TPU v7x, 32 devices: a whole 2x2x4 slice. The times are simulated.
32 devices in a mesh: ctx: 16 (over z, x, core), ch: 2 (over y).
Axes of the slice: x: 2, y: 2, z: 4, core: 2. Of those that a mesh axis runs over, the one named last changes fastest.
Arguments:
- q_in: bfloat16 [2048, 4096], P('ctx', 'ch'), may hold values from -6 to 6
- k_in: bfloat16 [2048, 4096], P('ctx', 'ch'), may hold values from -6 to 6
- v_in: bfloat16 [2048, 4096], P('ctx', 'ch'), may hold values from -6 to 6
- grad_out: bfloat16 [2048, 4096], P('ctx', 'ch'), may hold values from -30 to 30
- short_filter: float32 [3, 4096], P(None, 'ch'), may hold values from -3 to 3
- kernel: float32 [2048, 4096], P('ctx', 'ch'), may hold values from -0.125 to 0.125
- skip: float32 [4096], P('ch'), may hold values from -3 to 3
Outputs:
- mixed: bfloat16 [2048, 4096], P('ctx', 'ch')
- grad_q: bfloat16 [2048, 4096], P('ctx', 'ch')
- grad_k: bfloat16 [2048, 4096], P('ctx', 'ch')
- grad_v: bfloat16 [2048, 4096], P('ctx', 'ch')
- grad_short: float32 [3, 4096], P(None, 'ch')
- grad_skip: float32 [4096], P('ch')
- grad_kernel: float32 [2048, 4096], P('ctx', 'ch')
All inputs are finite; a program needn't handle non-finite values.
Results may differ from a plain program's by a relative error of at most 0.009.
Values may be sent and summed in bfloat16 or wider, within the bound.
No kernel may reach another device: no remote copies, remote signals or barrier semaphores. Data moves between devices by JAX's collectives and lax.ppermute only.
A program may use at most 128 MiB of HBM per device.

v0:
```python
import math

import jax
import jax.numpy as jnp
from jax import lax
from jax.sharding import PartitionSpec as P

highest = lax.Precision.HIGHEST


def shifted(shard, axis, by):
    size = lax.axis_size(axis)
    pairs = [(i, i + by) for i in range(size) if 0 <= i + by < size]
    return lax.ppermute(shard, axis, pairs)


def phase(left_idx, right_idx, period):
    product = left_idx[:, None] * right_idx[None, :] % period
    return product.astype(jnp.float32) * (2.0 * math.pi / period)


def forward_table(angle):
    cosine = jnp.cos(angle)
    sine = jnp.sin(angle)
    return jnp.stack([jnp.stack([cosine, sine]), jnp.stack([-sine, cosine])])


def inverse_table(angle):
    cosine = jnp.cos(angle)
    sine = jnp.sin(angle)
    return jnp.stack([jnp.stack([cosine, -sine]), jnp.stack([sine, cosine])])


def short_forward(extended, short_taps, rows_here):
    halo_rows = short_taps.shape[0] - 1
    result = short_taps[0] * extended[halo_rows : halo_rows + rows_here]
    for shift_idx in range(1, short_taps.shape[0]):
        result = (
            result
            + short_taps[shift_idx]
            * extended[halo_rows - shift_idx : halo_rows - shift_idx + rows_here]
        )
    return result


def short_backward(extended, short_taps, rows_here):
    result = short_taps[0] * extended[0:rows_here]
    for shift_idx in range(1, short_taps.shape[0]):
        result = result + short_taps[shift_idx] * extended[shift_idx : shift_idx + rows_here]
    return result


def spread_rows(signal, pieces):
    return lax.all_to_all(
        signal.reshape(pieces, signal.shape[0] // pieces, signal.shape[1]),
        "ctx",
        split_axis=0,
        concat_axis=0,
        tiled=True,
    )


def spectrum_tiles(section_in, here_idx, pieces):
    signals, _, slice_rows, channels = section_in.shape
    rows_here = pieces * slice_rows
    fft_len = 2 * pieces * rows_here
    outer_angle = phase(jnp.arange(2 * pieces), jnp.arange(pieces), 2 * pieces)
    outer_table = jnp.stack([jnp.cos(outer_angle), -jnp.sin(outer_angle)])
    part = jnp.einsum("pba,garc->pgbrc", outer_table, section_in, precision=highest)
    part_re = part[0]
    part_im = part[1]
    twist_angle = phase(
        jnp.arange(2 * pieces), here_idx * slice_rows + jnp.arange(slice_rows), fft_len
    )
    twist_cos = jnp.cos(twist_angle)[None, :, :, None]
    twist_sin = jnp.sin(twist_angle)[None, :, :, None]
    turn_re = part_re * twist_cos + part_im * twist_sin
    turn_im = part_im * twist_cos - part_re * twist_sin
    stacked = jnp.stack([turn_re, turn_im]).reshape(2, signals, pieces, 2, slice_rows, channels)
    arrived = lax.all_to_all(stacked, "ctx", split_axis=2, concat_axis=4, tiled=True).reshape(
        2, signals, 2, rows_here, channels
    )
    inner_angle = phase(jnp.arange(rows_here), jnp.arange(rows_here), rows_here)
    spec = jnp.einsum("pqer,qgjrc->pgjec", forward_table(inner_angle), arrived, precision=highest)
    return (spec[0], spec[1])


def rows_from_spectrum(spec_re, spec_im, here_idx, pieces):
    signals, _, rows_here, channels = spec_re.shape
    slice_rows = rows_here // pieces
    fft_len = 2 * pieces * rows_here
    inner_angle = phase(jnp.arange(rows_here), jnp.arange(rows_here), rows_here)
    part = jnp.einsum(
        "pqre,qgjec->pgjrc",
        inverse_table(inner_angle),
        jnp.stack([spec_re, spec_im]),
        precision=highest,
    )
    part_re = part[0]
    part_im = part[1]
    twist_angle = phase(2 * here_idx + jnp.arange(2), jnp.arange(rows_here), fft_len)
    twist_cos = jnp.cos(twist_angle)[None, :, :, None]
    twist_sin = jnp.sin(twist_angle)[None, :, :, None]
    turn_re = part_re * twist_cos - part_im * twist_sin
    turn_im = part_im * twist_cos + part_re * twist_sin
    stacked = jnp.stack([turn_re, turn_im]).reshape(2, signals, 2, pieces, slice_rows, channels)
    arrived = lax.all_to_all(stacked, "ctx", split_axis=3, concat_axis=2, tiled=True).reshape(
        2, signals, 2 * pieces, slice_rows, channels
    )
    outer_angle = phase(jnp.arange(pieces), jnp.arange(2 * pieces), 2 * pieces)
    outer_table = jnp.stack([jnp.cos(outer_angle), -jnp.sin(outer_angle)])
    time_rows = jnp.einsum("qab,qgbrc->garc", outer_table, arrived, precision=highest) / fft_len
    returned = lax.all_to_all(time_rows, "ctx", split_axis=1, concat_axis=1, tiled=True)
    return returned.reshape(signals, rows_here, channels)


def body(q_in, k_in, v_in, grad_out, short_filter, kernel, skip):
    pieces = lax.axis_size("ctx")
    here_idx = lax.axis_index("ctx")
    rows_here, channels = q_in.shape
    seq_len = pieces * rows_here
    halo_rows = short_filter.shape[0] - 1
    lead = shifted(
        (
            q_in[rows_here - halo_rows :],
            k_in[rows_here - halo_rows :],
            v_in[rows_here - halo_rows :],
        ),
        "ctx",
        1,
    )
    q_ext = jnp.concatenate([lead[0], q_in], axis=0).astype(jnp.float32)
    k_ext = jnp.concatenate([lead[1], k_in], axis=0).astype(jnp.float32)
    v_ext = jnp.concatenate([lead[2], v_in], axis=0).astype(jnp.float32)
    q_short = short_forward(q_ext, short_filter, rows_here)
    k_short = short_forward(k_ext, short_filter, rows_here)
    v_short = short_forward(v_ext, short_filter, rows_here)
    product = (k_short * v_short).astype(jnp.bfloat16)
    product_wide = product.astype(jnp.float32)
    slice_rows = rows_here // pieces
    kernel_tiles = lax.all_to_all(
        kernel.reshape(pieces, slice_rows, channels), "ctx", split_axis=0, concat_axis=0, tiled=True
    )
    product_tiles = spread_rows(product, pieces).astype(jnp.float32)
    spec_re, spec_im = spectrum_tiles(jnp.stack([product_tiles, kernel_tiles]), here_idx, pieces)
    signal_re = spec_re[0]
    signal_im = spec_im[0]
    kernel_re = spec_re[1]
    kernel_im = spec_im[1]
    conv_re = signal_re * kernel_re - signal_im * kernel_im
    conv_im = signal_re * kernel_im + signal_im * kernel_re
    conv = rows_from_spectrum(conv_re[None], conv_im[None], here_idx, pieces)[0]
    filtered = conv + skip[None, :] * product_wide
    mixed = (q_short * filtered).astype(jnp.bfloat16)
    upstream = grad_out.astype(jnp.float32)
    back_q = upstream * filtered
    back_mix = upstream * q_short
    back_cast = back_mix.astype(jnp.bfloat16)
    cotan_tiles = spread_rows(back_cast, pieces).astype(jnp.float32)
    cotan_re, cotan_im = spectrum_tiles(cotan_tiles[None], here_idx, pieces)
    grad_re = cotan_re[0]
    grad_im = cotan_im[0]
    corr_re = kernel_re * grad_re + kernel_im * grad_im
    corr_im = kernel_re * grad_im - kernel_im * grad_re
    lag_re = signal_re * grad_re + signal_im * grad_im
    lag_im = signal_re * grad_im - signal_im * grad_re
    returned = rows_from_spectrum(
        jnp.stack([corr_re, lag_re]), jnp.stack([corr_im, lag_im]), here_idx, pieces
    )
    correlate = returned[0]
    kernel_grad = returned[1]
    back_prod = correlate + skip[None, :] * back_mix
    back_k = back_prod * v_short
    back_v = back_prod * k_short
    tail = shifted((back_q[:halo_rows], back_k[:halo_rows], back_v[:halo_rows]), "ctx", -1)
    grad_q = short_backward(
        jnp.concatenate([back_q, tail[0]], axis=0), short_filter, rows_here
    ).astype(jnp.bfloat16)
    grad_k = short_backward(
        jnp.concatenate([back_k, tail[1]], axis=0), short_filter, rows_here
    ).astype(jnp.bfloat16)
    grad_v = short_backward(
        jnp.concatenate([back_v, tail[2]], axis=0), short_filter, rows_here
    ).astype(jnp.bfloat16)
    tap_rows = []
    for shift_idx in range(short_filter.shape[0]):
        first = halo_rows - shift_idx
        tap_rows.append(
            jnp.sum(
                back_q * q_ext[first : first + rows_here]
                + back_k * k_ext[first : first + rows_here]
                + back_v * v_ext[first : first + rows_here],
                axis=0,
            )
        )
    short_grad = jnp.stack(tap_rows)
    skip_grad = jnp.sum(back_mix * product_wide, axis=0)
    kernel_square = jnp.sum(kernel_grad * kernel_grad)
    summed = lax.psum((short_grad, skip_grad, kernel_square), "ctx")
    local_square = jnp.sum(summed[0] * summed[0]) + jnp.sum(summed[1] * summed[1]) + summed[2]
    norm_sq = lax.psum(local_square, "ch")
    clip_limit = math.sqrt(float(seq_len * channels * lax.axis_size("ch")))
    factor = clip_limit / jnp.maximum(jnp.sqrt(norm_sq), clip_limit)
    return (
        mixed,
        grad_q,
        grad_k,
        grad_v,
        factor * summed[0],
        factor * summed[1],
        factor * kernel_grad,
    )


def solution(mesh):
    in_specs = (
        P("ctx", "ch"),
        P("ctx", "ch"),
        P("ctx", "ch"),
        P("ctx", "ch"),
        P(None, "ch"),
        P("ctx", "ch"),
        P("ch"),
    )
    out_specs = (
        P("ctx", "ch"),
        P("ctx", "ch"),
        P("ctx", "ch"),
        P("ctx", "ch"),
        P(None, "ch"),
        P("ch"),
        P("ctx", "ch"),
    )
    return jax.shard_map(body, mesh=mesh, in_specs=in_specs, out_specs=out_specs, check_vma=False)
```

profile of v0, /device:TPU:0, one launch (start us, length us, event | category | flops | bytes accessed | tf_op | source)
XLA Modules:
  0.0 877.3 jit_solution(11594147346714436012)
XLA Ops:
  1.5 2.4 collective-permute-start.2
  4.6 4.5 collective-permute-start.1
  9.9 1.9 collective-permute-start
  12.7 1.2 maximum_convert_fusion
  14.0 1.2 maximum_convert_fusion.1
  15.2 1.2 maximum_convert_fusion.2
  16.4 2.6 fusion.49
  19.0 8.1 all-to-all-start
  27.1 2.3 convert_bitcast_fusion
  29.3 12.3 %all-to-all-done = bf16[16,8,2048]{2,1,0:T(8,128)(2,1)} async-done(((bf16[16,8,2048]{2,1,0:T(8,128)(2,1)}), bf16[16,8,2048]{2,1,0:T(8,128)(2,1)}, u32[]{:S(2)}, u32[]{:S(2)}) %all-to-all-start) | async-done | bytes 524320 | tf_op jit(solution)/shard_map/all_to_all | solution.py:54
  41.6 18.7 %all_to_all.85 = bf16[16,8,2048]{2,1,0:T(8,128)(2,1)} all-to-all(bf16[16,8,2048]{2,1,0:T(8,128)(2,1)} %convert_bitcast_fusion), channel_id=1, replica_groups=mesh['ctx'=16,'ch'=2] {'ctx'}, dimensions={0} | all-to-all | bytes 1048576 | tf_op jit(solution)/shard_map/all_to_all | solution.py:54
  60.3 4.4 all-to-all-start.1
  64.8 3.5 convolution_bitcast_fusion.1
  69.3 1.2 copy.110
  70.5 1.2 copy.111
  71.7 2.3 pad_maximum_fusion.3
  74.0 13.6 %all-to-all-done.1 = f32[16,8,2048]{2,1,0:T(8,128)} async-done(((f32[16,8,2048]{2,1,0:T(8,128)}), f32[16,8,2048]{2,1,0:T(8,128)}, u32[]{:S(2)}, u32[]{:S(2)}) %all-to-all-start.1) | async-done | bytes 1048608 | tf_op jit(solution)/shard_map/all_to_all | solution.py:141
  87.6 7.1 all-to-all-start.6
  94.7 1.4 bitcast_convert_fusion
  96.0 1.8 copy.148
  97.9 10.9 %convolution_bitcast_fusion = f32[2,2,32,8,2048]{4,2,0,3,1:T(8,128)S(1)} fusion(f32[1,16,8,2048]{3,1,2,0:T(8,128)S(1)} %bitcast.270, f32[1,16,8,2048]{3,1,2,0:T(8,128)S(1)} %bitcast_convert_fusion, f32[1,32,16]{1,2,0:T(8,128)S(1)} %get-tuple-element.50, f32[1,32,16]{1,2,0:T(8,128)S(1)} %get-tuple-element.51), kind=kOutput, calls=%fused_computation.10 | convolution fusion | flops 403178496 | bytes 10489856 | tf_op jit(solution)/shard_map/pba,garc->pgbrc/dot_general | solution.py:69
  108.8 4.5 multiply_add_fusion
  113.3 6.2 stack.159
  119.5 7.9 copy.56
  127.4 5.9 stack.160
  133.3 6.1 copy.57
  139.5 3.9 pad_maximum_fusion
  143.4 29.0 %all-to-all-done.6 = f32[2,1,16,2,8,2048]{5,4,3,0,1,2:T(8,128)} async-done(((f32[2,1,16,2,8,2048]{5,4,3,0,1,2:T(8,128)}), f32[2,1,16,2,8,2048]{5,4,3,0,1,2:T(8,128)}, u32[]{:S(2)}, u32[]{:S(2)}) %all-to-all-start.6) | async-done | bytes 4194336 | tf_op jit(solution)/shard_map/all_to_all | solution.py:80
  172.3 20.2 %all-to-all-start.2 = ((f32[2,2,16,2,8,2048]{5,4,3,1,0,2:T(8,128)}), f32[2,2,16,2,8,2048]{5,4,3,1,0,2:T(8,128)}, u32[]{:S(2)}, u32[]{:S(2)}) async-start(f32[2,2,16,2,8,2048]{5,4,3,1,0,2:T(8,128)} %pad_maximum_fusion), calls=%async_computation.2 | async-start | bytes 16777216 | tf_op jit(solution)/shard_map/all_to_all | solution.py:80
  194.5 9.9 %fusion.18 = f32[2,1,2,128,2048]{3,4,2,1,0:T(8,128)} fusion(f32[2,1,16,2,8,2048]{5,4,3,0,1,2:T(8,128)} %all-to-all-done.6, f32[1,2,128,128]{3,2,1,0:T(8,128)S(1)} %get-tuple-element.35, f32[1,2,128,128]{3,2,1,0:T(8,128)S(1)} %get-tuple-element.38), kind=kOutput, calls=%fused_computation.26 | convolution fusion | flops 3221291008 | bytes 8650752 | tf_op jit(solution)/shard_map/pqer,qgjrc->pgjec/dot_general | solution.py:84
  204.4 138.8 %all-to-all-done.2 = f32[2,2,16,2,8,2048]{5,4,3,1,0,2:T(8,128)} async-done(((f32[2,2,16,2,8,2048]{5,4,3,1,0,2:T(8,128)}), f32[2,2,16,2,8,2048]{5,4,3,1,0,2:T(8,128)}, u32[]{:S(2)}, u32[]{:S(2)}) %all-to-all-start.2) | async-done | bytes 8388640 | tf_op jit(solution)/shard_map/all_to_all | solution.py:80
  343.2 15.6 %fusion.4 = f32[2,2,2,128,2048]{3,4,0,2,1:T(8,128)S(1)} fusion(f32[1,2,128,128]{3,2,1,0:T(8,128)S(1)} %get-tuple-element.35, f32[1,2,128,128]{3,2,1,0:T(8,128)} %copy-done.14, f32[2,2,16,2,8,2048]{5,4,3,1,0,2:T(8,128)} %all-to-all-done.2), kind=kOutput, calls=%fused_computation.8 | convolution fusion | flops 6442516480 | bytes 17039360 | tf_op jit(solution)/shard_map/pqer,qgjrc->pgjec/dot_general | solution.py:84
  359.2 2.9 copy-done
  362.1 6.0 fusion.32
  368.1 5.5 fusion.15
  375.0 2.3 copy.107
  377.3 36.8 %all-to-all-start.3 = ((f32[2,1,2,16,8,2048]{5,4,2,1,0,3:T(8,128)}), f32[2,1,2,16,8,2048]{5,4,2,1,0,3:T(8,128)}, u32[]{:S(2)}, u32[]{:S(2)}) async-start(f32[2,1,2,16,8,2048]{5,4,2,1,0,3:T(8,128)} %copy.107), calls=%async_computation.3 | async-start | bytes 8388608 | tf_op jit(solution)/shard_map/all_to_all | solution.py:107
  414.0 2.6 maximum_bitcast_fusion.2
  417.5 3.0 fusion.28
  421.4 8.5 fusion.7
  429.9 2.1 subtract_bitcast_fusion
  432.0 1.1 pad_maximum_fusion.1
  433.1 3.8 copy.117
  436.9 54.8 %all-to-all-done.3 = f32[2,1,2,16,8,2048]{5,4,2,1,0,3:T(8,128)} async-done(((f32[2,1,2,16,8,2048]{5,4,2,1,0,3:T(8,128)}), f32[2,1,2,16,8,2048]{5,4,2,1,0,3:T(8,128)}, u32[]{:S(2)}, u32[]{:S(2)}) %all-to-all-start.3) | async-done | bytes 4194336 | tf_op jit(solution)/shard_map/all_to_all | solution.py:107
  491.7 20.0 %all-to-all-start.7 = ((f32[2,2,2,16,8,2048]{5,4,2,1,0,3:T(8,128)}), f32[2,2,2,16,8,2048]{5,4,2,1,0,3:T(8,128)}, u32[]{:S(2)}, u32[]{:S(2)}) async-start(f32[2,2,2,16,8,2048]{5,4,2,1,0,3:T(8,128)} %copy.117), calls=%async_computation.7 | async-start | bytes 16777216 | tf_op jit(solution)/shard_map/all_to_all | solution.py:107
  511.7 7.5 copy.68
  519.1 6.0 reshape.562
  525.2 4.0 fusion.24
  529.2 1.6 copy.69
  530.8 131.5 %all-to-all-done.7 = f32[2,2,2,16,8,2048]{5,4,2,1,0,3:T(8,128)} async-done(((f32[2,2,2,16,8,2048]{5,4,2,1,0,3:T(8,128)}), f32[2,2,2,16,8,2048]{5,4,2,1,0,3:T(8,128)}, u32[]{:S(2)}, u32[]{:S(2)}) %all-to-all-start.7) | async-done | bytes 8388640 | tf_op jit(solution)/shard_map/all_to_all | solution.py:107
  662.3 36.8 %all-to-all-start.4 = ((f32[1,16,8,2048]{3,2,0,1:T(8,128)}), f32[1,16,8,2048]{3,2,0,1:T(8,128)}, u32[]{:S(2)}, u32[]{:S(2)}) async-start(f32[1,16,8,2048]{3,2,0,1:T(8,128)} %copy.69), calls=%async_computation.4 | async-start | bytes 2097152 | tf_op jit(solution)/shard_map/all_to_all | solution.py:113
  699.2 15.5 %copy.82 = f32[2,2,16,2,1,8,2048]{6,3,2,0,5,1,4:T(2,128)} copy(f32[2,2,16,2,1,8,2048]{6,5,3,1,0,2,4:T(8,128)} %bitcast.83) | data formatting | bytes 16777216 | tf_op jit(solution)/shard_map/all_to_all | solution.py:107
  714.7 11.0 %reshape.565 = f32[2,2,32,8,2048]{4,2,0,3,1:T(8,128)} reshape(f32[2,2,16,2,1,8,2048]{6,3,2,0,5,1,4:T(2,128)} %copy.82) | data formatting | bytes 16777216 | tf_op jit(solution)/shard_map/reshape | solution.py:107
  725.7 6.8 fusion.22
  732.5 2.6 copy.83
  735.1 53.7 %all_to_all.86 = f32[2,16,8,2048]{3,2,0,1:T(8,128)S(1)} all-to-all(f32[2,16,8,2048]{3,2,0,1:T(8,128)} %copy.83), channel_id=1, replica_groups=mesh['ctx'=16,'ch'=2] {'ctx'}, dimensions={1} | all-to-all | bytes 4194304 | tf_op jit(solution)/shard_map/all_to_all | solution.py:113
  788.8 4.2 add_reduce_fusion.2
  794.0 61.4 %all-reduce = (f32[3,2048]{1,0:T(4,128)S(1)}, f32[2048]{0:T(1024)S(1)}, f32[]{:T(128)}) all-reduce(f32[3,2048]{1,0:T(4,128)S(1)} %pad_maximum_fusion.17, f32[2048]{0:T(1024)S(1)} %get-tuple-element.13, f32[]{:T(128)} %multiply_reduce_fusion), channel_id=1, replica_groups=mesh['ctx'=16,'ch'=2] {'ctx'}, use_global_device_ids=true, to_apply=%region_3.4 | all-reduce | flops 8193 | bytes 65544 | tf_op jit(solution)/shard_map/psum | solution.py:199
  858.5 5.4 psum.31
  867.9 1.3 collective-permute-start.3
  869.1 1.3 collective-permute-start.4
  870.4 1.3 collective-permute-start.5
  871.7 2.3 multiply_bitcast_fusion
  874.8 2.0 fusion.37
  (71 shorter events, 15.9 us)
Async XLA Ops:
  0.6 15.7 %copy-start.7 = (bf16[128,2048]{1,0:T(8,128)(2,1)S(1)}, bf16[128,2048]{1,0:T(8,128)(2,1)}, u32[]{:S(2)}) copy-start(bf16[128,2048]{1,0:T(8,128)(2,1)} %param.10) | copy-start | bytes 1572868
  1.5 13.7 %collective-permute-start.2 = (bf16[2,2048]{1,0:T(2,128)(2,1)S(1)}, bf16[2,2048]{1,0:T(2,128)(2,1)S(1)}, u32[]{:S(2)}, u32[]{:S(2)}) collective-permute-start(bf16[2,2048]{1,0:T(2,128)(2,1)S(1)} %slice.167), channel_id=1, source_target_pairs={{0,2},{2,4},{4,6},{6,8},{8,10},{10,12},{12,14},{14,16},{16,18},{18... | collective-permute-start | bytes 24584 | tf_op jit(solution)/shard_map/ppermute | solution.py:14
  4.6 9.3 %collective-permute-start.1 = (bf16[2,2048]{1,0:T(2,128)(2,1)S(1)}, bf16[2,2048]{1,0:T(2,128)(2,1)S(1)}, u32[]{:S(2)}, u32[]{:S(2)}) collective-permute-start(bf16[2,2048]{1,0:T(2,128)(2,1)S(1)} %slice.163), channel_id=1, source_target_pairs={{0,2},{2,4},{4,6},{6,8},{8,10},{10,12},{12,14},{14,16},{16,18},{18... | collective-permute-start | bytes 24584 | tf_op jit(solution)/shard_map/ppermute | solution.py:14
  9.9 2.8 collective-permute-start
  19.0 22.6 %all-to-all-start = ((bf16[16,8,2048]{2,1,0:T(8,128)(2,1)}), bf16[16,8,2048]{2,1,0:T(8,128)(2,1)}, u32[]{:S(2)}, u32[]{:S(2)}) async-start(bf16[16,8,2048]{2,1,0:T(8,128)(2,1)} %bitcast.269), calls=%async_computation | async-start | bytes 1048576 | tf_op jit(solution)/shard_map/all_to_all | solution.py:54
  60.3 27.3 %all-to-all-start.1 = ((f32[16,8,2048]{2,1,0:T(8,128)}), f32[16,8,2048]{2,1,0:T(8,128)}, u32[]{:S(2)}, u32[]{:S(2)}) async-start(f32[16,8,2048]{2,1,0:T(8,128)} %bitcast.272), calls=%async_computation.1 | async-start | bytes 2097152 | tf_op jit(solution)/shard_map/all_to_all | solution.py:141
  87.6 84.7 %all-to-all-start.6 = ((f32[2,1,16,2,8,2048]{5,4,3,0,1,2:T(8,128)}), f32[2,1,16,2,8,2048]{5,4,3,0,1,2:T(8,128)}, u32[]{:S(2)}, u32[]{:S(2)}) async-start(f32[2,1,16,2,8,2048]{5,4,3,0,1,2:T(8,128)} %pad_maximum_fusion.3), calls=%async_computation.6 | async-start | bytes 8388608 | tf_op jit(solution)/shard_map/all_to_all | solution.py:80
  133.3 6.2 copy-start.2
  172.3 170.9 %all-to-all-start.2 = ((f32[2,2,16,2,8,2048]{5,4,3,1,0,2:T(8,128)}), f32[2,2,16,2,8,2048]{5,4,3,1,0,2:T(8,128)}, u32[]{:S(2)}, u32[]{:S(2)}) async-start(f32[2,2,16,2,8,2048]{5,4,3,1,0,2:T(8,128)} %pad_maximum_fusion), calls=%async_computation.2 | async-start | bytes 16777216 | tf_op jit(solution)/shard_map/all_to_all | solution.py:80
  193.8 0.7 copy-start.14
  358.8 3.3 copy-start
  362.1 6.0 copy-start.15
  362.1 6.0 copy-start.16
  377.3 114.4 %all-to-all-start.3 = ((f32[2,1,2,16,8,2048]{5,4,2,1,0,3:T(8,128)}), f32[2,1,2,16,8,2048]{5,4,2,1,0,3:T(8,128)}, u32[]{:S(2)}, u32[]{:S(2)}) async-start(f32[2,1,2,16,8,2048]{5,4,2,1,0,3:T(8,128)} %copy.107), calls=%async_computation.3 | async-start | bytes 8388608 | tf_op jit(solution)/shard_map/all_to_all | solution.py:107
  414.0 3.5 copy-start.1
  417.5 3.0 copy-start.5
  420.5 0.9 copy-start.17
  491.7 170.6 %all-to-all-start.7 = ((f32[2,2,2,16,8,2048]{5,4,2,1,0,3:T(8,128)}), f32[2,2,2,16,8,2048]{5,4,2,1,0,3:T(8,128)}, u32[]{:S(2)}, u32[]{:S(2)}) async-start(f32[2,2,2,16,8,2048]{5,4,2,1,0,3:T(8,128)} %copy.117), calls=%async_computation.7 | async-start | bytes 16777216 | tf_op jit(solution)/shard_map/all_to_all | solution.py:107
  662.3 72.8 %all-to-all-start.4 = ((f32[1,16,8,2048]{3,2,0,1:T(8,128)}), f32[1,16,8,2048]{3,2,0,1:T(8,128)}, u32[]{:S(2)}, u32[]{:S(2)}) async-start(f32[1,16,8,2048]{3,2,0,1:T(8,128)} %copy.69), calls=%async_computation.4 | async-start | bytes 2097152 | tf_op jit(solution)/shard_map/all_to_all | solution.py:113
  732.5 56.3 %copy-start.18 = (f32[2048]{0:T(1024)S(1)}, f32[2048]{0:T(1024)}, u32[]{:S(2)}) copy-start(f32[2048]{0:T(1024)} %param.13) | copy-start | bytes 24580
  735.1 53.7 %copy-start.4 = (f32[128,2048]{1,0:T(8,128)S(1)}, f32[128,2048]{1,0:T(8,128)}, u32[]{:S(2)}) copy-start(f32[128,2048]{1,0:T(8,128)} %get-tuple-element.17) | copy-start | bytes 3145732
  735.1 53.7 %copy-start.6 = (bf16[128,2048]{1,0:T(8,128)(2,1)S(1)}, bf16[128,2048]{1,0:T(8,128)(2,1)}, u32[]{:S(2)}) copy-start(bf16[128,2048]{1,0:T(8,128)(2,1)} %get-tuple-element.14) | copy-start | bytes 1572868
  735.1 53.7 %copy-start.8 = (bf16[128,2048]{1,0:T(8,128)(2,1)S(1)}, bf16[128,2048]{1,0:T(8,128)(2,1)}, u32[]{:S(2)}) copy-start(bf16[128,2048]{1,0:T(8,128)(2,1)} %param.10) | copy-start | bytes 1572868
  735.1 53.7 %copy-start.12 = (f32[128,2048]{1,0:T(8,128)S(1)}, f32[128,2048]{1,0:T(8,128)}, u32[]{:S(2)}) copy-start(f32[128,2048]{1,0:T(8,128)} %get-tuple-element.15) | copy-start | bytes 3145732
  735.1 53.7 %copy-start.13 = (f32[128,2048]{1,0:T(8,128)S(1)}, f32[128,2048]{1,0:T(8,128)}, u32[]{:S(2)}) copy-start(f32[128,2048]{1,0:T(8,128)} %get-tuple-element.16) | copy-start | bytes 3145732
  788.8 4.3 copy-start.3
  793.1 81.7 %copy-start.9 = (f32[128,2048]{1,0:T(8,128)S(1)}, f32[128,2048]{1,0:T(8,128)}, u32[]{:S(2)}) copy-start(f32[128,2048]{1,0:T(8,128)} %get-tuple-element.18) | copy-start | bytes 3145732
  793.1 81.7 %copy-start.10 = (f32[128,2048]{1,0:T(8,128)S(1)}, f32[128,2048]{1,0:T(8,128)}, u32[]{:S(2)}) copy-start(f32[128,2048]{1,0:T(8,128)} %get-tuple-element.19) | copy-start | bytes 3145732
  793.1 81.7 %copy-start.11 = (f32[128,2048]{1,0:T(8,128)S(1)}, f32[128,2048]{1,0:T(8,128)}, u32[]{:S(2)}) copy-start(f32[128,2048]{1,0:T(8,128)} %get-tuple-element.20) | copy-start | bytes 3145732
  867.9 6.8 collective-permute-start.3
  869.1 5.5 collective-permute-start.4
  870.4 4.3 collective-permute-start.5
where the time goes:
time: 888 us; the launch traced here: 877 us
  waiting for transfers between devices  380 us (43%)
  starting transfers between devices  146 us (16%)
  blocking collectives  139 us (16%)
  local copies, waits for them, and re-layouts  91.4 us (10%)
  matrix products  64.8 us (7%)
  other arithmetic  51.7 us (6%)
    all_to_all x2, waiting for transfers between devices, rows_from_spectrum(): lax.all_to_all(stacked, 'ctx', split_axis=3, concat_axis=2, tiled=True)  186 us
    all_to_all x2, waiting for transfers between devices, spectrum_tiles(): lax.all_to_all(stacked, 'ctx', split_axis=2, concat_axis=4, tiled=True)  168 us
    psum x1, blocking collectives, body(): summed = lax.psum((short_grad, skip_grad, kernel_square), 'ctx')  61.4 us
    all_to_all x2, starting transfers between devices, rows_from_spectrum(): lax.all_to_all(stacked, 'ctx', split_axis=3, concat_axis=2, tiled=True)  56.7 us
    all_to_all x1, blocking collectives, rows_from_spectrum(): lax.all_to_all(time_rows, 'ctx', split_axis=1, concat_axis=1, tiled=True)  53.7 us
    all_to_all x1, starting transfers between devices, rows_from_spectrum(): lax.all_to_all(time_rows, 'ctx', split_axis=1, concat_axis=1, tiled=True)  36.8 us
    another operation x6, local copies, waits for them, and re-layouts, spectrum_tiles(): jnp.stack([turn_re, turn_im])  28.6 us
    all_to_all x2, starting transfers between devices, spectrum_tiles(): lax.all_to_all(stacked, 'ctx', split_axis=2, concat_axis=4, tiled=True)  27.3 us
  transfers between devices with their start and end apart: 13, of which 7 were waited for; matrix products, arithmetic and copies ran while one was open for 18% of the time, Pallas kernels for 0%

commit v1 on v0

v1 whole, which is shorter than its diff:
```python
import math

import jax
import jax.numpy as jnp
import ml_dtypes
import numpy as np
from jax import lax
from jax.experimental import pallas as pl
from jax.experimental.pallas import tpu as pltpu
from jax.sharding import PartitionSpec as P

LANES = 128
SPAN = 256
CHUNK = 16
PAD = 8
VMEM_BYTES = 40 * 1024 * 1024

f32 = jnp.float32
bf16 = jnp.bfloat16


def leaf_phases(count, phase=0.25):
    if count == 1:
        return [phase]
    return leaf_phases(count // 2, phase / 2) + leaf_phases(count // 2, phase / 2 + 0.5)


def turn(re, im, phase):
    cosine = math.cos(2.0 * math.pi * phase)
    sine = math.sin(2.0 * math.pi * phase)
    if im is None:
        return re * cosine, re * (-sine)
    return re * cosine + im * sine, im * cosine - re * sine


def to_leaves(parts, phase=0.25):
    count = len(parts)
    if count == 1:
        return parts
    half = count // 2
    first = []
    second = []
    for low, high in zip(parts[:half], parts[half:]):
        high_re, high_im = turn(high[0], high[1], phase / 2)
        first.append((low[0] + high_re, high_im if low[1] is None else low[1] + high_im))
        second.append((low[0] - high_re, -high_im if low[1] is None else low[1] - high_im))
    return to_leaves(first, phase / 2) + to_leaves(second, phase / 2 + 0.5)


def from_leaves(leaves, phase=0.25, real_only=True):
    count = len(leaves)
    if count == 1:
        return leaves
    half = count // 2
    first = from_leaves(leaves[:half], phase / 2, False)
    second = from_leaves(leaves[half:], phase / 2 + 0.5, False)
    cosine = math.cos(math.pi * phase)
    sine = math.sin(math.pi * phase)
    low = []
    high = []
    for one, two in zip(first, second):
        diff_re = one[0] - two[0]
        diff_im = one[1] - two[1]
        if real_only:
            low.append((one[0] + two[0], None))
            high.append((diff_re * cosine - diff_im * sine, None))
        else:
            low.append((one[0] + two[0], one[1] + two[1]))
            high.append((diff_re * cosine - diff_im * sine, diff_im * cosine + diff_re * sine))
    return low + high


def dft_matrix():
    idx = np.arange(SPAN)
    angle = (idx[:, None] * idx[None, :] % SPAN) * (2.0 * np.pi / SPAN)
    cosine, sine = np.cos(angle), np.sin(angle)
    return np.block([[cosine, sine], [-sine, cosine]])


def twist_table(outer):
    angle = np.asarray(leaf_phases(outer))[:, None] * np.arange(SPAN)[None, :] * (2.0 * np.pi / SPAN)
    return np.stack([np.cos(angle), np.sin(angle)])


def halves(matrix):
    high = matrix.astype(ml_dtypes.bfloat16)
    low = (matrix - high.astype(np.float64)).astype(ml_dtypes.bfloat16)
    return np.concatenate([high, high, low], axis=1)


def split_store(ref, rows, lanes, value):
    high = value.astype(bf16)
    ref[pl.ds(rows, CHUNK), lanes] = high
    ref[pl.ds(2 * SPAN + rows, CHUNK), lanes] = (value - high.astype(f32)).astype(bf16)


def wide_dot(matrix_ref, split_ref, result_ref):
    split = 4 * SPAN
    width = 2 * LANES
    for start in range(0, result_ref.shape[1], width):
        lanes = slice(start, start + width)
        result_ref[:, lanes] = jnp.dot(
            matrix_ref[:, :split], split_ref[:, lanes], preferred_element_type=f32
        ) + jnp.dot(matrix_ref[:, split:], split_ref[: 2 * SPAN, lanes], preferred_element_type=f32)


def signal_spectrum(signal_ref, twist_ref, forward_ref, split_ref, spec_ref):
    outer = signal_ref.shape[0]

    def step(idx, carry):
        row = pl.multiple_of(idx * CHUNK, CHUNK)
        here = pl.ds(row, CHUNK)
        leaves = to_leaves([(signal_ref[part, here, :].astype(f32), None) for part in range(outer)])
        for leaf, (re, im) in enumerate(leaves):
            cosine = twist_ref[0, leaf, here, :]
            sine = twist_ref[1, leaf, here, :]
            lanes = slice(leaf * LANES, (leaf + 1) * LANES)
            split_store(split_ref, row, lanes, re * cosine + im * sine)
            split_store(split_ref, SPAN + row, lanes, im * cosine - re * sine)
        return carry

    lax.fori_loop(0, SPAN // CHUNK, step, 0)
    wide_dot(forward_ref, split_ref, spec_ref)


def combine(left_ref, right_ref, split_ref, conjugate):
    def step(idx, carry):
        row = pl.multiple_of(idx * CHUNK, CHUNK)
        for start in range(0, left_ref.shape[1], LANES):
            lanes = slice(start, start + LANES)
            left_re = left_ref[pl.ds(row, CHUNK), lanes]
            left_im = left_ref[pl.ds(SPAN + row, CHUNK), lanes]
            right_re = right_ref[pl.ds(row, CHUNK), lanes]
            right_im = right_ref[pl.ds(SPAN + row, CHUNK), lanes]
            if conjugate:
                re = left_re * right_re + left_im * right_im
                im = left_re * right_im - left_im * right_re
            else:
                re = left_re * right_re - left_im * right_im
                im = left_re * right_im + left_im * right_re
            split_store(split_ref, row, lanes, re)
            split_store(split_ref, SPAN + row, lanes, im)
        return carry

    lax.fori_loop(0, SPAN // CHUNK, step, 0)


def spectrum_signal(split_ref, inverse_ref, twist_ref, time_ref, signal_ref, square_ref=None):
    outer = signal_ref.shape[0]
    wide_dot(inverse_ref, split_ref, time_ref)

    def step(idx, carry):
        row = pl.multiple_of(idx * CHUNK, CHUNK)
        here = pl.ds(row, CHUNK)
        leaves = []
        for leaf in range(outer):
            cosine = twist_ref[0, leaf, here, :]
            sine = twist_ref[1, leaf, here, :]
            lanes = slice(leaf * LANES, (leaf + 1) * LANES)
            re = time_ref[here, lanes]
            im = time_ref[pl.ds(SPAN + row, CHUNK), lanes]
            leaves.append((re * cosine - im * sine, im * cosine + re * sine))
        parts = from_leaves(leaves)
        for part in range(outer):
            signal_ref[part, here, :] = parts[part][0].astype(bf16)
            if square_ref is not None:
                carry = carry + parts[part][0] * parts[part][0]
        return carry

    total = lax.fori_loop(0, SPAN // CHUNK, step, jnp.zeros((CHUNK, LANES), f32))
    if square_ref is not None:
        square_ref[...] = total


def filter_kernel(filter_ref, twist_ref, forward_ref, spec_ref, split_ref):
    signal_spectrum(filter_ref, twist_ref, forward_ref, split_ref, spec_ref)


def conv_kernel(
    product_ref, filter_spec_ref, twist_ref, forward_ref, inverse_ref,
    conv_ref, product_spec_ref, split_ref, time_ref,
):
    signal_spectrum(product_ref, twist_ref, forward_ref, split_ref, product_spec_ref)
    combine(filter_spec_ref, product_spec_ref, split_ref, False)
    spectrum_signal(split_ref, inverse_ref, twist_ref, time_ref, conv_ref)


def corr_kernel(
    cotan_ref, filter_spec_ref, product_spec_ref, twist_ref, forward_ref, inverse_ref,
    corr_ref, lag_ref, square_ref, cotan_spec_ref, split_ref, time_ref,
):
    signal_spectrum(cotan_ref, twist_ref, forward_ref, split_ref, cotan_spec_ref)
    combine(filter_spec_ref, cotan_spec_ref, split_ref, True)
    spectrum_signal(split_ref, inverse_ref, twist_ref, time_ref, corr_ref)
    combine(product_spec_ref, cotan_spec_ref, split_ref, True)
    spectrum_signal(split_ref, inverse_ref, twist_ref, time_ref, lag_ref, square_ref)


def call(kernel, outs, scratch, *args, **options):
    return pl.pallas_call(
        kernel,
        out_shape=outs,
        scratch_shapes=scratch,
        compiler_params=pltpu.CompilerParams(vmem_limit_bytes=VMEM_BYTES),
        **options,
    )(*args)


class Transforms:
    def __init__(self, seq_len):
        self.outer = seq_len // SPAN
        matrix = dft_matrix()
        self.forward = jnp.asarray(halves(matrix))
        self.inverse = jnp.asarray(halves(matrix.T / seq_len))
        twist = twist_table(self.outer).astype(np.float32)[..., None]
        self.twist = jnp.broadcast_to(jnp.asarray(twist), twist.shape[:3] + (LANES,))
        self.spec = jax.ShapeDtypeStruct((2 * SPAN, self.outer * LANES), f32)
        self.time = jax.ShapeDtypeStruct((self.outer, SPAN, LANES), bf16)
        self.square = jax.ShapeDtypeStruct((CHUNK, LANES), f32)
        self.split = pltpu.VMEM((4 * SPAN, self.outer * LANES), bf16)
        self.work = pltpu.VMEM(self.spec.shape, f32)

    def filter(self, kernel):
        return call(
            filter_kernel, self.spec, [self.split],
            kernel.reshape(self.time.shape), self.twist, self.forward,
        )

    def conv(self, product, filter_spec):
        return call(
            conv_kernel, (self.time, self.spec), [self.split, self.work],
            product.reshape(self.time.shape), filter_spec, self.twist, self.forward, self.inverse,
        )

    def corr(self, cotan, filter_spec, product_spec):
        return call(
            corr_kernel, (self.time, self.time, self.square), [self.work, self.split, self.work],
            cotan.reshape(self.time.shape), filter_spec, product_spec,
            self.twist, self.forward, self.inverse,
        )


class PlainTransforms:
    def __init__(self, seq_len):
        self.seq_len = seq_len
        self.outer = seq_len // SPAN
        idx = np.arange(SPAN)
        angle = (idx[:, None] * idx[None, :] % SPAN) * (2.0 * np.pi / SPAN)
        self.cosine = jnp.asarray(np.cos(angle), f32)
        self.sine = jnp.asarray(np.sin(angle), f32)
        self.twist = jnp.asarray(twist_table(self.outer), f32)[..., None]

    def dot(self, matrix, signal):
        return jnp.einsum("fs,tsc->tfc", matrix, signal, precision=lax.Precision.HIGHEST)

    def filter(self, signal):
        parts = signal.astype(f32).reshape(self.outer, SPAN, -1)
        leaves = to_leaves([(parts[part], None) for part in range(self.outer)])
        re = jnp.stack([leaf[0] for leaf in leaves])
        im = jnp.stack([leaf[1] for leaf in leaves])
        twist_re = re * self.twist[0] + im * self.twist[1]
        twist_im = im * self.twist[0] - re * self.twist[1]
        return (
            self.dot(self.cosine, twist_re) + self.dot(self.sine, twist_im),
            self.dot(self.cosine, twist_im) - self.dot(self.sine, twist_re),
        )

    def back(self, re, im):
        time_re = self.dot(self.cosine, re) - self.dot(self.sine, im)
        time_im = self.dot(self.cosine, im) + self.dot(self.sine, re)
        leaf_re = time_re * self.twist[0] - time_im * self.twist[1]
        leaf_im = time_im * self.twist[0] + time_re * self.twist[1]
        parts = from_leaves([(leaf_re[leaf], leaf_im[leaf]) for leaf in range(self.outer)])
        return jnp.stack([part[0] for part in parts]) * (1.0 / self.seq_len)

    def conv(self, product, filter_spec):
        spec = self.filter(product)
        re = filter_spec[0] * spec[0] - filter_spec[1] * spec[1]
        im = filter_spec[0] * spec[1] + filter_spec[1] * spec[0]
        return self.back(re, im).astype(bf16), spec

    def corr(self, cotan, filter_spec, product_spec):
        spec = self.filter(cotan)
        results = []
        for other in (filter_spec, product_spec):
            re = other[0] * spec[0] + other[1] * spec[1]
            im = other[0] * spec[1] - other[1] * spec[0]
            results.append(self.back(re, im))
        squares = jnp.sum(results[1] * results[1], axis=(0, 1))[None, :]
        return results[0].astype(bf16), results[1].astype(bf16), squares


def group(idx):
    return slice(idx * LANES, (idx + 1) * LANES)


def pack_kernel(wide_ref, packed_ref):
    for idx in range(packed_ref.shape[0]):
        packed_ref[idx] = wide_ref[:, group(idx)].astype(packed_ref.dtype)


def extend_rows(lead, rows, ext_ref):
    halo_rows = lead.shape[0]
    ext_ref[PAD - halo_rows : PAD, :] = lead.astype(f32)
    ext_ref[PAD:, :] = rows.astype(f32)


def delayed(ext_ref, by):
    return ext_ref[PAD - by : ext_ref.shape[0] - by, :]


def short_conv(ext_ref, taps):
    result = taps[0:1] * delayed(ext_ref, 0)
    for shift_idx in range(1, taps.shape[0]):
        result = result + taps[shift_idx : shift_idx + 1] * delayed(ext_ref, shift_idx)
    return result


def signals_kernel(
    q_ref, k_ref, v_ref, grad_ref, lead_ref, taps_ref, product_ref, cotan_ref, q_ext, k_ext, v_ext
):
    halo_rows = taps_ref.shape[0] - 1
    for idx in range(product_ref.shape[0]):
        lanes = group(idx)
        taps = taps_ref[:, lanes]
        for place, (ref, ext) in enumerate(((q_ref, q_ext), (k_ref, k_ext), (v_ref, v_ext))):
            extend_rows(lead_ref[place * halo_rows : (place + 1) * halo_rows, lanes], ref[:, lanes], ext)
        product_ref[idx] = (short_conv(k_ext, taps) * short_conv(v_ext, taps)).astype(bf16)
        cotan_ref[idx] = (grad_ref[:, lanes].astype(f32) * short_conv(q_ext, taps)).astype(bf16)


def finish_kernel(
    q_ref, k_ref, v_ref, grad_ref, lead_ref, taps_ref, skip_ref, conv_ref, corr_ref,
    mixed_ref, grad_q_ref, grad_k_ref, grad_v_ref, edge_ref, sums_ref,
    q_ext, k_ext, v_ext, back_ext,
):
    taps_count = taps_ref.shape[0]
    halo_rows = taps_count - 1
    rows_here = q_ref.shape[0]
    sums_ref[...] = jnp.zeros_like(sums_ref)
    back_ext[rows_here:, :] = jnp.zeros((PAD, LANES), f32)
    for idx in range(conv_ref.shape[0]):
        lanes = group(idx)
        taps = taps_ref[:, lanes]
        skip = skip_ref[:, lanes]
        exts = (q_ext, k_ext, v_ext)
        for place, (ref, ext) in enumerate(zip((q_ref, k_ref, v_ref), exts)):
            extend_rows(lead_ref[place * halo_rows : (place + 1) * halo_rows, lanes], ref[:, lanes], ext)
        q_short = short_conv(q_ext, taps)
        k_short = short_conv(k_ext, taps)
        v_short = short_conv(v_ext, taps)
        product = (k_short * v_short).astype(bf16).astype(f32)
        filtered = conv_ref[idx].astype(f32) + skip * product
        mixed_ref[:, lanes] = (q_short * filtered).astype(bf16)
        upstream = grad_ref[:, lanes].astype(f32)
        back_q = upstream * filtered
        back_mix = upstream * q_short
        back_prod = corr_ref[idx].astype(f32) + skip * back_mix
        sums_ref[idx, taps_count : taps_count + 1, :] = jnp.sum(back_mix * product, axis=0, keepdims=True)
        backs = (back_q, back_prod * v_short, back_prod * k_short)
        taps_sums = [0.0] * taps_count
        for place, (back, ext, out_ref) in enumerate(
            zip(backs, exts, (grad_q_ref, grad_k_ref, grad_v_ref))
        ):
            for shift_idx in range(taps_count):
                taps_sums[shift_idx] = taps_sums[shift_idx] + back * delayed(ext, shift_idx)
            back_ext[:rows_here, :] = back
            grad = taps[0:1] * back
            for shift_idx in range(1, taps_count):
                grad = grad + taps[shift_idx : shift_idx + 1] * back_ext[shift_idx : shift_idx + rows_here, :]
            out_ref[:, lanes] = grad.astype(bf16)
            edge_ref[place, 0:halo_rows, lanes] = back[:halo_rows]
            edge_ref[place, halo_rows : 2 * halo_rows, lanes] = grad[rows_here - halo_rows :]
        for shift_idx in range(taps_count):
            sums_ref[idx, shift_idx : shift_idx + 1, :] = jnp.sum(taps_sums[shift_idx], axis=0, keepdims=True)


def edges_kernel(edge_ref, tail_ref, taps_ref, q_ref, k_ref, v_ref, q_out, k_out, v_out, work_ref):
    taps_count = taps_ref.shape[0]
    halo_rows = taps_count - 1
    block_rows = q_ref.shape[0]
    for place, (ref, out_ref) in enumerate(((q_ref, q_out), (k_ref, k_out), (v_ref, v_out))):
        work_ref[...] = ref[...].astype(f32)
        for row in range(halo_rows):
            total = edge_ref[place, halo_rows + row : halo_rows + row + 1, :]
            for shift_idx in range(halo_rows - row, taps_count):
                source = row + shift_idx - halo_rows
                total = total + taps_ref[shift_idx : shift_idx + 1, :] * tail_ref[place, source : source + 1, :]
            at = block_rows - halo_rows + row
            work_ref[at : at + 1, :] = total
        out_ref[...] = work_ref[...].astype(bf16)


def scale_kernel(here_ref, limit, all_ref, lag_ref, taps_out, skip_out, kernel_out):
    taps_count = taps_out.shape[0]
    pieces = all_ref.shape[0]
    squares = jnp.sum(all_ref[:, :, taps_count + 1, :])
    factor = limit / jnp.maximum(jnp.sqrt(jnp.full((1, LANES), squares)), limit)
    share = all_ref.shape[-1]
    for piece in range(pieces):
        own = all_ref[piece, here_ref[0]]
        lanes = slice(piece * share, (piece + 1) * share)
        taps_out[:, lanes] = own[0:taps_count] * factor[:, :share]
        skip_out[:, lanes] = own[taps_count : taps_count + 1] * factor[:, :share]
    for idx in range(lag_ref.shape[0]):
        kernel_out[:, group(idx)] = lag_ref[idx].astype(f32) * factor


def exchange(pieces_first, axes="ctx"):
    return lax.all_to_all(pieces_first, axes, split_axis=0, concat_axis=0, tiled=True)


def to_pieces(groups, pieces):
    count, rows, lanes = groups.shape
    if count == pieces:
        return groups
    share = count * lanes // pieces
    split = groups.reshape(count, rows, lanes // share, share)
    return split.transpose(0, 2, 1, 3).reshape(pieces, rows, share)


def to_groups(parts):
    pieces, rows, share = parts.shape
    if share == LANES:
        return parts
    joined = parts.reshape(pieces * share // LANES, LANES // share, rows, share)
    return joined.transpose(0, 2, 1, 3).reshape(-1, rows, LANES)


def body(q_in, k_in, v_in, grad_out, short_filter, kernel, skip):
    pieces = lax.axis_size("ctx")
    sides = lax.axis_size("ch")
    rows_here, channels = q_in.shape
    seq_len = pieces * rows_here
    taps_count = short_filter.shape[0]
    halo_rows = taps_count - 1
    groups = channels // LANES
    share = channels // pieces
    at_once = min(groups, 4)
    steps = groups // at_once
    width = at_once * LANES
    skip_row = skip.reshape(1, channels)
    transforms = (Transforms if share == LANES else PlainTransforms)(seq_len)

    rows_spec = pl.BlockSpec((rows_here, width), lambda i: (0, i))
    group_spec = pl.BlockSpec((at_once, rows_here, LANES), lambda i: (i, 0, 0))
    lead_spec = pl.BlockSpec((3 * halo_rows, width), lambda i: (0, i))
    taps_spec = pl.BlockSpec((taps_count, width), lambda i: (0, i))
    skip_spec = pl.BlockSpec((1, width), lambda i: (0, i))
    sums_spec = pl.BlockSpec((at_once, PAD, LANES), lambda i: (i, 0, 0))
    edge_spec = pl.BlockSpec((3, 2 * halo_rows, width), lambda i: (0, 0, i))
    grouped = jax.ShapeDtypeStruct((groups, rows_here, LANES), bf16)
    flat = jax.ShapeDtypeStruct((rows_here, channels), bf16)
    ext = pltpu.VMEM((rows_here + PAD, LANES), f32)

    lead = jnp.concatenate([x[rows_here - halo_rows :] for x in (q_in, k_in, v_in)], axis=0)
    lead = lax.ppermute(lead, "ctx", [(i, i + 1) for i in range(pieces - 1)])

    packed = call(pack_kernel, grouped, [], kernel, grid=(steps,), in_specs=[rows_spec], out_specs=group_spec)
    filter_here = exchange(to_pieces(packed, pieces))
    product, cotan = call(
        signals_kernel, (grouped, grouped), [ext, ext, ext],
        q_in, k_in, v_in, grad_out, lead, short_filter,
        grid=(steps,),
        in_specs=[rows_spec] * 4 + [lead_spec, taps_spec],
        out_specs=(group_spec, group_spec),
    )
    product_here = exchange(to_pieces(product, pieces))
    cotan_here = exchange(to_pieces(cotan, pieces))

    filter_spec = transforms.filter(filter_here)
    conv, product_spec = transforms.conv(product_here, filter_spec)
    conv = to_groups(exchange(conv.reshape(pieces, rows_here, share)))
    corr, lag, lag_squares = transforms.corr(cotan_here, filter_spec, product_spec)
    corr = to_groups(exchange(corr.reshape(pieces, rows_here, share)))
    lag = to_groups(exchange(lag.reshape(pieces, rows_here, share)))

    mixed, grad_q, grad_k, grad_v, edge, sums = call(
        finish_kernel,
        (
            flat, flat, flat, flat,
            jax.ShapeDtypeStruct((3, 2 * halo_rows, channels), f32),
            jax.ShapeDtypeStruct((groups, PAD, LANES), f32),
        ),
        [ext, ext, ext, ext],
        q_in, k_in, v_in, grad_out, lead, short_filter, skip_row, conv, corr,
        grid=(steps,),
        in_specs=[rows_spec] * 4 + [lead_spec, taps_spec, skip_spec, group_spec, group_spec],
        out_specs=(rows_spec,) * 4 + (edge_spec, sums_spec),
    )

    sums_here = jnp.sum(exchange(to_pieces(sums, pieces)), axis=0)
    squares = jnp.sum(lag_squares, axis=0) + jnp.sum(sums_here * sums_here, axis=0)
    shared = jnp.concatenate([sums_here[: taps_count + 1], squares[None], sums_here[taps_count + 2 :]], axis=0)
    everyone = exchange(
        jnp.broadcast_to(shared[None], (pieces * sides,) + shared.shape), ("ctx", "ch")
    ).reshape(pieces, sides, PAD, share)

    tail = lax.ppermute(edge[:, :halo_rows], "ctx", [(i, i - 1) for i in range(1, pieces)])
    last_block = 16
    last_spec = pl.BlockSpec((last_block, channels), lambda i: (rows_here // last_block - 1, 0))
    whole = lambda *dims: pl.BlockSpec(dims, lambda i: (0,) * len(dims))
    grad_q, grad_k, grad_v = call(
        edges_kernel, (flat, flat, flat), [pltpu.VMEM((last_block, channels), f32)],
        edge, tail, short_filter, grad_q, grad_k, grad_v,
        grid=(1,),
        in_specs=[whole(*edge.shape), whole(*tail.shape), whole(*short_filter.shape)] + [last_spec] * 3,
        out_specs=(last_spec,) * 3,
        input_output_aliases={3: 0, 4: 1, 5: 2},
    )

    limit = math.sqrt(float(seq_len * channels * sides))
    grad_short, grad_skip, grad_kernel = call(
        lambda here, *refs: scale_kernel(here, limit, *refs),
        (
            jax.ShapeDtypeStruct((taps_count, channels), f32),
            jax.ShapeDtypeStruct((1, channels), f32),
            jax.ShapeDtypeStruct((rows_here, channels), f32),
        ),
        [],
        lax.axis_index("ch").reshape(1), everyone, lag,
        in_specs=[pl.BlockSpec(memory_space=pltpu.SMEM)] + [pl.BlockSpec(memory_space=pltpu.VMEM)] * 2,
        out_specs=(pl.BlockSpec(memory_space=pltpu.VMEM),) * 3,
    )
    return mixed, grad_q, grad_k, grad_v, grad_short, grad_skip.reshape(channels), grad_kernel


def solution(mesh):
    in_specs = (
        P("ctx", "ch"),
        P("ctx", "ch"),
        P("ctx", "ch"),
        P("ctx", "ch"),
        P(None, "ch"),
        P("ctx", "ch"),
        P("ch"),
    )
    out_specs = (
        P("ctx", "ch"),
        P("ctx", "ch"),
        P("ctx", "ch"),
        P("ctx", "ch"),
        P(None, "ch"),
        P("ch"),
        P("ctx", "ch"),
    )
    return jax.shard_map(body, mesh=mesh, in_specs=in_specs, out_specs=out_specs, check_vma=False)
```

time: 888 us -> 163 us (0.18); the launches traced: 877 us -> 161 us
  waiting for transfers between devices: 380 us -> 29.8 us
  starting transfers between devices: 146 us -> 28.7 us
  blocking collectives: 139 us -> 51.7 us
  local copies, waits for them, and re-layouts: 91.4 us -> 16.9 us
  matrix products: 64.8 us -> 0 us
  other arithmetic: 51.7 us -> 0.11 us
  Pallas kernels: 0 us -> 33.2 us
    all_to_all x7 -> x5, waiting for transfers between devices: 380 us -> 27.2 us  [exchange(): lax.all_to_all(pieces_first, axes, split_axis=0, concat_axis=0, tiled=True)]
    all_to_all x7 -> x5, starting transfers between devices: 133 us -> 25.1 us  [exchange(): lax.all_to_all(pieces_first, axes, split_axis=0, concat_axis=0, tiled=True)]
    psum x2 -> x0, blocking collectives: 66.8 us -> none  [the longest x1 61.4 us: body(): summed = lax.psum((short_grad, skip_grad, kernel_square), 'ctx')]
    dot_general x8 -> x0, matrix products: 64.8 us -> none  [the longest x2 25.5 us: spectrum_tiles(): jnp.einsum('pqer,qgjrc->pgjec', forward_table(inner_angle), arrived, prec...]
    another operation x9 -> x0, local copies, waits for them, and re-layouts: 40.7 us -> none  [the longest x6 28.6 us: spectrum_tiles(): jnp.stack([turn_re, turn_im])]
    pallas_call x0 -> x8, Pallas kernels: none -> 33.2 us  [call(): pl.pallas_call(kernel, out_shape=outs, scratch_shapes=scratch, compiler_p...]
    all_to_all x3 -> x0, local copies, waits for them, and re-layouts: 24.8 us -> none  [the longest x2 23 us: rows_from_spectrum(): lax.all_to_all(stacked, 'ctx', split_axis=3, concat_axis=2, tiled=True)]
    all_to_all x2 -> x3, blocking collectives: 72.4 us -> 51.7 us  [exchange(): lax.all_to_all(pieces_first, axes, split_axis=0, concat_axis=0, tiled=True)]
  transfers between devices with their start and end apart: 13 -> 7, of which waited for: 7 -> 5; matrix products, arithmetic and copies ran while one was open for 18% -> 0% of each run, Pallas kernels for 0% -> 15%
where the time goes in v1:
time: 163 us; the launch traced here: 161 us
  blocking collectives  51.7 us (32%)
  Pallas kernels  33.2 us (20%)
  waiting for transfers between devices  29.8 us (18%)
  starting transfers between devices  28.7 us (18%)
  local copies, waits for them, and re-layouts  16.9 us (10%)
    all_to_all x3, blocking collectives, exchange(): lax.all_to_all(pieces_first, axes, split_axis=0, concat_axis=0, tiled=True)  51.7 us
    pallas_call x8, Pallas kernels, call(): pl.pallas_call(kernel, out_shape=outs, scratch_shapes=scratch, compiler_p...  33.2 us
    all_to_all x5, waiting for transfers between devices, exchange(): lax.all_to_all(pieces_first, axes, split_axis=0, concat_axis=0, tiled=True)  27.2 us
    all_to_all x5, starting transfers between devices, exchange(): lax.all_to_all(pieces_first, axes, split_axis=0, concat_axis=0, tiled=True)  25.1 us
    unnamed x46, local copies, waits for them, and re-layouts  15.6 us
  transfers between devices with their start and end apart: 7, of which 5 were waited for; matrix products, arithmetic and copies ran while one was open for 0% of the time, Pallas kernels for 15%

profile of v1, /device:TPU:0, one launch (start us, length us, event | category | flops | bytes accessed | tf_op | source)
XLA Modules:
  0.0 161.4 jit_solution(18405777922515421184)
XLA Ops:
  0.6 0.0 copy-start.8
  0.6 0.0 copy-start.7
  0.7 0.0 copy-start.6
  0.7 0.0 copy-start.14
  0.7 0.0 copy-start.17
  0.7 1.4 copy-done.17
  2.0 0.0 copy-start.20
  2.0 1.5 shard_map.154
  3.5 7.4 %all-to-all-start.1 = ((bf16[16,128,128]{2,1,0:T(8,128)(2,1)}), bf16[16,128,128]{2,1,0:T(8,128)(2,1)S(1)}, u32[]{:S(2)}, u32[]{:S(2)}) async-start(bf16[16,128,128]{2,1,0:T(8,128)(2,1)} %shard_map.154), calls=%async_computation.1 | async-start | bytes 1048576 | tf_op jit(solution)/shard_map/all_to_all | solution.py:410
  10.9 0.0 copy-done.8
  10.9 0.0 copy-done.7
  10.9 0.0 copy-done.6
  11.0 0.0 copy-start.22
  11.0 2.3 %collective-permute-start = (bf16[6,2048]{1,0:T(8,128)(2,1)S(1)}, bf16[6,2048]{1,0:T(8,128)(2,1)S(1)}, u32[]{:S(2)}, u32[]{:S(2)}) collective-permute-start(bf16[6,2048]{1,0:T(8,128)(2,1)S(1)} %pad_maximum_fusion), channel_id=1, source_target_pairs={{0,2},{2,4},{4,6},{6,8},{8,10},{10,12},{12,14},{14,16},{16,18},{18... | collective-permute-start | bytes 73736 | tf_op jit(solution)/shard_map/ppermute | solution.py:457
  13.3 0.8 collective-permute-done.lead_ref
  14.2 0.0 copy-done.14
  14.2 0.0 copy-done.20
  14.2 2.2 %shard_map.153 = (bf16[16,128,128]{2,1,0:T(8,128)(2,1)S(1)}, bf16[16,128,128]{2,1,0:T(8,128)(2,1)}) custom-call(bf16[128,2048]{1,0:T(8,128)(2,1)S(1)} %copy-done.6, bf16[128,2048]{1,0:T(8,128)(2,1)S(1)} %copy-done.7, bf16[128,2048]{1,0:T(8,128)(2,1)S(1)} %copy-done.8, bf16[128,2048]{1,0:T(8,128)(2,1)S(1)} %copy-done.14, ...), custom_call_target="tpu_custom_call" | custom-call | tf_op jit(solution)/shard_map/pallas_call | solution.py:200
  16.4 9.0 %all-to-all-done.1 = bf16[16,128,128]{2,1,0:T(8,128)(2,1)S(1)} async-done(((bf16[16,128,128]{2,1,0:T(8,128)(2,1)}), bf16[16,128,128]{2,1,0:T(8,128)(2,1)S(1)}, u32[]{:S(2)}, u32[]{:S(2)}) %all-to-all-start.1) | async-done | bytes 524320 | tf_op jit(solution)/shard_map/all_to_all | solution.py:410
  25.3 0.0 copy-start.12
  25.3 20.5 %all_to_all.40 = bf16[16,128,128]{2,1,0:T(8,128)(2,1)} all-to-all(bf16[16,128,128]{2,1,0:T(8,128)(2,1)S(1)} %get-tuple-element.26), channel_id=1, replica_groups=mesh['ctx'=16,'ch'=2] {'ctx'}, dimensions={0} | all-to-all | bytes 1048576 | tf_op jit(solution)/shard_map/all_to_all | solution.py:410
  45.8 4.3 %all-to-all-start.3 = ((bf16[16,128,128]{2,1,0:T(8,128)(2,1)}), bf16[16,128,128]{2,1,0:T(8,128)(2,1)}, u32[]{:S(2)}, u32[]{:S(2)}) async-start(bf16[16,128,128]{2,1,0:T(8,128)(2,1)} %get-tuple-element.28), calls=%async_computation.3 | async-start | bytes 1048576 | tf_op jit(solution)/shard_map/all_to_all | solution.py:410
  50.1 0.0 copy-done.12
  50.1 0.0 copy-done.22
  50.1 0.0 copy-start.13
  50.1 0.6 broadcast_in_dim.7.twist_ref
  50.7 0.4 copy-done.13
  51.2 0.0 copy-start.2
  51.2 1.4 copy-done.2
  52.6 0.0 copy-start.4
  52.6 0.0 copy-start.16
  52.6 3.0 %shard_map.155.filter_spec_ref = f32[512,1024]{1,0:T(8,128)S(1)} custom-call(bf16[8,256,128]{2,1,0:T(8,128)(2,1)S(1)} %bitcast.12, f32[2,8,256,128]{3,2,1,0:T(8,128)S(1)} %broadcast_in_dim.7.twist_ref, bf16[512,1536]{1,0:T(8,128)(2,1)S(1)} %copy-done.2), custom_call_target="tpu_custom_call" | custom-call | tf_op jit(solution)/shard_map/pallas_call | solution.py:200
  55.6 0.0 copy-done.4
  55.6 0.0 copy-done.16
  55.6 6.3 %shard_map.156 = (bf16[8,256,128]{2,1,0:T(8,128)(2,1)S(1)}, f32[512,1024]{1,0:T(8,128)S(1)}) custom-call(bf16[8,256,128]{2,1,0:T(8,128)(2,1)S(1)} %bitcast.13, f32[512,1024]{1,0:T(8,128)S(1)} %shard_map.155.filter_spec_ref, f32[2,8,256,128]{3,2,1,0:T(8,128)S(1)} %broadcast_in_dim.7.twist_ref, bf16[512,1536]{1,0:T(8,128)(2,1)S(1)} %copy-done.2, ...), custom_call_target="tpu_custom_call" | custom-call | tf_op jit(solution)/shard_map/pallas_call | solution.py:200
  62.0 0.0 copy-start
  62.0 1.4 copy-done
  63.3 1.3 copy-done.10
  64.6 0.8 copy-done.18
  65.4 0.0 all-to-all-done.3
  65.4 6.0 %all-to-all-start.2 = ((bf16[16,128,128]{2,1,0:T(8,128)(2,1)}), bf16[16,128,128]{2,1,0:T(8,128)(2,1)}, u32[]{:S(2)}, u32[]{:S(2)}) async-start(bf16[16,128,128]{2,1,0:T(8,128)(2,1)} %bitcast.14), calls=%async_computation.2 | async-start | bytes 1048576 | tf_op jit(solution)/shard_map/all_to_all | solution.py:410
  71.4 0.0 copy-start.1
  71.4 1.6 copy-done.1
  73.0 1.4 copy-done.3
  74.4 1.4 copy-done.5
  75.8 1.6 copy-done.11
  77.4 11.5 %shard_map.157 = (bf16[8,256,128]{2,1,0:T(8,128)(2,1)S(1)}, bf16[8,256,128]{2,1,0:T(8,128)(2,1)}, f32[16,128]{1,0:T(8,128)S(1)}) custom-call(bf16[8,256,128]{2,1,0:T(8,128)(2,1)} %bitcast.4.cotan_ref, f32[512,1024]{1,0:T(8,128)S(1)} %copy-done.1, f32[512,1024]{1,0:T(8,128)S(1)} %copy-done.11, f32[2,8,256,128]{3,2,1,0:T(8,128)S(1)} %broadcast_in_dim.7.twist_ref, ...), custom_call_target="tpu_custom_call" | custom-call | tf_op jit(solution)/shard_map/pallas_call | solution.py:200
  88.9 0.8 copy-done.19
  89.7 0.0 all-to-all-done.2.conv_ref
  89.7 20.4 %all_to_all.41.corr_ref = bf16[16,128,128]{2,1,0:T(8,128)(2,1)S(1)} all-to-all(bf16[16,128,128]{2,1,0:T(8,128)(2,1)} %bitcast.15), channel_id=1, replica_groups=mesh['ctx'=16,'ch'=2] {'ctx'}, dimensions={0} | all-to-all | bytes 1048576 | tf_op jit(solution)/shard_map/all_to_all | solution.py:410
  110.2 0.0 copy-done.21
  110.2 1.0 copy-done.9
  111.2 1.0 copy-done.15
  112.2 5.8 %shard_map.158 = (bf16[128,2048]{1,0:T(8,128)(2,1)}, bf16[128,2048]{1,0:T(8,128)(2,1)}, bf16[128,2048]{1,0:T(8,128)(2,1)}, bf16[128,2048]{1,0:T(8,128)(2,1)}, f3...) custom-call(bf16[128,2048]{1,0:T(8,128)(2,1)S(1)} %copy-done.6, bf16[128,2048]{1,0:T(8,128)(2,1)S(1)} %copy-done.7, ...), custom_call_target="tpu_custom_call" | custom-call | tf_op jit(solution)/shard_map/pallas_call | solution.py:200
  118.1 10.8 %all_to_all.42 = f32[16,8,128]{2,1,0:T(8,128)S(1)} all-to-all(f32[16,8,128]{2,1,0:T(8,128)S(1)} %get-tuple-element.39), channel_id=1, replica_groups=mesh['ctx'=16,'ch'=2] {'ctx'}, dimensions={0} | all-to-all | bytes 131072 | tf_op jit(solution)/shard_map/all_to_all | solution.py:410
  128.8 3.6 %all-to-all-start.7 = ((bf16[16,128,128]{2,1,0:T(8,128)(2,1)}), bf16[16,128,128]{2,1,0:T(8,128)(2,1)S(1)}, u32[]{:S(2)}, u32[]{:S(2)}) async-start(bf16[16,128,128]{2,1,0:T(8,128)(2,1)} %bitcast.9), calls=%async_computation.7 | async-start | bytes 1048576 | tf_op jit(solution)/shard_map/all_to_all | solution.py:410
  132.5 14.3 %all-to-all-done.7.refs_1_ = bf16[16,128,128]{2,1,0:T(8,128)(2,1)S(1)} async-done(((bf16[16,128,128]{2,1,0:T(8,128)(2,1)}), bf16[16,128,128]{2,1,0:T(8,128)(2,1)S(1)}, u32[]{:S(2)}, u32[]{:S(2)}) %all-to-all-start.7) | async-done | bytes 524320 | tf_op jit(solution)/shard_map/all_to_all | solution.py:410
  146.8 0.7 broadcast_in_dim.16
  147.5 4.0 %all-to-all-start.6 = ((f32[32,8,128]{2,1,0:T(8,128)}), f32[32,8,128]{2,1,0:T(8,128)S(1)}, u32[]{:S(2)}, u32[]{:S(2)}) async-start(f32[32,8,128]{2,1,0:T(8,128)} %broadcast_in_dim.16), calls=%async_computation.6 | async-start | bytes 262144 | tf_op jit(solution)/shard_map/all_to_all | solution.py:410
  151.5 1.3 collective-permute-start.1
  152.8 1.8 %collective-permute-done.1.tail_ref = f32[3,2,2048]{2,1,0:T(2,128)S(1)} collective-permute-done((f32[3,2,2048]{2,1,0:T(2,128)S(1)}, f32[3,2,2048]{2,1,0:T(2,128)S(1)}, u32[]{:S(2)}, u32[]{:S(2)}) %collective-permute-start.1) | collective-permute-done | bytes 49184 | tf_op jit(solution)/shard_map/ppermute | solution.py:499
  154.6 1.6 shard_map.159
  156.2 3.9 %all-to-all-done.6 = f32[32,8,128]{2,1,0:T(8,128)S(1)} async-done(((f32[32,8,128]{2,1,0:T(8,128)}), f32[32,8,128]{2,1,0:T(8,128)S(1)}, u32[]{:S(2)}, u32[]{:S(2)}) %all-to-all-start.6) | async-done | bytes 131104 | tf_op jit(solution)/shard_map/all_to_all | solution.py:410
  160.1 1.3 shard_map.160
  (21 shorter events, 0.2 us)
Async XLA Ops:
  0.6 10.2 %copy-start.8 = (bf16[128,2048]{1,0:T(8,128)(2,1)S(1)}, bf16[128,2048]{1,0:T(8,128)(2,1)}, u32[]{:S(2)}) copy-start(bf16[128,2048]{1,0:T(8,128)(2,1)} %v_ref.3) | copy-start | bytes 1572868
  0.6 10.3 %copy-start.7 = (bf16[128,2048]{1,0:T(8,128)(2,1)S(1)}, bf16[128,2048]{1,0:T(8,128)(2,1)}, u32[]{:S(2)}) copy-start(bf16[128,2048]{1,0:T(8,128)(2,1)} %k_ref.3) | copy-start | bytes 1572868
  0.7 10.3 %copy-start.6 = (bf16[128,2048]{1,0:T(8,128)(2,1)S(1)}, bf16[128,2048]{1,0:T(8,128)(2,1)}, u32[]{:S(2)}) copy-start(bf16[128,2048]{1,0:T(8,128)(2,1)} %q_ref.3) | copy-start | bytes 1572868
  0.7 13.5 %copy-start.14 = (bf16[128,2048]{1,0:T(8,128)(2,1)S(1)}, bf16[128,2048]{1,0:T(8,128)(2,1)}, u32[]{:S(2)}) copy-start(bf16[128,2048]{1,0:T(8,128)(2,1)} %grad_ref.3) | copy-start | bytes 1572868
  0.7 1.4 copy-start.17
  2.0 12.1 %copy-start.20 = (f32[3,2048]{1,0:T(4,128)S(1)}, f32[3,2048]{1,0:T(4,128)}, u32[]{:S(2)}) copy-start(f32[3,2048]{1,0:T(4,128)} %taps_ref.5) | copy-start | bytes 73732
  3.5 21.8 %all-to-all-start.1 = ((bf16[16,128,128]{2,1,0:T(8,128)(2,1)}), bf16[16,128,128]{2,1,0:T(8,128)(2,1)S(1)}, u32[]{:S(2)}, u32[]{:S(2)}) async-start(bf16[16,128,128]{2,1,0:T(8,128)(2,1)} %shard_map.154), calls=%async_computation.1 | async-start | bytes 1048576 | tf_op jit(solution)/shard_map/all_to_all | solution.py:410
  11.0 39.1 %copy-start.22 = (f32[2,8,256]{2,1,0:T(8,128)S(1)}, f32[2,8,256]{2,1,0:T(8,128)}, u32[]{:S(2)}) copy-start(f32[2,8,256]{2,1,0:T(8,128)} %constant.15) | copy-start | bytes 49156
  11.0 3.2 %collective-permute-start = (bf16[6,2048]{1,0:T(8,128)(2,1)S(1)}, bf16[6,2048]{1,0:T(8,128)(2,1)S(1)}, u32[]{:S(2)}, u32[]{:S(2)}) collective-permute-start(bf16[6,2048]{1,0:T(8,128)(2,1)S(1)} %pad_maximum_fusion), channel_id=1, source_target_pairs={{0,2},{2,4},{4,6},{6,8},{8,10},{10,12},{12,14},{14,16},{16,18},{18... | collective-permute-start | bytes 73736 | tf_op jit(solution)/shard_map/ppermute | solution.py:457
  25.3 24.8 %copy-start.12 = (bf16[16,128,128]{2,1,0:T(8,128)(2,1)}, bf16[16,128,128]{2,1,0:T(8,128)(2,1)S(1)}, u32[]{:S(2)}) copy-start(bf16[16,128,128]{2,1,0:T(8,128)(2,1)S(1)} %all-to-all-done.1) | copy-start | bytes 1572868
  45.8 19.6 %all-to-all-start.3 = ((bf16[16,128,128]{2,1,0:T(8,128)(2,1)}), bf16[16,128,128]{2,1,0:T(8,128)(2,1)}, u32[]{:S(2)}, u32[]{:S(2)}) async-start(bf16[16,128,128]{2,1,0:T(8,128)(2,1)} %get-tuple-element.28), calls=%async_computation.3 | async-start | bytes 1048576 | tf_op jit(solution)/shard_map/all_to_all | solution.py:410
  50.1 1.0 copy-start.13
  51.2 1.4 copy-start.2
  52.6 3.0 %copy-start.4 = (bf16[512,1536]{1,0:T(8,128)(2,1)S(1)}, bf16[512,1536]{1,0:T(8,128)(2,1)}, u32[]{:S(2)}) copy-start(bf16[512,1536]{1,0:T(8,128)(2,1)} %constant.13.clone.inverse_ref) | copy-start | bytes 4718596
  52.6 3.0 %copy-start.16 = (bf16[16,128,128]{2,1,0:T(8,128)(2,1)S(1)}, bf16[16,128,128]{2,1,0:T(8,128)(2,1)}, u32[]{:S(2)}) copy-start(bf16[16,128,128]{2,1,0:T(8,128)(2,1)} %all_to_all.40) | copy-start | bytes 1572868
  62.0 1.4 copy-start
  63.3 1.3 copy-start.10
  64.6 0.8 copy-start.18
  65.4 24.3 %all-to-all-start.2 = ((bf16[16,128,128]{2,1,0:T(8,128)(2,1)}), bf16[16,128,128]{2,1,0:T(8,128)(2,1)}, u32[]{:S(2)}, u32[]{:S(2)}) async-start(bf16[16,128,128]{2,1,0:T(8,128)(2,1)} %bitcast.14), calls=%async_computation.2 | async-start | bytes 1048576 | tf_op jit(solution)/shard_map/all_to_all | solution.py:410
  71.4 1.6 copy-start.1
  73.0 1.4 copy-start.3
  74.4 1.4 copy-start.5
  75.8 1.6 copy-start.11
  77.4 32.8 %copy-start.21 = (f32[2048]{0:T(1024)S(1)}, f32[2048]{0:T(1024)}, u32[]{:S(2)}) copy-start(f32[2048]{0:T(1024)} %param.16) | copy-start | bytes 24580
  88.9 0.8 copy-start.19
  110.2 1.0 copy-start.9
  111.2 1.0 copy-start.15
  128.8 18.0 %all-to-all-start.7 = ((bf16[16,128,128]{2,1,0:T(8,128)(2,1)}), bf16[16,128,128]{2,1,0:T(8,128)(2,1)S(1)}, u32[]{:S(2)}, u32[]{:S(2)}) async-start(bf16[16,128,128]{2,1,0:T(8,128)(2,1)} %bitcast.9), calls=%async_computation.7 | async-start | bytes 1048576 | tf_op jit(solution)/shard_map/all_to_all | solution.py:410
  147.5 12.6 %all-to-all-start.6 = ((f32[32,8,128]{2,1,0:T(8,128)}), f32[32,8,128]{2,1,0:T(8,128)S(1)}, u32[]{:S(2)}, u32[]{:S(2)}) async-start(f32[32,8,128]{2,1,0:T(8,128)} %broadcast_in_dim.16), calls=%async_computation.6 | async-start | bytes 262144 | tf_op jit(solution)/shard_map/all_to_all | solution.py:410
  151.5 3.1 %collective-permute-start.1 = (f32[3,2,2048]{2,1,0:T(2,128)S(1)}, f32[3,2,2048]{2,1,0:T(2,128)S(1)}, u32[]{:S(2)}, u32[]{:S(2)}) collective-permute-start(f32[3,2,2048]{2,1,0:T(2,128)S(1)} %slice.21), channel_id=1, source_target_pairs={{2,0},{4,2},{6,4},{8,6},{10,8},{12,10},{14,12},{16,14},{18,16},{20... | collective-permute-start | bytes 147464 | tf_op jit(solution)/shard_map/ppermute | solution.py:499

commit v2 on v1

v2 whole, which is shorter than its diff:
```python
import math

import jax
import jax.numpy as jnp
import ml_dtypes
import numpy as np
from jax import lax
from jax.experimental import pallas as pl
from jax.experimental.pallas import tpu as pltpu
from jax.sharding import PartitionSpec as P

LANES = 128
SPAN = 256
CHUNK = 16
PAD = 8
BOTH = 2 * SPAN
VMEM_BYTES = 58 * 1024 * 1024
SMALL_VMEM_BYTES = 8 * 1024 * 1024

f32 = jnp.float32
bf16 = jnp.bfloat16


def leaf_phases(count, phase=0.25):
    if count == 1:
        return [phase]
    return leaf_phases(count // 2, phase / 2) + leaf_phases(count // 2, phase / 2 + 0.5)


def turn(re, im, phase):
    cosine = math.cos(2.0 * math.pi * phase)
    sine = math.sin(2.0 * math.pi * phase)
    if im is None:
        return re * cosine, re * (-sine)
    return re * cosine + im * sine, im * cosine - re * sine


def to_leaves(parts, phase=0.25):
    count = len(parts)
    if count == 1:
        return parts
    half = count // 2
    first = []
    second = []
    for low, high in zip(parts[:half], parts[half:]):
        high_re, high_im = turn(high[0], high[1], phase / 2)
        first.append((low[0] + high_re, high_im if low[1] is None else low[1] + high_im))
        second.append((low[0] - high_re, -high_im if low[1] is None else low[1] - high_im))
    return to_leaves(first, phase / 2) + to_leaves(second, phase / 2 + 0.5)


def from_leaves(leaves, phase=0.25, real_only=True):
    count = len(leaves)
    if count == 1:
        return leaves
    half = count // 2
    first = from_leaves(leaves[:half], phase / 2, False)
    second = from_leaves(leaves[half:], phase / 2 + 0.5, False)
    cosine = math.cos(math.pi * phase)
    sine = math.sin(math.pi * phase)
    low = []
    high = []
    for one, two in zip(first, second):
        diff_re = one[0] - two[0]
        diff_im = one[1] - two[1]
        if real_only:
            low.append((one[0] + two[0], None))
            high.append((diff_re * cosine - diff_im * sine, None))
        else:
            low.append((one[0] + two[0], one[1] + two[1]))
            high.append((diff_re * cosine - diff_im * sine, diff_im * cosine + diff_re * sine))
    return low + high


def dft_matrix():
    idx = np.arange(SPAN)
    angle = (idx[:, None] * idx[None, :] % SPAN) * (2.0 * np.pi / SPAN)
    cosine, sine = np.cos(angle), np.sin(angle)
    return np.block([[cosine, sine], [-sine, cosine]])


def twist_table(outer):
    angle = np.asarray(leaf_phases(outer))[:, None] * np.arange(SPAN)[None, :] * (2.0 * np.pi / SPAN)
    return np.stack([np.cos(angle), np.sin(angle)])


def halves(matrix):
    high = matrix.astype(ml_dtypes.bfloat16)
    low = (matrix - high.astype(np.float64)).astype(ml_dtypes.bfloat16)
    return np.stack([high, low])


def leaf_lanes(leaf):
    return slice(leaf * LANES, (leaf + 1) * LANES)


def split_store(ref, row, lanes, value):
    high = value.astype(bf16)
    low = (value - high.astype(f32)).astype(bf16)
    ref[pl.ds(row, CHUNK), lanes] = high
    ref[pl.ds(BOTH + row, CHUNK), lanes] = low
    ref[pl.ds(2 * BOTH + row, CHUNK), lanes] = high


def matrix_copies(matrix_hbm, matrix_ref, sems):
    return [
        pltpu.make_async_copy(
            matrix_hbm.at[half], matrix_ref.at[:, pl.ds(place * BOTH, BOTH)], sems.at[place]
        )
        for place, half in enumerate((0, 0, 1))
    ]


def transform(matrix_ref, split_ref, result_ref):
    for start in range(0, result_ref.shape[1], 2 * LANES):
        lanes = slice(start, start + 2 * LANES)
        result_ref[:, lanes] = jnp.dot(matrix_ref[...], split_ref[:, lanes], preferred_element_type=f32)


def spread_twist(column_ref, twist_ref):
    outer = twist_ref.shape[1]

    def step(idx, carry):
        here = pl.ds(pl.multiple_of(idx * CHUNK, CHUNK), CHUNK)
        columns = column_ref[here, :]
        for leaf in range(outer):
            for side in range(2):
                column = columns[:, side * outer + leaf : side * outer + leaf + 1]
                twist_ref[side, leaf, here, :] = jnp.broadcast_to(column, (CHUNK, LANES))
        return carry

    lax.fori_loop(0, SPAN // CHUNK, step, 0)


def over_chunks(rows_here, step, carry=0):
    for piece in range(SPAN // rows_here):

        def inner(idx, carry, piece=piece):
            row = pl.multiple_of(idx * CHUNK, CHUNK)
            return step(piece, row, pl.multiple_of(piece * rows_here + row, CHUNK), carry)

        carry = lax.fori_loop(0, rows_here // CHUNK, inner, carry)
    return carry


def leaves_of(read, rows_here, twist_ref, split_ref):
    outer = twist_ref.shape[1]
    ratio = SPAN // rows_here

    def step(piece, row, span_row, carry):
        here = pl.ds(span_row, CHUNK)
        parts = [(read(part * ratio + piece, pl.ds(row, CHUNK)).astype(f32), None) for part in range(outer)]
        for leaf, (re, im) in enumerate(to_leaves(parts)):
            cosine = twist_ref[0, leaf, here, :]
            sine = twist_ref[1, leaf, here, :]
            split_store(split_ref, span_row, leaf_lanes(leaf), re * cosine + im * sine)
            split_store(split_ref, SPAN + span_row, leaf_lanes(leaf), im * cosine - re * sine)
        return carry

    over_chunks(rows_here, step)


def combine(left_ref, right_ref, split_ref, conjugate):
    def step(idx, carry):
        row = pl.multiple_of(idx * CHUNK, CHUNK)
        for leaf in range(left_ref.shape[1] // LANES):
            lanes = leaf_lanes(leaf)
            left_re = left_ref[pl.ds(row, CHUNK), lanes]
            left_im = left_ref[pl.ds(SPAN + row, CHUNK), lanes]
            right_re = right_ref[pl.ds(row, CHUNK), lanes]
            right_im = right_ref[pl.ds(SPAN + row, CHUNK), lanes]
            if conjugate:
                re = left_re * right_re + left_im * right_im
                minus_im = left_im * right_re - left_re * right_im
            else:
                re = left_re * right_re - left_im * right_im
                minus_im = -left_re * right_im - left_im * right_re
            split_store(split_ref, row, lanes, re)
            split_store(split_ref, SPAN + row, lanes, minus_im)
        return carry

    lax.fori_loop(0, SPAN // CHUNK, step, 0)


def signal_of(time_ref, twist_ref, rows_here, write, carry=0):
    outer = twist_ref.shape[1]
    ratio = SPAN // rows_here
    scale = 1.0 / (SPAN * outer)

    def step(piece, row, span_row, carry):
        here = pl.ds(span_row, CHUNK)
        leaves = []
        for leaf in range(outer):
            cosine = twist_ref[0, leaf, here, :]
            sine = twist_ref[1, leaf, here, :]
            re = time_ref[here, leaf_lanes(leaf)]
            minus_im = time_ref[pl.ds(SPAN + span_row, CHUNK), leaf_lanes(leaf)]
            leaves.append((re * cosine + minus_im * sine, re * sine - minus_im * cosine))
        for part, (value, _) in enumerate(from_leaves(leaves)):
            carry = write(part * ratio + piece, pl.ds(row, CHUNK), value * scale, carry)
        return carry

    return over_chunks(rows_here, step, carry)


def filter_kernel(filter_ref, column_ref, matrix_hbm, spec_ref, twist_ref, matrix_ref, split_ref, sems):
    copies = matrix_copies(matrix_hbm, matrix_ref, sems)
    for copy in copies:
        copy.start()
    spread_twist(column_ref, twist_ref)
    leaves_of(lambda piece, rows: filter_ref[piece, rows, :], filter_ref.shape[1], twist_ref, split_ref)
    for copy in copies:
        copy.wait()
    transform(matrix_ref, split_ref, spec_ref)


def products_kernel(
    signals_ref, column_ref, matrix_hbm, filter_hbm, results_ref, lag_hbm,
    twist_ref, matrix_ref, split_ref, lag_split_ref, filter_ref, product_ref, cotan_ref, time_ref, sems,
):
    rows_here = signals_ref.shape[2]
    copies = matrix_copies(matrix_hbm, matrix_ref, sems)
    filter_copy = pltpu.make_async_copy(filter_hbm, filter_ref, sems.at[3])
    lag_copy = pltpu.make_async_copy(lag_split_ref, lag_hbm, sems.at[4])
    for copy in copies + [filter_copy]:
        copy.start()
    spread_twist(column_ref, twist_ref)
    leaves_of(lambda piece, rows: signals_ref[piece, 0, rows, :], rows_here, twist_ref, split_ref)
    for copy in copies:
        copy.wait()
    transform(matrix_ref, split_ref, product_ref)
    leaves_of(lambda piece, rows: signals_ref[piece, 1, rows, :], rows_here, twist_ref, split_ref)
    transform(matrix_ref, split_ref, cotan_ref)
    combine(product_ref, cotan_ref, lag_split_ref, True)
    lag_copy.start()
    filter_copy.wait()
    for place, (other_ref, conjugate) in enumerate(((product_ref, False), (cotan_ref, True))):
        combine(filter_ref, other_ref, split_ref, conjugate)
        transform(matrix_ref, split_ref, time_ref)

        def write(piece, rows, value, carry, place=place):
            results_ref[piece, place, rows, :] = value.astype(bf16)
            return carry

        signal_of(time_ref, twist_ref, rows_here, write)
    lag_copy.wait()


def lag_kernel(
    split_hbm, column_ref, matrix_hbm, lag_ref, square_ref, twist_ref, matrix_ref, split_ref, time_ref, sems
):
    copies = matrix_copies(matrix_hbm, matrix_ref, sems)
    copies.append(pltpu.make_async_copy(split_hbm, split_ref, sems.at[3]))
    for copy in copies:
        copy.start()
    spread_twist(column_ref, twist_ref)
    for copy in copies:
        copy.wait()
    transform(matrix_ref, split_ref, time_ref)

    def write(piece, rows, value, carry):
        lag_ref[piece, rows, :] = value.astype(bf16)
        return carry + value * value

    square_ref[...] = signal_of(
        time_ref, twist_ref, lag_ref.shape[1], write, jnp.zeros((CHUNK, LANES), f32)
    )


def call(kernel, outs, scratch, *args, vmem_bytes=VMEM_BYTES, **options):
    return pl.pallas_call(
        kernel,
        out_shape=outs,
        scratch_shapes=scratch,
        compiler_params=pltpu.CompilerParams(vmem_limit_bytes=vmem_bytes),
        **options,
    )(*args)


IN_VMEM = pl.BlockSpec(memory_space=pltpu.VMEM)
ANYWHERE = pl.BlockSpec(memory_space=pl.ANY)


class Transforms:
    def __init__(self, pieces, rows_here):
        outer = pieces * rows_here // SPAN
        self.matrix = jnp.asarray(halves(dft_matrix()))
        twist = twist_table(outer).astype(np.float32).reshape(2 * outer, SPAN)
        self.column = jnp.asarray(np.ascontiguousarray(twist.T))
        self.spec = jax.ShapeDtypeStruct((BOTH, outer * LANES), f32)
        self.split = jax.ShapeDtypeStruct((3 * BOTH, outer * LANES), bf16)
        self.signal = jax.ShapeDtypeStruct((pieces, rows_here, LANES), bf16)
        self.pair = jax.ShapeDtypeStruct((pieces, 2, rows_here, LANES), bf16)
        self.square = jax.ShapeDtypeStruct((CHUNK, LANES), f32)
        self.work = pltpu.VMEM(self.spec.shape, f32)
        self.split_work = pltpu.VMEM(self.split.shape, bf16)
        self.tables = [pltpu.VMEM((2, outer, SPAN, LANES), f32), pltpu.VMEM((BOTH, 3 * BOTH), bf16)]

    def filter(self, signal):
        return call(
            filter_kernel, self.spec, self.tables + [self.split_work, pltpu.SemaphoreType.DMA((3,))],
            signal, self.column, self.matrix,
            in_specs=[IN_VMEM, IN_VMEM, ANYWHERE],
            out_specs=IN_VMEM,
        )

    def products(self, signals, filter_spec):
        return call(
            products_kernel, (self.pair, self.split),
            self.tables
            + [self.split_work, self.split_work, self.work, self.work, self.work, self.work]
            + [pltpu.SemaphoreType.DMA((5,))],
            signals, self.column, self.matrix, filter_spec,
            in_specs=[IN_VMEM, IN_VMEM, ANYWHERE, ANYWHERE],
            out_specs=(IN_VMEM, ANYWHERE),
        )

    def lag(self, lag_split):
        return call(
            lag_kernel, (self.signal, self.square),
            self.tables + [self.split_work, self.work, pltpu.SemaphoreType.DMA((4,))],
            lag_split, self.column, self.matrix,
            in_specs=[ANYWHERE, IN_VMEM, ANYWHERE],
            out_specs=(IN_VMEM, IN_VMEM),
        )


class PlainTransforms:
    def __init__(self, pieces, rows_here):
        self.seq_len = pieces * rows_here
        self.pieces = pieces
        self.outer = self.seq_len // SPAN
        idx = np.arange(SPAN)
        angle = (idx[:, None] * idx[None, :] % SPAN) * (2.0 * np.pi / SPAN)
        self.cosine = jnp.asarray(np.cos(angle), f32)
        self.sine = jnp.asarray(np.sin(angle), f32)
        self.twist = jnp.asarray(twist_table(self.outer), f32)[..., None]

    def dot(self, matrix, signal):
        return jnp.einsum("fs,tsc->tfc", matrix, signal, precision=lax.Precision.HIGHEST)

    def filter(self, signal):
        parts = signal.astype(f32).reshape(self.outer, SPAN, -1)
        leaves = to_leaves([(parts[part], None) for part in range(self.outer)])
        re = jnp.stack([leaf[0] for leaf in leaves])
        im = jnp.stack([leaf[1] for leaf in leaves])
        twist_re = re * self.twist[0] + im * self.twist[1]
        twist_im = im * self.twist[0] - re * self.twist[1]
        return (
            self.dot(self.cosine, twist_re) + self.dot(self.sine, twist_im),
            self.dot(self.cosine, twist_im) - self.dot(self.sine, twist_re),
        )

    def back(self, re, im):
        time_re = self.dot(self.cosine, re) - self.dot(self.sine, im)
        time_im = self.dot(self.cosine, im) + self.dot(self.sine, re)
        leaf_re = time_re * self.twist[0] - time_im * self.twist[1]
        leaf_im = time_im * self.twist[0] + time_re * self.twist[1]
        parts = from_leaves([(leaf_re[leaf], leaf_im[leaf]) for leaf in range(self.outer)])
        signal = jnp.stack([part[0] for part in parts]) * (1.0 / self.seq_len)
        return signal.reshape(self.pieces, self.seq_len // self.pieces, -1)

    def products(self, signals, filter_spec):
        product = self.filter(signals[:, 0])
        cotan = self.filter(signals[:, 1])
        conv = self.back(
            filter_spec[0] * product[0] - filter_spec[1] * product[1],
            filter_spec[0] * product[1] + filter_spec[1] * product[0],
        )
        corr = self.back(
            filter_spec[0] * cotan[0] + filter_spec[1] * cotan[1],
            filter_spec[0] * cotan[1] - filter_spec[1] * cotan[0],
        )
        lag = (
            product[0] * cotan[0] + product[1] * cotan[1],
            product[0] * cotan[1] - product[1] * cotan[0],
        )
        return jnp.stack([conv, corr], axis=1).astype(bf16), lag

    def lag(self, lag_spec):
        lag = self.back(*lag_spec)
        return lag.astype(bf16), jnp.sum(lag * lag, axis=(0, 1))[None, :]


def group(idx):
    return slice(idx * LANES, (idx + 1) * LANES)


def pack_kernel(wide_ref, packed_ref):
    for idx in range(packed_ref.shape[0]):
        packed_ref[idx] = wide_ref[:, group(idx)].astype(packed_ref.dtype)


def extend_rows(lead, rows, ext_ref):
    halo_rows = lead.shape[0]
    ext_ref[PAD - halo_rows : PAD, :] = lead.astype(f32)
    ext_ref[PAD:, :] = rows.astype(f32)


def delayed(ext_ref, by):
    return ext_ref[PAD - by : ext_ref.shape[0] - by, :]


def short_conv(ext_ref, taps):
    result = taps[0:1] * delayed(ext_ref, 0)
    for shift_idx in range(1, taps.shape[0]):
        result = result + taps[shift_idx : shift_idx + 1] * delayed(ext_ref, shift_idx)
    return result


def signals_kernel(
    q_ref, k_ref, v_ref, grad_ref, lead_ref, taps_ref, signals_ref, short_ref, q_ext, k_ext, v_ext
):
    halo_rows = taps_ref.shape[0] - 1
    for idx in range(signals_ref.shape[0]):
        lanes = group(idx)
        taps = taps_ref[:, lanes]
        shorts = []
        for place, (ref, ext) in enumerate(((q_ref, q_ext), (k_ref, k_ext), (v_ref, v_ext))):
            extend_rows(lead_ref[place * halo_rows : (place + 1) * halo_rows, lanes], ref[:, lanes], ext)
            shorts.append(short_conv(ext, taps))
            short_ref[place, :, lanes] = shorts[place]
        signals_ref[idx, 0] = (shorts[1] * shorts[2]).astype(bf16)
        signals_ref[idx, 1] = (grad_ref[:, lanes].astype(f32) * shorts[0]).astype(bf16)


def finish_kernel(
    q_ref, k_ref, v_ref, grad_ref, short_ref, lead_ref, taps_ref, skip_ref, long_ref,
    mixed_ref, grad_q_ref, grad_k_ref, grad_v_ref, edge_ref, sums_ref,
    q_back, k_back, v_back,
):
    taps_count = taps_ref.shape[0]
    halo_rows = taps_count - 1
    rows_here = q_ref.shape[0]
    for ext in (q_back, k_back, v_back):
        ext[rows_here:, :] = jnp.zeros((PAD, LANES), f32)
    for idx in range(long_ref.shape[0]):
        lanes = group(idx)
        taps = taps_ref[:, lanes]
        skip = skip_ref[:, lanes]
        q_short = short_ref[0, :, lanes]
        k_short = short_ref[1, :, lanes]
        v_short = short_ref[2, :, lanes]
        product = (k_short * v_short).astype(bf16).astype(f32)
        filtered = long_ref[idx, 0].astype(f32) + skip * product
        mixed_ref[:, lanes] = (q_short * filtered).astype(bf16)
        upstream = grad_ref[:, lanes].astype(f32)
        back_mix = upstream * q_short
        back_prod = long_ref[idx, 1].astype(f32) + skip * back_mix
        sums_ref[taps_count : taps_count + 1, lanes] = jnp.sum(back_mix * product, axis=0, keepdims=True)
        backs = (upstream * filtered, back_prod * v_short, back_prod * k_short)
        sums = [0.0] * taps_count
        heads = [0.0] * taps_count
        for place, (back, ext, in_ref, out_ref) in enumerate(
            zip(backs, (q_back, k_back, v_back), (q_ref, k_ref, v_ref), (grad_q_ref, grad_k_ref, grad_v_ref))
        ):
            ext[:rows_here, :] = back
            signal = in_ref[:, lanes].astype(f32)
            lead = lead_ref[place * halo_rows : (place + 1) * halo_rows, lanes].astype(f32)
            sums[0] = sums[0] + back * signal
            grad = taps[0:1] * back
            for shift_idx in range(1, taps_count):
                ahead = ext[shift_idx : shift_idx + rows_here, :]
                grad = grad + taps[shift_idx : shift_idx + 1] * ahead
                sums[shift_idx] = sums[shift_idx] + ahead * signal
                heads[shift_idx] = heads[shift_idx] + jnp.sum(
                    back[:shift_idx] * lead[halo_rows - shift_idx :], axis=0, keepdims=True
                )
            out_ref[:, lanes] = grad.astype(bf16)
            edge_ref[place, 0:halo_rows, lanes] = back[:halo_rows]
            edge_ref[place, halo_rows : 2 * halo_rows, lanes] = grad[rows_here - halo_rows :]
        for shift_idx in range(taps_count):
            sums_ref[shift_idx : shift_idx + 1, lanes] = heads[shift_idx] + jnp.sum(
                sums[shift_idx], axis=0, keepdims=True
            )


def edges_kernel(edge_ref, tail_ref, taps_ref, q_ref, k_ref, v_ref, q_out, k_out, v_out, work_ref):
    taps_count = taps_ref.shape[0]
    halo_rows = taps_count - 1
    block_rows = q_ref.shape[0]
    for place, (ref, out_ref) in enumerate(((q_ref, q_out), (k_ref, k_out), (v_ref, v_out))):
        work_ref[...] = ref[...].astype(f32)
        for row in range(halo_rows):
            total = edge_ref[place, halo_rows + row : halo_rows + row + 1, :]
            for shift_idx in range(halo_rows - row, taps_count):
                source = row + shift_idx - halo_rows
                total = total + taps_ref[shift_idx : shift_idx + 1, :] * tail_ref[place, source : source + 1, :]
            at = block_rows - halo_rows + row
            work_ref[at : at + 1, :] = total
        out_ref[...] = work_ref[...].astype(bf16)


def scale_kernel(limit, totals_ref, norm_ref, lag_ref, taps_out, skip_out, kernel_out):
    taps_count = taps_out.shape[0]
    channels = taps_out.shape[1]
    factor = limit / jnp.maximum(jnp.sqrt(norm_ref[...]), limit)
    for idx in range(channels // LANES):
        taps_out[:, group(idx)] = totals_ref[0:taps_count, group(idx)] * factor
        skip_out[:, group(idx)] = totals_ref[taps_count : taps_count + 1, group(idx)] * factor
        kernel_out[:, group(idx)] = lag_ref[idx].astype(f32) * factor


def exchange(pieces_first):
    return lax.all_to_all(pieces_first, "ctx", split_axis=0, concat_axis=0, tiled=True)


def to_pieces(groups, pieces):
    count, kinds, rows, lanes = groups.shape
    if count == pieces:
        return groups
    share = count * lanes // pieces
    split = groups.reshape(count, kinds, rows, lanes // share, share)
    return split.transpose(0, 3, 1, 2, 4).reshape(pieces, kinds, rows, share)


def to_groups(parts):
    pieces, kinds, rows, share = parts.shape
    if share == LANES:
        return parts
    joined = parts.reshape(pieces * share // LANES, LANES // share, kinds, rows, share)
    return joined.transpose(0, 2, 3, 1, 4).reshape(-1, kinds, rows, LANES)


def total_over(value, axis):
    size = lax.axis_size(axis)
    step = 1
    while step < size:
        value = value + lax.ppermute(value, axis, [(i, i ^ step) for i in range(size)])
        step *= 2
    return value


def body(q_in, k_in, v_in, grad_out, short_filter, kernel, skip):
    pieces = lax.axis_size("ctx")
    sides = lax.axis_size("ch")
    rows_here, channels = q_in.shape
    seq_len = pieces * rows_here
    taps_count = short_filter.shape[0]
    halo_rows = taps_count - 1
    groups = channels // LANES
    share = channels // pieces
    at_once = min(groups, 4)
    steps = groups // at_once
    width = at_once * LANES
    transforms = (Transforms if share == LANES else PlainTransforms)(pieces, rows_here)

    rows_spec = pl.BlockSpec((rows_here, width), lambda i: (0, i))
    short_spec = pl.BlockSpec((3, rows_here, width), lambda i: (0, 0, i))
    group_spec = pl.BlockSpec((at_once, rows_here, LANES), lambda i: (i, 0, 0))
    pair_spec = pl.BlockSpec((at_once, 2, rows_here, LANES), lambda i: (i, 0, 0, 0))
    edge_spec = pl.BlockSpec((3, 2 * halo_rows, width), lambda i: (0, 0, i))

    def flat_spec(rows):
        return pl.BlockSpec((rows, width), lambda i: (0, i))

    flat = jax.ShapeDtypeStruct((rows_here, channels), bf16)
    ext = pltpu.VMEM((rows_here + PAD, LANES), f32)

    lead = jnp.concatenate([x[rows_here - halo_rows :] for x in (q_in, k_in, v_in)], axis=0)
    lead = lax.ppermute(lead, "ctx", [(i, i + 1) for i in range(pieces - 1)])

    packed = call(
        pack_kernel, jax.ShapeDtypeStruct((groups, rows_here, LANES), bf16), [], kernel,
        grid=(steps,), in_specs=[rows_spec], out_specs=group_spec,
    )
    filter_here = exchange(to_pieces(packed[:, None], pieces))[:, 0]
    signals, short = call(
        signals_kernel,
        (
            jax.ShapeDtypeStruct((groups, 2, rows_here, LANES), bf16),
            jax.ShapeDtypeStruct((3, rows_here, channels), f32),
        ),
        [ext, ext, ext],
        q_in, k_in, v_in, grad_out, lead, short_filter,
        grid=(steps,),
        in_specs=[rows_spec] * 4 + [flat_spec(3 * halo_rows), flat_spec(taps_count)],
        out_specs=(pair_spec, short_spec),
    )
    signals_here = exchange(to_pieces(signals, pieces))
    filter_spec = transforms.filter(filter_here)
    long_here, lag_spec = transforms.products(signals_here, filter_spec)
    long = to_groups(exchange(long_here))
    lag_here, lag_squares = transforms.lag(lag_spec)
    lag = to_groups(exchange(lag_here[:, None]))[:, 0]

    mixed, grad_q, grad_k, grad_v, edge, sums = call(
        finish_kernel,
        (
            flat, flat, flat, flat,
            jax.ShapeDtypeStruct((3, 2 * halo_rows, channels), f32),
            jax.ShapeDtypeStruct((taps_count + 1, channels), f32),
        ),
        [ext, ext, ext],
        q_in, k_in, v_in, grad_out, short, lead, short_filter, skip.reshape(1, channels), long,
        grid=(steps,),
        in_specs=[rows_spec] * 4
        + [short_spec, flat_spec(3 * halo_rows), flat_spec(taps_count), flat_spec(1), pair_spec],
        out_specs=(rows_spec,) * 4 + (edge_spec, flat_spec(taps_count + 1)),
    )

    extra = jnp.zeros((taps_count + 1, LANES), f32).at[0, :share].set(jnp.sum(lag_squares, axis=0))
    totals = total_over(jnp.concatenate([sums, extra], axis=1), "ctx")
    square = jnp.sum(totals[:, :channels] * totals[:, :channels]) + jnp.sum(totals[0, channels:])
    norm_sq = total_over(jnp.full((1, LANES), square), "ch")

    tail = lax.ppermute(edge[:, :halo_rows], "ctx", [(i, i - 1) for i in range(1, pieces)])
    last_block = 16
    last_spec = pl.BlockSpec((last_block, channels), lambda i: (rows_here // last_block - 1, 0))
    whole = lambda *dims: pl.BlockSpec(dims, lambda i: (0,) * len(dims))
    grad_q, grad_k, grad_v = call(
        edges_kernel, (flat, flat, flat), [pltpu.VMEM((last_block, channels), f32)],
        edge, tail, short_filter, grad_q, grad_k, grad_v,
        vmem_bytes=SMALL_VMEM_BYTES,
        grid=(1,),
        in_specs=[whole(*edge.shape), whole(*tail.shape), whole(*short_filter.shape)] + [last_spec] * 3,
        out_specs=(last_spec,) * 3,
        input_output_aliases={3: 0, 4: 1, 5: 2},
    )

    limit = math.sqrt(float(seq_len * channels * sides))
    grad_short, grad_skip, grad_kernel = call(
        lambda *refs: scale_kernel(limit, *refs),
        (
            jax.ShapeDtypeStruct((taps_count, channels), f32),
            jax.ShapeDtypeStruct((1, channels), f32),
            jax.ShapeDtypeStruct((rows_here, channels), f32),
        ),
        [],
        totals, norm_sq, lag,
        vmem_bytes=SMALL_VMEM_BYTES,
        in_specs=[IN_VMEM] * 3,
        out_specs=(IN_VMEM,) * 3,
    )
    return mixed, grad_q, grad_k, grad_v, grad_short, grad_skip.reshape(channels), grad_kernel


def solution(mesh):
    in_specs = (
        P("ctx", "ch"),
        P("ctx", "ch"),
        P("ctx", "ch"),
        P("ctx", "ch"),
        P(None, "ch"),
        P("ctx", "ch"),
        P("ch"),
    )
    out_specs = (
        P("ctx", "ch"),
        P("ctx", "ch"),
        P("ctx", "ch"),
        P("ctx", "ch"),
        P(None, "ch"),
        P("ch"),
        P("ctx", "ch"),
    )
    return jax.shard_map(body, mesh=mesh, in_specs=in_specs, out_specs=out_specs, check_vma=False)
```

time: 163 us -> 149 us (0.914)
  blocking collectives: 51.7 us -> 0 us
  Pallas kernels: 33.2 us -> 50.2 us
  waiting for transfers between devices: 29.8 us -> 43.3 us
  starting transfers between devices: 28.7 us -> 41.9 us
  local copies, waits for them, and re-layouts: 16.9 us -> 6.68 us
  other arithmetic: 0.11 us -> 3.54 us
    all_to_all x3 -> x0, blocking collectives: 51.7 us -> none  [exchange(): lax.all_to_all(pieces_first, axes, split_axis=0, concat_axis=0, tiled=True)]
    pallas_call x8, Pallas kernels: 33.2 us -> 50.2 us  [call(): pl.pallas_call(kernel, out_shape=outs, scratch_shapes=scratch, compiler_p...]
    unnamed x46 -> x12, local copies, waits for them, and re-layouts: 15.6 us -> 3.45 us
    ppermute x0 -> x5, waiting for transfers between devices: none -> 8.26 us  [total_over(): lax.ppermute(value, axis, [(i, i ^ step) for i in range(size)])]
    ppermute x0 -> x5, starting transfers between devices: none -> 8.04 us  [total_over(): lax.ppermute(value, axis, [(i, i ^ step) for i in range(size)])]
    all_to_all x5 -> x4, waiting for transfers between devices: 27.2 us -> 34.2 us  [exchange(): lax.all_to_all(pieces_first, 'ctx', split_axis=0, concat_axis=0, tiled=True)]
    all_to_all x5 -> x4, starting transfers between devices: 25.1 us -> 30.2 us  [exchange(): lax.all_to_all(pieces_first, 'ctx', split_axis=0, concat_axis=0, tiled=True)]
    slice x3, local copies, waits for them, and re-layouts: 0.04 us -> 2.32 us  [body(): x[rows_here - halo_rows:]]
  transfers between devices with their start and end apart: 7 -> 11, of which waited for: 5 -> 6; matrix products, arithmetic and copies ran while one was open for 0% -> 4% of each run, Pallas kernels for 15% -> 14%
where the time goes in v2:
time: 149 us; the launch traced here: 148 us
  Pallas kernels  50.2 us (34%)
  waiting for transfers between devices  43.3 us (29%)
  starting transfers between devices  41.9 us (28%)
  local copies, waits for them, and re-layouts  6.68 us (4%)
  other arithmetic  3.54 us (2%)
  between operations  2.09 us (1%)
    pallas_call x8, Pallas kernels, call(): pl.pallas_call(kernel, out_shape=outs, scratch_shapes=scratch, compiler_p...  50.2 us
    all_to_all x4, waiting for transfers between devices, exchange(): lax.all_to_all(pieces_first, 'ctx', split_axis=0, concat_axis=0, tiled=True)  34.2 us
    all_to_all x4, starting transfers between devices, exchange(): lax.all_to_all(pieces_first, 'ctx', split_axis=0, concat_axis=0, tiled=True)  30.2 us
    ppermute x5, waiting for transfers between devices, total_over(): lax.ppermute(value, axis, [(i, i ^ step) for i in range(size)])  8.26 us
    ppermute x5, starting transfers between devices, total_over(): lax.ppermute(value, axis, [(i, i ^ step) for i in range(size)])  8.04 us
    unnamed x12, local copies, waits for them, and re-layouts  3.45 us
  transfers between devices with their start and end apart: 11, of which 6 were waited for; matrix products, arithmetic and copies ran while one was open for 4% of the time, Pallas kernels for 14%

profile of v2, /device:TPU:0, one launch (start us, length us, event | category | flops | bytes accessed | tf_op | source)
XLA Modules:
  0.0 147.7 jit_solution(344337311458259719)
XLA Ops:
  0.6 3.3 %shard_map.145 = bf16[16,128,128]{2,1,0:T(8,128)(2,1)} custom-call(f32[128,2048]{1,0:T(8,128)} %wide_ref.1), custom_call_target="tpu_custom_call" | custom-call | tf_op jit(solution)/shard_map/pallas_call | solution.py:271
  3.9 7.4 %all-to-all-start.1 = ((bf16[16,1,128,128]{3,2,1,0:T(8,128)(2,1)}), bf16[16,1,128,128]{3,2,1,0:T(8,128)(2,1)S(1)}, u32[]{:S(2)}, u32[]{:S(2)}) async-start(bf16[16,1,128,128]{3,2,1,0:T(8,128)(2,1)} %bitcast.12), calls=%async_computation.1 | async-start | bytes 1048576 | tf_op jit(solution)/shard_map/all_to_all | solution.py:505
  11.3 0.8 slice.33
  12.0 0.8 slice.34
  12.8 0.8 slice.35
  13.6 2.3 %collective-permute-start = (bf16[6,2048]{1,0:T(8,128)(2,1)S(1)}, bf16[6,2048]{1,0:T(8,128)(2,1)S(1)}, u32[]{:S(2)}, u32[]{:S(2)}) collective-permute-start(bf16[6,2048]{1,0:T(8,128)(2,1)S(1)} %pad_maximum_fusion), channel_id=1, source_target_pairs={{0,2},{2,4},{4,6},{6,8},{8,10},{10,12},{12,14},{14,16},{16,18},{18... | collective-permute-start | bytes 73736 | tf_op jit(solution)/shard_map/ppermute | solution.py:561
  16.0 0.8 collective-permute-done.lead_ref
  16.8 0.0 copy-start.5
  16.8 0.6 copy-done.5
  17.4 4.8 %shard_map.144 = (bf16[16,2,128,128]{3,2,1,0:T(8,128)(2,1)}, f32[3,128,2048]{2,1,0:T(8,128)}) custom-call(bf16[128,2048]{1,0:T(8,128)(2,1)} %q_ref.3, bf16[128,2048]{1,0:T(8,128)(2,1)} %k_ref.3, bf16[128,2048]{1,0:T(8,128)(2,1)} %v_ref.3, bf16[128,2048]{1,0:T(8,128)(2,1)} %grad_ref.3, bf16[6,2048]{1,0:T(8,128)(2,1)} %copy-done.5, f32[3,2048]{1,0:T(4,128)} %taps_ref.5), custom_call_target="tpu_custom_call" | custom-call | tf_op jit(solution)/shard_map/pallas_call | solution.py:271
  22.2 3.5 %all-to-all-done.1 = bf16[16,1,128,128]{3,2,1,0:T(8,128)(2,1)S(1)} async-done(((bf16[16,1,128,128]{3,2,1,0:T(8,128)(2,1)}), bf16[16,1,128,128]{3,2,1,0:T(8,128)(2,1)S(1)}, u32[]{:S(2)}, u32[]{:S(2)}) %all-to-all-start.1) | async-done | bytes 524320 | tf_op jit(solution)/shard_map/all_to_all | solution.py:505
  25.7 0.0 copy-start.4
  25.7 9.4 %all-to-all-start = ((bf16[16,2,128,128]{3,2,1,0:T(8,128)(2,1)}), bf16[16,2,128,128]{3,2,1,0:T(8,128)(2,1)S(1)}, u32[]{:S(2)}, u32[]{:S(2)}) async-start(bf16[16,2,128,128]{3,2,1,0:T(8,128)(2,1)} %get-tuple-element.38), calls=%async_computation | async-start | bytes 2097152 | tf_op jit(solution)/shard_map/all_to_all | solution.py:505
  35.2 0.0 copy-done.4
  35.2 7.6 %shard_map.146.filter_hbm = f32[512,1024]{1,0:T(8,128)} custom-call(bf16[16,128,128]{2,1,0:T(8,128)(2,1)} %bitcast.13, f32[256,16]{1,0:T(8,128)} %constant.34.clone.column_ref, bf16[2,512,512]{2,1,0:T(8,128)(2,1)} %constant.33.clone.matrix_hbm), custom_call_target="tpu_custom_call" | custom-call | tf_op jit(solution)/shard_map/pallas_call | solution.py:271
  42.8 15.3 %all-to-all-done.signals_ref = bf16[16,2,128,128]{3,2,1,0:T(8,128)(2,1)S(1)} async-done(((bf16[16,2,128,128]{3,2,1,0:T(8,128)(2,1)}), bf16[16,2,128,128]{3,2,1,0:T(8,128)(2,1)S(1)}, u32[]{:S(2)}, u32[]{:S(2)}) %all-to-all-start) | async-done | bytes 1048608 | tf_op jit(solution)/shard_map/all_to_all | solution.py:505
  58.1 0.0 copy-start.3
  58.1 1.0 copy-done.3
  59.1 18.9 %shard_map.147 = (bf16[16,2,128,128]{3,2,1,0:T(8,128)(2,1)}, bf16[1536,1024]{1,0:T(8,128)(2,1)}) custom-call(bf16[16,2,128,128]{3,2,1,0:T(8,128)(2,1)} %copy-done.3, f32[256,16]{1,0:T(8,128)} %constant.34.clone.column_ref, bf16[2,512,512]{2,1,0:T(8,128)(2,1)} %constant.33.clone.matrix_hbm, f32[512,1024]{1,0:T(8,128)} %shard_map.146.filter_hbm), custom_call_target="tpu_custom_call" | custom-call | tf_op jit(solution)/shard_map/pallas_call | solution.py:271
  78.0 6.9 %all-to-all-start.2 = ((bf16[16,2,128,128]{3,2,1,0:T(8,128)(2,1)}), bf16[16,2,128,128]{3,2,1,0:T(8,128)(2,1)S(1)}, u32[]{:S(2)}, u32[]{:S(2)}) async-start(bf16[16,2,128,128]{3,2,1,0:T(8,128)(2,1)} %get-tuple-element.39), calls=%async_computation.2 | async-start | bytes 2097152 | tf_op jit(solution)/shard_map/all_to_all | solution.py:505
  84.8 6.9 %shard_map.150 = (bf16[16,128,128]{2,1,0:T(8,128)(2,1)}, f32[16,128]{1,0:T(8,128)}) custom-call(bf16[1536,1024]{1,0:T(8,128)(2,1)} %get-tuple-element.49.split_hbm, f32[256,16]{1,0:T(8,128)} %constant.34.clone.column_ref, bf16[2,512,512]{2,1,0:T(8,128)(2,1)} %constant.33.clone.matrix_hbm), custom_call_target="tpu_custom_call" | custom-call | tf_op jit(solution)/shard_map/pallas_call | solution.py:271
  91.7 0.7 reduce_sum.27
  92.4 15.4 %all-to-all-done.2.long_ref = bf16[16,2,128,128]{3,2,1,0:T(8,128)(2,1)S(1)} async-done(((bf16[16,2,128,128]{3,2,1,0:T(8,128)(2,1)}), bf16[16,2,128,128]{3,2,1,0:T(8,128)(2,1)S(1)}, u32[]{:S(2)}, u32[]{:S(2)}) %all-to-all-start.2) | async-done | bytes 1048608 | tf_op jit(solution)/shard_map/all_to_all | solution.py:505
  107.8 0.0 copy-start.2
  107.8 1.0 copy-done.2
  108.8 0.0 copy-start
  108.8 6.1 %shard_map.148 = (bf16[128,2048]{1,0:T(8,128)(2,1)}, bf16[128,2048]{1,0:T(8,128)(2,1)}, bf16[128,2048]{1,0:T(8,128)(2,1)}, bf16[128,2048]{1,0:T(8,128)(2,1)}, f32[3,4,2048]{2,1,0:T(4,128)}, /*index=5*/f32[4,2048]{1,0:T(4,128)}) custom-call(bf16[128,2048]{1,0:T(8,128)(2,1)} %q_ref.3, bf16[128,2048]{1,0:T(8,128)(2,1)} %k_ref.3, bf16[128,2048]{1,0:T(8,128)(2,1)} %v_ref.3, ...), custom_call_target="tpu_custom_call" | custom-call | tf_op jit(solution)/shard_map/pallas_call | solution.py:271
  114.8 0.8 select_maximum_fusion
  115.6 0.7 collective-permute-start.2
  116.3 6.6 %all-to-all-start.3 = ((bf16[16,1,128,128]{3,2,1,0:T(8,128)(2,1)}), bf16[16,1,128,128]{3,2,1,0:T(8,128)(2,1)S(1)}, u32[]{:S(2)}, u32[]{:S(2)}) async-start(bf16[16,1,128,128]{3,2,1,0:T(8,128)(2,1)} %bitcast.6), calls=%async_computation.3 | async-start | bytes 1048576 | tf_op jit(solution)/shard_map/all_to_all | solution.py:505
  122.8 0.0 collective-permute-done.2
  122.9 0.8 fusion.1
  123.6 2.0 %collective-permute-start.3 = (f32[4,2176]{1,0:T(4,128)S(1)}, f32[4,2176]{1,0:T(4,128)S(1)}, u32[]{:S(2)}, u32[]{:S(2)}) collective-permute-start(f32[4,2176]{1,0:T(4,128)S(1)} %fusion.1), channel_id=1, source_target_pairs={{0,4},{2,6},{4,0},{6,2},{8,12},{10,14},{12,8},{14,10},{16,20},{18,... | collective-permute-start | bytes 104456 | tf_op jit(solution)/shard_map/ppermute | solution.py:529
  125.6 4.0 %collective-permute-done.3 = f32[4,2176]{1,0:T(4,128)S(1)} collective-permute-done((f32[4,2176]{1,0:T(4,128)S(1)}, f32[4,2176]{1,0:T(4,128)S(1)}, u32[]{:S(2)}, u32[]{:S(2)}) %collective-permute-start.3) | collective-permute-done | bytes 34848 | tf_op jit(solution)/shard_map/ppermute | solution.py:529
  129.6 0.1 collective-permute-start.4
  129.7 4.3 %collective-permute-done.4 = f32[4,2176]{1,0:T(4,128)S(1)} collective-permute-done((f32[4,2176]{1,0:T(4,128)S(1)}, f32[4,2176]{1,0:T(4,128)S(1)}, u32[]{:S(2)}, u32[]{:S(2)}) %collective-permute-start.4) | collective-permute-done | bytes 34848 | tf_op jit(solution)/shard_map/ppermute | solution.py:529
  134.0 3.7 %collective-permute-start.5 = (f32[4,2176]{1,0:T(4,128)S(1)}, f32[4,2176]{1,0:T(4,128)S(1)}, u32[]{:S(2)}, u32[]{:S(2)}) collective-permute-start(f32[4,2176]{1,0:T(4,128)S(1)} %add.24), channel_id=1, source_target_pairs={{0,16},{2,18},{4,20},{6,22},{8,24},{10,26},{12,28},{14,30},{16,0},... | collective-permute-start | bytes 104456 | tf_op jit(solution)/shard_map/ppermute | solution.py:529
  137.7 0.9 slice.36
  138.6 1.3 collective-permute-start.1
  139.9 0.0 collective-permute-done.5
  139.9 0.6 fusion
  140.6 0.6 slice_reduce_fusion
  142.5 1.6 %collective-permute-start.6 = (f32[1,128]{1,0:T(1,128)S(1)}, f32[1,128]{1,0:T(1,128)S(1)}, u32[]{:S(2)}, u32[]{:S(2)}) collective-permute-start(f32[1,128]{1,0:T(1,128)S(1)} %broadcast_in_dim.11), channel_id=1, source_target_pairs={{0,1},{1,0},{2,3},{3,2},{4,5},{5,4},{6,7},{7,6},{8,9},{9,8},{10,11... | collective-permute-start | bytes 1544 | tf_op jit(solution)/shard_map/ppermute | solution.py:529
  144.1 0.0 collective-permute-done.1.tail_ref
  144.1 0.0 copy-done
  144.1 0.0 copy-start.1
  144.1 0.9 copy-done.1
  145.0 1.6 %shard_map.149 = (bf16[128,2048]{1,0:T(8,128)(2,1)}, bf16[128,2048]{1,0:T(8,128)(2,1)}, bf16[128,2048]{1,0:T(8,128)(2,1)}) custom-call(f32[3,4,2048]{2,1,0:T(4,128)S(1)} %copy-done.1, f32[3,2,2048]{2,1,0:T(2,128)S(1)} %collective-permute-done.1.tail_ref, f32[3,2048]{1,0:T(4,128)S(1)} %copy-done, ...), custom_call_target="tpu_custom_call", output_to_operand_aliasing={{0}: (3, {}), {1}: (4, {}), {2}: (5, {})} | custom-call | tf_op jit(solution)/shard_map/pallas_call | solution.py:271
  146.6 0.0 collective-permute-done.6
  146.6 0.0 all-to-all-done.3
  146.6 1.1 shard_map.151
  (6 shorter events, 0.1 us)
Async XLA Ops:
  3.9 21.8 %all-to-all-start.1 = ((bf16[16,1,128,128]{3,2,1,0:T(8,128)(2,1)}), bf16[16,1,128,128]{3,2,1,0:T(8,128)(2,1)S(1)}, u32[]{:S(2)}, u32[]{:S(2)}) async-start(bf16[16,1,128,128]{3,2,1,0:T(8,128)(2,1)} %bitcast.12), calls=%async_computation.1 | async-start | bytes 1048576 | tf_op jit(solution)/shard_map/all_to_all | solution.py:505
  13.6 3.2 %collective-permute-start = (bf16[6,2048]{1,0:T(8,128)(2,1)S(1)}, bf16[6,2048]{1,0:T(8,128)(2,1)S(1)}, u32[]{:S(2)}, u32[]{:S(2)}) collective-permute-start(bf16[6,2048]{1,0:T(8,128)(2,1)S(1)} %pad_maximum_fusion), channel_id=1, source_target_pairs={{0,2},{2,4},{4,6},{6,8},{8,10},{10,12},{12,14},{14,16},{16,18},{18... | collective-permute-start | bytes 73736 | tf_op jit(solution)/shard_map/ppermute | solution.py:561
  16.8 0.6 copy-start.5
  25.7 9.4 %copy-start.4 = (bf16[16,1,128,128]{3,2,1,0:T(8,128)(2,1)}, bf16[16,1,128,128]{3,2,1,0:T(8,128)(2,1)S(1)}, u32[]{:S(2)}) copy-start(bf16[16,1,128,128]{3,2,1,0:T(8,128)(2,1)S(1)} %all-to-all-done.1) | copy-start | bytes 1572868
  25.7 32.4 %all-to-all-start = ((bf16[16,2,128,128]{3,2,1,0:T(8,128)(2,1)}), bf16[16,2,128,128]{3,2,1,0:T(8,128)(2,1)S(1)}, u32[]{:S(2)}, u32[]{:S(2)}) async-start(bf16[16,2,128,128]{3,2,1,0:T(8,128)(2,1)} %get-tuple-element.38), calls=%async_computation | async-start | bytes 2097152 | tf_op jit(solution)/shard_map/all_to_all | solution.py:505
  58.1 1.0 copy-start.3
  78.0 29.8 %all-to-all-start.2 = ((bf16[16,2,128,128]{3,2,1,0:T(8,128)(2,1)}), bf16[16,2,128,128]{3,2,1,0:T(8,128)(2,1)S(1)}, u32[]{:S(2)}, u32[]{:S(2)}) async-start(bf16[16,2,128,128]{3,2,1,0:T(8,128)(2,1)} %get-tuple-element.39), calls=%async_computation.2 | async-start | bytes 2097152 | tf_op jit(solution)/shard_map/all_to_all | solution.py:505
  107.8 1.0 copy-start.2
  108.8 35.3 %copy-start = (f32[3,2048]{1,0:T(4,128)S(1)}, f32[3,2048]{1,0:T(4,128)}, u32[]{:S(2)}) copy-start(f32[3,2048]{1,0:T(4,128)} %taps_ref.5) | copy-start | bytes 73732
  115.6 7.2 %collective-permute-start.2 = (f32[4,2176]{1,0:T(4,128)S(1)}, f32[4,2176]{1,0:T(4,128)S(1)}, u32[]{:S(2)}, u32[]{:S(2)}) collective-permute-start(f32[4,2176]{1,0:T(4,128)S(1)} %select_maximum_fusion), channel_id=1, source_target_pairs={{0,2},{2,0},{4,6},{6,4},{8,10},{10,8},{12,14},{14,12},{16,18},{18,... | collective-permute-start | bytes 104456 | tf_op jit(solution)/shard_map/ppermute | solution.py:529
  116.3 30.3 %all-to-all-start.3 = ((bf16[16,1,128,128]{3,2,1,0:T(8,128)(2,1)}), bf16[16,1,128,128]{3,2,1,0:T(8,128)(2,1)S(1)}, u32[]{:S(2)}, u32[]{:S(2)}) async-start(bf16[16,1,128,128]{3,2,1,0:T(8,128)(2,1)} %bitcast.6), calls=%async_computation.3 | async-start | bytes 1048576 | tf_op jit(solution)/shard_map/all_to_all | solution.py:505
  123.6 6.0 %collective-permute-start.3 = (f32[4,2176]{1,0:T(4,128)S(1)}, f32[4,2176]{1,0:T(4,128)S(1)}, u32[]{:S(2)}, u32[]{:S(2)}) collective-permute-start(f32[4,2176]{1,0:T(4,128)S(1)} %fusion.1), channel_id=1, source_target_pairs={{0,4},{2,6},{4,0},{6,2},{8,12},{10,14},{12,8},{14,10},{16,20},{18,... | collective-permute-start | bytes 104456 | tf_op jit(solution)/shard_map/ppermute | solution.py:529
  129.6 4.4 %collective-permute-start.4 = (f32[4,2176]{1,0:T(4,128)S(1)}, f32[4,2176]{1,0:T(4,128)S(1)}, u32[]{:S(2)}, u32[]{:S(2)}) collective-permute-start(f32[4,2176]{1,0:T(4,128)S(1)} %add.23), channel_id=1, source_target_pairs={{0,8},{2,10},{4,12},{6,14},{8,0},{10,2},{12,4},{14,6},{16,24},{18,... | collective-permute-start | bytes 104456 | tf_op jit(solution)/shard_map/ppermute | solution.py:529
  134.0 5.9 %collective-permute-start.5 = (f32[4,2176]{1,0:T(4,128)S(1)}, f32[4,2176]{1,0:T(4,128)S(1)}, u32[]{:S(2)}, u32[]{:S(2)}) collective-permute-start(f32[4,2176]{1,0:T(4,128)S(1)} %add.24), channel_id=1, source_target_pairs={{0,16},{2,18},{4,20},{6,22},{8,24},{10,26},{12,28},{14,30},{16,0},... | collective-permute-start | bytes 104456 | tf_op jit(solution)/shard_map/ppermute | solution.py:529
  138.6 5.4 %collective-permute-start.1 = (f32[3,2,2048]{2,1,0:T(2,128)S(1)}, f32[3,2,2048]{2,1,0:T(2,128)S(1)}, u32[]{:S(2)}, u32[]{:S(2)}) collective-permute-start(f32[3,2,2048]{2,1,0:T(2,128)S(1)} %slice.36), channel_id=1, source_target_pairs={{2,0},{4,2},{6,4},{8,6},{10,8},{12,10},{14,12},{16,14},{18,16},{20... | collective-permute-start | bytes 147464 | tf_op jit(solution)/shard_map/ppermute | solution.py:607
  142.5 4.1 %collective-permute-start.6 = (f32[1,128]{1,0:T(1,128)S(1)}, f32[1,128]{1,0:T(1,128)S(1)}, u32[]{:S(2)}, u32[]{:S(2)}) collective-permute-start(f32[1,128]{1,0:T(1,128)S(1)} %broadcast_in_dim.11), channel_id=1, source_target_pairs={{0,1},{1,0},{2,3},{3,2},{4,5},{5,4},{6,7},{7,6},{8,9},{9,8},{10,11... | collective-permute-start | bytes 1544 | tf_op jit(solution)/shard_map/ppermute | solution.py:529
  144.1 0.9 copy-start.1

commit v3 on v0

v3 whole, which is shorter than its diff:
```python
import functools
import math

import jax
import jax.numpy as jnp
import ml_dtypes
import numpy as np
from jax import lax
from jax.experimental import pallas as pl
from jax.experimental.pallas import tpu as pltpu
from jax.sharding import PartitionSpec as P

LANES = 128
SPAN = 256
BOTH = 2 * SPAN
CHUNK = 16
CHUNKS = SPAN // CHUNK
PAD = 8
ROWS = 32
PASSES = 2
VMEM_BYTES = 60 * 1024 * 1024
SMALL_VMEM_BYTES = 8 * 1024 * 1024

f32 = jnp.float32
bf16 = jnp.bfloat16

IN_VMEM = pl.BlockSpec(memory_space=pltpu.VMEM)
IN_SMEM = pl.BlockSpec(memory_space=pltpu.SMEM)
ANYWHERE = pl.BlockSpec(memory_space=pl.ANY)


def call(kernel, outs, scratch, *args, vmem_bytes=VMEM_BYTES, **options):
    return pl.pallas_call(
        kernel,
        out_shape=outs,
        scratch_shapes=scratch,
        compiler_params=pltpu.CompilerParams(vmem_limit_bytes=vmem_bytes),
        **options,
    )(*args)


def leaf_phases(count):
    return [(4 * leaf + 1) / (4 * count) for leaf in range(count)]


def root_times(re, im, num, den, sign):
    if num == 0:
        return re, im
    if 4 * num == den:
        return (im, -re) if sign < 0 else (-im, re)
    cosine = math.cos(2.0 * math.pi * num / den)
    sine = sign * math.sin(2.0 * math.pi * num / den)
    if 8 * num == den:
        return ((re + im) * cosine, (im - re) * cosine) if sign < 0 else ((re - im) * cosine, (re + im) * cosine)
    if 8 * num == 3 * den:
        return ((re - im) * cosine, (re + im) * cosine) if sign < 0 else ((re + im) * cosine, (im - re) * cosine)
    return re * cosine - im * sine, im * cosine + re * sine


def short_fft(values, sign):
    count = len(values)
    if count == 1:
        return values
    even = short_fft(values[0::2], sign)
    odd = short_fft(values[1::2], sign)
    first = []
    second = []
    for num in range(count // 2):
        re, im = root_times(*odd[num], num, count, sign)
        first.append((even[num][0] + re, even[num][1] + im))
        second.append((even[num][0] - re, even[num][1] - im))
    return first + second


def to_leaves(parts):
    count = len(parts)
    turned = []
    for idx, part in enumerate(parts):
        angle = 2.0 * math.pi * idx / (4 * count)
        turned.append((part * math.cos(angle), part * (-math.sin(angle))) if idx else (part, jnp.zeros_like(part)))
    return short_fft(turned, -1)


def from_leaves(leaves, scale):
    count = len(leaves)
    parts = []
    for idx, (re, im) in enumerate(short_fft(leaves, 1)):
        angle = 2.0 * math.pi * idx / (4 * count)
        if idx == 0:
            parts.append(re * scale)
        else:
            parts.append(re * (math.cos(angle) * scale) - im * (math.sin(angle) * scale))
    return parts


def dft_matrix():
    idx = np.arange(SPAN)
    angle = (idx[:, None] * idx[None, :] % SPAN) * (2.0 * np.pi / SPAN)
    cosine, sine = np.cos(angle), np.sin(angle)
    return np.block([[cosine, sine], [-sine, cosine]])


def twist_angles(outer, inner):
    return np.asarray(leaf_phases(outer))[:, None] * np.asarray(inner)[None, :] * (2.0 * np.pi / SPAN)


def matrix_blocks():
    matrix = dft_matrix()
    high = matrix.astype(ml_dtypes.bfloat16)
    low = (matrix - high.astype(np.float64)).astype(ml_dtypes.bfloat16)
    return np.concatenate([high, low, high][:PASSES], axis=1)


def leaf_place(leaf):
    return leaf // 2, slice((leaf % 2) * LANES, (leaf % 2 + 1) * LANES)


def split_store(ref, leaf, row, value):
    pair, lanes = leaf_place(leaf)
    high = value.astype(bf16)
    for block in range(PASSES):
        part = high
        if PASSES == 3 and block == 2:
            part = (value - high.astype(f32)).astype(bf16)
        ref[pair, pl.ds(block * BOTH + row, CHUNK), lanes] = part


def run(stages, matmul=None):
    tiles = matmul[2].shape[0] if matmul else 4

    def step(tile, carry):
        if matmul:
            matrix_ref, split_ref, result_ref = matmul
            result_ref[tile] = jnp.dot(matrix_ref[...], split_ref[tile], preferred_element_type=f32)
        for part in range(CHUNKS // tiles):
            for stage in stages:
                carry = stage(tile * (CHUNKS // tiles) + part, carry)
        return carry

    return step, tiles


def run_all(stages, matmul=None, carry=0):
    step, tiles = run(stages, matmul)
    return lax.fori_loop(0, tiles, step, carry)


def chunk_row(idx):
    return pl.multiple_of(idx * CHUNK, CHUNK)


def twist_stage(coarse_ref, fine_ref, twist_ref):
    outer = twist_ref.shape[1]

    def stage(idx, carry):
        here = pl.ds(chunk_row(idx), CHUNK)
        for leaf in range(outer):
            far_cosine = coarse_ref[idx, leaf]
            far_sine = coarse_ref[idx, outer + leaf]
            cosine = fine_ref[0, leaf]
            sine = fine_ref[1, leaf]
            twist_ref[0, leaf, here, :] = far_cosine * cosine - far_sine * sine
            twist_ref[1, leaf, here, :] = far_sine * cosine + far_cosine * sine
        return carry

    return stage


def piece_place(idx, part, rows_here):
    ratio = SPAN // rows_here
    in_piece = rows_here // CHUNK
    return part * ratio + idx // in_piece, pl.ds(chunk_row(idx % in_piece), CHUNK)


def leaves_stage(signals_ref, kind, twist_ref, split_ref):
    outer = twist_ref.shape[1]
    rows_here = signals_ref.shape[2]

    def stage(idx, carry):
        row = chunk_row(idx)
        parts = []
        for part in range(outer):
            piece, rows = piece_place(idx, part, rows_here)
            parts.append(signals_ref[piece, kind, rows, :].astype(f32))
        for leaf, (re, im) in enumerate(to_leaves(parts)):
            cosine = twist_ref[0, leaf, pl.ds(row, CHUNK), :]
            sine = twist_ref[1, leaf, pl.ds(row, CHUNK), :]
            split_store(split_ref, leaf, row, re * cosine + im * sine)
            split_store(split_ref, leaf, SPAN + row, im * cosine - re * sine)
        return carry

    return stage


def combine_stage(left_ref, right_ref, split_ref, conjugate):
    def stage(idx, carry):
        row = chunk_row(idx)
        for leaf in range(2 * left_ref.shape[0]):
            pair, lanes = leaf_place(leaf)
            left_re = left_ref[pair, pl.ds(row, CHUNK), lanes]
            left_im = left_ref[pair, pl.ds(SPAN + row, CHUNK), lanes]
            right_re = right_ref[pair, pl.ds(row, CHUNK), lanes]
            right_im = right_ref[pair, pl.ds(SPAN + row, CHUNK), lanes]
            if conjugate:
                re = left_re * right_re + left_im * right_im
                minus_im = left_im * right_re - left_re * right_im
            else:
                re = left_re * right_re - left_im * right_im
                minus_im = -(left_re * right_im + left_im * right_re)
            split_store(split_ref, leaf, row, re)
            split_store(split_ref, leaf, SPAN + row, minus_im)
        return carry

    return stage


def signal_stage(time_ref, twist_ref, rows_here, write):
    outer = twist_ref.shape[1]
    scale = 1.0 / (SPAN * outer)

    def stage(idx, carry):
        row = chunk_row(idx)
        leaves = []
        for leaf in range(outer):
            pair, lanes = leaf_place(leaf)
            cosine = twist_ref[0, leaf, pl.ds(row, CHUNK), :]
            sine = twist_ref[1, leaf, pl.ds(row, CHUNK), :]
            re = time_ref[pair, pl.ds(row, CHUNK), lanes]
            minus_im = time_ref[pair, pl.ds(SPAN + row, CHUNK), lanes]
            leaves.append((re * cosine + minus_im * sine, re * sine - minus_im * cosine))
        for part, value in enumerate(from_leaves(leaves, scale)):
            piece, rows = piece_place(idx, part, rows_here)
            carry = write(piece, rows, value, carry)
        return carry

    return stage


def products_kernel(
    signals_hbm, coarse_ref, fine_ref, matrix_hbm, results_hbm, lag_hbm,
    twist_ref, matrix_ref, signals_ref, results_ref, one_split, two_split, lag_split,
    filter_ref, product_ref, cotan_ref, time_ref, sems,
):
    rows_here = signals_ref.shape[2]
    arrivals = [
        pltpu.make_async_copy(signals_hbm.at[:, kind], signals_ref.at[:, kind], sems.at[kind]) for kind in range(3)
    ]
    matrix_copy = pltpu.make_async_copy(matrix_hbm, matrix_ref, sems.at[3])
    lag_copy = pltpu.make_async_copy(lag_split, lag_hbm, sems.at[4])
    returns = [
        pltpu.make_async_copy(results_ref.at[:, kind], results_hbm.at[:, kind], sems.at[5 + kind]) for kind in range(2)
    ]

    def leaves(kind, split_ref):
        return leaves_stage(signals_ref, kind, twist_ref, split_ref)

    def result(kind, from_ref):
        def write(piece, rows, value, carry):
            results_ref[piece, kind, rows, :] = value.astype(bf16)
            return carry

        return signal_stage(from_ref, twist_ref, rows_here, write)

    for copy in (arrivals[2], arrivals[0], matrix_copy, arrivals[1]):
        copy.start()
    run_all([twist_stage(coarse_ref, fine_ref, twist_ref)])
    arrivals[2].wait()
    run_all([leaves(2, one_split)])
    arrivals[0].wait()
    matrix_copy.wait()
    run_all([leaves(0, two_split)], (matrix_ref, one_split, filter_ref))
    arrivals[1].wait()
    run_all([leaves(1, one_split)], (matrix_ref, two_split, product_ref))
    run_all([combine_stage(filter_ref, product_ref, two_split, False)], (matrix_ref, one_split, cotan_ref))
    run_all([combine_stage(filter_ref, cotan_ref, one_split, True)], (matrix_ref, two_split, time_ref))
    run_all([combine_stage(product_ref, cotan_ref, lag_split, True), result(0, time_ref)], (matrix_ref, one_split, filter_ref))
    lag_copy.start()
    returns[0].start()
    run_all([result(1, filter_ref)])
    returns[1].start()
    lag_copy.wait()
    returns[0].wait()
    returns[1].wait()


def lag_kernel(
    split_hbm, coarse_ref, fine_ref, matrix_hbm, lag_ref, square_ref, twist_ref, matrix_ref, split_ref, time_ref, sems
):
    copies = [
        pltpu.make_async_copy(matrix_hbm, matrix_ref, sems.at[0]),
        pltpu.make_async_copy(split_hbm, split_ref, sems.at[1]),
    ]
    for copy in copies:
        copy.start()
    for copy in copies:
        copy.wait()
    run_all([twist_stage(coarse_ref, fine_ref, twist_ref)], (matrix_ref, split_ref, time_ref))

    def write(piece, rows, value, carry):
        lag_ref[piece, rows, :] = value.astype(bf16)
        return carry + value * value

    square_ref[...] = run_all(
        [signal_stage(time_ref, twist_ref, lag_ref.shape[1], write)], None, jnp.zeros((CHUNK, LANES), f32)
    )


class Transforms:
    def __init__(self, pieces, rows_here):
        outer = pieces * rows_here // SPAN
        pairs = outer // 2
        self.matrix = jnp.asarray(matrix_blocks())
        coarse = twist_angles(outer, CHUNK * np.arange(CHUNKS)).T
        self.coarse = jnp.asarray(np.concatenate([np.cos(coarse), np.sin(coarse)], axis=1), f32)
        fine = twist_angles(outer, np.arange(CHUNK))
        fine = jnp.asarray(np.stack([np.cos(fine), np.sin(fine)]), f32)[..., None]
        self.fine = jnp.broadcast_to(fine, fine.shape[:3] + (LANES,))
        self.split = jax.ShapeDtypeStruct((pairs, PASSES * BOTH, 2 * LANES), bf16)
        self.signal = jax.ShapeDtypeStruct((pieces, rows_here, LANES), bf16)
        self.result = jax.ShapeDtypeStruct((pieces, 2, rows_here, LANES), bf16)
        self.square = jax.ShapeDtypeStruct((CHUNK, LANES), f32)
        self.signals_work = pltpu.VMEM((pieces, 3, rows_here, LANES), bf16)
        self.results_work = pltpu.VMEM(self.result.shape, bf16)
        self.work = pltpu.VMEM((pairs, BOTH, 2 * LANES), f32)
        self.split_work = pltpu.VMEM(self.split.shape, bf16)
        self.tables = [pltpu.VMEM((2, outer, SPAN, LANES), f32), pltpu.VMEM(self.matrix.shape, bf16)]

    def products(self, signals):
        return call(
            products_kernel, (self.result, self.split),
            self.tables
            + [self.signals_work, self.results_work]
            + [self.split_work] * 3
            + [self.work] * 4
            + [pltpu.SemaphoreType.DMA((7,))],
            signals, self.coarse, self.fine, self.matrix,
            in_specs=[ANYWHERE, IN_SMEM, IN_VMEM, ANYWHERE],
            out_specs=(ANYWHERE, ANYWHERE),
        )

    def lag(self, lag_split):
        return call(
            lag_kernel, (self.signal, self.square),
            self.tables + [self.split_work, self.work, pltpu.SemaphoreType.DMA((2,))],
            lag_split, self.coarse, self.fine, self.matrix,
            in_specs=[ANYWHERE, IN_SMEM, IN_VMEM, ANYWHERE],
            out_specs=(IN_VMEM, IN_VMEM),
        )


class PlainTransforms:
    def __init__(self, pieces, rows_here):
        self.seq_len = pieces * rows_here
        self.pieces = pieces
        self.outer = self.seq_len // SPAN
        idx = np.arange(SPAN)
        angle = (idx[:, None] * idx[None, :] % SPAN) * (2.0 * np.pi / SPAN)
        self.cosine = jnp.asarray(np.cos(angle), f32)
        self.sine = jnp.asarray(np.sin(angle), f32)
        twist = twist_angles(self.outer, idx)
        self.twist = jnp.asarray(np.stack([np.cos(twist), np.sin(twist)]), f32)[..., None]

    def dot(self, matrix, signal):
        return jnp.einsum("fs,tsc->tfc", matrix, signal, precision=lax.Precision.HIGHEST)

    def spectrum(self, signal):
        parts = signal.astype(f32).reshape(self.outer, SPAN, -1)
        leaves = to_leaves([parts[part] for part in range(self.outer)])
        re = jnp.stack([leaf[0] for leaf in leaves])
        im = jnp.stack([leaf[1] for leaf in leaves])
        twist_re = re * self.twist[0] + im * self.twist[1]
        twist_im = im * self.twist[0] - re * self.twist[1]
        return (
            self.dot(self.cosine, twist_re) + self.dot(self.sine, twist_im),
            self.dot(self.cosine, twist_im) - self.dot(self.sine, twist_re),
        )

    def back(self, re, im):
        time_re = self.dot(self.cosine, re) - self.dot(self.sine, im)
        time_im = self.dot(self.cosine, im) + self.dot(self.sine, re)
        leaf_re = time_re * self.twist[0] - time_im * self.twist[1]
        leaf_im = time_im * self.twist[0] + time_re * self.twist[1]
        parts = from_leaves([(leaf_re[leaf], leaf_im[leaf]) for leaf in range(self.outer)], 1.0 / self.seq_len)
        return jnp.stack(parts).reshape(self.pieces, self.seq_len // self.pieces, -1)

    def products(self, signals):
        product, cotan, taps = (self.spectrum(signals[:, kind]) for kind in range(3))
        conv = self.back(taps[0] * product[0] - taps[1] * product[1], taps[0] * product[1] + taps[1] * product[0])
        corr = self.back(taps[0] * cotan[0] + taps[1] * cotan[1], taps[0] * cotan[1] - taps[1] * cotan[0])
        lag = (
            product[0] * cotan[0] + product[1] * cotan[1],
            product[0] * cotan[1] - product[1] * cotan[0],
        )
        return jnp.stack([conv, corr], axis=1).astype(bf16), lag

    def lag(self, lag_spec):
        lag = self.back(*lag_spec)
        return lag.astype(bf16), jnp.sum(lag * lag, axis=(0, 1))[None, :]


def group(idx):
    return pl.ds(pl.multiple_of(idx * LANES, LANES), LANES)


def streamed(work, steps, per_step, places, in_count, out_count, *refs):
    hbm = refs[: in_count + out_count]
    held = refs[in_count + out_count : 2 * (in_count + out_count)]
    scratch = refs[2 * (in_count + out_count) : -1]
    sems = refs[-1]

    def copy(place, step):
        outside = hbm[place].at[places[place][0](step)]
        inside = held[place].at[places[place][1](step)]
        ends = (outside, inside) if place < in_count else (inside, outside)
        return pltpu.make_async_copy(*ends, sems.at[place, step])

    for step in range(steps):
        for place in range(in_count):
            copy(place, step).start()
    for step in range(steps):
        for place in range(in_count):
            copy(place, step).wait()

        def one(idx, carry):
            work(idx, held[:in_count], held[in_count:], scratch)
            return carry

        lax.fori_loop(step * per_step, (step + 1) * per_step, one, 0)
        for place in range(in_count, in_count + out_count):
            copy(place, step).start()
    for step in range(steps):
        for place in range(in_count, in_count + out_count):
            copy(place, step).wait()


def stream_call(work, steps, per_step, operands, results, scratch=(), aliases=None):
    arrays = [operand[0] for operand in operands]
    shapes = [jax.ShapeDtypeStruct(array.shape, array.dtype) for array in arrays] + [result[0] for result in results]
    cuts = [entry[1] for entry in operands] + [entry[1] for entry in results]
    held = [pltpu.VMEM(entry[2] or shape.shape, shape.dtype) for entry, shape in zip(operands + results, shapes)]
    extra = list(aliases or ())
    kernel = functools.partial(streamed, work, steps, per_step, cuts, len(arrays), len(results))

    def with_aliases(*refs):
        kernel(*refs[: len(arrays)], *refs[len(arrays) + len(extra) :])

    return call(
        with_aliases,
        tuple(result[0] for result in results),
        held + list(scratch) + [pltpu.SemaphoreType.DMA((len(shapes), steps))],
        *arrays, *extra,
        in_specs=[ANYWHERE] * (len(arrays) + len(extra)),
        out_specs=(ANYWHERE,) * len(results),
        input_output_aliases={len(arrays) + idx: idx for idx in range(len(extra))},
    )


def cut_lanes(width, rank):
    def place(step):
        return (slice(None),) * (rank - 1) + (pl.ds(step * width, width),)

    return place, place


def cut_groups(per_step, kinds=None):
    def outside(step):
        here = pl.ds(step * per_step, per_step)
        return (here,) if kinds is None else (here, kinds)

    def inside(step):
        return (pl.ds(step * per_step, per_step),)

    return outside, inside


def row_blocks(rows_here):
    return [slice(start, start + ROWS) for start in range(0, rows_here, ROWS)]


def pack_work(idx, operands, results, scratch):
    results[0][idx] = operands[0][:, group(idx)].astype(bf16)


def extend_rows(lead, in_ref, lanes, ext_ref):
    ext_ref[PAD - lead.shape[0] : PAD, :] = lead
    ext_ref[PAD:, :] = in_ref[:, lanes].astype(f32)


def short_conv(ext_ref, taps, rows):
    result = None
    for shift_idx in range(taps.shape[0]):
        term = taps[shift_idx : shift_idx + 1] * ext_ref[PAD + rows.start - shift_idx : PAD + rows.stop - shift_idx, :]
        result = term if result is None else result + term
    return result


def extend_three(idx, operands, lead_ref, halo_rows, exts):
    lead = lead_ref[:, group(idx)]
    for place, ext in enumerate(exts):
        extend_rows(lead[place * halo_rows : (place + 1) * halo_rows], operands[place], group(idx), ext)


def signals_work(idx, operands, results, exts):
    q_ref, k_ref, v_ref, grad_ref, lead_ref, taps_ref = operands
    taps = taps_ref[:, group(idx)]
    extend_three(idx, operands, lead_ref, taps.shape[0] - 1, exts)
    for rows in row_blocks(q_ref.shape[0]):
        q_short, k_short, v_short = (short_conv(ext, taps, rows) for ext in exts)
        results[0][idx, 0, rows, :] = (k_short * v_short).astype(bf16)
        results[0][idx, 1, rows, :] = (grad_ref[rows, group(idx)].astype(f32) * q_short).astype(bf16)


def short_work(idx, operands, results, exts):
    q_ref, k_ref, v_ref, lead_ref, taps_ref = operands
    taps = taps_ref[:, group(idx)]
    extend_three(idx, operands, lead_ref, taps.shape[0] - 1, exts)
    for rows in row_blocks(q_ref.shape[0]):
        for place, ext in enumerate(exts):
            results[0][place, rows, group(idx)] = short_conv(ext, taps, rows)


def fold(value):
    return jnp.sum(value.reshape(-1, 8, LANES), axis=0)


def finish_work(idx, operands, results, exts):
    q_ref, k_ref, v_ref, grad_ref, short_ref, lead_ref, taps_ref, skip_ref, long_ref = operands
    mixed_ref, grad_q_ref, grad_k_ref, grad_v_ref, front_ref, back_ref, sums_ref = results
    lanes = group(idx)
    taps = taps_ref[:, lanes]
    skip = skip_ref[:, lanes]
    lead = lead_ref[:, lanes]
    taps_count = taps.shape[0]
    halo_rows = taps_count - 1
    rows_here = q_ref.shape[0]
    sums = [jnp.zeros((8, LANES), f32) for _ in range(taps_count + 1)]
    for ext in exts:
        ext[rows_here:, :] = jnp.zeros((PAD, LANES), f32)
    for rows in row_blocks(rows_here):
        q_short, k_short, v_short = (short_ref[place, rows, lanes] for place in range(3))
        product = (k_short * v_short).astype(bf16).astype(f32)
        filtered = long_ref[idx, 0, rows, :].astype(f32) + skip * product
        mixed_ref[rows, lanes] = (q_short * filtered).astype(bf16)
        upstream = grad_ref[rows, lanes].astype(f32)
        back_mix = upstream * q_short
        back_prod = long_ref[idx, 1, rows, :].astype(f32) + skip * back_mix
        sums[taps_count] = sums[taps_count] + fold(back_mix * product)
        exts[0][rows, :] = upstream * filtered
        exts[1][rows, :] = back_prod * v_short
        exts[2][rows, :] = back_prod * k_short
    for place, (ext, in_ref, out_ref) in enumerate(
        zip(exts, (q_ref, k_ref, v_ref), (grad_q_ref, grad_k_ref, grad_v_ref))
    ):
        for rows in row_blocks(rows_here):
            signal = in_ref[rows, lanes].astype(f32)
            grad = None
            for shift_idx in range(taps_count):
                ahead = ext[rows.start + shift_idx : rows.stop + shift_idx, :]
                term = taps[shift_idx : shift_idx + 1] * ahead
                grad = term if grad is None else grad + term
                sums[shift_idx] = sums[shift_idx] + fold(ahead * signal)
            out_ref[rows, lanes] = grad.astype(bf16)
        back_ref[place * halo_rows : (place + 1) * halo_rows, lanes] = grad[ROWS - halo_rows :]
        front_ref[place * halo_rows : (place + 1) * halo_rows, lanes] = ext[0:halo_rows, :]
    for shift_idx in range(taps_count + 1):
        total = jnp.sum(sums[shift_idx], axis=0, keepdims=True)
        for place in range(3 if shift_idx < taps_count else 0):
            for row in range(shift_idx):
                at = place * halo_rows + halo_rows - shift_idx + row
                total = total + lead[at : at + 1] * exts[place][row : row + 1, :]
        sums_ref[shift_idx : shift_idx + 1, lanes] = total


def lead_kernel(q_ref, k_ref, v_ref, lead_ref):
    halo_rows = lead_ref.shape[0] // 3
    for place, ref in enumerate((q_ref, k_ref, v_ref)):
        rows = ref[...].astype(f32)
        lead_ref[place * halo_rows : (place + 1) * halo_rows, :] = rows[rows.shape[0] - halo_rows :]


def edges_kernel(back_ref, tail_ref, taps_ref, q_ref, k_ref, v_ref, q_out, k_out, v_out, work_ref):
    taps_count = taps_ref.shape[0]
    halo_rows = taps_count - 1
    block_rows = q_ref.shape[0]
    for place, (ref, out_ref) in enumerate(((q_ref, q_out), (k_ref, k_out), (v_ref, v_out))):
        work_ref[...] = ref[...].astype(f32)
        first = place * halo_rows
        for row in range(halo_rows):
            total = back_ref[first + row : first + row + 1, :]
            for shift_idx in range(halo_rows - row, taps_count):
                source = first + row + shift_idx - halo_rows
                total = total + taps_ref[shift_idx : shift_idx + 1, :] * tail_ref[source : source + 1, :]
            at = block_rows - halo_rows + row
            work_ref[at : at + 1, :] = total
        out_ref[...] = work_ref[...].astype(bf16)


def norm_kernel(*refs):
    values, totals_ref, square_ref = refs[:-2], refs[-2], refs[-1]
    channels = totals_ref.shape[1] - LANES
    totals = values[0][...]
    if len(values) == 4:
        totals = (totals + values[1][...]) + (values[2][...] + values[3][...])
    totals_ref[...] = totals
    square = jnp.sum(totals[:, :channels] * totals[:, :channels]) + jnp.sum(totals[0:1, channels:])
    square_ref[...] = jnp.full(square_ref.shape, square)


def scale_kernel(limit, totals_ref, norm_ref, lag_hbm, taps_out, skip_out, kernel_out, lag_ref, sems):
    taps_count, channels = taps_out.shape
    groups = lag_ref.shape[0]
    per_step = max(groups // 4, 1)
    copies = []
    for step in range(groups // per_step):
        here = pl.ds(step * per_step, per_step)
        copies.append(pltpu.make_async_copy(lag_hbm.at[here], lag_ref.at[here], sems.at[step]))
        copies[step].start()
    factor = limit / jnp.maximum(jnp.sqrt(norm_ref[...]), limit)
    for idx in range(groups):
        lanes = slice(idx * LANES, (idx + 1) * LANES)
        taps_out[:, lanes] = totals_ref[0:taps_count, lanes] * factor
        skip_out[:, lanes] = totals_ref[taps_count : taps_count + 1, lanes] * factor
    for step, copy in enumerate(copies):
        copy.wait()
        for idx in range(step * per_step, (step + 1) * per_step):
            kernel_out[:, idx * LANES : (idx + 1) * LANES] = lag_ref[idx].astype(f32) * factor


def exchange(pieces_first):
    return lax.all_to_all(pieces_first, "ctx", split_axis=0, concat_axis=0, tiled=True)


def to_pieces(groups, pieces):
    count, kinds, rows, lanes = groups.shape
    if count == pieces:
        return groups
    share = count * lanes // pieces
    split = groups.reshape(count, kinds, rows, lanes // share, share)
    return split.transpose(0, 3, 1, 2, 4).reshape(pieces, kinds, rows, share)


def to_groups(parts):
    pieces, kinds, rows, share = parts.shape
    if share == LANES:
        return parts
    joined = parts.reshape(pieces * share // LANES, LANES // share, kinds, rows, share)
    return joined.transpose(0, 2, 3, 1, 4).reshape(-1, kinds, rows, LANES)


def partners(value, axis, steps):
    size = lax.axis_size(axis)
    return [value] + [lax.ppermute(value, axis, [(i, i ^ step) for i in range(size)]) for step in steps]


def rounds_of(size):
    rounds = []
    step = 1
    while step < size:
        rounds.append((step, 2 * step, 3 * step) if size // step >= 4 else (step,))
        step *= 4 if size // step >= 4 else 2
    return rounds


def add_up(values):
    if len(values) == 2:
        return values[0] + values[1]
    return (values[0] + values[1]) + (values[2] + values[3])


def body(q_in, k_in, v_in, grad_out, short_filter, kernel, skip):
    pieces = lax.axis_size("ctx")
    sides = lax.axis_size("ch")
    rows_here, channels = q_in.shape
    seq_len = pieces * rows_here
    taps_count = short_filter.shape[0]
    halo_rows = taps_count - 1
    groups = channels // LANES
    share = channels // pieces
    per_step = min(groups, 4)
    steps = groups // per_step
    lanes2 = cut_lanes(per_step * LANES, 2)
    lanes3 = cut_lanes(per_step * LANES, 3)
    transforms = (Transforms if share == LANES else PlainTransforms)(pieces, rows_here)
    stream = functools.partial(stream_call, steps=steps, per_step=per_step)

    flat = jax.ShapeDtypeStruct((rows_here, channels), bf16)
    halo = jax.ShapeDtypeStruct((3 * halo_rows, channels), f32)
    sent = jax.ShapeDtypeStruct((groups, 3, rows_here, LANES), bf16)
    exts = [pltpu.VMEM((rows_here + PAD, LANES), f32)] * 3
    last_block = 16
    last_spec = pl.BlockSpec((last_block, channels), lambda i: (rows_here // last_block - 1, 0))

    def whole(array):
        return pl.BlockSpec(array.shape, lambda i: (0,) * len(array.shape))

    lead = call(
        lead_kernel, halo, [], q_in, k_in, v_in,
        grid=(1,), in_specs=[last_spec] * 3, out_specs=whole(halo),
    )
    lead = lax.ppermute(lead, "ctx", [(i, i + 1) for i in range(pieces - 1)])

    (packed,) = stream(
        pack_work,
        operands=[(kernel, lanes2, None)],
        results=[(sent, cut_groups(per_step, 2), (groups, rows_here, LANES))],
    )
    (signals,) = stream(
        signals_work,
        operands=[(x, lanes2, None) for x in (q_in, k_in, v_in, grad_out, lead, short_filter)],
        results=[(sent, cut_groups(per_step, pl.ds(0, 2)), (groups, 2, rows_here, LANES))],
        scratch=exts,
        aliases=[packed],
    )
    signals_here = exchange(to_pieces(signals, pieces))
    (short,) = stream(
        short_work,
        operands=[(x, lanes2, None) for x in (q_in, k_in, v_in, lead, short_filter)],
        results=[(jax.ShapeDtypeStruct((3, rows_here, channels), f32), lanes3, None)],
        scratch=exts,
    )
    long_here, lag_spec = transforms.products(signals_here)
    long = to_groups(exchange(long_here))
    lag_here, lag_squares = transforms.lag(lag_spec)

    mixed, grad_q, grad_k, grad_v, front, back, sums = stream(
        finish_work,
        operands=[(x, lanes2, None) for x in (q_in, k_in, v_in, grad_out)]
        + [(short, lanes3, None)]
        + [(x, lanes2, None) for x in (lead, short_filter, skip.reshape(1, channels))]
        + [(long, cut_groups(per_step), None)],
        results=[(flat, lanes2, None)] * 4
        + [(halo, lanes2, None)] * 2
        + [(jax.ShapeDtypeStruct((taps_count + 1, channels), f32), lanes2, None)],
        scratch=exts,
    )
    lag = to_groups(exchange(lag_here[:, None]))[:, 0]

    extra = jnp.zeros((taps_count + 1, LANES), f32).at[0, :share].set(jnp.sum(lag_squares, axis=0))
    totals = jnp.concatenate([sums, extra], axis=1)
    rounds = rounds_of(pieces)
    for steps_of in rounds[:-1]:
        totals = add_up(partners(totals, "ctx", steps_of))
    last = partners(totals, "ctx", rounds[-1])
    if len(last) == 2:
        last = [last[0] + last[1]]
    totals, norm_sq = call(
        norm_kernel,
        (jax.ShapeDtypeStruct(totals.shape, f32), jax.ShapeDtypeStruct((1, LANES), f32)),
        [], *last,
        vmem_bytes=SMALL_VMEM_BYTES,
        in_specs=[IN_VMEM] * len(last), out_specs=(IN_VMEM, IN_VMEM),
    )
    for steps_of in rounds_of(sides):
        norm_sq = add_up(partners(norm_sq, "ch", steps_of))

    tail = lax.ppermute(front, "ctx", [(i, i - 1) for i in range(1, pieces)])
    grad_q, grad_k, grad_v = call(
        edges_kernel, (flat, flat, flat), [pltpu.VMEM((last_block, channels), f32)],
        back, tail, short_filter, grad_q, grad_k, grad_v,
        vmem_bytes=SMALL_VMEM_BYTES,
        grid=(1,),
        in_specs=[whole(back), whole(tail), whole(short_filter)] + [last_spec] * 3,
        out_specs=(last_spec,) * 3,
        input_output_aliases={3: 0, 4: 1, 5: 2},
    )

    limit = math.sqrt(float(seq_len * channels * sides))
    grad_short, grad_skip, grad_kernel = call(
        functools.partial(scale_kernel, limit),
        (
            jax.ShapeDtypeStruct((taps_count, channels), f32),
            jax.ShapeDtypeStruct((1, channels), f32),
            jax.ShapeDtypeStruct((rows_here, channels), f32),
        ),
        [pltpu.VMEM(lag.shape, bf16), pltpu.SemaphoreType.DMA((4,))],
        totals, norm_sq, lag,
        vmem_bytes=SMALL_VMEM_BYTES,
        in_specs=[IN_VMEM, IN_VMEM, ANYWHERE],
        out_specs=(IN_VMEM,) * 3,
    )
    return mixed, grad_q, grad_k, grad_v, grad_short, grad_skip.reshape(channels), grad_kernel


def solution(mesh):
    in_specs = (
        P("ctx", "ch"),
        P("ctx", "ch"),
        P("ctx", "ch"),
        P("ctx", "ch"),
        P(None, "ch"),
        P("ctx", "ch"),
        P("ch"),
    )
    out_specs = (
        P("ctx", "ch"),
        P("ctx", "ch"),
        P("ctx", "ch"),
        P("ctx", "ch"),
        P(None, "ch"),
        P("ch"),
        P("ctx", "ch"),
    )
    return jax.shard_map(body, mesh=mesh, in_specs=in_specs, out_specs=out_specs, check_vma=False)
```

time: 888 us -> 134 us (0.15); the launches traced: 877 us -> 133 us
  waiting for transfers between devices: 380 us -> 18.8 us
  starting transfers between devices: 146 us -> 23.8 us
  blocking collectives: 139 us -> 45 us
  local copies, waits for them, and re-layouts: 91.4 us -> 2.22 us
  matrix products: 64.8 us -> 0 us
  other arithmetic: 51.7 us -> 2.27 us
  Pallas kernels: 0 us -> 40.4 us
    all_to_all x7 -> x2, waiting for transfers between devices: 380 us -> 12.7 us  [exchange(): lax.all_to_all(pieces_first, 'ctx', split_axis=0, concat_axis=0, tiled=True)]
    all_to_all x7 -> x2, starting transfers between devices: 133 us -> 11.9 us  [exchange(): lax.all_to_all(pieces_first, 'ctx', split_axis=0, concat_axis=0, tiled=True)]
    psum x2 -> x0, blocking collectives: 66.8 us -> none  [the longest x1 61.4 us: body(): summed = lax.psum((short_grad, skip_grad, kernel_square), 'ctx')]
    dot_general x8 -> x0, matrix products: 64.8 us -> none  [the longest x2 25.5 us: spectrum_tiles(): jnp.einsum('pqer,qgjrc->pgjec', forward_table(inner_angle), arrived, prec...]
    another operation x9 -> x0, local copies, waits for them, and re-layouts: 40.7 us -> none  [the longest x6 28.6 us: spectrum_tiles(): jnp.stack([turn_re, turn_im])]
    pallas_call x0 -> x10, Pallas kernels: none -> 40.4 us  [call(): pl.pallas_call(kernel, out_shape=outs, scratch_shapes=scratch, compiler_p...]
    all_to_all x2 -> x1, blocking collectives: 72.4 us -> 45 us  [exchange(): lax.all_to_all(pieces_first, 'ctx', split_axis=0, concat_axis=0, tiled=True)]
    all_to_all x3 -> x0, local copies, waits for them, and re-layouts: 24.8 us -> none  [the longest x2 23 us: rows_from_spectrum(): lax.all_to_all(stacked, 'ctx', split_axis=3, concat_axis=2, tiled=True)]
  transfers between devices with their start and end apart: 13 -> 11, of which waited for: 7 -> 5; matrix products, arithmetic and copies ran while one was open for 18% -> 2% of each run, Pallas kernels for 0% -> 14%
where the time goes in v3:
time: 134 us; the launch traced here: 133 us
  blocking collectives  45 us (34%)
  Pallas kernels  40.4 us (30%)
  starting transfers between devices  23.8 us (18%)
  waiting for transfers between devices  18.8 us (14%)
  other arithmetic  2.27 us (2%)
  local copies, waits for them, and re-layouts  2.22 us (2%)
    all_to_all x1, blocking collectives, exchange(): lax.all_to_all(pieces_first, 'ctx', split_axis=0, concat_axis=0, tiled=True)  45 us
    pallas_call x10, Pallas kernels, call(): pl.pallas_call(kernel, out_shape=outs, scratch_shapes=scratch, compiler_p...  40.4 us
    all_to_all x2, waiting for transfers between devices, exchange(): lax.all_to_all(pieces_first, 'ctx', split_axis=0, concat_axis=0, tiled=True)  12.7 us
    all_to_all x2, starting transfers between devices, exchange(): lax.all_to_all(pieces_first, 'ctx', split_axis=0, concat_axis=0, tiled=True)  11.9 us
    ppermute x7, starting transfers between devices, partners(): lax.ppermute(value, axis, [(i, i ^ step) for i in range(size)])  8.24 us
    ppermute x7, waiting for transfers between devices, partners(): lax.ppermute(value, axis, [(i, i ^ step) for i in range(size)])  6.09 us
  transfers between devices with their start and end apart: 11, of which 5 were waited for; matrix products, arithmetic and copies ran while one was open for 2% of the time, Pallas kernels for 14%

profile of v3, /device:TPU:0, one launch (start us, length us, event | category | flops | bytes accessed | tf_op | source)
XLA Modules:
  0.0 133.2 jit_solution(16648250780287924149)
XLA Ops:
  0.6 1.6 %shard_map.153 = f32[6,2048]{1,0:T(8,128)} custom-call(bf16[128,2048]{1,0:T(8,128)(2,1)} %refs_0_.7, bf16[128,2048]{1,0:T(8,128)(2,1)} %refs_1_.5, bf16[128,2048]{1,0:T(8,128)(2,1)} %refs_2_.5), custom_call_target="tpu_custom_call" | custom-call | tf_op jit(solution)/shard_map/pallas_call | solution.py:33
  2.2 2.3 %collective-permute-start = (f32[6,2048]{1,0:T(8,128)}, f32[6,2048]{1,0:T(8,128)S(1)}, u32[]{:S(2)}, u32[]{:S(2)}) collective-permute-start(f32[6,2048]{1,0:T(8,128)} %shard_map.153), channel_id=1, source_target_pairs={{0,2},{2,4},{4,6},{6,8},{8,10},{10,12},{12,14},{14,16},{16,18},{18... | collective-permute-start | bytes 147464 | tf_op jit(solution)/shard_map/ppermute | solution.py:700
  4.5 2.0 %shard_map.155.refs_6_ = bf16[16,3,128,128]{3,2,1,0:T(8,128)(2,1)} custom-call(f32[128,2048]{1,0:T(8,128)} %refs_0_.5), custom_call_target="tpu_custom_call" | custom-call | tf_op jit(solution)/shard_map/pallas_call | solution.py:33
  6.5 0.0 collective-permute-done.refs_3_.refs_4_.refs_5_
  6.5 0.0 copy-start.3
  6.5 0.6 copy-done.3
  7.1 3.3 %shard_map.156 = bf16[16,3,128,128]{3,2,1,0:T(8,128)(2,1)} custom-call(bf16[128,2048]{1,0:T(8,128)(2,1)} %refs_0_.7, bf16[128,2048]{1,0:T(8,128)(2,1)} %refs_1_.5, bf16[128,2048]{1,0:T(8,128)(2,1)} %refs_2_.5, bf16[128,2048]{1,0:T(8,128)(2,1)} %refs_3_.3, f32[6,2048]{1,0:T(8,128)} %copy-done.3, f32[3,2048]{1,0:T(4,128)} %taps_ref.1, ...), custom_call_target="tpu_custom_call", output_to_operand_aliasing={{}: (6, {})} | custom-call | tf_op jit(solution)/shard_map/pallas_call | solution.py:33
  10.4 0.0 copy-start.4
  10.4 45.0 %all_to_all.15.signals_hbm = bf16[16,3,128,128]{3,2,1,0:T(8,128)(2,1)} all-to-all(bf16[16,3,128,128]{3,2,1,0:T(8,128)(2,1)} %shard_map.156), channel_id=1, replica_groups=mesh['ctx'=16,'ch'=2] {'ctx'}, dimensions={0} | all-to-all | bytes 3145728 | tf_op jit(solution)/shard_map/all_to_all | solution.py:630
  55.4 0.0 copy-done.4
  55.4 0.8 broadcast_in_dim.4.fine_ref
  56.2 15.3 %shard_map.157 = (bf16[16,2,128,128]{3,2,1,0:T(8,128)(2,1)}, bf16[4,1024,256]{2,1,0:T(8,128)(2,1)}) custom-call(bf16[16,3,128,128]{3,2,1,0:T(8,128)(2,1)} %all_to_all.15.signals_hbm, f32[16,16]{1,0:T(8,128)} %constant.36.clone.coarse_ref, f32[2,8,16,128]{3,2,1,0:T(8,128)} %broadcast_in_dim.4.fine_ref, bf16[512,1024]{1,0:T(8,128)(2,1)} %constant.35.clone.matrix_hbm), custom_call_target="tpu_custom_call" | custom-call | tf_op jit(solution)/shard_map/pallas_call | solution.py:33
  71.5 5.0 %all-to-all-start.1 = ((bf16[16,2,128,128]{3,2,1,0:T(8,128)(2,1)}), bf16[16,2,128,128]{3,2,1,0:T(8,128)(2,1)S(1)}, u32[]{:S(2)}, u32[]{:S(2)}) async-start(bf16[16,2,128,128]{3,2,1,0:T(8,128)(2,1)} %get-tuple-element.38), calls=%async_computation.1 | async-start | bytes 2097152 | tf_op jit(solution)/shard_map/all_to_all | solution.py:630
  76.5 3.4 %shard_map.154.refs_4_ = f32[3,128,2048]{2,1,0:T(8,128)} custom-call(bf16[128,2048]{1,0:T(8,128)(2,1)} %refs_0_.7, bf16[128,2048]{1,0:T(8,128)(2,1)} %refs_1_.5, bf16[128,2048]{1,0:T(8,128)(2,1)} %refs_2_.5, f32[6,2048]{1,0:T(8,128)} %copy-done.3, f32[3,2048]{1,0:T(4,128)} %taps_ref.1), custom_call_target="tpu_custom_call" | custom-call | tf_op jit(solution)/shard_map/pallas_call | solution.py:33
  79.9 6.2 %shard_map.160 = (bf16[16,128,128]{2,1,0:T(8,128)(2,1)}, f32[16,128]{1,0:T(8,128)}) custom-call(bf16[4,1024,256]{2,1,0:T(8,128)(2,1)} %get-tuple-element.49.split_hbm, f32[16,16]{1,0:T(8,128)} %constant.36.clone.coarse_ref, f32[2,8,16,128]{3,2,1,0:T(8,128)} %broadcast_in_dim.4.fine_ref, bf16[512,1024]{1,0:T(8,128)(2,1)} %constant.35.clone.matrix_hbm), custom_call_target="tpu_custom_call" | custom-call | tf_op jit(solution)/shard_map/pallas_call | solution.py:33
  86.1 0.7 reduce_sum.9
  86.8 12.7 %all-to-all-done.1.refs_8_ = bf16[16,2,128,128]{3,2,1,0:T(8,128)(2,1)S(1)} async-done(((bf16[16,2,128,128]{3,2,1,0:T(8,128)(2,1)}), bf16[16,2,128,128]{3,2,1,0:T(8,128)(2,1)S(1)}, u32[]{:S(2)}, u32[]{:S(2)}) %all-to-all-start.1) | async-done | bytes 1048608 | tf_op jit(solution)/shard_map/all_to_all | solution.py:630
  99.5 0.0 copy-start.2
  99.5 6.9 %all-to-all-start.2 = ((bf16[16,1,128,128]{3,2,1,0:T(8,128)(2,1)}), bf16[16,1,128,128]{3,2,1,0:T(8,128)(2,1)S(1)}, u32[]{:S(2)}, u32[]{:S(2)}) async-start(bf16[16,1,128,128]{3,2,1,0:T(8,128)(2,1)} %bitcast.8), calls=%async_computation.2 | async-start | bytes 1048576 | tf_op jit(solution)/shard_map/all_to_all | solution.py:630
  106.3 0.0 copy-done.2
  106.4 0.0 copy-start
  106.4 5.2 %shard_map.158 = (bf16[128,2048]{1,0:T(8,128)(2,1)}, bf16[128,2048]{1,0:T(8,128)(2,1)}, bf16[128,2048]{1,0:T(8,128)(2,1)}, bf16[128,2048]{1,0:T(8,128)(2,1)}, f3...) custom-call(bf16[128,2048]{1,0:T(8,128)(2,1)} %refs_0_.7, bf16[128,2048]{1,0:T(8,128)(2,1)} %refs_1_.5, ...), custom_call_target="tpu_custom_call" | custom-call | tf_op jit(solution)/shard_map/pallas_call | solution.py:33
  111.6 0.8 select_maximum_fusion
  112.3 2.0 %collective-permute-start.3 = (f32[4,2176]{1,0:T(4,128)S(1)}, f32[4,2176]{1,0:T(4,128)S(1)}, u32[]{:S(2)}, u32[]{:S(2)}) collective-permute-start(f32[4,2176]{1,0:T(4,128)S(1)} %select_maximum_fusion), channel_id=1, source_target_pairs={{0,4},{2,6},{4,0},{6,2},{8,12},{10,14},{12,8},{14,10},{16,20},{18,... | collective-permute-start | bytes 104456 | tf_op jit(solution)/shard_map/ppermute | solution.py:652
  114.3 0.0 collective-permute-start.4
  114.3 0.2 collective-permute-start.2
  114.5 1.3 collective-permute-start.1
  115.8 0.9 collective-permute-done.3
  116.7 1.3 collective-permute-done.4
  118.0 0.0 collective-permute-done.2
  118.0 0.8 add_add_fusion.refs_0_
  118.8 3.3 %collective-permute-start.7 = (f32[4,2176]{1,0:T(4,128)S(1)}, f32[4,2176]{1,0:T(4,128)S(1)}, u32[]{:S(2)}, u32[]{:S(2)}) collective-permute-start(f32[4,2176]{1,0:T(4,128)S(1)} %add_add_fusion.refs_0_), channel_id=1, source_target_pairs={{0,24},{2,26},{4,28},{6,30},{8,16},{10,18},{12,20},{14,22},{16,8},... | collective-permute-start | bytes 104456 | tf_op jit(solution)/shard_map/ppermute | solution.py:652
  122.1 0.4 collective-permute-start.6
  122.5 0.7 collective-permute-start.5
  123.2 1.4 %collective-permute-done.7.refs_3_ = f32[4,2176]{1,0:T(4,128)S(1)} collective-permute-done((f32[4,2176]{1,0:T(4,128)S(1)}, f32[4,2176]{1,0:T(4,128)S(1)}, u32[]{:S(2)}, u32[]{:S(2)}) %collective-permute-start.7) | collective-permute-done | bytes 34848 | tf_op jit(solution)/shard_map/ppermute | solution.py:652
  124.6 2.5 %collective-permute-done.6.refs_2_ = f32[4,2176]{1,0:T(4,128)S(1)} collective-permute-done((f32[4,2176]{1,0:T(4,128)S(1)}, f32[4,2176]{1,0:T(4,128)S(1)}, u32[]{:S(2)}, u32[]{:S(2)}) %collective-permute-start.6) | collective-permute-done | bytes 34848 | tf_op jit(solution)/shard_map/ppermute | solution.py:652
  127.2 0.0 collective-permute-done.5.refs_1_
  127.2 0.1 shard_map.161
  127.3 1.6 %collective-permute-start.8 = (f32[1,128]{1,0:T(1,128)S(1)}, f32[1,128]{1,0:T(1,128)S(1)}, u32[]{:S(2)}, u32[]{:S(2)}) collective-permute-start(f32[1,128]{1,0:T(1,128)S(1)} %get-tuple-element.52), channel_id=1, source_target_pairs={{0,1},{1,0},{2,3},{3,2},{4,5},{5,4},{6,7},{7,6},{8,9},{9,8},{10,11... | collective-permute-start | bytes 1544 | tf_op jit(solution)/shard_map/ppermute | solution.py:652
  128.9 0.0 collective-permute-done.1.tail_ref
  128.9 0.0 copy-done
  128.9 0.0 copy-start.1
  128.9 0.8 copy-done.1
  129.7 1.6 %shard_map.159 = (bf16[128,2048]{1,0:T(8,128)(2,1)}, bf16[128,2048]{1,0:T(8,128)(2,1)}, bf16[128,2048]{1,0:T(8,128)(2,1)}) custom-call(f32[6,2048]{1,0:T(8,128)S(1)} %copy-done.1, f32[6,2048]{1,0:T(8,128)S(1)} %collective-permute-done.1.tail_ref, f32[3,2048]{1,0:T(4,128)S(1)} %copy-done, ...), custom_call_target="tpu_custom_call", output_to_operand_aliasing={{0}: (3, {}), {1}: (4, {}), {2}: (5, {})} | custom-call | tf_op jit(solution)/shard_map/pallas_call | solution.py:33
  131.3 0.0 collective-permute-done.8
  131.4 0.0 all-to-all-done.2
  131.4 1.8 %shard_map.162 = (f32[3,2048]{1,0:T(4,128)}, f32[1,2048]{1,0:T(1,128)}, f32[128,2048]{1,0:T(8,128)}) custom-call(f32[4,2176]{1,0:T(4,128)S(1)} %get-tuple-element.51.totals_ref, f32[1,128]{1,0:T(1,128)S(1)} %add.19.norm_ref, bf16[16,128,128]{2,1,0:T(8,128)(2,1)S(1)} %bitcast.7), custom_call_target="tpu_custom_call" | custom-call | tf_op jit(solution)/shard_map/pallas_call | solution.py:33
  (1 shorter events, 0.0 us)
Async XLA Ops:
  2.2 4.3 %collective-permute-start = (f32[6,2048]{1,0:T(8,128)}, f32[6,2048]{1,0:T(8,128)S(1)}, u32[]{:S(2)}, u32[]{:S(2)}) collective-permute-start(f32[6,2048]{1,0:T(8,128)} %shard_map.153), channel_id=1, source_target_pairs={{0,2},{2,4},{4,6},{6,8},{8,10},{10,12},{12,14},{14,16},{16,18},{18... | collective-permute-start | bytes 147464 | tf_op jit(solution)/shard_map/ppermute | solution.py:700
  6.5 0.6 copy-start.3
  10.4 45.0 %copy-start.4 = (f32[2,8,16]{2,1,0:T(8,128)S(1)}, f32[2,8,16]{2,1,0:T(8,128)}, u32[]{:S(2)}) copy-start(f32[2,8,16]{2,1,0:T(8,128)} %constant.37.clone) | copy-start | bytes 3076
  71.5 28.0 %all-to-all-start.1 = ((bf16[16,2,128,128]{3,2,1,0:T(8,128)(2,1)}), bf16[16,2,128,128]{3,2,1,0:T(8,128)(2,1)S(1)}, u32[]{:S(2)}, u32[]{:S(2)}) async-start(bf16[16,2,128,128]{3,2,1,0:T(8,128)(2,1)} %get-tuple-element.38), calls=%async_computation.1 | async-start | bytes 2097152 | tf_op jit(solution)/shard_map/all_to_all | solution.py:630
  99.5 6.9 %copy-start.2 = (bf16[16,2,128,128]{3,2,1,0:T(8,128)(2,1)}, bf16[16,2,128,128]{3,2,1,0:T(8,128)(2,1)S(1)}, u32[]{:S(2)}) copy-start(bf16[16,2,128,128]{3,2,1,0:T(8,128)(2,1)S(1)} %all-to-all-done.1.refs_8_) | copy-start | bytes 3145732
  99.5 31.9 %all-to-all-start.2 = ((bf16[16,1,128,128]{3,2,1,0:T(8,128)(2,1)}), bf16[16,1,128,128]{3,2,1,0:T(8,128)(2,1)S(1)}, u32[]{:S(2)}, u32[]{:S(2)}) async-start(bf16[16,1,128,128]{3,2,1,0:T(8,128)(2,1)} %bitcast.8), calls=%async_computation.2 | async-start | bytes 1048576 | tf_op jit(solution)/shard_map/all_to_all | solution.py:630
  106.4 22.5 %copy-start = (f32[3,2048]{1,0:T(4,128)S(1)}, f32[3,2048]{1,0:T(4,128)}, u32[]{:S(2)}) copy-start(f32[3,2048]{1,0:T(4,128)} %taps_ref.1) | copy-start | bytes 73732
  112.3 4.3 %collective-permute-start.3 = (f32[4,2176]{1,0:T(4,128)S(1)}, f32[4,2176]{1,0:T(4,128)S(1)}, u32[]{:S(2)}, u32[]{:S(2)}) collective-permute-start(f32[4,2176]{1,0:T(4,128)S(1)} %select_maximum_fusion), channel_id=1, source_target_pairs={{0,4},{2,6},{4,0},{6,2},{8,12},{10,14},{12,8},{14,10},{16,20},{18,... | collective-permute-start | bytes 104456 | tf_op jit(solution)/shard_map/ppermute | solution.py:652
  114.3 3.7 %collective-permute-start.4 = (f32[4,2176]{1,0:T(4,128)S(1)}, f32[4,2176]{1,0:T(4,128)S(1)}, u32[]{:S(2)}, u32[]{:S(2)}) collective-permute-start(f32[4,2176]{1,0:T(4,128)S(1)} %select_maximum_fusion), channel_id=1, source_target_pairs={{0,6},{2,4},{4,2},{6,0},{8,14},{10,12},{12,10},{14,8},{16,22},{18,... | collective-permute-start | bytes 104456 | tf_op jit(solution)/shard_map/ppermute | solution.py:652
  114.3 3.7 %collective-permute-start.2 = (f32[4,2176]{1,0:T(4,128)S(1)}, f32[4,2176]{1,0:T(4,128)S(1)}, u32[]{:S(2)}, u32[]{:S(2)}) collective-permute-start(f32[4,2176]{1,0:T(4,128)S(1)} %select_maximum_fusion), channel_id=1, source_target_pairs={{0,2},{2,0},{4,6},{6,4},{8,10},{10,8},{12,14},{14,12},{16,18},{18,... | collective-permute-start | bytes 104456 | tf_op jit(solution)/shard_map/ppermute | solution.py:652
  114.5 14.4 %collective-permute-start.1 = (f32[6,2048]{1,0:T(8,128)}, f32[6,2048]{1,0:T(8,128)S(1)}, u32[]{:S(2)}, u32[]{:S(2)}) collective-permute-start(f32[6,2048]{1,0:T(8,128)} %get-tuple-element.41), channel_id=1, source_target_pairs={{2,0},{4,2},{6,4},{8,6},{10,8},{12,10},{14,12},{16,14},{18,16},{20... | collective-permute-start | bytes 147464 | tf_op jit(solution)/shard_map/ppermute | solution.py:756
  118.8 5.8 %collective-permute-start.7 = (f32[4,2176]{1,0:T(4,128)S(1)}, f32[4,2176]{1,0:T(4,128)S(1)}, u32[]{:S(2)}, u32[]{:S(2)}) collective-permute-start(f32[4,2176]{1,0:T(4,128)S(1)} %add_add_fusion.refs_0_), channel_id=1, source_target_pairs={{0,24},{2,26},{4,28},{6,30},{8,16},{10,18},{12,20},{14,22},{16,8},... | collective-permute-start | bytes 104456 | tf_op jit(solution)/shard_map/ppermute | solution.py:652
  122.1 5.0 %collective-permute-start.6 = (f32[4,2176]{1,0:T(4,128)S(1)}, f32[4,2176]{1,0:T(4,128)S(1)}, u32[]{:S(2)}, u32[]{:S(2)}) collective-permute-start(f32[4,2176]{1,0:T(4,128)S(1)} %add_add_fusion.refs_0_), channel_id=1, source_target_pairs={{0,16},{2,18},{4,20},{6,22},{8,24},{10,26},{12,28},{14,30},{16,0},... | collective-permute-start | bytes 104456 | tf_op jit(solution)/shard_map/ppermute | solution.py:652
  122.5 4.6 %collective-permute-start.5 = (f32[4,2176]{1,0:T(4,128)S(1)}, f32[4,2176]{1,0:T(4,128)S(1)}, u32[]{:S(2)}, u32[]{:S(2)}) collective-permute-start(f32[4,2176]{1,0:T(4,128)S(1)} %add_add_fusion.refs_0_), channel_id=1, source_target_pairs={{0,8},{2,10},{4,12},{6,14},{8,0},{10,2},{12,4},{14,6},{16,24},{18,... | collective-permute-start | bytes 104456 | tf_op jit(solution)/shard_map/ppermute | solution.py:652
  127.3 4.0 %collective-permute-start.8 = (f32[1,128]{1,0:T(1,128)S(1)}, f32[1,128]{1,0:T(1,128)S(1)}, u32[]{:S(2)}, u32[]{:S(2)}) collective-permute-start(f32[1,128]{1,0:T(1,128)S(1)} %get-tuple-element.52), channel_id=1, source_target_pairs={{0,1},{1,0},{2,3},{3,2},{4,5},{5,4},{6,7},{7,6},{8,9},{9,8},{10,11... | collective-permute-start | bytes 1544 | tf_op jit(solution)/shard_map/ppermute | solution.py:652
  128.9 0.8 copy-start.1

commit v4 on v3

--- a/solution.py
+++ b/solution.py
@@ -115,45 +115,51 @@
     return leaf // 2, slice((leaf % 2) * LANES, (leaf % 2 + 1) * LANES)
 
 
-def split_store(ref, leaf, row, value):
+def split_store(ref, leaf, below, here, value):
     pair, lanes = leaf_place(leaf)
     high = value.astype(bf16)
     for block in range(PASSES):
         part = high
         if PASSES == 3 and block == 2:
             part = (value - high.astype(f32)).astype(bf16)
-        ref[pair, pl.ds(block * BOTH + row, CHUNK), lanes] = part
-
-
-def run(stages, matmul=None):
+        ref[pair, shifted_rows(here, block * BOTH + below), lanes] = part
+
+
+def run_all(stages, rows_here, matmul=None, carry=0):
     tiles = matmul[2].shape[0] if matmul else 4
-
-    def step(tile, carry):
-        if matmul:
-            matrix_ref, split_ref, result_ref = matmul
-            result_ref[tile] = jnp.dot(matrix_ref[...], split_ref[tile], preferred_element_type=f32)
-        for part in range(CHUNKS // tiles):
-            for stage in stages:
-                carry = stage(tile * (CHUNKS // tiles) + part, carry)
-        return carry
-
-    return step, tiles
-
-
-def run_all(stages, matmul=None, carry=0):
-    step, tiles = run(stages, matmul)
-    return lax.fori_loop(0, tiles, step, carry)
+    ratio = SPAN // rows_here
+    in_part = tiles // ratio
+    per_tile = CHUNKS // tiles
+    for part in range(ratio):
+
+        def step(tile, carry, part=part):
+            if matmul:
+                matrix_ref, split_ref, result_ref = matmul
+                place = part * in_part + tile
+                result_ref[place] = jnp.dot(matrix_ref[...], split_ref[place], preferred_element_type=f32)
+            for chunk in range(per_tile):
+                for stage in stages:
+                    carry = stage(part, chunk_row(tile * per_tile + chunk), carry)
+            return carry
+
+        carry = lax.fori_loop(0, in_part, step, carry)
+    return carry
 
 
 def chunk_row(idx):
     return pl.multiple_of(idx * CHUNK, CHUNK)
 
 
-def twist_stage(coarse_ref, fine_ref, twist_ref):
+def in_span(part, row, rows_here):
+    return pl.ds(pl.multiple_of(part * rows_here + row, CHUNK), CHUNK)
+
+
+def twist_stage(coarse_ref, fine_ref, twist_ref, rows_here):
     outer = twist_ref.shape[1]
 
-    def stage(idx, carry):
-        here = pl.ds(chunk_row(idx), CHUNK)
+    def stage(part, row, carry):
+        here = in_span(part, row, rows_here)
+        idx = part * (rows_here // CHUNK) + row // CHUNK
         for leaf in range(outer):
             far_cosine = coarse_ref[idx, leaf]
             far_sine = coarse_ref[idx, outer + leaf]
@@ -166,49 +172,48 @@
     return stage
 
 
-def piece_place(idx, part, rows_here):
-    ratio = SPAN // rows_here
-    in_piece = rows_here // CHUNK
-    return part * ratio + idx // in_piece, pl.ds(chunk_row(idx % in_piece), CHUNK)
-
-
 def leaves_stage(signals_ref, kind, twist_ref, split_ref):
     outer = twist_ref.shape[1]
     rows_here = signals_ref.shape[2]
-
-    def stage(idx, carry):
-        row = chunk_row(idx)
-        parts = []
-        for part in range(outer):
-            piece, rows = piece_place(idx, part, rows_here)
-            parts.append(signals_ref[piece, kind, rows, :].astype(f32))
+    ratio = SPAN // rows_here
+
+    def stage(part, row, carry):
+        here = in_span(part, row, rows_here)
+        parts = [
+            signals_ref[place * ratio + part, kind, pl.ds(row, CHUNK), :].astype(f32) for place in range(outer)
+        ]
         for leaf, (re, im) in enumerate(to_leaves(parts)):
-            cosine = twist_ref[0, leaf, pl.ds(row, CHUNK), :]
-            sine = twist_ref[1, leaf, pl.ds(row, CHUNK), :]
-            split_store(split_ref, leaf, row, re * cosine + im * sine)
-            split_store(split_ref, leaf, SPAN + row, im * cosine - re * sine)
+            cosine = twist_ref[0, leaf, here, :]
+            sine = twist_ref[1, leaf, here, :]
+            split_store(split_ref, leaf, 0, here, re * cosine + im * sine)
+            split_store(split_ref, leaf, SPAN, here, im * cosine - re * sine)
         return carry
 
     return stage
 
 
-def combine_stage(left_ref, right_ref, split_ref, conjugate):
-    def stage(idx, carry):
-        row = chunk_row(idx)
+def shifted_rows(here, by):
+    return pl.ds(here.start + by, here.size)
+
+
+def combine_stage(left_ref, right_ref, split_ref, rows_here, conjugate):
+    def stage(part, row, carry):
+        here = in_span(part, row, rows_here)
+        below = shifted_rows(here, SPAN)
         for leaf in range(2 * left_ref.shape[0]):
             pair, lanes = leaf_place(leaf)
-            left_re = left_ref[pair, pl.ds(row, CHUNK), lanes]
-            left_im = left_ref[pair, pl.ds(SPAN + row, CHUNK), lanes]
-            right_re = right_ref[pair, pl.ds(row, CHUNK), lanes]
-            right_im = right_ref[pair, pl.ds(SPAN + row, CHUNK), lanes]
+            left_re = left_ref[pair, here, lanes]
+            left_im = left_ref[pair, below, lanes]
+            right_re = right_ref[pair, here, lanes]
+            right_im = right_ref[pair, below, lanes]
             if conjugate:
                 re = left_re * right_re + left_im * right_im
                 minus_im = left_im * right_re - left_re * right_im
             else:
                 re = left_re * right_re - left_im * right_im
                 minus_im = -(left_re * right_im + left_im * right_re)
-            split_store(split_ref, leaf, row, re)
-            split_store(split_ref, leaf, SPAN + row, minus_im)
+            split_store(split_ref, leaf, 0, here, re)
+            split_store(split_ref, leaf, SPAN, here, minus_im)
         return carry
 
     return stage
@@ -216,36 +221,47 @@
 
 def signal_stage(time_ref, twist_ref, rows_here, write):
     outer = twist_ref.shape[1]
+    ratio = SPAN // rows_here
     scale = 1.0 / (SPAN * outer)
 
-    def stage(idx, carry):
-        row = chunk_row(idx)
+    def stage(part, row, carry):
+        here = in_span(part, row, rows_here)
+        below = shifted_rows(here, SPAN)
         leaves = []
         for leaf in range(outer):
             pair, lanes = leaf_place(leaf)
-            cosine = twist_ref[0, leaf, pl.ds(row, CHUNK), :]
-            sine = twist_ref[1, leaf, pl.ds(row, CHUNK), :]
-            re = time_ref[pair, pl.ds(row, CHUNK), lanes]
-            minus_im = time_ref[pair, pl.ds(SPAN + row, CHUNK), lanes]
+            cosine = twist_ref[0, leaf, here, :]
+            sine = twist_ref[1, leaf, here, :]
+            re = time_ref[pair, here, lanes]
+            minus_im = time_ref[pair, below, lanes]
             leaves.append((re * cosine + minus_im * sine, re * sine - minus_im * cosine))
-        for part, value in enumerate(from_leaves(leaves, scale)):
-            piece, rows = piece_place(idx, part, rows_here)
-            carry = write(piece, rows, value, carry)
+        for place, value in enumerate(from_leaves(leaves, scale)):
+            carry = write(place * ratio + part, pl.ds(row, CHUNK), value, carry)
         return carry
 
     return stage
 
 
+def filter_kernel(
+    filter_ref, coarse_ref, fine_ref, matrix_ref, spec_ref, twist_ref, split_ref,
+):
+    rows_here = filter_ref.shape[2]
+    run_all([twist_stage(coarse_ref, fine_ref, twist_ref, rows_here)], rows_here)
+    run_all([leaves_stage(filter_ref, 0, twist_ref, split_ref)], rows_here)
+    run_all([], rows_here, (matrix_ref, split_ref, spec_ref))
+
+
 def products_kernel(
-    signals_hbm, coarse_ref, fine_ref, matrix_hbm, results_hbm, lag_hbm,
+    signals_hbm, filter_hbm, coarse_ref, fine_ref, matrix_hbm, results_hbm, lag_hbm,
     twist_ref, matrix_ref, signals_ref, results_ref, one_split, two_split, lag_split,
     filter_ref, product_ref, cotan_ref, time_ref, sems,
 ):
     rows_here = signals_ref.shape[2]
     arrivals = [
-        pltpu.make_async_copy(signals_hbm.at[:, kind], signals_ref.at[:, kind], sems.at[kind]) for kind in range(3)
+        pltpu.make_async_copy(signals_hbm.at[:, kind], signals_ref.at[:, kind], sems.at[kind]) for kind in range(2)
     ]
-    matrix_copy = pltpu.make_async_copy(matrix_hbm, matrix_ref, sems.at[3])
+    matrix_copy = pltpu.make_async_copy(matrix_hbm, matrix_ref, sems.at[2])
+    filter_copy = pltpu.make_async_copy(filter_hbm, filter_ref, sems.at[3])
     lag_copy = pltpu.make_async_copy(lag_split, lag_hbm, sems.at[4])
     returns = [
         pltpu.make_async_copy(results_ref.at[:, kind], results_hbm.at[:, kind], sems.at[5 + kind]) for kind in range(2)
@@ -254,6 +270,9 @@
     def leaves(kind, split_ref):
         return leaves_stage(signals_ref, kind, twist_ref, split_ref)
 
+    def combine(left_ref, right_ref, split_ref, conjugate):
+        return combine_stage(left_ref, right_ref, split_ref, rows_here, conjugate)
+
     def result(kind, from_ref):
         def write(piece, rows, value, carry):
             results_ref[piece, kind, rows, :] = value.astype(bf16)
@@ -261,22 +280,24 @@
 
         return signal_stage(from_ref, twist_ref, rows_here, write)
 
-    for copy in (arrivals[2], arrivals[0], matrix_copy, arrivals[1]):
+    for copy in (arrivals[0], matrix_copy, arrivals[1], filter_copy):
         copy.start()
-    run_all([twist_stage(coarse_ref, fine_ref, twist_ref)])
-    arrivals[2].wait()
-    run_all([leaves(2, one_split)])
+    run_all([twist_stage(coarse_ref, fine_ref, twist_ref, rows_here)], rows_here)
     arrivals[0].wait()
+    run_all([leaves(0, one_split)], rows_here)
+    arrivals[1].wait()
     matrix_copy.wait()
-    run_all([leaves(0, two_split)], (matrix_ref, one_split, filter_ref))
-    arrivals[1].wait()
-    run_all([leaves(1, one_split)], (matrix_ref, two_split, product_ref))
-    run_all([combine_stage(filter_ref, product_ref, two_split, False)], (matrix_ref, one_split, cotan_ref))
-    run_all([combine_stage(filter_ref, cotan_ref, one_split, True)], (matrix_ref, two_split, time_ref))
-    run_all([combine_stage(product_ref, cotan_ref, lag_split, True), result(0, time_ref)], (matrix_ref, one_split, filter_ref))
+    run_all([leaves(1, two_split)], rows_here, (matrix_ref, one_split, product_ref))
+    filter_copy.wait()
+    run_all([combine(filter_ref, product_ref, one_split, False)], rows_here, (matrix_ref, two_split, cotan_ref))
+    run_all([combine(filter_ref, cotan_ref, two_split, True)], rows_here, (matrix_ref, one_split, time_ref))
+    run_all(
+        [combine(product_ref, cotan_ref, lag_split, True), result(0, time_ref)],
+        rows_here, (matrix_ref, two_split, filter_ref),
+    )
     lag_copy.start()
     returns[0].start()
-    run_all([result(1, filter_ref)])
+    run_all([result(1, filter_ref)], rows_here)
     returns[1].start()
     lag_copy.wait()
     returns[0].wait()
@@ -286,63 +307,75 @@
 def lag_kernel(
     split_hbm, coarse_ref, fine_ref, matrix_hbm, lag_ref, square_ref, twist_ref, matrix_ref, split_ref, time_ref, sems
 ):
+    rows_here = lag_ref.shape[1]
     copies = [
         pltpu.make_async_copy(matrix_hbm, matrix_ref, sems.at[0]),
         pltpu.make_async_copy(split_hbm, split_ref, sems.at[1]),
     ]
     for copy in copies:
         copy.start()
+    run_all([twist_stage(coarse_ref, fine_ref, twist_ref, rows_here)], rows_here)
     for copy in copies:
         copy.wait()
-    run_all([twist_stage(coarse_ref, fine_ref, twist_ref)], (matrix_ref, split_ref, time_ref))
+    run_all([], rows_here, (matrix_ref, split_ref, time_ref))
 
     def write(piece, rows, value, carry):
         lag_ref[piece, rows, :] = value.astype(bf16)
         return carry + value * value
 
-    square_ref[...] = run_all(
-        [signal_stage(time_ref, twist_ref, lag_ref.shape[1], write)], None, jnp.zeros((CHUNK, LANES), f32)
-    )
+    square = run_all(
+        [signal_stage(time_ref, twist_ref, rows_here, write)], rows_here, None, jnp.zeros((CHUNK, LANES), f32)
+    )
+    square_ref[...] = jnp.sum(square, axis=0, keepdims=True)
 
 
 class Transforms:
     def __init__(self, pieces, rows_here):
         outer = pieces * rows_here // SPAN
         pairs = outer // 2
-        self.matrix = jnp.asarray(matrix_blocks())
         coarse = twist_angles(outer, CHUNK * np.arange(CHUNKS)).T
-        self.coarse = jnp.asarray(np.concatenate([np.cos(coarse), np.sin(coarse)], axis=1), f32)
-        fine = twist_angles(outer, np.arange(CHUNK))
-        fine = jnp.asarray(np.stack([np.cos(fine), np.sin(fine)]), f32)[..., None]
-        self.fine = jnp.broadcast_to(fine, fine.shape[:3] + (LANES,))
+        fine = twist_angles(outer, np.arange(CHUNK))[..., None] * np.ones(LANES)
+        self.tables = [
+            jnp.asarray(np.concatenate([np.cos(coarse), np.sin(coarse)], axis=1).astype(np.float32)),
+            jnp.asarray(np.stack([np.cos(fine), np.sin(fine)]).astype(np.float32)),
+            jnp.asarray(matrix_blocks()),
+        ]
+        self.spec = jax.ShapeDtypeStruct((pairs, BOTH, 2 * LANES), f32)
         self.split = jax.ShapeDtypeStruct((pairs, PASSES * BOTH, 2 * LANES), bf16)
         self.signal = jax.ShapeDtypeStruct((pieces, rows_here, LANES), bf16)
         self.result = jax.ShapeDtypeStruct((pieces, 2, rows_here, LANES), bf16)
-        self.square = jax.ShapeDtypeStruct((CHUNK, LANES), f32)
-        self.signals_work = pltpu.VMEM((pieces, 3, rows_here, LANES), bf16)
-        self.results_work = pltpu.VMEM(self.result.shape, bf16)
-        self.work = pltpu.VMEM((pairs, BOTH, 2 * LANES), f32)
+        self.square = jax.ShapeDtypeStruct((1, LANES), f32)
+        self.pair_work = pltpu.VMEM(self.result.shape, bf16)
+        self.work = pltpu.VMEM(self.spec.shape, f32)
         self.split_work = pltpu.VMEM(self.split.shape, bf16)
-        self.tables = [pltpu.VMEM((2, outer, SPAN, LANES), f32), pltpu.VMEM(self.matrix.shape, bf16)]
-
-    def products(self, signals):
+        self.twist_work = pltpu.VMEM((2, outer, SPAN, LANES), f32)
+        self.matrix_work = pltpu.VMEM(self.tables[2].shape, bf16)
+
+    def filter(self, signal):
+        return call(
+            filter_kernel, self.spec, [self.twist_work, self.split_work],
+            signal, *self.tables,
+            in_specs=[IN_VMEM, IN_SMEM, IN_VMEM, IN_VMEM],
+            out_specs=IN_VMEM,
+        )
+
+    def products(self, signals, filter_spec):
         return call(
             products_kernel, (self.result, self.split),
-            self.tables
-            + [self.signals_work, self.results_work]
+            [self.twist_work, self.matrix_work, self.pair_work, self.pair_work]
             + [self.split_work] * 3
             + [self.work] * 4
             + [pltpu.SemaphoreType.DMA((7,))],
-            signals, self.coarse, self.fine, self.matrix,
-            in_specs=[ANYWHERE, IN_SMEM, IN_VMEM, ANYWHERE],
+            signals, filter_spec, *self.tables,
+            in_specs=[ANYWHERE, ANYWHERE, IN_SMEM, IN_VMEM, ANYWHERE],
             out_specs=(ANYWHERE, ANYWHERE),
         )
 
     def lag(self, lag_split):
         return call(
             lag_kernel, (self.signal, self.square),
-            self.tables + [self.split_work, self.work, pltpu.SemaphoreType.DMA((2,))],
-            lag_split, self.coarse, self.fine, self.matrix,
+            [self.twist_work, self.matrix_work, self.split_work, self.work, pltpu.SemaphoreType.DMA((2,))],
+            lag_split, *self.tables,
             in_specs=[ANYWHERE, IN_SMEM, IN_VMEM, ANYWHERE],
             out_specs=(IN_VMEM, IN_VMEM),
         )
@@ -383,8 +416,11 @@
         parts = from_leaves([(leaf_re[leaf], leaf_im[leaf]) for leaf in range(self.outer)], 1.0 / self.seq_len)
         return jnp.stack(parts).reshape(self.pieces, self.seq_len // self.pieces, -1)
 
-    def products(self, signals):
-        product, cotan, taps = (self.spectrum(signals[:, kind]) for kind in range(3))
+    def filter(self, signal):
+        return self.spectrum(signal[:, 0])
+
+    def products(self, signals, taps):
+        product, cotan = (self.spectrum(signals[:, kind]) for kind in range(2))
         conv = self.back(taps[0] * product[0] - taps[1] * product[1], taps[0] * product[1] + taps[1] * product[0])
         corr = self.back(taps[0] * cotan[0] + taps[1] * cotan[1], taps[0] * cotan[1] - taps[1] * cotan[0])
         lag = (
@@ -395,17 +431,20 @@
 
     def lag(self, lag_spec):
         lag = self.back(*lag_spec)
-        return lag.astype(bf16), jnp.sum(lag * lag, axis=(0, 1))[None, :]
+        squares = jnp.sum(lag * lag, axis=(0, 1))
+        return lag.astype(bf16), jnp.zeros((1, LANES), f32).at[0, : squares.shape[0]].set(squares)
 
 
 def group(idx):
     return pl.ds(pl.multiple_of(idx * LANES, LANES), LANES)
 
 
-def streamed(work, steps, per_step, places, in_count, out_count, *refs):
-    hbm = refs[: in_count + out_count]
-    held = refs[in_count + out_count : 2 * (in_count + out_count)]
-    scratch = refs[2 * (in_count + out_count) : -1]
+def streamed(work, steps, per_step, places, in_count, out_count, kept, *refs):
+    moved = in_count + out_count
+    hbm = refs[:moved]
+    kept_refs = refs[moved : moved + kept]
+    held = refs[moved + kept : 2 * moved + kept]
+    scratch = refs[2 * moved + kept : -1]
     sems = refs[-1]
 
     def copy(place, step):
@@ -414,43 +453,46 @@
         ends = (outside, inside) if place < in_count else (inside, outside)
         return pltpu.make_async_copy(*ends, sems.at[place, step])
 
+    def arrivals(step):
+        return [copy(place, step) for place in range(in_count) if places[place][0](step) is not None]
+
     for step in range(steps):
-        for place in range(in_count):
+        for arrival in arrivals(step):
+            arrival.start()
+    for step in range(steps):
+        for arrival in arrivals(step):
+            arrival.wait()
+
+        def one(idx, carry):
+            work(idx, held[:in_count], held[in_count:] + kept_refs, scratch)
+            return carry
+
+        lax.fori_loop(step * per_step, (step + 1) * per_step, one, 0)
+        for place in range(in_count, moved):
             copy(place, step).start()
     for step in range(steps):
-        for place in range(in_count):
+        for place in range(in_count, moved):
             copy(place, step).wait()
 
-        def one(idx, carry):
-            work(idx, held[:in_count], held[in_count:], scratch)
-            return carry
-
-        lax.fori_loop(step * per_step, (step + 1) * per_step, one, 0)
-        for place in range(in_count, in_count + out_count):
-            copy(place, step).start()
-    for step in range(steps):
-        for place in range(in_count, in_count + out_count):
-            copy(place, step).wait()
-
-
-def stream_call(work, steps, per_step, operands, results, scratch=(), aliases=None):
+
+def stream_call(work, steps, per_step, operands, results, scratch=(), aliases=(), kept=()):
     arrays = [operand[0] for operand in operands]
     shapes = [jax.ShapeDtypeStruct(array.shape, array.dtype) for array in arrays] + [result[0] for result in results]
     cuts = [entry[1] for entry in operands] + [entry[1] for entry in results]
     held = [pltpu.VMEM(entry[2] or shape.shape, shape.dtype) for entry, shape in zip(operands + results, shapes)]
-    extra = list(aliases or ())
-    kernel = functools.partial(streamed, work, steps, per_step, cuts, len(arrays), len(results))
+    extra = list(aliases)
+    kernel = functools.partial(streamed, work, steps, per_step, cuts, len(arrays), len(results), len(kept))
 
     def with_aliases(*refs):
         kernel(*refs[: len(arrays)], *refs[len(arrays) + len(extra) :])
 
     return call(
         with_aliases,
-        tuple(result[0] for result in results),
+        tuple(result[0] for result in results) + tuple(kept),
         held + list(scratch) + [pltpu.SemaphoreType.DMA((len(shapes), steps))],
         *arrays, *extra,
         in_specs=[ANYWHERE] * (len(arrays) + len(extra)),
-        out_specs=(ANYWHERE,) * len(results),
+        out_specs=(ANYWHERE,) * len(results) + (IN_VMEM,) * len(kept),
         input_output_aliases={len(arrays) + idx: idx for idx in range(len(extra))},
     )
 
@@ -462,15 +504,15 @@
     return place, place
 
 
-def cut_groups(per_step, kinds=None):
-    def outside(step):
-        here = pl.ds(step * per_step, per_step)
-        return (here,) if kinds is None else (here, kinds)
-
-    def inside(step):
+def cut_groups(per_step):
+    def place(step):
         return (pl.ds(step * per_step, per_step),)
 
-    return outside, inside
+    return place, place
+
+
+def cut_none(step):
+    return None if step else (slice(None),)
 
 
 def row_blocks(rows_here):
@@ -478,7 +520,7 @@
 
 
 def pack_work(idx, operands, results, scratch):
-    results[0][idx] = operands[0][:, group(idx)].astype(bf16)
+    results[0][idx, 0] = operands[0][:, group(idx)].astype(bf16)
 
 
 def extend_rows(lead, in_ref, lanes, ext_ref):
@@ -524,7 +566,7 @@
 
 
 def finish_work(idx, operands, results, exts):
-    q_ref, k_ref, v_ref, grad_ref, short_ref, lead_ref, taps_ref, skip_ref, long_ref = operands
+    q_ref, k_ref, v_ref, grad_ref, short_ref, lead_ref, taps_ref, skip_ref, long_ref, squares_ref = operands
     mixed_ref, grad_q_ref, grad_k_ref, grad_v_ref, front_ref, back_ref, sums_ref = results
     lanes = group(idx)
     taps = taps_ref[:, lanes]
@@ -562,6 +604,9 @@
             out_ref[rows, lanes] = grad.astype(bf16)
         back_ref[place * halo_rows : (place + 1) * halo_rows, lanes] = grad[ROWS - halo_rows :]
         front_ref[place * halo_rows : (place + 1) * halo_rows, lanes] = ext[0:halo_rows, :]
+    extra = slice(sums_ref.shape[1] - LANES, sums_ref.shape[1])
+    sums_ref[:, extra] = jnp.zeros((taps_count + 1, LANES), f32)
+    sums_ref[0:1, extra] = squares_ref[...]
     for shift_idx in range(taps_count + 1):
         total = jnp.sum(sums[shift_idx], axis=0, keepdims=True)
         for place in range(3 if shift_idx < taps_count else 0):
@@ -606,24 +651,31 @@
     square_ref[...] = jnp.full(square_ref.shape, square)
 
 
-def scale_kernel(limit, totals_ref, norm_ref, lag_hbm, taps_out, skip_out, kernel_out, lag_ref, sems):
+def scale_kernel(limit, totals_ref, norm_ref, lag_hbm, taps_out, skip_out, kernel_hbm, lag_ref, kernel_ref, sems):
     taps_count, channels = taps_out.shape
     groups = lag_ref.shape[0]
     per_step = max(groups // 4, 1)
-    copies = []
-    for step in range(groups // per_step):
+    steps = groups // per_step
+    arrivals = []
+    returns = []
+    for step in range(steps):
         here = pl.ds(step * per_step, per_step)
-        copies.append(pltpu.make_async_copy(lag_hbm.at[here], lag_ref.at[here], sems.at[step]))
-        copies[step].start()
+        lanes = pl.ds(step * per_step * LANES, per_step * LANES)
+        arrivals.append(pltpu.make_async_copy(lag_hbm.at[here], lag_ref.at[here], sems.at[0, step]))
+        returns.append(pltpu.make_async_copy(kernel_ref.at[:, lanes], kernel_hbm.at[:, lanes], sems.at[1, step]))
+        arrivals[step].start()
     factor = limit / jnp.maximum(jnp.sqrt(norm_ref[...]), limit)
+    for step in range(steps):
+        arrivals[step].wait()
+        for idx in range(step * per_step, (step + 1) * per_step):
+            kernel_ref[:, idx * LANES : (idx + 1) * LANES] = lag_ref[idx].astype(f32) * factor
+        returns[step].start()
     for idx in range(groups):
         lanes = slice(idx * LANES, (idx + 1) * LANES)
         taps_out[:, lanes] = totals_ref[0:taps_count, lanes] * factor
         skip_out[:, lanes] = totals_ref[taps_count : taps_count + 1, lanes] * factor
-    for step, copy in enumerate(copies):
-        copy.wait()
-        for idx in range(step * per_step, (step + 1) * per_step):
-            kernel_out[:, idx * LANES : (idx + 1) * LANES] = lag_ref[idx].astype(f32) * factor
+    for step in range(steps):
+        returns[step].wait()
 
 
 def exchange(pieces_first):
@@ -685,7 +737,8 @@
 
     flat = jax.ShapeDtypeStruct((rows_here, channels), bf16)
     halo = jax.ShapeDtypeStruct((3 * halo_rows, channels), f32)
-    sent = jax.ShapeDtypeStruct((groups, 3, rows_here, LANES), bf16)
+    one_sent = jax.ShapeDtypeStruct((groups, 1, rows_here, LANES), bf16)
+    two_sent = jax.ShapeDtypeStruct((groups, 2, rows_here, LANES), bf16)
     exts = [pltpu.VMEM((rows_here + PAD, LANES), f32)] * 3
     last_block = 16
     last_spec = pl.BlockSpec((last_block, channels), lambda i: (rows_here // last_block - 1, 0))
@@ -702,14 +755,14 @@
     (packed,) = stream(
         pack_work,
         operands=[(kernel, lanes2, None)],
-        results=[(sent, cut_groups(per_step, 2), (groups, rows_here, LANES))],
-    )
+        results=[(one_sent, cut_groups(per_step), None)],
+    )
+    filter_here = exchange(to_pieces(packed, pieces))
     (signals,) = stream(
         signals_work,
         operands=[(x, lanes2, None) for x in (q_in, k_in, v_in, grad_out, lead, short_filter)],
-        results=[(sent, cut_groups(per_step, pl.ds(0, 2)), (groups, 2, rows_here, LANES))],
+        results=[(two_sent, cut_groups(per_step), None)],
         scratch=exts,
-        aliases=[packed],
     )
     signals_here = exchange(to_pieces(signals, pieces))
     (short,) = stream(
@@ -718,7 +771,8 @@
         results=[(jax.ShapeDtypeStruct((3, rows_here, channels), f32), lanes3, None)],
         scratch=exts,
     )
-    long_here, lag_spec = transforms.products(signals_here)
+    filter_spec = transforms.filter(filter_here)
+    long_here, lag_spec = transforms.products(signals_here, filter_spec)
     long = to_groups(exchange(long_here))
     lag_here, lag_squares = transforms.lag(lag_spec)
 
@@ -727,31 +781,21 @@
         operands=[(x, lanes2, None) for x in (q_in, k_in, v_in, grad_out)]
         + [(short, lanes3, None)]
         + [(x, lanes2, None) for x in (lead, short_filter, skip.reshape(1, channels))]
-        + [(long, cut_groups(per_step), None)],
-        results=[(flat, lanes2, None)] * 4
-        + [(halo, lanes2, None)] * 2
-        + [(jax.ShapeDtypeStruct((taps_count + 1, channels), f32), lanes2, None)],
+        + [(long, cut_groups(per_step), None), (lag_squares, (cut_none, cut_none), None)],
+        results=[(flat, lanes2, None)] * 4,
         scratch=exts,
-    )
+        kept=[halo, halo, jax.ShapeDtypeStruct((taps_count + 1, channels + LANES), f32)],
+    )
+    lag_here, sums = lax.optimization_barrier((lag_here, sums))
     lag = to_groups(exchange(lag_here[:, None]))[:, 0]
 
-    extra = jnp.zeros((taps_count + 1, LANES), f32).at[0, :share].set(jnp.sum(lag_squares, axis=0))
-    totals = jnp.concatenate([sums, extra], axis=1)
+    totals = sums
     rounds = rounds_of(pieces)
     for steps_of in rounds[:-1]:
         totals = add_up(partners(totals, "ctx", steps_of))
     last = partners(totals, "ctx", rounds[-1])
     if len(last) == 2:
         last = [last[0] + last[1]]
-    totals, norm_sq = call(
-        norm_kernel,
-        (jax.ShapeDtypeStruct(totals.shape, f32), jax.ShapeDtypeStruct((1, LANES), f32)),
-        [], *last,
-        vmem_bytes=SMALL_VMEM_BYTES,
-        in_specs=[IN_VMEM] * len(last), out_specs=(IN_VMEM, IN_VMEM),
-    )
-    for steps_of in rounds_of(sides):
-        norm_sq = add_up(partners(norm_sq, "ch", steps_of))
 
     tail = lax.ppermute(front, "ctx", [(i, i - 1) for i in range(1, pieces)])
     grad_q, grad_k, grad_v = call(
@@ -763,6 +807,17 @@
         out_specs=(last_spec,) * 3,
         input_output_aliases={3: 0, 4: 1, 5: 2},
     )
+    grad_q, grad_k, grad_v, *last = lax.optimization_barrier((grad_q, grad_k, grad_v, *last))
+
+    totals, norm_sq = call(
+        norm_kernel,
+        (jax.ShapeDtypeStruct(totals.shape, f32), jax.ShapeDtypeStruct((1, LANES), f32)),
+        [], *last,
+        vmem_bytes=SMALL_VMEM_BYTES,
+        in_specs=[IN_VMEM] * len(last), out_specs=(IN_VMEM, IN_VMEM),
+    )
+    for steps_of in rounds_of(sides):
+        norm_sq = add_up(partners(norm_sq, "ch", steps_of))
 
     limit = math.sqrt(float(seq_len * channels * sides))
     grad_short, grad_skip, grad_kernel = call(
@@ -772,11 +827,11 @@
             jax.ShapeDtypeStruct((1, channels), f32),
             jax.ShapeDtypeStruct((rows_here, channels), f32),
         ),
-        [pltpu.VMEM(lag.shape, bf16), pltpu.SemaphoreType.DMA((4,))],
+        [pltpu.VMEM(lag.shape, bf16), pltpu.VMEM((rows_here, channels), f32), pltpu.SemaphoreType.DMA((2, 4))],
         totals, norm_sq, lag,
         vmem_bytes=SMALL_VMEM_BYTES,
         in_specs=[IN_VMEM, IN_VMEM, ANYWHERE],
-        out_specs=(IN_VMEM,) * 3,
+        out_specs=(IN_VMEM, IN_VMEM, ANYWHERE),
     )
     return mixed, grad_q, grad_k, grad_v, grad_short, grad_skip.reshape(channels), grad_kernel
 

time: 134 us -> 139 us (1.037)
  blocking collectives: 45 us -> 0 us
  waiting for transfers between devices: 18.8 us -> 47 us
  starting transfers between devices: 23.8 us -> 41.6 us
  Pallas kernels: 40.4 us -> 44.7 us
  other arithmetic: 2.27 us -> 0.79 us
    all_to_all x1 -> x0, blocking collectives: 45 us -> none  [exchange(): lax.all_to_all(pieces_first, 'ctx', split_axis=0, concat_axis=0, tiled=True)]
    all_to_all x2 -> x4, waiting for transfers between devices: 12.7 us -> 36.4 us  [exchange(): lax.all_to_all(pieces_first, 'ctx', split_axis=0, concat_axis=0, tiled=True)]
    all_to_all x2 -> x4, starting transfers between devices: 11.9 us -> 29.4 us  [exchange(): lax.all_to_all(pieces_first, 'ctx', split_axis=0, concat_axis=0, tiled=True)]
    pallas_call x10 -> x11, Pallas kernels: 40.4 us -> 44.7 us  [call(): pl.pallas_call(kernel, out_shape=outs, scratch_shapes=scratch, compiler_p...]
    ppermute x7, waiting for transfers between devices: 6.09 us -> 9.46 us  [partners(): lax.ppermute(value, axis, [(i, i ^ step) for i in range(size)])]
    unnamed x10 -> x12, local copies, waits for them, and re-layouts: 1.47 us -> 3.42 us
  transfers between devices with their start and end apart: 11 -> 13, of which waited for: 5 -> 8; matrix products, arithmetic and copies ran while one was open for 2% -> 1% of each run, Pallas kernels for 14% -> 16%
where the time goes in v4:
time: 139 us; the launch traced here: 138 us
  waiting for transfers between devices  47 us (34%)
  Pallas kernels  44.7 us (32%)
  starting transfers between devices  41.6 us (30%)
  local copies, waits for them, and re-layouts  3.42 us (2%)
    pallas_call x11, Pallas kernels, call(): pl.pallas_call(kernel, out_shape=outs, scratch_shapes=scratch, compiler_p...  44.7 us
    all_to_all x4, waiting for transfers between devices, exchange(): lax.all_to_all(pieces_first, 'ctx', split_axis=0, concat_axis=0, tiled=True)  36.4 us
    all_to_all x4, starting transfers between devices, exchange(): lax.all_to_all(pieces_first, 'ctx', split_axis=0, concat_axis=0, tiled=True)  29.4 us
    ppermute x7, waiting for transfers between devices, partners(): lax.ppermute(value, axis, [(i, i ^ step) for i in range(size)])  9.46 us
    ppermute x7, starting transfers between devices, partners(): lax.ppermute(value, axis, [(i, i ^ step) for i in range(size)])  8.59 us
    unnamed x12, local copies, waits for them, and re-layouts  3.42 us
  transfers between devices with their start and end apart: 13, of which 8 were waited for; matrix products, arithmetic and copies ran while one was open for 1% of the time, Pallas kernels for 16%

profile of v4, /device:TPU:0, one launch (start us, length us, event | category | flops | bytes accessed | tf_op | source)
XLA Modules:
  0.0 138.2 jit_solution(1556302654811803174)
XLA Ops:
  0.6 2.0 %shard_map.156 = bf16[16,1,128,128]{3,2,1,0:T(8,128)(2,1)} custom-call(f32[128,2048]{1,0:T(8,128)} %refs_0_.6), custom_call_target="tpu_custom_call" | custom-call | tf_op jit(solution)/shard_map/pallas_call | solution.py:33
  2.6 7.4 %all-to-all-start.1 = ((bf16[16,1,128,128]{3,2,1,0:T(8,128)(2,1)}), bf16[16,1,128,128]{3,2,1,0:T(8,128)(2,1)S(1)}, u32[]{:S(2)}, u32[]{:S(2)}) async-start(bf16[16,1,128,128]{3,2,1,0:T(8,128)(2,1)} %shard_map.156), calls=%async_computation.1 | async-start | bytes 1048576 | tf_op jit(solution)/shard_map/all_to_all | solution.py:682
  10.0 1.6 %shard_map.153 = f32[6,2048]{1,0:T(8,128)} custom-call(bf16[128,2048]{1,0:T(8,128)(2,1)} %refs_0_.7, bf16[128,2048]{1,0:T(8,128)(2,1)} %refs_1_.5, bf16[128,2048]{1,0:T(8,128)(2,1)} %refs_2_.5), custom_call_target="tpu_custom_call" | custom-call | tf_op jit(solution)/shard_map/pallas_call | solution.py:33
  11.5 2.3 %collective-permute-start = (f32[6,2048]{1,0:T(8,128)}, f32[6,2048]{1,0:T(8,128)S(1)}, u32[]{:S(2)}, u32[]{:S(2)}) collective-permute-start(f32[6,2048]{1,0:T(8,128)} %shard_map.153), channel_id=1, source_target_pairs={{0,2},{2,4},{4,6},{6,8},{8,10},{10,12},{12,14},{14,16},{16,18},{18... | collective-permute-start | bytes 147464 | tf_op jit(solution)/shard_map/ppermute | solution.py:753
  13.8 1.1 collective-permute-done.refs_3_.refs_4_.refs_5_
  14.9 0.0 copy-start.5
  14.9 0.6 copy-done.5
  15.6 3.3 %shard_map.155 = bf16[16,2,128,128]{3,2,1,0:T(8,128)(2,1)} custom-call(bf16[128,2048]{1,0:T(8,128)(2,1)} %refs_0_.7, bf16[128,2048]{1,0:T(8,128)(2,1)} %refs_1_.5, bf16[128,2048]{1,0:T(8,128)(2,1)} %refs_2_.5, bf16[128,2048]{1,0:T(8,128)(2,1)} %refs_3_.3, f32[6,2048]{1,0:T(8,128)} %copy-done.5, f32[3,2048]{1,0:T(4,128)} %taps_ref.1), custom_call_target="tpu_custom_call" | custom-call | tf_op jit(solution)/shard_map/pallas_call | solution.py:33
  18.9 5.6 %all-to-all-done.1.filter_ref = bf16[16,1,128,128]{3,2,1,0:T(8,128)(2,1)S(1)} async-done(((bf16[16,1,128,128]{3,2,1,0:T(8,128)(2,1)}), bf16[16,1,128,128]{3,2,1,0:T(8,128)(2,1)S(1)}, u32[]{:S(2)}, u32[]{:S(2)}) %all-to-all-start.1) | async-done | bytes 524320 | tf_op jit(solution)/shard_map/all_to_all | solution.py:682
  24.4 0.0 copy-start.4
  24.4 8.3 %all-to-all-start = ((bf16[16,2,128,128]{3,2,1,0:T(8,128)(2,1)}), bf16[16,2,128,128]{3,2,1,0:T(8,128)(2,1)S(1)}, u32[]{:S(2)}, u32[]{:S(2)}) async-start(bf16[16,2,128,128]{3,2,1,0:T(8,128)(2,1)} %shard_map.155), calls=%async_computation | async-start | bytes 2097152 | tf_op jit(solution)/shard_map/all_to_all | solution.py:682
  32.8 0.0 copy-done.4
  32.8 5.6 %shard_map.157.filter_hbm = f32[4,512,256]{2,1,0:T(8,128)} custom-call(bf16[16,1,128,128]{3,2,1,0:T(8,128)(2,1)} %copy-done.4, f32[16,16]{1,0:T(8,128)} %constant.6.clone.coarse_ref, f32[2,8,16,128]{3,2,1,0:T(8,128)} %constant.7.clone.fine_ref, bf16[512,1024]{1,0:T(8,128)(2,1)} %constant.8.clone.matrix_ref.matrix_hbm), custom_call_target="tpu_custom_call" | custom-call | tf_op jit(solution)/shard_map/pallas_call | solution.py:33
  38.4 17.3 %all-to-all-done.signals_hbm = bf16[16,2,128,128]{3,2,1,0:T(8,128)(2,1)S(1)} async-done(((bf16[16,2,128,128]{3,2,1,0:T(8,128)(2,1)}), bf16[16,2,128,128]{3,2,1,0:T(8,128)(2,1)S(1)}, u32[]{:S(2)}, u32[]{:S(2)}) %all-to-all-start) | async-done | bytes 1048608 | tf_op jit(solution)/shard_map/all_to_all | solution.py:682
  55.7 0.0 copy-start.3
  55.7 1.0 copy-done.3
  56.7 13.0 %shard_map.158 = (bf16[16,2,128,128]{3,2,1,0:T(8,128)(2,1)}, bf16[4,1024,256]{2,1,0:T(8,128)(2,1)}) custom-call(bf16[16,2,128,128]{3,2,1,0:T(8,128)(2,1)} %copy-done.3, f32[4,512,256]{2,1,0:T(8,128)} %shard_map.157.filter_hbm, f32[16,16]{1,0:T(8,128)} %constant.6.clone.coarse_ref, f32[2,8,16,128]{3,2,1,0:T(8,128)} %constant.7.clone.fine_ref, ...), custom_call_target="tpu_custom_call" | custom-call | tf_op jit(solution)/shard_map/pallas_call | solution.py:33
  69.7 6.9 %all-to-all-start.2 = ((bf16[16,2,128,128]{3,2,1,0:T(8,128)(2,1)}), bf16[16,2,128,128]{3,2,1,0:T(8,128)(2,1)S(1)}, u32[]{:S(2)}, u32[]{:S(2)}) async-start(bf16[16,2,128,128]{3,2,1,0:T(8,128)(2,1)} %get-tuple-element.35), calls=%async_computation.2 | async-start | bytes 2097152 | tf_op jit(solution)/shard_map/all_to_all | solution.py:682
  76.5 3.3 %shard_map.154.refs_4_ = f32[3,128,2048]{2,1,0:T(8,128)} custom-call(bf16[128,2048]{1,0:T(8,128)(2,1)} %refs_0_.7, bf16[128,2048]{1,0:T(8,128)(2,1)} %refs_1_.5, bf16[128,2048]{1,0:T(8,128)(2,1)} %refs_2_.5, f32[6,2048]{1,0:T(8,128)} %copy-done.5, f32[3,2048]{1,0:T(4,128)} %taps_ref.1), custom_call_target="tpu_custom_call" | custom-call | tf_op jit(solution)/shard_map/pallas_call | solution.py:33
  79.9 6.1 %shard_map.159 = (bf16[16,128,128]{2,1,0:T(8,128)(2,1)}, f32[1,128]{1,0:T(1,128)}) custom-call(bf16[4,1024,256]{2,1,0:T(8,128)(2,1)} %get-tuple-element.36.split_hbm, f32[16,16]{1,0:T(8,128)} %constant.6.clone.coarse_ref, f32[2,8,16,128]{3,2,1,0:T(8,128)} %constant.7.clone.fine_ref, bf16[512,1024]{1,0:T(8,128)(2,1)} %constant.8.clone.matrix_ref.matrix_hbm), custom_call_target="tpu_custom_call" | custom-call | tf_op jit(solution)/shard_map/pallas_call | solution.py:33
  86.0 13.5 %all-to-all-done.2.refs_8_ = bf16[16,2,128,128]{3,2,1,0:T(8,128)(2,1)S(1)} async-done(((bf16[16,2,128,128]{3,2,1,0:T(8,128)(2,1)}), bf16[16,2,128,128]{3,2,1,0:T(8,128)(2,1)S(1)}, u32[]{:S(2)}, u32[]{:S(2)}) %all-to-all-start.2) | async-done | bytes 1048608 | tf_op jit(solution)/shard_map/all_to_all | solution.py:682
  99.5 0.0 copy-start.2
  99.5 1.0 copy-done.2
  100.5 0.0 copy-start
  100.5 5.8 %shard_map.160 = (bf16[128,2048]{1,0:T(8,128)(2,1)}, bf16[128,2048]{1,0:T(8,128)(2,1)}, bf16[128,2048]{1,0:T(8,128)(2,1)}, bf16[128,2048]{1,0:T(8,128)(2,1)}, f3...) custom-call(bf16[128,2048]{1,0:T(8,128)(2,1)} %refs_0_.7, bf16[128,2048]{1,0:T(8,128)(2,1)} %refs_1_.5, ...), custom_call_target="tpu_custom_call" | custom-call | tf_op jit(solution)/shard_map/pallas_call | solution.py:33
  106.3 6.9 %all-to-all-start.3 = ((bf16[16,1,128,128]{3,2,1,0:T(8,128)(2,1)}), bf16[16,1,128,128]{3,2,1,0:T(8,128)(2,1)S(1)}, u32[]{:S(2)}, u32[]{:S(2)}) async-start(bf16[16,1,128,128]{3,2,1,0:T(8,128)(2,1)} %bitcast.2), calls=%async_computation.3 | async-start | bytes 1048576 | tf_op jit(solution)/shard_map/all_to_all | solution.py:682
  113.1 1.7 %collective-permute-start.4 = (f32[4,2176]{1,0:T(4,128)}, f32[4,2176]{1,0:T(4,128)S(1)}, u32[]{:S(2)}, u32[]{:S(2)}) collective-permute-start(f32[4,2176]{1,0:T(4,128)} %get-tuple-element.49), channel_id=1, source_target_pairs={{0,6},{2,4},{4,2},{6,0},{8,14},{10,12},{12,10},{14,8},{16,22},{18,... | collective-permute-start | bytes 104456 | tf_op jit(solution)/shard_map/ppermute | solution.py:704
  114.8 0.4 collective-permute-start.3
  115.2 0.0 collective-permute-start.2
  115.2 1.3 collective-permute-start.1
  116.5 2.7 %collective-permute-done.4 = f32[4,2176]{1,0:T(4,128)S(1)} collective-permute-done((f32[4,2176]{1,0:T(4,128)}, f32[4,2176]{1,0:T(4,128)S(1)}, u32[]{:S(2)}, u32[]{:S(2)}) %collective-permute-start.4) | collective-permute-done | bytes 34848 | tf_op jit(solution)/shard_map/ppermute | solution.py:704
  119.2 1.8 %collective-permute-done.3 = f32[4,2176]{1,0:T(4,128)S(1)} collective-permute-done((f32[4,2176]{1,0:T(4,128)}, f32[4,2176]{1,0:T(4,128)S(1)}, u32[]{:S(2)}, u32[]{:S(2)}) %collective-permute-start.3) | collective-permute-done | bytes 34848 | tf_op jit(solution)/shard_map/ppermute | solution.py:704
  121.0 0.0 collective-permute-done.2
  121.0 0.8 add_add_fusion.refs_0_
  121.8 4.3 %collective-permute-start.7 = (f32[4,2176]{1,0:T(4,128)S(1)}, f32[4,2176]{1,0:T(4,128)S(1)}, u32[]{:S(2)}, u32[]{:S(2)}) collective-permute-start(f32[4,2176]{1,0:T(4,128)S(1)} %add_add_fusion.refs_0_), channel_id=1, source_target_pairs={{0,24},{2,26},{4,28},{6,30},{8,16},{10,18},{12,20},{14,22},{16,8},... | collective-permute-start | bytes 104456 | tf_op jit(solution)/shard_map/ppermute | solution.py:704
  126.1 0.0 collective-permute-start.6
  126.1 0.6 collective-permute-start.5
  126.7 0.0 collective-permute-done.1.tail_ref
  126.7 0.0 copy-done
  126.7 0.0 copy-start.1
  126.7 0.8 copy-done.1
  127.6 1.6 %shard_map.161 = (bf16[128,2048]{1,0:T(8,128)(2,1)}, bf16[128,2048]{1,0:T(8,128)(2,1)}, bf16[128,2048]{1,0:T(8,128)(2,1)}) custom-call(f32[6,2048]{1,0:T(8,128)S(1)} %copy-done.1, f32[6,2048]{1,0:T(8,128)S(1)} %collective-permute-done.1.tail_ref, f32[3,2048]{1,0:T(4,128)S(1)} %copy-done, ...), custom_call_target="tpu_custom_call", output_to_operand_aliasing={{0}: (3, {}), {1}: (4, {}), {2}: (5, {})} | custom-call | tf_op jit(solution)/shard_map/pallas_call | solution.py:33
  129.2 0.0 collective-permute-done.7.refs_3_
  129.2 2.9 %collective-permute-done.6.refs_2_ = f32[4,2176]{1,0:T(4,128)S(1)} collective-permute-done((f32[4,2176]{1,0:T(4,128)S(1)}, f32[4,2176]{1,0:T(4,128)S(1)}, u32[]{:S(2)}, u32[]{:S(2)}) %collective-permute-start.6) | collective-permute-done | bytes 34848 | tf_op jit(solution)/shard_map/ppermute | solution.py:704
  132.1 0.0 collective-permute-done.5.refs_1_
  132.1 0.1 shard_map.162
  132.3 1.6 %collective-permute-start.8 = (f32[1,128]{1,0:T(1,128)S(1)}, f32[1,128]{1,0:T(1,128)S(1)}, u32[]{:S(2)}, u32[]{:S(2)}) collective-permute-start(f32[1,128]{1,0:T(1,128)S(1)} %get-tuple-element.58), channel_id=1, source_target_pairs={{0,1},{1,0},{2,3},{3,2},{4,5},{5,4},{6,7},{7,6},{8,9},{9,8},{10,11... | collective-permute-start | bytes 1544 | tf_op jit(solution)/shard_map/ppermute | solution.py:704
  133.9 2.0 %collective-permute-done.8 = f32[1,128]{1,0:T(1,128)S(1)} collective-permute-done((f32[1,128]{1,0:T(1,128)S(1)}, f32[1,128]{1,0:T(1,128)S(1)}, u32[]{:S(2)}, u32[]{:S(2)}) %collective-permute-start.8) | collective-permute-done | bytes 544 | tf_op jit(solution)/shard_map/ppermute | solution.py:704
  135.9 0.0 all-to-all-done.3
  135.9 2.4 %shard_map.163 = (f32[3,2048]{1,0:T(4,128)}, f32[1,2048]{1,0:T(1,128)}, f32[128,2048]{1,0:T(8,128)}) custom-call(f32[4,2176]{1,0:T(4,128)S(1)} %get-tuple-element.57.totals_ref, f32[1,128]{1,0:T(1,128)S(1)} %add.15.norm_ref, bf16[16,128,128]{2,1,0:T(8,128)(2,1)S(1)} %bitcast.6), custom_call_target="tpu_custom_call" | custom-call | tf_op jit(solution)/shard_map/pallas_call | solution.py:33
  (1 shorter events, 0.0 us)
Async XLA Ops:
  2.6 21.8 %all-to-all-start.1 = ((bf16[16,1,128,128]{3,2,1,0:T(8,128)(2,1)}), bf16[16,1,128,128]{3,2,1,0:T(8,128)(2,1)S(1)}, u32[]{:S(2)}, u32[]{:S(2)}) async-start(bf16[16,1,128,128]{3,2,1,0:T(8,128)(2,1)} %shard_map.156), calls=%async_computation.1 | async-start | bytes 1048576 | tf_op jit(solution)/shard_map/all_to_all | solution.py:682
  11.5 3.4 %collective-permute-start = (f32[6,2048]{1,0:T(8,128)}, f32[6,2048]{1,0:T(8,128)S(1)}, u32[]{:S(2)}, u32[]{:S(2)}) collective-permute-start(f32[6,2048]{1,0:T(8,128)} %shard_map.153), channel_id=1, source_target_pairs={{0,2},{2,4},{4,6},{6,8},{8,10},{10,12},{12,14},{14,16},{16,18},{18... | collective-permute-start | bytes 147464 | tf_op jit(solution)/shard_map/ppermute | solution.py:753
  14.9 0.6 copy-start.5
  24.4 8.3 %copy-start.4 = (bf16[16,1,128,128]{3,2,1,0:T(8,128)(2,1)}, bf16[16,1,128,128]{3,2,1,0:T(8,128)(2,1)S(1)}, u32[]{:S(2)}) copy-start(bf16[16,1,128,128]{3,2,1,0:T(8,128)(2,1)S(1)} %all-to-all-done.1.filter_ref) | copy-start | bytes 1572868
  24.4 31.3 %all-to-all-start = ((bf16[16,2,128,128]{3,2,1,0:T(8,128)(2,1)}), bf16[16,2,128,128]{3,2,1,0:T(8,128)(2,1)S(1)}, u32[]{:S(2)}, u32[]{:S(2)}) async-start(bf16[16,2,128,128]{3,2,1,0:T(8,128)(2,1)} %shard_map.155), calls=%async_computation | async-start | bytes 2097152 | tf_op jit(solution)/shard_map/all_to_all | solution.py:682
  55.7 1.0 copy-start.3
  69.7 29.8 %all-to-all-start.2 = ((bf16[16,2,128,128]{3,2,1,0:T(8,128)(2,1)}), bf16[16,2,128,128]{3,2,1,0:T(8,128)(2,1)S(1)}, u32[]{:S(2)}, u32[]{:S(2)}) async-start(bf16[16,2,128,128]{3,2,1,0:T(8,128)(2,1)} %get-tuple-element.35), calls=%async_computation.2 | async-start | bytes 2097152 | tf_op jit(solution)/shard_map/all_to_all | solution.py:682
  99.5 1.0 copy-start.2
  100.5 26.3 %copy-start = (f32[3,2048]{1,0:T(4,128)S(1)}, f32[3,2048]{1,0:T(4,128)}, u32[]{:S(2)}) copy-start(f32[3,2048]{1,0:T(4,128)} %taps_ref.1) | copy-start | bytes 73732
  106.3 29.6 %all-to-all-start.3 = ((bf16[16,1,128,128]{3,2,1,0:T(8,128)(2,1)}), bf16[16,1,128,128]{3,2,1,0:T(8,128)(2,1)S(1)}, u32[]{:S(2)}, u32[]{:S(2)}) async-start(bf16[16,1,128,128]{3,2,1,0:T(8,128)(2,1)} %bitcast.2), calls=%async_computation.3 | async-start | bytes 1048576 | tf_op jit(solution)/shard_map/all_to_all | solution.py:682
  113.1 6.1 %collective-permute-start.4 = (f32[4,2176]{1,0:T(4,128)}, f32[4,2176]{1,0:T(4,128)S(1)}, u32[]{:S(2)}, u32[]{:S(2)}) collective-permute-start(f32[4,2176]{1,0:T(4,128)} %get-tuple-element.49), channel_id=1, source_target_pairs={{0,6},{2,4},{4,2},{6,0},{8,14},{10,12},{12,10},{14,8},{16,22},{18,... | collective-permute-start | bytes 104456 | tf_op jit(solution)/shard_map/ppermute | solution.py:704
  114.8 6.2 %collective-permute-start.3 = (f32[4,2176]{1,0:T(4,128)}, f32[4,2176]{1,0:T(4,128)S(1)}, u32[]{:S(2)}, u32[]{:S(2)}) collective-permute-start(f32[4,2176]{1,0:T(4,128)} %get-tuple-element.49), channel_id=1, source_target_pairs={{0,4},{2,6},{4,0},{6,2},{8,12},{10,14},{12,8},{14,10},{16,20},{18,... | collective-permute-start | bytes 104456 | tf_op jit(solution)/shard_map/ppermute | solution.py:704
  115.2 5.8 %collective-permute-start.2 = (f32[4,2176]{1,0:T(4,128)}, f32[4,2176]{1,0:T(4,128)S(1)}, u32[]{:S(2)}, u32[]{:S(2)}) collective-permute-start(f32[4,2176]{1,0:T(4,128)} %get-tuple-element.49), channel_id=1, source_target_pairs={{0,2},{2,0},{4,6},{6,4},{8,10},{10,8},{12,14},{14,12},{16,18},{18,... | collective-permute-start | bytes 104456 | tf_op jit(solution)/shard_map/ppermute | solution.py:704
  115.2 11.6 %collective-permute-start.1 = (f32[6,2048]{1,0:T(8,128)}, f32[6,2048]{1,0:T(8,128)S(1)}, u32[]{:S(2)}, u32[]{:S(2)}) collective-permute-start(f32[6,2048]{1,0:T(8,128)} %get-tuple-element.40), channel_id=1, source_target_pairs={{2,0},{4,2},{6,4},{8,6},{10,8},{12,10},{14,12},{16,14},{18,16},{20... | collective-permute-start | bytes 147464 | tf_op jit(solution)/shard_map/ppermute | solution.py:800
  121.8 7.4 %collective-permute-start.7 = (f32[4,2176]{1,0:T(4,128)S(1)}, f32[4,2176]{1,0:T(4,128)S(1)}, u32[]{:S(2)}, u32[]{:S(2)}) collective-permute-start(f32[4,2176]{1,0:T(4,128)S(1)} %add_add_fusion.refs_0_), channel_id=1, source_target_pairs={{0,24},{2,26},{4,28},{6,30},{8,16},{10,18},{12,20},{14,22},{16,8},... | collective-permute-start | bytes 104456 | tf_op jit(solution)/shard_map/ppermute | solution.py:704
  126.1 6.0 %collective-permute-start.6 = (f32[4,2176]{1,0:T(4,128)S(1)}, f32[4,2176]{1,0:T(4,128)S(1)}, u32[]{:S(2)}, u32[]{:S(2)}) collective-permute-start(f32[4,2176]{1,0:T(4,128)S(1)} %add_add_fusion.refs_0_), channel_id=1, source_target_pairs={{0,16},{2,18},{4,20},{6,22},{8,24},{10,26},{12,28},{14,30},{16,0},... | collective-permute-start | bytes 104456 | tf_op jit(solution)/shard_map/ppermute | solution.py:704
  126.1 6.0 %collective-permute-start.5 = (f32[4,2176]{1,0:T(4,128)S(1)}, f32[4,2176]{1,0:T(4,128)S(1)}, u32[]{:S(2)}, u32[]{:S(2)}) collective-permute-start(f32[4,2176]{1,0:T(4,128)S(1)} %add_add_fusion.refs_0_), channel_id=1, source_target_pairs={{0,8},{2,10},{4,12},{6,14},{8,0},{10,2},{12,4},{14,6},{16,24},{18,... | collective-permute-start | bytes 104456 | tf_op jit(solution)/shard_map/ppermute | solution.py:704
  126.7 0.8 copy-start.1
  132.3 3.6 %collective-permute-start.8 = (f32[1,128]{1,0:T(1,128)S(1)}, f32[1,128]{1,0:T(1,128)S(1)}, u32[]{:S(2)}, u32[]{:S(2)}) collective-permute-start(f32[1,128]{1,0:T(1,128)S(1)} %get-tuple-element.58), channel_id=1, source_target_pairs={{0,1},{1,0},{2,3},{3,2},{4,5},{5,4},{6,7},{7,6},{8,9},{9,8},{10,11... | collective-permute-start | bytes 1544 | tf_op jit(solution)/shard_map/ppermute | solution.py:704

commit v5 on v4

--- a/solution.py
+++ b/solution.py
@@ -37,6 +37,28 @@
         compiler_params=pltpu.CompilerParams(vmem_limit_bytes=vmem_bytes),
         **options,
     )(*args)
+
+
+def spread_copies(held_ref, outside, me, sems):
+    if len(outside) == 1:
+        return [pltpu.make_async_copy(held_ref, outside[0], sems.at[0])]
+    return [pltpu.make_async_copy(held_ref.at[me ^ idx], ref, sems.at[idx]) for idx, ref in enumerate(outside)]
+
+
+def collect_copies(outside, held_ref, me, sems):
+    if len(outside) == 1:
+        return [pltpu.make_async_copy(outside[0], held_ref, sems.at[0])]
+    return [pltpu.make_async_copy(ref, held_ref.at[me ^ idx], sems.at[idx]) for idx, ref in enumerate(outside)]
+
+
+def start_all(copies):
+    for copy in copies:
+        copy.start()
+
+
+def wait_all(copies):
+    for copy in copies:
+        copy.wait()
 
 
 def leaf_phases(count):
@@ -242,30 +264,21 @@
     return stage
 
 
-def filter_kernel(
-    filter_ref, coarse_ref, fine_ref, matrix_ref, spec_ref, twist_ref, split_ref,
+def products_kernel(
+    count, me_ref, coarse_ref, fine_ref, matrix_hbm, *refs
 ):
-    rows_here = filter_ref.shape[2]
-    run_all([twist_stage(coarse_ref, fine_ref, twist_ref, rows_here)], rows_here)
-    run_all([leaves_stage(filter_ref, 0, twist_ref, split_ref)], rows_here)
-    run_all([], rows_here, (matrix_ref, split_ref, spec_ref))
-
-
-def products_kernel(
-    signals_hbm, filter_hbm, coarse_ref, fine_ref, matrix_hbm, results_hbm, lag_hbm,
-    twist_ref, matrix_ref, signals_ref, results_ref, one_split, two_split, lag_split,
-    filter_ref, product_ref, cotan_ref, time_ref, sems,
-):
+    signals_hbm = refs[:count]
+    results_hbm = refs[count : 2 * count]
+    (
+        lag_hbm, twist_ref, matrix_ref, signals_ref, results_ref, one_split, two_split, lag_split,
+        filter_ref, product_ref, cotan_ref, time_ref, arrival_sems, return_sems, sems,
+    ) = refs[2 * count :]
+    me = me_ref[0]
     rows_here = signals_ref.shape[2]
-    arrivals = [
-        pltpu.make_async_copy(signals_hbm.at[:, kind], signals_ref.at[:, kind], sems.at[kind]) for kind in range(2)
-    ]
-    matrix_copy = pltpu.make_async_copy(matrix_hbm, matrix_ref, sems.at[2])
-    filter_copy = pltpu.make_async_copy(filter_hbm, filter_ref, sems.at[3])
-    lag_copy = pltpu.make_async_copy(lag_split, lag_hbm, sems.at[4])
-    returns = [
-        pltpu.make_async_copy(results_ref.at[:, kind], results_hbm.at[:, kind], sems.at[5 + kind]) for kind in range(2)
-    ]
+    arrivals = collect_copies(signals_hbm, signals_ref, me, arrival_sems)
+    returns = spread_copies(results_ref, results_hbm, me, return_sems)
+    matrix_copy = pltpu.make_async_copy(matrix_hbm, matrix_ref, sems.at[0])
+    lag_copy = pltpu.make_async_copy(lag_split, lag_hbm, sems.at[1])
 
     def leaves(kind, split_ref):
         return leaves_stage(signals_ref, kind, twist_ref, split_ref)
@@ -280,43 +293,40 @@
 
         return signal_stage(from_ref, twist_ref, rows_here, write)
 
-    for copy in (arrivals[0], matrix_copy, arrivals[1], filter_copy):
-        copy.start()
+    start_all(arrivals)
+    matrix_copy.start()
     run_all([twist_stage(coarse_ref, fine_ref, twist_ref, rows_here)], rows_here)
-    arrivals[0].wait()
-    run_all([leaves(0, one_split)], rows_here)
-    arrivals[1].wait()
+    wait_all(arrivals)
+    run_all([leaves(2, one_split)], rows_here)
     matrix_copy.wait()
-    run_all([leaves(1, two_split)], rows_here, (matrix_ref, one_split, product_ref))
-    filter_copy.wait()
-    run_all([combine(filter_ref, product_ref, one_split, False)], rows_here, (matrix_ref, two_split, cotan_ref))
-    run_all([combine(filter_ref, cotan_ref, two_split, True)], rows_here, (matrix_ref, one_split, time_ref))
+    run_all([leaves(0, two_split)], rows_here, (matrix_ref, one_split, filter_ref))
+    run_all([leaves(1, one_split)], rows_here, (matrix_ref, two_split, product_ref))
+    run_all([combine(filter_ref, product_ref, two_split, False)], rows_here, (matrix_ref, one_split, cotan_ref))
+    run_all([combine(filter_ref, cotan_ref, one_split, True)], rows_here, (matrix_ref, two_split, time_ref))
     run_all(
         [combine(product_ref, cotan_ref, lag_split, True), result(0, time_ref)],
-        rows_here, (matrix_ref, two_split, filter_ref),
+        rows_here, (matrix_ref, one_split, filter_ref),
     )
     lag_copy.start()
-    returns[0].start()
     run_all([result(1, filter_ref)], rows_here)
-    returns[1].start()
+    start_all(returns)
     lag_copy.wait()
-    returns[0].wait()
-    returns[1].wait()
+    wait_all(returns)
 
 
 def lag_kernel(
-    split_hbm, coarse_ref, fine_ref, matrix_hbm, lag_ref, square_ref, twist_ref, matrix_ref, split_ref, time_ref, sems
+    count, me_ref, split_hbm, coarse_ref, fine_ref, matrix_hbm, *refs
 ):
+    lag_hbm = refs[:count]
+    square_ref, lag_ref, twist_ref, matrix_ref, split_ref, time_ref, return_sems, sems = refs[count:]
     rows_here = lag_ref.shape[1]
     copies = [
         pltpu.make_async_copy(matrix_hbm, matrix_ref, sems.at[0]),
         pltpu.make_async_copy(split_hbm, split_ref, sems.at[1]),
     ]
-    for copy in copies:
-        copy.start()
+    start_all(copies)
     run_all([twist_stage(coarse_ref, fine_ref, twist_ref, rows_here)], rows_here)
-    for copy in copies:
-        copy.wait()
+    wait_all(copies)
     run_all([], rows_here, (matrix_ref, split_ref, time_ref))
 
     def write(piece, rows, value, carry):
@@ -326,13 +336,18 @@
     square = run_all(
         [signal_stage(time_ref, twist_ref, rows_here, write)], rows_here, None, jnp.zeros((CHUNK, LANES), f32)
     )
+    returns = spread_copies(lag_ref, lag_hbm, me_ref[0], return_sems)
+    start_all(returns)
     square_ref[...] = jnp.sum(square, axis=0, keepdims=True)
+    wait_all(returns)
 
 
 class Transforms:
-    def __init__(self, pieces, rows_here):
+    def __init__(self, pieces, rows_here, me):
         outer = pieces * rows_here // SPAN
         pairs = outer // 2
+        self.me = me
+        self.pieces = pieces
         coarse = twist_angles(outer, CHUNK * np.arange(CHUNKS)).T
         fine = twist_angles(outer, np.arange(CHUNK))[..., None] * np.ones(LANES)
         self.tables = [
@@ -340,49 +355,44 @@
             jnp.asarray(np.stack([np.cos(fine), np.sin(fine)]).astype(np.float32)),
             jnp.asarray(matrix_blocks()),
         ]
-        self.spec = jax.ShapeDtypeStruct((pairs, BOTH, 2 * LANES), f32)
         self.split = jax.ShapeDtypeStruct((pairs, PASSES * BOTH, 2 * LANES), bf16)
-        self.signal = jax.ShapeDtypeStruct((pieces, rows_here, LANES), bf16)
-        self.result = jax.ShapeDtypeStruct((pieces, 2, rows_here, LANES), bf16)
+        self.signal = jax.ShapeDtypeStruct((rows_here, LANES), bf16)
+        self.result = jax.ShapeDtypeStruct((2, rows_here, LANES), bf16)
         self.square = jax.ShapeDtypeStruct((1, LANES), f32)
-        self.pair_work = pltpu.VMEM(self.result.shape, bf16)
-        self.work = pltpu.VMEM(self.spec.shape, f32)
+        self.work = pltpu.VMEM((pairs, BOTH, 2 * LANES), f32)
         self.split_work = pltpu.VMEM(self.split.shape, bf16)
         self.twist_work = pltpu.VMEM((2, outer, SPAN, LANES), f32)
         self.matrix_work = pltpu.VMEM(self.tables[2].shape, bf16)
 
-    def filter(self, signal):
-        return call(
-            filter_kernel, self.spec, [self.twist_work, self.split_work],
-            signal, *self.tables,
-            in_specs=[IN_VMEM, IN_SMEM, IN_VMEM, IN_VMEM],
-            out_specs=IN_VMEM,
-        )
-
-    def products(self, signals, filter_spec):
-        return call(
-            products_kernel, (self.result, self.split),
-            [self.twist_work, self.matrix_work, self.pair_work, self.pair_work]
+    def products(self, signals):
+        *results, lag_split = call(
+            functools.partial(products_kernel, self.pieces), (self.result,) * self.pieces + (self.split,),
+            [self.twist_work, self.matrix_work]
+            + [pltpu.VMEM((self.pieces, kinds) + self.signal.shape, bf16) for kinds in (3, 2)]
             + [self.split_work] * 3
             + [self.work] * 4
-            + [pltpu.SemaphoreType.DMA((7,))],
-            signals, filter_spec, *self.tables,
-            in_specs=[ANYWHERE, ANYWHERE, IN_SMEM, IN_VMEM, ANYWHERE],
-            out_specs=(ANYWHERE, ANYWHERE),
+            + [pltpu.SemaphoreType.DMA((count,)) for count in (self.pieces, self.pieces, 2)],
+            self.me, *self.tables, *signals,
+            in_specs=[IN_SMEM, IN_SMEM, IN_VMEM, ANYWHERE] + [ANYWHERE] * self.pieces,
+            out_specs=(ANYWHERE,) * (self.pieces + 1),
         )
+        return results, lag_split
 
     def lag(self, lag_split):
-        return call(
-            lag_kernel, (self.signal, self.square),
-            [self.twist_work, self.matrix_work, self.split_work, self.work, pltpu.SemaphoreType.DMA((2,))],
-            lag_split, *self.tables,
-            in_specs=[ANYWHERE, IN_SMEM, IN_VMEM, ANYWHERE],
-            out_specs=(IN_VMEM, IN_VMEM),
+        *results, squares = call(
+            functools.partial(lag_kernel, self.pieces), (self.signal,) * self.pieces + (self.square,),
+            [pltpu.VMEM((self.pieces,) + self.signal.shape, bf16)]
+            + [self.twist_work, self.matrix_work, self.split_work, self.work]
+            + [pltpu.SemaphoreType.DMA((count,)) for count in (self.pieces, 2)],
+            self.me, lag_split, *self.tables,
+            in_specs=[IN_SMEM, ANYWHERE, IN_SMEM, IN_VMEM, ANYWHERE],
+            out_specs=(ANYWHERE,) * self.pieces + (IN_VMEM,),
         )
+        return results, squares
 
 
 class PlainTransforms:
-    def __init__(self, pieces, rows_here):
+    def __init__(self, pieces, rows_here, me):
         self.seq_len = pieces * rows_here
         self.pieces = pieces
         self.outer = self.seq_len // SPAN
@@ -416,84 +426,98 @@
         parts = from_leaves([(leaf_re[leaf], leaf_im[leaf]) for leaf in range(self.outer)], 1.0 / self.seq_len)
         return jnp.stack(parts).reshape(self.pieces, self.seq_len // self.pieces, -1)
 
-    def filter(self, signal):
-        return self.spectrum(signal[:, 0])
-
-    def products(self, signals, taps):
-        product, cotan = (self.spectrum(signals[:, kind]) for kind in range(2))
+    def products(self, signals):
+        product, cotan, taps = (self.spectrum(signals[0][:, kind]) for kind in range(3))
         conv = self.back(taps[0] * product[0] - taps[1] * product[1], taps[0] * product[1] + taps[1] * product[0])
         corr = self.back(taps[0] * cotan[0] + taps[1] * cotan[1], taps[0] * cotan[1] - taps[1] * cotan[0])
         lag = (
             product[0] * cotan[0] + product[1] * cotan[1],
             product[0] * cotan[1] - product[1] * cotan[0],
         )
-        return jnp.stack([conv, corr], axis=1).astype(bf16), lag
+        return [jnp.stack([conv, corr], axis=1).astype(bf16)], lag
 
     def lag(self, lag_spec):
         lag = self.back(*lag_spec)
         squares = jnp.sum(lag * lag, axis=(0, 1))
-        return lag.astype(bf16), jnp.zeros((1, LANES), f32).at[0, : squares.shape[0]].set(squares)
+        return [lag.astype(bf16)], jnp.zeros((1, LANES), f32).at[0, : squares.shape[0]].set(squares)
 
 
 def group(idx):
     return pl.ds(pl.multiple_of(idx * LANES, LANES), LANES)
 
 
-def streamed(work, steps, per_step, places, in_count, out_count, kept, *refs):
-    moved = in_count + out_count
-    hbm = refs[:moved]
-    kept_refs = refs[moved : moved + kept]
-    held = refs[moved + kept : 2 * moved + kept]
-    scratch = refs[2 * moved + kept : -1]
-    sems = refs[-1]
+def streamed(work, steps, per_step, cuts, counts, me_ref, *refs):
+    refs = list(refs)
+
+    def take(count):
+        taken = refs[:count]
+        del refs[:count]
+        return taken
+
+    ins, gathered, outs, spread, kept = (take(count) for count in counts)
+    in_held = take(len(ins))
+    gathered_held = take(min(len(gathered), 1))
+    out_held = take(len(outs))
+    spread_held = take(min(len(spread), 1))
+    partner_sems, sems = refs[-2:]
+    me = me_ref[0]
+    moved = len(ins) + len(outs)
 
     def copy(place, step):
-        outside = hbm[place].at[places[place][0](step)]
-        inside = held[place].at[places[place][1](step)]
-        ends = (outside, inside) if place < in_count else (inside, outside)
+        outside = (ins + outs)[place].at[cuts[place](step)]
+        inside = (in_held + out_held)[place].at[cuts[place](step)]
+        ends = (outside, inside) if place < len(ins) else (inside, outside)
         return pltpu.make_async_copy(*ends, sems.at[place, step])
 
     def arrivals(step):
-        return [copy(place, step) for place in range(in_count) if places[place][0](step) is not None]
-
+        return [copy(place, step) for place in range(len(ins)) if cuts[place](step) is not None]
+
+    from_partners = collect_copies(gathered, gathered_held[0], me, partner_sems.at[0]) if gathered else []
+    to_partners = spread_copies(spread_held[0], spread, me, partner_sems.at[1]) if spread else []
+    start_all(from_partners)
     for step in range(steps):
-        for arrival in arrivals(step):
-            arrival.start()
+        start_all(arrivals(step))
+    wait_all(from_partners)
     for step in range(steps):
-        for arrival in arrivals(step):
-            arrival.wait()
+        wait_all(arrivals(step))
 
         def one(idx, carry):
-            work(idx, held[:in_count], held[in_count:] + kept_refs, scratch)
+            work(idx, in_held + gathered_held, out_held + spread_held + kept, refs[:-2])
             return carry
 
         lax.fori_loop(step * per_step, (step + 1) * per_step, one, 0)
-        for place in range(in_count, moved):
-            copy(place, step).start()
+        start_all([copy(place, step) for place in range(len(ins), moved)])
+    start_all(to_partners)
     for step in range(steps):
-        for place in range(in_count, moved):
-            copy(place, step).wait()
-
-
-def stream_call(work, steps, per_step, operands, results, scratch=(), aliases=(), kept=()):
-    arrays = [operand[0] for operand in operands]
-    shapes = [jax.ShapeDtypeStruct(array.shape, array.dtype) for array in arrays] + [result[0] for result in results]
-    cuts = [entry[1] for entry in operands] + [entry[1] for entry in results]
-    held = [pltpu.VMEM(entry[2] or shape.shape, shape.dtype) for entry, shape in zip(operands + results, shapes)]
-    extra = list(aliases)
-    kernel = functools.partial(streamed, work, steps, per_step, cuts, len(arrays), len(results), len(kept))
-
-    def with_aliases(*refs):
-        kernel(*refs[: len(arrays)], *refs[len(arrays) + len(extra) :])
-
+        wait_all([copy(place, step) for place in range(len(ins), moved)])
+    wait_all(to_partners)
+
+
+def stream_call(
+    work, steps, per_step, me, operands=(), gathered=(), results=(), spread=(), kept=(), held=None, scratch=()
+):
+    ins = [operand[0] for operand in operands]
+    outs = [result[0] for result in results]
+    cuts = [entry[1] for entry in list(operands) + list(results)]
+    counts = [len(part) for part in (ins, gathered, outs, spread, kept)]
+
+    def room(arrays):
+        return [pltpu.VMEM(array.shape, array.dtype) for array in arrays]
+
+    partner_room = [pltpu.VMEM(held, bf16)] if held else []
+    most = max(len(gathered), len(spread), 1)
     return call(
-        with_aliases,
-        tuple(result[0] for result in results) + tuple(kept),
-        held + list(scratch) + [pltpu.SemaphoreType.DMA((len(shapes), steps))],
-        *arrays, *extra,
-        in_specs=[ANYWHERE] * (len(arrays) + len(extra)),
-        out_specs=(ANYWHERE,) * len(results) + (IN_VMEM,) * len(kept),
-        input_output_aliases={len(arrays) + idx: idx for idx in range(len(extra))},
+        functools.partial(streamed, work, steps, per_step, cuts, counts),
+        tuple(outs) + tuple(spread) + tuple(kept),
+        room(ins)
+        + (partner_room if gathered else [])
+        + room(outs)
+        + (partner_room if spread else [])
+        + list(scratch)
+        + [pltpu.SemaphoreType.DMA((2, most)), pltpu.SemaphoreType.DMA((max(len(cuts), 1), steps))],
+        me, *ins, *gathered,
+        in_specs=[IN_SMEM] + [ANYWHERE] * (len(ins) + len(gathered)),
+        out_specs=(ANYWHERE,) * (len(outs) + len(spread)) + (IN_VMEM,) * len(kept),
     )
 
 
@@ -501,14 +525,7 @@
     def place(step):
         return (slice(None),) * (rank - 1) + (pl.ds(step * width, width),)
 
-    return place, place
-
-
-def cut_groups(per_step):
-    def place(step):
-        return (pl.ds(step * per_step, per_step),)
-
-    return place, place
+    return place
 
 
 def cut_none(step):
@@ -517,10 +534,6 @@
 
 def row_blocks(rows_here):
     return [slice(start, start + ROWS) for start in range(0, rows_here, ROWS)]
-
-
-def pack_work(idx, operands, results, scratch):
-    results[0][idx, 0] = operands[0][:, group(idx)].astype(bf16)
 
 
 def extend_rows(lead, in_ref, lanes, ext_ref):
@@ -543,13 +556,14 @@
 
 
 def signals_work(idx, operands, results, exts):
-    q_ref, k_ref, v_ref, grad_ref, lead_ref, taps_ref = operands
+    q_ref, k_ref, v_ref, grad_ref, kernel_ref, lead_ref, taps_ref = operands
     taps = taps_ref[:, group(idx)]
     extend_three(idx, operands, lead_ref, taps.shape[0] - 1, exts)
     for rows in row_blocks(q_ref.shape[0]):
         q_short, k_short, v_short = (short_conv(ext, taps, rows) for ext in exts)
         results[0][idx, 0, rows, :] = (k_short * v_short).astype(bf16)
         results[0][idx, 1, rows, :] = (grad_ref[rows, group(idx)].astype(f32) * q_short).astype(bf16)
+        results[0][idx, 2, rows, :] = kernel_ref[rows, group(idx)].astype(bf16)
 
 
 def short_work(idx, operands, results, exts):
@@ -566,7 +580,7 @@
 
 
 def finish_work(idx, operands, results, exts):
-    q_ref, k_ref, v_ref, grad_ref, short_ref, lead_ref, taps_ref, skip_ref, long_ref, squares_ref = operands
+    q_ref, k_ref, v_ref, grad_ref, short_ref, lead_ref, taps_ref, skip_ref, squares_ref, long_ref = operands
     mixed_ref, grad_q_ref, grad_k_ref, grad_v_ref, front_ref, back_ref, sums_ref = results
     lanes = group(idx)
     taps = taps_ref[:, lanes]
@@ -651,31 +665,28 @@
     square_ref[...] = jnp.full(square_ref.shape, square)
 
 
-def scale_kernel(limit, totals_ref, norm_ref, lag_hbm, taps_out, skip_out, kernel_hbm, lag_ref, kernel_ref, sems):
+def scale_kernel(limit, count, me_ref, totals_ref, norm_ref, *refs):
+    lag_hbm = refs[:count]
+    taps_out, skip_out, kernel_hbm, lag_ref, kernel_ref, arrival_sems, return_sems = refs[count:]
     taps_count, channels = taps_out.shape
     groups = lag_ref.shape[0]
-    per_step = max(groups // 4, 1)
-    steps = groups // per_step
-    arrivals = []
-    returns = []
-    for step in range(steps):
-        here = pl.ds(step * per_step, per_step)
-        lanes = pl.ds(step * per_step * LANES, per_step * LANES)
-        arrivals.append(pltpu.make_async_copy(lag_hbm.at[here], lag_ref.at[here], sems.at[0, step]))
-        returns.append(pltpu.make_async_copy(kernel_ref.at[:, lanes], kernel_hbm.at[:, lanes], sems.at[1, step]))
-        arrivals[step].start()
+    arrivals = collect_copies(lag_hbm, lag_ref, me_ref[0], arrival_sems)
+    start_all(arrivals)
     factor = limit / jnp.maximum(jnp.sqrt(norm_ref[...]), limit)
-    for step in range(steps):
-        arrivals[step].wait()
-        for idx in range(step * per_step, (step + 1) * per_step):
-            kernel_ref[:, idx * LANES : (idx + 1) * LANES] = lag_ref[idx].astype(f32) * factor
-        returns[step].start()
     for idx in range(groups):
         lanes = slice(idx * LANES, (idx + 1) * LANES)
         taps_out[:, lanes] = totals_ref[0:taps_count, lanes] * factor
         skip_out[:, lanes] = totals_ref[taps_count : taps_count + 1, lanes] * factor
-    for step in range(steps):
-        returns[step].wait()
+    wait_all(arrivals)
+    per_step = max(groups // 4, 1)
+    returns = []
+    for step in range(groups // per_step):
+        for idx in range(step * per_step, (step + 1) * per_step):
+            kernel_ref[:, idx * LANES : (idx + 1) * LANES] = lag_ref[idx].astype(f32) * factor
+        lanes = pl.ds(step * per_step * LANES, per_step * LANES)
+        returns.append(pltpu.make_async_copy(kernel_ref.at[:, lanes], kernel_hbm.at[:, lanes], return_sems.at[step]))
+        returns[step].start()
+    wait_all(returns)
 
 
 def exchange(pieces_first):
@@ -697,6 +708,16 @@
         return parts
     joined = parts.reshape(pieces * share // LANES, LANES // share, kinds, rows, share)
     return joined.transpose(0, 2, 3, 1, 4).reshape(-1, kinds, rows, LANES)
+
+
+def send(arrays, to_all, from_all):
+    size = lax.axis_size("ctx")
+    if len(arrays) == 1:
+        return [from_all(exchange(to_all(arrays[0])))]
+    received = {0: arrays[0]}
+    for idx in reversed(range(1, size)):
+        received[idx] = lax.ppermute(arrays[idx], "ctx", [(i, i ^ idx) for i in range(size)])
+    return [received[idx] for idx in range(size)]
 
 
 def partners(value, axis, steps):
@@ -732,13 +753,15 @@
     steps = groups // per_step
     lanes2 = cut_lanes(per_step * LANES, 2)
     lanes3 = cut_lanes(per_step * LANES, 3)
-    transforms = (Transforms if share == LANES else PlainTransforms)(pieces, rows_here)
-    stream = functools.partial(stream_call, steps=steps, per_step=per_step)
+    me = lax.axis_index("ctx").reshape(1)
+    direct = share == LANES
+    transforms = (Transforms if direct else PlainTransforms)(pieces, rows_here, me)
+    stream = functools.partial(stream_call, steps=steps, per_step=per_step, me=me)
 
     flat = jax.ShapeDtypeStruct((rows_here, channels), bf16)
     halo = jax.ShapeDtypeStruct((3 * halo_rows, channels), f32)
-    one_sent = jax.ShapeDtypeStruct((groups, 1, rows_here, LANES), bf16)
-    two_sent = jax.ShapeDtypeStruct((groups, 2, rows_here, LANES), bf16)
+    sent_dims = (groups, 3, rows_here, LANES)
+    sent = jax.ShapeDtypeStruct(sent_dims[1:] if direct else sent_dims, bf16)
     exts = [pltpu.VMEM((rows_here + PAD, LANES), f32)] * 3
     last_block = 16
     last_spec = pl.BlockSpec((last_block, channels), lambda i: (rows_here // last_block - 1, 0))
@@ -752,42 +775,37 @@
     )
     lead = lax.ppermute(lead, "ctx", [(i, i + 1) for i in range(pieces - 1)])
 
-    (packed,) = stream(
-        pack_work,
-        operands=[(kernel, lanes2, None)],
-        results=[(one_sent, cut_groups(per_step), None)],
-    )
-    filter_here = exchange(to_pieces(packed, pieces))
-    (signals,) = stream(
+    signals = stream(
         signals_work,
-        operands=[(x, lanes2, None) for x in (q_in, k_in, v_in, grad_out, lead, short_filter)],
-        results=[(two_sent, cut_groups(per_step), None)],
+        operands=[(x, lanes2) for x in (q_in, k_in, v_in, grad_out, kernel, lead, short_filter)],
+        spread=(sent,) * (pieces if direct else 1),
+        held=sent_dims,
         scratch=exts,
     )
-    signals_here = exchange(to_pieces(signals, pieces))
+    signals_here = send(signals, lambda x: to_pieces(x, pieces), lambda x: x)
     (short,) = stream(
         short_work,
-        operands=[(x, lanes2, None) for x in (q_in, k_in, v_in, lead, short_filter)],
-        results=[(jax.ShapeDtypeStruct((3, rows_here, channels), f32), lanes3, None)],
+        operands=[(x, lanes2) for x in (q_in, k_in, v_in, lead, short_filter)],
+        results=[(jax.ShapeDtypeStruct((3, rows_here, channels), f32), lanes3)],
         scratch=exts,
     )
-    filter_spec = transforms.filter(filter_here)
-    long_here, lag_spec = transforms.products(signals_here, filter_spec)
-    long = to_groups(exchange(long_here))
+    long_here, lag_spec = transforms.products(signals_here)
+    long = send(long_here, lambda x: x, to_groups)
     lag_here, lag_squares = transforms.lag(lag_spec)
+    lag = send(lag_here, lambda x: x[:, None], lambda x: to_groups(x)[:, 0])
 
     mixed, grad_q, grad_k, grad_v, front, back, sums = stream(
         finish_work,
-        operands=[(x, lanes2, None) for x in (q_in, k_in, v_in, grad_out)]
-        + [(short, lanes3, None)]
-        + [(x, lanes2, None) for x in (lead, short_filter, skip.reshape(1, channels))]
-        + [(long, cut_groups(per_step), None), (lag_squares, (cut_none, cut_none), None)],
-        results=[(flat, lanes2, None)] * 4,
+        operands=[(x, lanes2) for x in (q_in, k_in, v_in, grad_out)]
+        + [(short, lanes3)]
+        + [(x, lanes2) for x in (lead, short_filter, skip.reshape(1, channels))]
+        + [(lag_squares, cut_none)],
+        gathered=long,
+        held=(groups, 2, rows_here, LANES),
+        results=[(flat, lanes2)] * 4,
         scratch=exts,
         kept=[halo, halo, jax.ShapeDtypeStruct((taps_count + 1, channels + LANES), f32)],
     )
-    lag_here, sums = lax.optimization_barrier((lag_here, sums))
-    lag = to_groups(exchange(lag_here[:, None]))[:, 0]
 
     totals = sums
     rounds = rounds_of(pieces)
@@ -821,16 +839,19 @@
 
     limit = math.sqrt(float(seq_len * channels * sides))
     grad_short, grad_skip, grad_kernel = call(
-        functools.partial(scale_kernel, limit),
+        functools.partial(scale_kernel, limit, len(lag)),
         (
             jax.ShapeDtypeStruct((taps_count, channels), f32),
             jax.ShapeDtypeStruct((1, channels), f32),
             jax.ShapeDtypeStruct((rows_here, channels), f32),
         ),
-        [pltpu.VMEM(lag.shape, bf16), pltpu.VMEM((rows_here, channels), f32), pltpu.SemaphoreType.DMA((2, 4))],
-        totals, norm_sq, lag,
+        [
+            pltpu.VMEM((groups, rows_here, LANES), bf16), pltpu.VMEM((rows_here, channels), f32),
+            pltpu.SemaphoreType.DMA((len(lag),)), pltpu.SemaphoreType.DMA((4,)),
+        ],
+        me, totals, norm_sq, *lag,
         vmem_bytes=SMALL_VMEM_BYTES,
-        in_specs=[IN_VMEM, IN_VMEM, ANYWHERE],
+        in_specs=[IN_SMEM, IN_VMEM, IN_VMEM] + [ANYWHERE] * len(lag),
         out_specs=(IN_VMEM, IN_VMEM, ANYWHERE),
     )
     return mixed, grad_q, grad_k, grad_v, grad_short, grad_skip.reshape(channels), grad_kernel

time: 139 us -> 167 us (1.20)
  starting transfers between devices: 41.6 us -> 97.6 us
  waiting for transfers between devices: 47 us -> 20.3 us
    ppermute x0 -> x45, starting transfers between devices: none -> 84.2 us  [send(): lax.ppermute(arrays[idx], 'ctx', [(i, i ^ idx) for i in range(size)])]
    all_to_all x4 -> x0, waiting for transfers between devices: 36.4 us -> none  [exchange(): lax.all_to_all(pieces_first, 'ctx', split_axis=0, concat_axis=0, tiled=True)]
    all_to_all x4 -> x0, starting transfers between devices: 29.4 us -> none  [exchange(): lax.all_to_all(pieces_first, 'ctx', split_axis=0, concat_axis=0, tiled=True)]
    ppermute x0 -> x45, waiting for transfers between devices: none -> 18.8 us  [send(): lax.ppermute(arrays[idx], 'ctx', [(i, i ^ idx) for i in range(size)])]
    ppermute x7, waiting for transfers between devices: 9.46 us -> 0.41 us  [partners(): lax.ppermute(value, axis, [(i, i ^ step) for i in range(size)])]
    pallas_call x11 -> x9, Pallas kernels: 44.7 us -> 43.7 us  [call(): pl.pallas_call(kernel, out_shape=outs, scratch_shapes=scratch, compiler_p...]
    unnamed x12 -> x98, local copies, waits for them, and re-layouts: 3.42 us -> 2.78 us
  transfers between devices with their start and end apart: 13 -> 54, of which waited for: 8 -> 10; matrix products, arithmetic and copies ran while one was open for 1% -> 0% of each run, Pallas kernels for 16% -> 7%
where the time goes in v5:
time: 167 us; the launch traced here: 166 us
  starting transfers between devices  97.6 us (58%)
  Pallas kernels  43.7 us (26%)
  waiting for transfers between devices  20.3 us (12%)
  local copies, waits for them, and re-layouts  2.78 us (2%)
    ppermute x45, starting transfers between devices, send(): lax.ppermute(arrays[idx], 'ctx', [(i, i ^ idx) for i in range(size)])  84.2 us
    pallas_call x9, Pallas kernels, call(): pl.pallas_call(kernel, out_shape=outs, scratch_shapes=scratch, compiler_p...  43.7 us
    ppermute x45, waiting for transfers between devices, send(): lax.ppermute(arrays[idx], 'ctx', [(i, i ^ idx) for i in range(size)])  18.8 us
    ppermute x7, starting transfers between devices, partners(): lax.ppermute(value, axis, [(i, i ^ step) for i in range(size)])  9.73 us
  transfers between devices with their start and end apart: 54, of which 10 were waited for; matrix products, arithmetic and copies ran while one was open for 0% of the time, Pallas kernels for 7%

profile of v5, /device:TPU:0, one launch (start us, length us, event | category | flops | bytes accessed | tf_op | source)
XLA Modules:
  0.0 166.4 jit_solution(41326108004846921)
XLA Ops:
  0.6 1.6 shard_map.153
  2.2 2.3 %collective-permute-start = (f32[6,2048]{1,0:T(8,128)}, f32[6,2048]{1,0:T(8,128)S(1)}, u32[]{:S(2)}, u32[]{:S(2)}) collective-permute-start(f32[6,2048]{1,0:T(8,128)} %shard_map.153), channel_id=1, source_target_pairs={{0,2},{2,4},{4,6},{6,8},{8,10},{10,12},{12,14},{14,16},{16,18},{18... | collective-permute-start | bytes 147464 | tf_op jit(solution)/shard_map/ppermute | solution.py:776
  4.5 1.1 collective-permute-done.refs_3_.refs_5_
  5.6 0.6 copy-done.3
  6.3 4.2 %shard_map.155 = (bf16[3,128,128]{2,1,0:T(8,128)(2,1)}, bf16[3,128,128]{2,1,0:T(8,128)(2,1)}, bf16[3,128,128]{2,1,0:T(8,128)(2,1)}, bf16[3,128,128]{2,1,0:T(8,12...) custom-call(s32[1]{0:T(128)} %bitcast.me_ref, ...), custom_call_target="tpu_custom_call" | custom-call | tf_op jit(solution)/shard_map/pallas_call | solution.py:33
  10.4 3.2 %collective-permute-start.1 = (bf16[3,128,128]{2,1,0:T(8,128)(2,1)}, bf16[3,128,128]{2,1,0:T(8,128)(2,1)S(1)}, u32[]{:S(2)}, u32[]{:S(2)}) collective-permute-start(bf16[3,128,128]{2,1,0:T(8,128)(2,1)} %get-tuple-element.80), channel_id=1, source_target_pairs={{0,2},{2,0},{4,6},{6,4},{8,10},{10,8},{12,14},{14,12},{16,18},{18,... | collective-permute-start | bytes 294920 | tf_op jit(solution)/shard_map/ppermute | solution.py:719
  13.6 2.2 %collective-permute-start.2 = (bf16[3,128,128]{2,1,0:T(8,128)(2,1)}, bf16[3,128,128]{2,1,0:T(8,128)(2,1)S(1)}, u32[]{:S(2)}, u32[]{:S(2)}) collective-permute-start(bf16[3,128,128]{2,1,0:T(8,128)(2,1)} %get-tuple-element.81), channel_id=1, source_target_pairs={{0,4},{2,6},{4,0},{6,2},{8,12},{10,14},{12,8},{14,10},{16,20},{18,... | collective-permute-start | bytes 294920 | tf_op jit(solution)/shard_map/ppermute | solution.py:719
  15.9 2.7 %collective-permute-start.4 = (bf16[3,128,128]{2,1,0:T(8,128)(2,1)}, bf16[3,128,128]{2,1,0:T(8,128)(2,1)S(1)}, u32[]{:S(2)}, u32[]{:S(2)}) collective-permute-start(bf16[3,128,128]{2,1,0:T(8,128)(2,1)} %get-tuple-element.83), channel_id=1, source_target_pairs={{0,8},{2,10},{4,12},{6,14},{8,0},{10,2},{12,4},{14,6},{16,24},{18,... | collective-permute-start | bytes 294920 | tf_op jit(solution)/shard_map/ppermute | solution.py:719
  18.6 1.7 %collective-permute-start.6 = (bf16[3,128,128]{2,1,0:T(8,128)(2,1)}, bf16[3,128,128]{2,1,0:T(8,128)(2,1)S(1)}, u32[]{:S(2)}, u32[]{:S(2)}) collective-permute-start(bf16[3,128,128]{2,1,0:T(8,128)(2,1)} %get-tuple-element.85), channel_id=1, source_target_pairs={{0,12},{2,14},{4,8},{6,10},{8,4},{10,6},{12,0},{14,2},{16,28},{18,... | collective-permute-start | bytes 294920 | tf_op jit(solution)/shard_map/ppermute | solution.py:719
  20.4 1.1 collective-permute-start.7
  21.5 3.4 %collective-permute-start.8 = (bf16[3,128,128]{2,1,0:T(8,128)(2,1)}, bf16[3,128,128]{2,1,0:T(8,128)(2,1)S(1)}, u32[]{:S(2)}, u32[]{:S(2)}) collective-permute-start(bf16[3,128,128]{2,1,0:T(8,128)(2,1)} %get-tuple-element.87), channel_id=1, source_target_pairs={{0,16},{2,18},{4,20},{6,22},{8,24},{10,26},{12,28},{14,30},{16,0},... | collective-permute-start | bytes 294920 | tf_op jit(solution)/shard_map/ppermute | solution.py:719
  25.1 3.4 %collective-permute-start.10 = (bf16[3,128,128]{2,1,0:T(8,128)(2,1)}, bf16[3,128,128]{2,1,0:T(8,128)(2,1)S(1)}, u32[]{:S(2)}, u32[]{:S(2)}) collective-permute-start(bf16[3,128,128]{2,1,0:T(8,128)(2,1)} %get-tuple-element.89), channel_id=1, source_target_pairs={{0,20},{2,22},{4,16},{6,18},{8,28},{10,30},{12,24},{14,26},{16,4},... | collective-permute-start | bytes 294920 | tf_op jit(solution)/shard_map/ppermute | solution.py:719
  28.5 0.7 collective-permute-start.11
  29.2 2.6 %collective-permute-done.7.refs_7_ = bf16[3,128,128]{2,1,0:T(8,128)(2,1)S(1)} collective-permute-done((bf16[3,128,128]{2,1,0:T(8,128)(2,1)}, bf16[3,128,128]{2,1,0:T(8,128)(2,1)S(1)}, u32[]{:S(2)}, u32[]{:S(2)}) %collective-permute-start.7) | collective-permute-done | bytes 98336 | tf_op jit(solution)/shard_map/ppermute | solution.py:719
  31.9 1.7 %collective-permute-start.12 = (bf16[3,128,128]{2,1,0:T(8,128)(2,1)}, bf16[3,128,128]{2,1,0:T(8,128)(2,1)S(1)}, u32[]{:S(2)}, u32[]{:S(2)}) collective-permute-start(bf16[3,128,128]{2,1,0:T(8,128)(2,1)} %get-tuple-element.91), channel_id=1, source_target_pairs={{0,24},{2,26},{4,28},{6,30},{8,16},{10,18},{12,20},{14,22},{16,8},... | collective-permute-start | bytes 294920 | tf_op jit(solution)/shard_map/ppermute | solution.py:719
  33.6 1.7 %collective-permute-start.13 = (bf16[3,128,128]{2,1,0:T(8,128)(2,1)}, bf16[3,128,128]{2,1,0:T(8,128)(2,1)S(1)}, u32[]{:S(2)}, u32[]{:S(2)}) collective-permute-start(bf16[3,128,128]{2,1,0:T(8,128)(2,1)} %get-tuple-element.92), channel_id=1, source_target_pairs={{0,26},{2,24},{4,30},{6,28},{8,18},{10,16},{12,22},{14,20},{16,10}... | collective-permute-start | bytes 294920 | tf_op jit(solution)/shard_map/ppermute | solution.py:719
  35.3 10.4 %collective-permute-start.14 = (bf16[3,128,128]{2,1,0:T(8,128)(2,1)}, bf16[3,128,128]{2,1,0:T(8,128)(2,1)S(1)}, u32[]{:S(2)}, u32[]{:S(2)}) collective-permute-start(bf16[3,128,128]{2,1,0:T(8,128)(2,1)} %get-tuple-element.93), channel_id=1, source_target_pairs={{0,28},{2,30},{4,24},{6,26},{8,20},{10,22},{12,16},{14,18},{16,12}... | collective-permute-start | bytes 294920 | tf_op jit(solution)/shard_map/ppermute | solution.py:719
  45.7 1.4 collective-permute-done.10.refs_10_
  47.1 1.3 collective-permute-start.15
  48.7 5.5 %collective-permute-done.15.refs_15_ = bf16[3,128,128]{2,1,0:T(8,128)(2,1)S(1)} collective-permute-done((bf16[3,128,128]{2,1,0:T(8,128)(2,1)}, bf16[3,128,128]{2,1,0:T(8,128)(2,1)S(1)}, u32[]{:S(2)}, u32[]{:S(2)}) %collective-permute-start.15) | collective-permute-done | bytes 98336 | tf_op jit(solution)/shard_map/ppermute | solution.py:719
  54.3 0.5 copy-done.18
  54.8 16.0 %shard_map.156 = (bf16[2,128,128]{2,1,0:T(8,128)(2,1)}, bf16[2,128,128]{2,1,0:T(8,128)(2,1)}, bf16[2,128,128]{2,1,0:T(8,128)(2,1)}, bf16[2,128,128]{2,1,0:T(8,12...) custom-call(s32[1]{0:T(128)} %bitcast.me_ref, ...), custom_call_target="tpu_custom_call" | custom-call | tf_op jit(solution)/shard_map/pallas_call | solution.py:33
  70.9 0.9 collective-permute-start.17
  71.8 1.0 collective-permute-start.18
  72.8 7.0 %collective-permute-start.19 = (bf16[2,128,128]{2,1,0:T(8,128)(2,1)}, bf16[2,128,128]{2,1,0:T(8,128)(2,1)S(1)}, u32[]{:S(2)}, u32[]{:S(2)}) collective-permute-start(bf16[2,128,128]{2,1,0:T(8,128)(2,1)} %get-tuple-element.101), channel_id=1, source_target_pairs={{0,8},{2,10},{4,12},{6,14},{8,0},{10,2},{12,4},{14,6},{16,24},{18,... | collective-permute-start | bytes 196616 | tf_op jit(solution)/shard_map/ppermute | solution.py:719
  79.8 2.3 %collective-permute-start.21 = (bf16[2,128,128]{2,1,0:T(8,128)(2,1)}, bf16[2,128,128]{2,1,0:T(8,128)(2,1)S(1)}, u32[]{:S(2)}, u32[]{:S(2)}) collective-permute-start(bf16[2,128,128]{2,1,0:T(8,128)(2,1)} %get-tuple-element.103), channel_id=1, source_target_pairs={{0,12},{2,14},{4,8},{6,10},{8,4},{10,6},{12,0},{14,2},{16,28},{18,... | collective-permute-start | bytes 196616 | tf_op jit(solution)/shard_map/ppermute | solution.py:719
  82.2 3.5 %collective-permute-start.23 = (bf16[2,128,128]{2,1,0:T(8,128)(2,1)}, bf16[2,128,128]{2,1,0:T(8,128)(2,1)S(1)}, u32[]{:S(2)}, u32[]{:S(2)}) collective-permute-start(bf16[2,128,128]{2,1,0:T(8,128)(2,1)} %get-tuple-element.105), channel_id=1, source_target_pairs={{0,16},{2,18},{4,20},{6,22},{8,24},{10,26},{12,28},{14,30},{16,0},... | collective-permute-start | bytes 196616 | tf_op jit(solution)/shard_map/ppermute | solution.py:719
  85.9 3.4 %collective-permute-start.25 = (bf16[2,128,128]{2,1,0:T(8,128)(2,1)}, bf16[2,128,128]{2,1,0:T(8,128)(2,1)S(1)}, u32[]{:S(2)}, u32[]{:S(2)}) collective-permute-start(bf16[2,128,128]{2,1,0:T(8,128)(2,1)} %get-tuple-element.107), channel_id=1, source_target_pairs={{0,20},{2,22},{4,16},{6,18},{8,28},{10,30},{12,24},{14,26},{16,4},... | collective-permute-start | bytes 196616 | tf_op jit(solution)/shard_map/ppermute | solution.py:719
  89.3 0.4 collective-permute-start.26
  89.7 2.4 %collective-permute-start.27 = (bf16[2,128,128]{2,1,0:T(8,128)(2,1)}, bf16[2,128,128]{2,1,0:T(8,128)(2,1)S(1)}, u32[]{:S(2)}, u32[]{:S(2)}) collective-permute-start(bf16[2,128,128]{2,1,0:T(8,128)(2,1)} %get-tuple-element.109), channel_id=1, source_target_pairs={{0,24},{2,26},{4,28},{6,30},{8,16},{10,18},{12,20},{14,22},{16,8},... | collective-permute-start | bytes 196616 | tf_op jit(solution)/shard_map/ppermute | solution.py:719
  92.2 7.4 %collective-permute-start.28 = (bf16[2,128,128]{2,1,0:T(8,128)(2,1)}, bf16[2,128,128]{2,1,0:T(8,128)(2,1)S(1)}, u32[]{:S(2)}, u32[]{:S(2)}) collective-permute-start(bf16[2,128,128]{2,1,0:T(8,128)(2,1)} %get-tuple-element.110), channel_id=1, source_target_pairs={{0,26},{2,24},{4,30},{6,28},{8,18},{10,16},{12,22},{14,20},{16,10}... | collective-permute-start | bytes 196616 | tf_op jit(solution)/shard_map/ppermute | solution.py:719
  99.6 1.2 collective-permute-start.29
  100.8 1.0 collective-permute-done.25.refs_19_
  101.8 1.2 collective-permute-start.30
  103.1 3.4 %shard_map.154.refs_4_ = f32[3,128,2048]{2,1,0:T(8,128)} custom-call(s32[1]{0:T(128)} %bitcast.me_ref, bf16[128,2048]{1,0:T(8,128)(2,1)} %refs_0_.5, bf16[128,2048]{1,0:T(8,128)(2,1)} %refs_1_.5, bf16[128,2048]{1,0:T(8,128)(2,1)} %refs_2_.5, f32[6,2048]{1,0:T(8,128)} %copy-done.3, f32[3,2048]{1,0:T(4,128)} %taps_ref.1), custom_call_target="tpu_custom_call" | custom-call | tf_op jit(solution)/shard_map/pallas_call | solution.py:33
  106.5 6.7 %shard_map.157 = (bf16[128,128]{1,0:T(8,128)(2,1)}, bf16[128,128]{1,0:T(8,128)(2,1)}, bf16[128,128]{1,0:T(8,128)(2,1)}, bf16[128,128]{1,0:T(8,128)(2,1)}, bf16[1...) custom-call(s32[1]{0:T(128)} %bitcast.me_ref, ...), custom_call_target="tpu_custom_call" | custom-call | tf_op jit(solution)/shard_map/pallas_call | solution.py:33
  113.4 0.5 copy-done.29
  114.1 7.5 %shard_map.158 = (bf16[128,2048]{1,0:T(8,128)(2,1)}, bf16[128,2048]{1,0:T(8,128)(2,1)}, bf16[128,2048]{1,0:T(8,128)(2,1)}, bf16[128,2048]{1,0:T(8,128)(2,1)}, f3...) custom-call(s32[1]{0:T(128)} %bitcast.me_ref, bf16[128,2048]{1,0:T(8,128)(2,1)} %refs_0_.5, ...), custom_call_target="tpu_custom_call" | custom-call | tf_op jit(solution)/shard_map/pallas_call | solution.py:33
  121.7 1.3 collective-permute-start.34
  123.0 1.8 %collective-permute-start.33 = (f32[4,2176]{1,0:T(4,128)}, f32[4,2176]{1,0:T(4,128)S(1)}, u32[]{:S(2)}, u32[]{:S(2)}) collective-permute-start(f32[4,2176]{1,0:T(4,128)} %get-tuple-element.122), channel_id=1, source_target_pairs={{0,4},{2,6},{4,0},{6,2},{8,12},{10,14},{12,8},{14,10},{16,20},{18,... | collective-permute-start | bytes 104456 | tf_op jit(solution)/shard_map/ppermute | solution.py:725
  124.7 0.5 collective-permute-start.39
  125.5 1.3 collective-permute-start.41
  126.8 0.4 collective-permute-done.33
  127.2 1.3 collective-permute-start.31
  128.5 0.8 add_add_fusion.refs_0_
  129.3 4.4 %collective-permute-start.37 = (f32[4,2176]{1,0:T(4,128)S(1)}, f32[4,2176]{1,0:T(4,128)S(1)}, u32[]{:S(2)}, u32[]{:S(2)}) collective-permute-start(f32[4,2176]{1,0:T(4,128)S(1)} %add_add_fusion.refs_0_), channel_id=1, source_target_pairs={{0,24},{2,26},{4,28},{6,30},{8,16},{10,18},{12,20},{14,22},{16,8},... | collective-permute-start | bytes 104456 | tf_op jit(solution)/shard_map/ppermute | solution.py:725
  133.8 0.6 collective-permute-start.35
  134.4 0.4 collective-permute-start.43
  134.8 3.3 %collective-permute-done.43.refs_5_ = bf16[128,128]{1,0:T(8,128)(2,1)S(1)} collective-permute-done((bf16[128,128]{1,0:T(8,128)(2,1)S(1)}, bf16[128,128]{1,0:T(8,128)(2,1)S(1)}, u32[]{:S(2)}, u32[]{:S(2)}) %collective-permute-start.43) | collective-permute-done | bytes 32800 | tf_op jit(solution)/shard_map/ppermute | solution.py:719
  138.1 2.1 %collective-permute-start.44 = (bf16[128,128]{1,0:T(8,128)(2,1)S(1)}, bf16[128,128]{1,0:T(8,128)(2,1)S(1)}, u32[]{:S(2)}, u32[]{:S(2)}) collective-permute-start(bf16[128,128]{1,0:T(8,128)(2,1)S(1)} %copy-done.43), channel_id=1, source_target_pairs={{0,12},{2,14},{4,8},{6,10},{8,4},{10,6},{12,0},{14,2},{16,28},{18,... | collective-permute-start | bytes 98312 | tf_op jit(solution)/shard_map/ppermute | solution.py:719
  140.3 0.7 collective-permute-start.45
  141.0 2.1 %collective-permute-start.46 = (bf16[128,128]{1,0:T(8,128)(2,1)S(1)}, bf16[128,128]{1,0:T(8,128)(2,1)S(1)}, u32[]{:S(2)}, u32[]{:S(2)}) collective-permute-start(bf16[128,128]{1,0:T(8,128)(2,1)S(1)} %copy-done.41), channel_id=1, source_target_pairs={{0,16},{2,18},{4,20},{6,22},{8,24},{10,26},{12,28},{14,30},{16,0},... | collective-permute-start | bytes 98312 | tf_op jit(solution)/shard_map/ppermute | solution.py:719
  143.5 2.4 %collective-permute-start.48 = (bf16[128,128]{1,0:T(8,128)(2,1)S(1)}, bf16[128,128]{1,0:T(8,128)(2,1)S(1)}, u32[]{:S(2)}, u32[]{:S(2)}) collective-permute-start(bf16[128,128]{1,0:T(8,128)(2,1)S(1)} %copy-done.39), channel_id=1, source_target_pairs={{0,20},{2,22},{4,16},{6,18},{8,28},{10,30},{12,24},{14,26},{16,4},... | collective-permute-start | bytes 98312 | tf_op jit(solution)/shard_map/ppermute | solution.py:719
  145.9 0.8 copy-done.1
  146.7 1.6 shard_map.159
  148.5 1.6 collective-permute-start.38
  150.1 1.1 collective-permute-start.49
  151.1 1.6 collective-permute-start.50
  152.7 2.0 %collective-permute-start.51 = (bf16[128,128]{1,0:T(8,128)(2,1)S(1)}, bf16[128,128]{1,0:T(8,128)(2,1)S(1)}, u32[]{:S(2)}, u32[]{:S(2)}) collective-permute-start(bf16[128,128]{1,0:T(8,128)(2,1)S(1)} %copy-done.36), channel_id=1, source_target_pairs={{0,26},{2,24},{4,30},{6,28},{8,18},{10,16},{12,22},{14,20},{16,10}... | collective-permute-start | bytes 98312 | tf_op jit(solution)/shard_map/ppermute | solution.py:719
  154.8 2.9 %collective-permute-start.52 = (bf16[128,128]{1,0:T(8,128)(2,1)S(1)}, bf16[128,128]{1,0:T(8,128)(2,1)S(1)}, u32[]{:S(2)}, u32[]{:S(2)}) collective-permute-start(bf16[128,128]{1,0:T(8,128)(2,1)S(1)} %copy-done.35), channel_id=1, source_target_pairs={{0,28},{2,30},{4,24},{6,26},{8,20},{10,22},{12,16},{14,18},{16,12}... | collective-permute-start | bytes 98312 | tf_op jit(solution)/shard_map/ppermute | solution.py:719
  157.7 1.4 collective-permute-start.53
  159.2 2.2 %collective-permute-done.52.refs_14_ = bf16[128,128]{1,0:T(8,128)(2,1)S(1)} collective-permute-done((bf16[128,128]{1,0:T(8,128)(2,1)S(1)}, bf16[128,128]{1,0:T(8,128)(2,1)S(1)}, u32[]{:S(2)}, u32[]{:S(2)}) %collective-permute-start.52) | collective-permute-done | bytes 32800 | tf_op jit(solution)/shard_map/ppermute | solution.py:719
  161.4 2.4 %collective-permute-done.53.refs_15_ = bf16[128,128]{1,0:T(8,128)(2,1)S(1)} collective-permute-done((bf16[128,128]{1,0:T(8,128)(2,1)S(1)}, bf16[128,128]{1,0:T(8,128)(2,1)S(1)}, u32[]{:S(2)}, u32[]{:S(2)}) %collective-permute-start.53) | collective-permute-done | bytes 32800 | tf_op jit(solution)/shard_map/ppermute | solution.py:719
  163.8 2.6 %shard_map.161 = (f32[3,2048]{1,0:T(4,128)}, f32[1,2048]{1,0:T(1,128)}, f32[128,2048]{1,0:T(8,128)}) custom-call(s32[1]{0:T(128)} %bitcast.me_ref, f32[4,2176]{1,0:T(4,128)S(1)} %get-tuple-element.130.totals_ref, f32[1,128]{1,0:T(1,128)S(1)} %add.15.norm_ref, bf16[128,128]{1,0:T(8,128)(2,1)S(1)} %copy-done.2, ...), custom_call_target="tpu_custom_call" | custom-call | tf_op jit(solution)/shard_map/pallas_call | solution.py:33
  (153 shorter events, 2.1 us)
Async XLA Ops:
  2.2 3.4 %collective-permute-start = (f32[6,2048]{1,0:T(8,128)}, f32[6,2048]{1,0:T(8,128)S(1)}, u32[]{:S(2)}, u32[]{:S(2)}) collective-permute-start(f32[6,2048]{1,0:T(8,128)} %shard_map.153), channel_id=1, source_target_pairs={{0,2},{2,4},{4,6},{6,8},{8,10},{10,12},{12,14},{14,16},{16,18},{18... | collective-permute-start | bytes 147464 | tf_op jit(solution)/shard_map/ppermute | solution.py:776
  10.4 8.2 %collective-permute-start.1 = (bf16[3,128,128]{2,1,0:T(8,128)(2,1)}, bf16[3,128,128]{2,1,0:T(8,128)(2,1)S(1)}, u32[]{:S(2)}, u32[]{:S(2)}) collective-permute-start(bf16[3,128,128]{2,1,0:T(8,128)(2,1)} %get-tuple-element.80), channel_id=1, source_target_pairs={{0,2},{2,0},{4,6},{6,4},{8,10},{10,8},{12,14},{14,12},{16,18},{18,... | collective-permute-start | bytes 294920 | tf_op jit(solution)/shard_map/ppermute | solution.py:719
  13.6 6.7 %collective-permute-start.2 = (bf16[3,128,128]{2,1,0:T(8,128)(2,1)}, bf16[3,128,128]{2,1,0:T(8,128)(2,1)S(1)}, u32[]{:S(2)}, u32[]{:S(2)}) collective-permute-start(bf16[3,128,128]{2,1,0:T(8,128)(2,1)} %get-tuple-element.81), channel_id=1, source_target_pairs={{0,4},{2,6},{4,0},{6,2},{8,12},{10,14},{12,8},{14,10},{16,20},{18,... | collective-permute-start | bytes 294920 | tf_op jit(solution)/shard_map/ppermute | solution.py:719
  15.8 5.6 %collective-permute-start.3 = (bf16[3,128,128]{2,1,0:T(8,128)(2,1)}, bf16[3,128,128]{2,1,0:T(8,128)(2,1)S(1)}, u32[]{:S(2)}, u32[]{:S(2)}) collective-permute-start(bf16[3,128,128]{2,1,0:T(8,128)(2,1)} %get-tuple-element.82), channel_id=1, source_target_pairs={{0,6},{2,4},{4,2},{6,0},{8,14},{10,12},{12,10},{14,8},{16,22},{18,... | collective-permute-start | bytes 294920 | tf_op jit(solution)/shard_map/ppermute | solution.py:719
  15.9 8.9 %collective-permute-start.4 = (bf16[3,128,128]{2,1,0:T(8,128)(2,1)}, bf16[3,128,128]{2,1,0:T(8,128)(2,1)S(1)}, u32[]{:S(2)}, u32[]{:S(2)}) collective-permute-start(bf16[3,128,128]{2,1,0:T(8,128)(2,1)} %get-tuple-element.83), channel_id=1, source_target_pairs={{0,8},{2,10},{4,12},{6,14},{8,0},{10,2},{12,4},{14,6},{16,24},{18,... | collective-permute-start | bytes 294920 | tf_op jit(solution)/shard_map/ppermute | solution.py:719
  18.6 6.5 %collective-permute-start.5 = (bf16[3,128,128]{2,1,0:T(8,128)(2,1)}, bf16[3,128,128]{2,1,0:T(8,128)(2,1)S(1)}, u32[]{:S(2)}, u32[]{:S(2)}) collective-permute-start(bf16[3,128,128]{2,1,0:T(8,128)(2,1)} %get-tuple-element.84), channel_id=1, source_target_pairs={{0,10},{2,8},{4,14},{6,12},{8,2},{10,0},{12,6},{14,4},{16,26},{18,... | collective-permute-start | bytes 294920 | tf_op jit(solution)/shard_map/ppermute | solution.py:719
  18.6 35.5 %copy-start.4 = (bf16[3,128,128]{2,1,0:T(8,128)(2,1)}, bf16[3,128,128]{2,1,0:T(8,128)(2,1)S(1)}, u32[]{:S(2)}) copy-start(bf16[3,128,128]{2,1,0:T(8,128)(2,1)S(1)} %collective-permute-done.1.refs_1_) | copy-start | bytes 294916
  18.6 9.9 %collective-permute-start.6 = (bf16[3,128,128]{2,1,0:T(8,128)(2,1)}, bf16[3,128,128]{2,1,0:T(8,128)(2,1)S(1)}, u32[]{:S(2)}, u32[]{:S(2)}) collective-permute-start(bf16[3,128,128]{2,1,0:T(8,128)(2,1)} %get-tuple-element.85), channel_id=1, source_target_pairs={{0,12},{2,14},{4,8},{6,10},{8,4},{10,6},{12,0},{14,2},{16,28},{18,... | collective-permute-start | bytes 294920 | tf_op jit(solution)/shard_map/ppermute | solution.py:719
  20.4 33.8 %copy-start.5 = (bf16[3,128,128]{2,1,0:T(8,128)(2,1)}, bf16[3,128,128]{2,1,0:T(8,128)(2,1)S(1)}, u32[]{:S(2)}) copy-start(bf16[3,128,128]{2,1,0:T(8,128)(2,1)S(1)} %collective-permute-done.2.refs_2_) | copy-start | bytes 294916
  20.4 11.5 %collective-permute-start.7 = (bf16[3,128,128]{2,1,0:T(8,128)(2,1)}, bf16[3,128,128]{2,1,0:T(8,128)(2,1)S(1)}, u32[]{:S(2)}, u32[]{:S(2)}) collective-permute-start(bf16[3,128,128]{2,1,0:T(8,128)(2,1)} %get-tuple-element.86), channel_id=1, source_target_pairs={{0,14},{2,12},{4,10},{6,8},{8,6},{10,4},{12,2},{14,0},{16,30},{18,... | collective-permute-start | bytes 294920 | tf_op jit(solution)/shard_map/ppermute | solution.py:719
  21.5 32.7 %copy-start.6 = (bf16[3,128,128]{2,1,0:T(8,128)(2,1)}, bf16[3,128,128]{2,1,0:T(8,128)(2,1)S(1)}, u32[]{:S(2)}) copy-start(bf16[3,128,128]{2,1,0:T(8,128)(2,1)S(1)} %collective-permute-done.3.refs_3_) | copy-start | bytes 294916
  21.5 12.1 %collective-permute-start.8 = (bf16[3,128,128]{2,1,0:T(8,128)(2,1)}, bf16[3,128,128]{2,1,0:T(8,128)(2,1)S(1)}, u32[]{:S(2)}, u32[]{:S(2)}) collective-permute-start(bf16[3,128,128]{2,1,0:T(8,128)(2,1)} %get-tuple-element.87), channel_id=1, source_target_pairs={{0,16},{2,18},{4,20},{6,22},{8,24},{10,26},{12,28},{14,30},{16,0},... | collective-permute-start | bytes 294920 | tf_op jit(solution)/shard_map/ppermute | solution.py:719
  24.9 10.5 %collective-permute-start.9 = (bf16[3,128,128]{2,1,0:T(8,128)(2,1)}, bf16[3,128,128]{2,1,0:T(8,128)(2,1)S(1)}, u32[]{:S(2)}, u32[]{:S(2)}) collective-permute-start(bf16[3,128,128]{2,1,0:T(8,128)(2,1)} %get-tuple-element.88), channel_id=1, source_target_pairs={{0,18},{2,16},{4,22},{6,20},{8,26},{10,24},{12,30},{14,28},{16,2},... | collective-permute-start | bytes 294920 | tf_op jit(solution)/shard_map/ppermute | solution.py:719
  25.1 22.0 %collective-permute-start.10 = (bf16[3,128,128]{2,1,0:T(8,128)(2,1)}, bf16[3,128,128]{2,1,0:T(8,128)(2,1)S(1)}, u32[]{:S(2)}, u32[]{:S(2)}) collective-permute-start(bf16[3,128,128]{2,1,0:T(8,128)(2,1)} %get-tuple-element.89), channel_id=1, source_target_pairs={{0,20},{2,22},{4,16},{6,18},{8,28},{10,30},{12,24},{14,26},{16,4},... | collective-permute-start | bytes 294920 | tf_op jit(solution)/shard_map/ppermute | solution.py:719
  28.5 19.9 %collective-permute-start.11 = (bf16[3,128,128]{2,1,0:T(8,128)(2,1)}, bf16[3,128,128]{2,1,0:T(8,128)(2,1)S(1)}, u32[]{:S(2)}, u32[]{:S(2)}) collective-permute-start(bf16[3,128,128]{2,1,0:T(8,128)(2,1)} %get-tuple-element.90), channel_id=1, source_target_pairs={{0,22},{2,20},{4,18},{6,16},{8,30},{10,28},{12,26},{14,24},{16,6},... | collective-permute-start | bytes 294920 | tf_op jit(solution)/shard_map/ppermute | solution.py:719
  31.9 16.5 %collective-permute-start.12 = (bf16[3,128,128]{2,1,0:T(8,128)(2,1)}, bf16[3,128,128]{2,1,0:T(8,128)(2,1)S(1)}, u32[]{:S(2)}, u32[]{:S(2)}) collective-permute-start(bf16[3,128,128]{2,1,0:T(8,128)(2,1)} %get-tuple-element.91), channel_id=1, source_target_pairs={{0,24},{2,26},{4,28},{6,30},{8,16},{10,18},{12,20},{14,22},{16,8},... | collective-permute-start | bytes 294920 | tf_op jit(solution)/shard_map/ppermute | solution.py:719
  33.6 14.8 %collective-permute-start.13 = (bf16[3,128,128]{2,1,0:T(8,128)(2,1)}, bf16[3,128,128]{2,1,0:T(8,128)(2,1)S(1)}, u32[]{:S(2)}, u32[]{:S(2)}) collective-permute-start(bf16[3,128,128]{2,1,0:T(8,128)(2,1)} %get-tuple-element.92), channel_id=1, source_target_pairs={{0,26},{2,24},{4,30},{6,28},{8,18},{10,16},{12,22},{14,20},{16,10}... | collective-permute-start | bytes 294920 | tf_op jit(solution)/shard_map/ppermute | solution.py:719
  35.3 13.3 %collective-permute-start.14 = (bf16[3,128,128]{2,1,0:T(8,128)(2,1)}, bf16[3,128,128]{2,1,0:T(8,128)(2,1)S(1)}, u32[]{:S(2)}, u32[]{:S(2)}) collective-permute-start(bf16[3,128,128]{2,1,0:T(8,128)(2,1)} %get-tuple-element.93), channel_id=1, source_target_pairs={{0,28},{2,30},{4,24},{6,26},{8,20},{10,22},{12,16},{14,18},{16,12}... | collective-permute-start | bytes 294920 | tf_op jit(solution)/shard_map/ppermute | solution.py:719
  47.1 7.0 %collective-permute-start.15 = (bf16[3,128,128]{2,1,0:T(8,128)(2,1)}, bf16[3,128,128]{2,1,0:T(8,128)(2,1)S(1)}, u32[]{:S(2)}, u32[]{:S(2)}) collective-permute-start(bf16[3,128,128]{2,1,0:T(8,128)(2,1)} %get-tuple-element.94), channel_id=1, source_target_pairs={{0,30},{2,28},{4,26},{6,24},{8,22},{10,20},{12,18},{14,16},{16,14}... | collective-permute-start | bytes 294920 | tf_op jit(solution)/shard_map/ppermute | solution.py:719
  70.8 9.0 %collective-permute-start.16 = (bf16[2,128,128]{2,1,0:T(8,128)(2,1)}, bf16[2,128,128]{2,1,0:T(8,128)(2,1)S(1)}, u32[]{:S(2)}, u32[]{:S(2)}) collective-permute-start(bf16[2,128,128]{2,1,0:T(8,128)(2,1)} %get-tuple-element.98), channel_id=1, source_target_pairs={{0,2},{2,0},{4,6},{6,4},{8,10},{10,8},{12,14},{14,12},{16,18},{18,... | collective-permute-start | bytes 196616 | tf_op jit(solution)/shard_map/ppermute | solution.py:719
  70.9 11.2 %collective-permute-start.17 = (bf16[2,128,128]{2,1,0:T(8,128)(2,1)}, bf16[2,128,128]{2,1,0:T(8,128)(2,1)S(1)}, u32[]{:S(2)}, u32[]{:S(2)}) collective-permute-start(bf16[2,128,128]{2,1,0:T(8,128)(2,1)} %get-tuple-element.99), channel_id=1, source_target_pairs={{0,4},{2,6},{4,0},{6,2},{8,12},{10,14},{12,8},{14,10},{16,20},{18,... | collective-permute-start | bytes 196616 | tf_op jit(solution)/shard_map/ppermute | solution.py:719
  71.8 10.4 %collective-permute-start.18 = (bf16[2,128,128]{2,1,0:T(8,128)(2,1)}, bf16[2,128,128]{2,1,0:T(8,128)(2,1)S(1)}, u32[]{:S(2)}, u32[]{:S(2)}) collective-permute-start(bf16[2,128,128]{2,1,0:T(8,128)(2,1)} %get-tuple-element.100), channel_id=1, source_target_pairs={{0,6},{2,4},{4,2},{6,0},{8,14},{10,12},{12,10},{14,8},{16,22},{18,... | collective-permute-start | bytes 196616 | tf_op jit(solution)/shard_map/ppermute | solution.py:719
  72.8 13.0 %collective-permute-start.19 = (bf16[2,128,128]{2,1,0:T(8,128)(2,1)}, bf16[2,128,128]{2,1,0:T(8,128)(2,1)S(1)}, u32[]{:S(2)}, u32[]{:S(2)}) collective-permute-start(bf16[2,128,128]{2,1,0:T(8,128)(2,1)} %get-tuple-element.101), channel_id=1, source_target_pairs={{0,8},{2,10},{4,12},{6,14},{8,0},{10,2},{12,4},{14,6},{16,24},{18,... | collective-permute-start | bytes 196616 | tf_op jit(solution)/shard_map/ppermute | solution.py:719
  79.8 6.1 %collective-permute-start.20 = (bf16[2,128,128]{2,1,0:T(8,128)(2,1)}, bf16[2,128,128]{2,1,0:T(8,128)(2,1)S(1)}, u32[]{:S(2)}, u32[]{:S(2)}) collective-permute-start(bf16[2,128,128]{2,1,0:T(8,128)(2,1)} %get-tuple-element.102), channel_id=1, source_target_pairs={{0,10},{2,8},{4,14},{6,12},{8,2},{10,0},{12,6},{14,4},{16,26},{18,... | collective-permute-start | bytes 196616 | tf_op jit(solution)/shard_map/ppermute | solution.py:719
  79.8 33.3 %copy-start.19 = (bf16[2,128,128]{2,1,0:T(8,128)(2,1)}, bf16[2,128,128]{2,1,0:T(8,128)(2,1)S(1)}, u32[]{:S(2)}) copy-start(bf16[2,128,128]{2,1,0:T(8,128)(2,1)S(1)} %collective-permute-done.16.refs_10_) | copy-start | bytes 196612
  79.8 9.5 %collective-permute-start.21 = (bf16[2,128,128]{2,1,0:T(8,128)(2,1)}, bf16[2,128,128]{2,1,0:T(8,128)(2,1)S(1)}, u32[]{:S(2)}, u32[]{:S(2)}) collective-permute-start(bf16[2,128,128]{2,1,0:T(8,128)(2,1)} %get-tuple-element.103), channel_id=1, source_target_pairs={{0,12},{2,14},{4,8},{6,10},{8,4},{10,6},{12,0},{14,2},{16,28},{18,... | collective-permute-start | bytes 196616 | tf_op jit(solution)/shard_map/ppermute | solution.py:719
  82.1 7.6 %collective-permute-start.22 = (bf16[2,128,128]{2,1,0:T(8,128)(2,1)}, bf16[2,128,128]{2,1,0:T(8,128)(2,1)S(1)}, u32[]{:S(2)}, u32[]{:S(2)}) collective-permute-start(bf16[2,128,128]{2,1,0:T(8,128)(2,1)} %get-tuple-element.104), channel_id=1, source_target_pairs={{0,14},{2,12},{4,10},{6,8},{8,6},{10,4},{12,2},{14,0},{16,30},{18,... | collective-permute-start | bytes 196616 | tf_op jit(solution)/shard_map/ppermute | solution.py:719
  82.2 9.9 %collective-permute-start.23 = (bf16[2,128,128]{2,1,0:T(8,128)(2,1)}, bf16[2,128,128]{2,1,0:T(8,128)(2,1)S(1)}, u32[]{:S(2)}, u32[]{:S(2)}) collective-permute-start(bf16[2,128,128]{2,1,0:T(8,128)(2,1)} %get-tuple-element.105), channel_id=1, source_target_pairs={{0,16},{2,18},{4,20},{6,22},{8,24},{10,26},{12,28},{14,30},{16,0},... | collective-permute-start | bytes 196616 | tf_op jit(solution)/shard_map/ppermute | solution.py:719
  85.7 13.9 %collective-permute-start.24 = (bf16[2,128,128]{2,1,0:T(8,128)(2,1)}, bf16[2,128,128]{2,1,0:T(8,128)(2,1)S(1)}, u32[]{:S(2)}, u32[]{:S(2)}) collective-permute-start(bf16[2,128,128]{2,1,0:T(8,128)(2,1)} %get-tuple-element.106), channel_id=1, source_target_pairs={{0,18},{2,16},{4,22},{6,20},{8,26},{10,24},{12,30},{14,28},{16,2},... | collective-permute-start | bytes 196616 | tf_op jit(solution)/shard_map/ppermute | solution.py:719
  85.9 15.9 %collective-permute-start.25 = (bf16[2,128,128]{2,1,0:T(8,128)(2,1)}, bf16[2,128,128]{2,1,0:T(8,128)(2,1)S(1)}, u32[]{:S(2)}, u32[]{:S(2)}) collective-permute-start(bf16[2,128,128]{2,1,0:T(8,128)(2,1)} %get-tuple-element.107), channel_id=1, source_target_pairs={{0,20},{2,22},{4,16},{6,18},{8,28},{10,30},{12,24},{14,26},{16,4},... | collective-permute-start | bytes 196616 | tf_op jit(solution)/shard_map/ppermute | solution.py:719
  89.3 23.9 %collective-permute-start.26 = (bf16[2,128,128]{2,1,0:T(8,128)(2,1)}, bf16[2,128,128]{2,1,0:T(8,128)(2,1)S(1)}, u32[]{:S(2)}, u32[]{:S(2)}) collective-permute-start(bf16[2,128,128]{2,1,0:T(8,128)(2,1)} %get-tuple-element.108), channel_id=1, source_target_pairs={{0,22},{2,20},{4,18},{6,16},{8,30},{10,28},{12,26},{14,24},{16,6},... | collective-permute-start | bytes 196616 | tf_op jit(solution)/shard_map/ppermute | solution.py:719
  89.7 23.6 %collective-permute-start.27 = (bf16[2,128,128]{2,1,0:T(8,128)(2,1)}, bf16[2,128,128]{2,1,0:T(8,128)(2,1)S(1)}, u32[]{:S(2)}, u32[]{:S(2)}) collective-permute-start(bf16[2,128,128]{2,1,0:T(8,128)(2,1)} %get-tuple-element.109), channel_id=1, source_target_pairs={{0,24},{2,26},{4,28},{6,30},{8,16},{10,18},{12,20},{14,22},{16,8},... | collective-permute-start | bytes 196616 | tf_op jit(solution)/shard_map/ppermute | solution.py:719
  92.2 21.2 %collective-permute-start.28 = (bf16[2,128,128]{2,1,0:T(8,128)(2,1)}, bf16[2,128,128]{2,1,0:T(8,128)(2,1)S(1)}, u32[]{:S(2)}, u32[]{:S(2)}) collective-permute-start(bf16[2,128,128]{2,1,0:T(8,128)(2,1)} %get-tuple-element.110), channel_id=1, source_target_pairs={{0,26},{2,24},{4,30},{6,28},{8,18},{10,16},{12,22},{14,20},{16,10}... | collective-permute-start | bytes 196616 | tf_op jit(solution)/shard_map/ppermute | solution.py:719
  99.6 13.7 %collective-permute-start.29 = (bf16[2,128,128]{2,1,0:T(8,128)(2,1)}, bf16[2,128,128]{2,1,0:T(8,128)(2,1)S(1)}, u32[]{:S(2)}, u32[]{:S(2)}) collective-permute-start(bf16[2,128,128]{2,1,0:T(8,128)(2,1)} %get-tuple-element.111), channel_id=1, source_target_pairs={{0,28},{2,30},{4,24},{6,26},{8,20},{10,22},{12,16},{14,18},{16,12}... | collective-permute-start | bytes 196616 | tf_op jit(solution)/shard_map/ppermute | solution.py:719
  101.8 11.5 %collective-permute-start.30 = (bf16[2,128,128]{2,1,0:T(8,128)(2,1)}, bf16[2,128,128]{2,1,0:T(8,128)(2,1)S(1)}, u32[]{:S(2)}, u32[]{:S(2)}) collective-permute-start(bf16[2,128,128]{2,1,0:T(8,128)(2,1)} %get-tuple-element.112), channel_id=1, source_target_pairs={{0,30},{2,28},{4,26},{6,24},{8,22},{10,20},{12,18},{14,16},{16,14}... | collective-permute-start | bytes 196616 | tf_op jit(solution)/shard_map/ppermute | solution.py:719
  114.1 36.0 %copy-start.38 = (bf16[128,128]{1,0:T(8,128)(2,1)S(1)}, bf16[128,128]{1,0:T(8,128)(2,1)}, u32[]{:S(2)}) copy-start(bf16[128,128]{1,0:T(8,128)(2,1)} %get-tuple-element.143) | copy-start | bytes 98308
  114.1 37.0 %copy-start.37 = (bf16[128,128]{1,0:T(8,128)(2,1)S(1)}, bf16[128,128]{1,0:T(8,128)(2,1)}, u32[]{:S(2)}) copy-start(bf16[128,128]{1,0:T(8,128)(2,1)} %get-tuple-element.144) | copy-start | bytes 98308
  114.1 38.6 %copy-start.36 = (bf16[128,128]{1,0:T(8,128)(2,1)S(1)}, bf16[128,128]{1,0:T(8,128)(2,1)}, u32[]{:S(2)}) copy-start(bf16[128,128]{1,0:T(8,128)(2,1)} %get-tuple-element.145) | copy-start | bytes 98308
  114.1 40.7 %copy-start.35 = (bf16[128,128]{1,0:T(8,128)(2,1)S(1)}, bf16[128,128]{1,0:T(8,128)(2,1)}, u32[]{:S(2)}) copy-start(bf16[128,128]{1,0:T(8,128)(2,1)} %get-tuple-element.146) | copy-start | bytes 98308
  114.1 43.6 %copy-start.34 = (bf16[128,128]{1,0:T(8,128)(2,1)S(1)}, bf16[128,128]{1,0:T(8,128)(2,1)}, u32[]{:S(2)}) copy-start(bf16[128,128]{1,0:T(8,128)(2,1)} %get-tuple-element.147) | copy-start | bytes 98308
  114.1 49.7 %copy-start.2 = (bf16[128,128]{1,0:T(8,128)(2,1)S(1)}, bf16[128,128]{1,0:T(8,128)(2,1)}, u32[]{:S(2)}) copy-start(bf16[128,128]{1,0:T(8,128)(2,1)} %get-tuple-element.132.refs_0_) | copy-start | bytes 98308
  121.7 3.8 %collective-permute-start.34 = (f32[4,2176]{1,0:T(4,128)}, f32[4,2176]{1,0:T(4,128)S(1)}, u32[]{:S(2)}, u32[]{:S(2)}) collective-permute-start(f32[4,2176]{1,0:T(4,128)} %get-tuple-element.122), channel_id=1, source_target_pairs={{0,6},{2,4},{4,2},{6,0},{8,14},{10,12},{12,10},{14,8},{16,22},{18,... | collective-permute-start | bytes 104456 | tf_op jit(solution)/shard_map/ppermute | solution.py:725
  123.0 4.3 %collective-permute-start.33 = (f32[4,2176]{1,0:T(4,128)}, f32[4,2176]{1,0:T(4,128)S(1)}, u32[]{:S(2)}, u32[]{:S(2)}) collective-permute-start(f32[4,2176]{1,0:T(4,128)} %get-tuple-element.122), channel_id=1, source_target_pairs={{0,4},{2,6},{4,0},{6,2},{8,12},{10,14},{12,8},{14,10},{16,20},{18,... | collective-permute-start | bytes 104456 | tf_op jit(solution)/shard_map/ppermute | solution.py:725
  124.7 2.5 %collective-permute-start.32 = (f32[4,2176]{1,0:T(4,128)}, f32[4,2176]{1,0:T(4,128)S(1)}, u32[]{:S(2)}, u32[]{:S(2)}) collective-permute-start(f32[4,2176]{1,0:T(4,128)} %get-tuple-element.122), channel_id=1, source_target_pairs={{0,2},{2,0},{4,6},{6,4},{8,10},{10,8},{12,14},{14,12},{16,18},{18,... | collective-permute-start | bytes 104456 | tf_op jit(solution)/shard_map/ppermute | solution.py:725
  124.7 4.6 %collective-permute-start.39 = (bf16[128,128]{1,0:T(8,128)(2,1)S(1)}, bf16[128,128]{1,0:T(8,128)(2,1)S(1)}, u32[]{:S(2)}, u32[]{:S(2)}) collective-permute-start(bf16[128,128]{1,0:T(8,128)(2,1)S(1)} %copy-done.48), channel_id=1, source_target_pairs={{0,2},{2,0},{4,6},{6,4},{8,10},{10,8},{12,14},{14,12},{16,18},{18,... | collective-permute-start | bytes 98312 | tf_op jit(solution)/shard_map/ppermute | solution.py:719
  125.3 8.5 %collective-permute-start.40 = (bf16[128,128]{1,0:T(8,128)(2,1)S(1)}, bf16[128,128]{1,0:T(8,128)(2,1)S(1)}, u32[]{:S(2)}, u32[]{:S(2)}) collective-permute-start(bf16[128,128]{1,0:T(8,128)(2,1)S(1)} %copy-done.47), channel_id=1, source_target_pairs={{0,4},{2,6},{4,0},{6,2},{8,12},{10,14},{12,8},{14,10},{16,20},{18,... | collective-permute-start | bytes 98312 | tf_op jit(solution)/shard_map/ppermute | solution.py:719
  125.5 8.3 %collective-permute-start.41 = (bf16[128,128]{1,0:T(8,128)(2,1)S(1)}, bf16[128,128]{1,0:T(8,128)(2,1)S(1)}, u32[]{:S(2)}, u32[]{:S(2)}) collective-permute-start(bf16[128,128]{1,0:T(8,128)(2,1)S(1)} %copy-done.46), channel_id=1, source_target_pairs={{0,6},{2,4},{4,2},{6,0},{8,14},{10,12},{12,10},{14,8},{16,22},{18,... | collective-permute-start | bytes 98312 | tf_op jit(solution)/shard_map/ppermute | solution.py:719
  127.2 7.2 %collective-permute-start.42 = (bf16[128,128]{1,0:T(8,128)(2,1)S(1)}, bf16[128,128]{1,0:T(8,128)(2,1)S(1)}, u32[]{:S(2)}, u32[]{:S(2)}) collective-permute-start(bf16[128,128]{1,0:T(8,128)(2,1)S(1)} %copy-done.45), channel_id=1, source_target_pairs={{0,8},{2,10},{4,12},{6,14},{8,0},{10,2},{12,4},{14,6},{16,24},{18,... | collective-permute-start | bytes 98312 | tf_op jit(solution)/shard_map/ppermute | solution.py:719
  127.2 13.0 %collective-permute-start.31 = (f32[6,2048]{1,0:T(8,128)}, f32[6,2048]{1,0:T(8,128)S(1)}, u32[]{:S(2)}, u32[]{:S(2)}) collective-permute-start(f32[6,2048]{1,0:T(8,128)} %get-tuple-element.115), channel_id=1, source_target_pairs={{2,0},{4,2},{6,4},{8,6},{10,8},{12,10},{14,12},{16,14},{18,16},{20... | collective-permute-start | bytes 147464 | tf_op jit(solution)/shard_map/ppermute | solution.py:818
  129.3 11.7 %collective-permute-start.37 = (f32[4,2176]{1,0:T(4,128)S(1)}, f32[4,2176]{1,0:T(4,128)S(1)}, u32[]{:S(2)}, u32[]{:S(2)}) collective-permute-start(f32[4,2176]{1,0:T(4,128)S(1)} %add_add_fusion.refs_0_), channel_id=1, source_target_pairs={{0,24},{2,26},{4,28},{6,30},{8,16},{10,18},{12,20},{14,22},{16,8},... | collective-permute-start | bytes 104456 | tf_op jit(solution)/shard_map/ppermute | solution.py:725
  133.8 9.3 %collective-permute-start.36 = (f32[4,2176]{1,0:T(4,128)S(1)}, f32[4,2176]{1,0:T(4,128)S(1)}, u32[]{:S(2)}, u32[]{:S(2)}) collective-permute-start(f32[4,2176]{1,0:T(4,128)S(1)} %add_add_fusion.refs_0_), channel_id=1, source_target_pairs={{0,16},{2,18},{4,20},{6,22},{8,24},{10,26},{12,28},{14,30},{16,0},... | collective-permute-start | bytes 104456 | tf_op jit(solution)/shard_map/ppermute | solution.py:725
  133.8 9.7 %collective-permute-start.35 = (f32[4,2176]{1,0:T(4,128)S(1)}, f32[4,2176]{1,0:T(4,128)S(1)}, u32[]{:S(2)}, u32[]{:S(2)}) collective-permute-start(f32[4,2176]{1,0:T(4,128)S(1)} %add_add_fusion.refs_0_), channel_id=1, source_target_pairs={{0,8},{2,10},{4,12},{6,14},{8,0},{10,2},{12,4},{14,6},{16,24},{18,... | collective-permute-start | bytes 104456 | tf_op jit(solution)/shard_map/ppermute | solution.py:725
  134.4 3.7 %collective-permute-start.43 = (bf16[128,128]{1,0:T(8,128)(2,1)S(1)}, bf16[128,128]{1,0:T(8,128)(2,1)S(1)}, u32[]{:S(2)}, u32[]{:S(2)}) collective-permute-start(bf16[128,128]{1,0:T(8,128)(2,1)S(1)} %copy-done.44), channel_id=1, source_target_pairs={{0,10},{2,8},{4,14},{6,12},{8,2},{10,0},{12,6},{14,4},{16,26},{18,... | collective-permute-start | bytes 98312 | tf_op jit(solution)/shard_map/ppermute | solution.py:719
  138.1 10.3 %collective-permute-start.44 = (bf16[128,128]{1,0:T(8,128)(2,1)S(1)}, bf16[128,128]{1,0:T(8,128)(2,1)S(1)}, u32[]{:S(2)}, u32[]{:S(2)}) collective-permute-start(bf16[128,128]{1,0:T(8,128)(2,1)S(1)} %copy-done.43), channel_id=1, source_target_pairs={{0,12},{2,14},{4,8},{6,10},{8,4},{10,6},{12,0},{14,2},{16,28},{18,... | collective-permute-start | bytes 98312 | tf_op jit(solution)/shard_map/ppermute | solution.py:719
  140.3 9.8 %collective-permute-start.45 = (bf16[128,128]{1,0:T(8,128)(2,1)S(1)}, bf16[128,128]{1,0:T(8,128)(2,1)S(1)}, u32[]{:S(2)}, u32[]{:S(2)}) collective-permute-start(bf16[128,128]{1,0:T(8,128)(2,1)S(1)} %copy-done.42), channel_id=1, source_target_pairs={{0,14},{2,12},{4,10},{6,8},{8,6},{10,4},{12,2},{14,0},{16,30},{18,... | collective-permute-start | bytes 98312 | tf_op jit(solution)/shard_map/ppermute | solution.py:719
  141.0 10.1 %collective-permute-start.46 = (bf16[128,128]{1,0:T(8,128)(2,1)S(1)}, bf16[128,128]{1,0:T(8,128)(2,1)S(1)}, u32[]{:S(2)}, u32[]{:S(2)}) collective-permute-start(bf16[128,128]{1,0:T(8,128)(2,1)S(1)} %copy-done.41), channel_id=1, source_target_pairs={{0,16},{2,18},{4,20},{6,22},{8,24},{10,26},{12,28},{14,30},{16,0},... | collective-permute-start | bytes 98312 | tf_op jit(solution)/shard_map/ppermute | solution.py:719
  143.1 9.6 %collective-permute-start.47 = (bf16[128,128]{1,0:T(8,128)(2,1)S(1)}, bf16[128,128]{1,0:T(8,128)(2,1)S(1)}, u32[]{:S(2)}, u32[]{:S(2)}) collective-permute-start(bf16[128,128]{1,0:T(8,128)(2,1)S(1)} %copy-done.40), channel_id=1, source_target_pairs={{0,18},{2,16},{4,22},{6,20},{8,26},{10,24},{12,30},{14,28},{16,2},... | collective-permute-start | bytes 98312 | tf_op jit(solution)/shard_map/ppermute | solution.py:719
  143.5 11.3 %collective-permute-start.48 = (bf16[128,128]{1,0:T(8,128)(2,1)S(1)}, bf16[128,128]{1,0:T(8,128)(2,1)S(1)}, u32[]{:S(2)}, u32[]{:S(2)}) collective-permute-start(bf16[128,128]{1,0:T(8,128)(2,1)S(1)} %copy-done.39), channel_id=1, source_target_pairs={{0,20},{2,22},{4,16},{6,18},{8,28},{10,30},{12,24},{14,26},{16,4},... | collective-permute-start | bytes 98312 | tf_op jit(solution)/shard_map/ppermute | solution.py:719
  148.5 9.2 %collective-permute-start.38 = (f32[1,128]{1,0:T(1,128)S(1)}, f32[1,128]{1,0:T(1,128)S(1)}, u32[]{:S(2)}, u32[]{:S(2)}) collective-permute-start(f32[1,128]{1,0:T(1,128)S(1)} %get-tuple-element.131), channel_id=1, source_target_pairs={{0,1},{1,0},{2,3},{3,2},{4,5},{5,4},{6,7},{7,6},{8,9},{9,8},{10,11... | collective-permute-start | bytes 1544 | tf_op jit(solution)/shard_map/ppermute | solution.py:725
  150.1 9.1 %collective-permute-start.49 = (bf16[128,128]{1,0:T(8,128)(2,1)S(1)}, bf16[128,128]{1,0:T(8,128)(2,1)S(1)}, u32[]{:S(2)}, u32[]{:S(2)}) collective-permute-start(bf16[128,128]{1,0:T(8,128)(2,1)S(1)} %copy-done.38), channel_id=1, source_target_pairs={{0,22},{2,20},{4,18},{6,16},{8,30},{10,28},{12,26},{14,24},{16,6},... | collective-permute-start | bytes 98312 | tf_op jit(solution)/shard_map/ppermute | solution.py:719
  151.1 8.0 %collective-permute-start.50 = (bf16[128,128]{1,0:T(8,128)(2,1)S(1)}, bf16[128,128]{1,0:T(8,128)(2,1)S(1)}, u32[]{:S(2)}, u32[]{:S(2)}) collective-permute-start(bf16[128,128]{1,0:T(8,128)(2,1)S(1)} %copy-done.37), channel_id=1, source_target_pairs={{0,24},{2,26},{4,28},{6,30},{8,16},{10,18},{12,20},{14,22},{16,8},... | collective-permute-start | bytes 98312 | tf_op jit(solution)/shard_map/ppermute | solution.py:719
  152.7 6.4 %collective-permute-start.51 = (bf16[128,128]{1,0:T(8,128)(2,1)S(1)}, bf16[128,128]{1,0:T(8,128)(2,1)S(1)}, u32[]{:S(2)}, u32[]{:S(2)}) collective-permute-start(bf16[128,128]{1,0:T(8,128)(2,1)S(1)} %copy-done.36), channel_id=1, source_target_pairs={{0,26},{2,24},{4,30},{6,28},{8,18},{10,16},{12,22},{14,20},{16,10}... | collective-permute-start | bytes 98312 | tf_op jit(solution)/shard_map/ppermute | solution.py:719
  154.8 6.6 %collective-permute-start.52 = (bf16[128,128]{1,0:T(8,128)(2,1)S(1)}, bf16[128,128]{1,0:T(8,128)(2,1)S(1)}, u32[]{:S(2)}, u32[]{:S(2)}) collective-permute-start(bf16[128,128]{1,0:T(8,128)(2,1)S(1)} %copy-done.35), channel_id=1, source_target_pairs={{0,28},{2,30},{4,24},{6,26},{8,20},{10,22},{12,16},{14,18},{16,12}... | collective-permute-start | bytes 98312 | tf_op jit(solution)/shard_map/ppermute | solution.py:719
  157.7 6.1 %collective-permute-start.53 = (bf16[128,128]{1,0:T(8,128)(2,1)S(1)}, bf16[128,128]{1,0:T(8,128)(2,1)S(1)}, u32[]{:S(2)}, u32[]{:S(2)}) collective-permute-start(bf16[128,128]{1,0:T(8,128)(2,1)S(1)} %copy-done.34), channel_id=1, source_target_pairs={{0,30},{2,28},{4,26},{6,24},{8,22},{10,20},{12,18},{14,16},{16,14}... | collective-permute-start | bytes 98312 | tf_op jit(solution)/shard_map/ppermute | solution.py:719
  (39 other events, 626.5 us)

commit v6 on v4

--- a/solution.py
+++ b/solution.py
@@ -17,7 +17,8 @@
 CHUNKS = SPAN // CHUNK
 PAD = 8
 ROWS = 32
-PASSES = 2
+PASSES = 1
+TILE_ROWS = 16
 VMEM_BYTES = 60 * 1024 * 1024
 SMALL_VMEM_BYTES = 8 * 1024 * 1024
 
@@ -172,16 +173,14 @@
     return stage
 
 
-def leaves_stage(signals_ref, kind, twist_ref, split_ref):
+def leaves_stage(signals_ref, first_row, rows_here, twist_ref, split_ref):
     outer = twist_ref.shape[1]
-    rows_here = signals_ref.shape[2]
     ratio = SPAN // rows_here
 
     def stage(part, row, carry):
         here = in_span(part, row, rows_here)
-        parts = [
-            signals_ref[place * ratio + part, kind, pl.ds(row, CHUNK), :].astype(f32) for place in range(outer)
-        ]
+        rows = pl.ds(pl.multiple_of(first_row + row, CHUNK), CHUNK)
+        parts = [signals_ref[place * ratio + part, rows, :].astype(f32) for place in range(outer)]
         for leaf, (re, im) in enumerate(to_leaves(parts)):
             cosine = twist_ref[0, leaf, here, :]
             sine = twist_ref[1, leaf, here, :]
@@ -242,33 +241,69 @@
     return stage
 
 
-def filter_kernel(
-    filter_ref, coarse_ref, fine_ref, matrix_ref, spec_ref, twist_ref, split_ref,
-):
-    rows_here = filter_ref.shape[2]
-    run_all([twist_stage(coarse_ref, fine_ref, twist_ref, rows_here)], rows_here)
-    run_all([leaves_stage(filter_ref, 0, twist_ref, split_ref)], rows_here)
-    run_all([], rows_here, (matrix_ref, split_ref, spec_ref))
+def first_rows(lead, first, taps):
+    count = len(lead)
+    rows = lead + first
+    return [
+        functools.reduce(lambda x, y: x + y, [taps[shift] * rows[count + row - shift] for shift in range(count + 1)])
+        for row in range(count)
+    ]
+
+
+def first_signals(ahead, own, taps):
+    count = len(taps) - 1
+
+    def kind(rows, idx):
+        return rows[idx * count : (idx + 1) * count]
+
+    q_short, k_short, v_short = (first_rows(kind(ahead, idx), kind(own, 3 + idx), taps) for idx in range(3))
+    product = [k_row * v_row for k_row, v_row in zip(k_short, v_short)]
+    cotan = [grad_row * q_row for grad_row, q_row in zip(kind(own, 6), q_short)]
+    return product, cotan
+
+
+def patch_first_rows(signals_ref, taps_ref, rows_here):
+    pieces, all_rows = signals_ref.shape[:2]
+    taps = [taps_ref[shift : shift + 1, :] for shift in range(taps_ref.shape[0])]
+    used = 7 * (len(taps) - 1)
+
+    def extra(piece):
+        rows = signals_ref[piece, 3 * rows_here : all_rows, :].astype(f32)
+        return [rows[idx : idx + 1] for idx in range(used)]
+
+    row_idx = lax.broadcasted_iota(jnp.int32, (TILE_ROWS, LANES), 0)
+    ahead = extra(0)
+    for piece in range(1, pieces):
+        own = extra(piece)
+        for kind, rows in enumerate(first_signals(ahead, own, taps)):
+            place = slice(kind * rows_here, kind * rows_here + TILE_ROWS)
+            tile = signals_ref[piece, place, :].astype(f32)
+            for row, value in enumerate(rows):
+                tile = jnp.where(row_idx == row, value, tile)
+            signals_ref[piece, place, :] = tile.astype(bf16)
+        ahead = own
 
 
 def products_kernel(
-    signals_hbm, filter_hbm, coarse_ref, fine_ref, matrix_hbm, results_hbm, lag_hbm,
+    rows_here, signals_hbm, taps_ref, coarse_ref, fine_ref, matrix_hbm, results_hbm, lag_hbm,
     twist_ref, matrix_ref, signals_ref, results_ref, one_split, two_split, lag_split,
     filter_ref, product_ref, cotan_ref, time_ref, sems,
 ):
-    rows_here = signals_ref.shape[2]
+    filter_rows = pl.ds(2 * rows_here, rows_here)
+    extra_rows = pl.ds(3 * rows_here, signals_ref.shape[1] - 3 * rows_here)
+    signal_rows = pl.ds(0, 2 * rows_here)
     arrivals = [
-        pltpu.make_async_copy(signals_hbm.at[:, kind], signals_ref.at[:, kind], sems.at[kind]) for kind in range(2)
+        pltpu.make_async_copy(signals_hbm.at[:, rows], signals_ref.at[:, rows], sems.at[idx])
+        for idx, rows in enumerate((filter_rows, extra_rows, signal_rows))
     ]
-    matrix_copy = pltpu.make_async_copy(matrix_hbm, matrix_ref, sems.at[2])
-    filter_copy = pltpu.make_async_copy(filter_hbm, filter_ref, sems.at[3])
+    matrix_copy = pltpu.make_async_copy(matrix_hbm, matrix_ref, sems.at[3])
     lag_copy = pltpu.make_async_copy(lag_split, lag_hbm, sems.at[4])
     returns = [
         pltpu.make_async_copy(results_ref.at[:, kind], results_hbm.at[:, kind], sems.at[5 + kind]) for kind in range(2)
     ]
 
     def leaves(kind, split_ref):
-        return leaves_stage(signals_ref, kind, twist_ref, split_ref)
+        return leaves_stage(signals_ref, kind * rows_here, rows_here, twist_ref, split_ref)
 
     def combine(left_ref, right_ref, split_ref, conjugate):
         return combine_stage(left_ref, right_ref, split_ref, rows_here, conjugate)
@@ -280,20 +315,22 @@
 
         return signal_stage(from_ref, twist_ref, rows_here, write)
 
-    for copy in (arrivals[0], matrix_copy, arrivals[1], filter_copy):
+    for copy in arrivals + [matrix_copy]:
         copy.start()
     run_all([twist_stage(coarse_ref, fine_ref, twist_ref, rows_here)], rows_here)
     arrivals[0].wait()
-    run_all([leaves(0, one_split)], rows_here)
+    run_all([leaves(2, one_split)], rows_here)
     arrivals[1].wait()
+    arrivals[2].wait()
+    patch_first_rows(signals_ref, taps_ref, rows_here)
     matrix_copy.wait()
-    run_all([leaves(1, two_split)], rows_here, (matrix_ref, one_split, product_ref))
-    filter_copy.wait()
-    run_all([combine(filter_ref, product_ref, one_split, False)], rows_here, (matrix_ref, two_split, cotan_ref))
-    run_all([combine(filter_ref, cotan_ref, two_split, True)], rows_here, (matrix_ref, one_split, time_ref))
+    run_all([leaves(0, two_split)], rows_here, (matrix_ref, one_split, filter_ref))
+    run_all([leaves(1, one_split)], rows_here, (matrix_ref, two_split, product_ref))
+    run_all([combine(filter_ref, product_ref, two_split, False)], rows_here, (matrix_ref, one_split, cotan_ref))
+    run_all([combine(filter_ref, cotan_ref, one_split, True)], rows_here, (matrix_ref, two_split, time_ref))
     run_all(
         [combine(product_ref, cotan_ref, lag_split, True), result(0, time_ref)],
-        rows_here, (matrix_ref, two_split, filter_ref),
+        rows_here, (matrix_ref, one_split, filter_ref),
     )
     lag_copy.start()
     returns[0].start()
@@ -340,34 +377,25 @@
             jnp.asarray(np.stack([np.cos(fine), np.sin(fine)]).astype(np.float32)),
             jnp.asarray(matrix_blocks()),
         ]
-        self.spec = jax.ShapeDtypeStruct((pairs, BOTH, 2 * LANES), f32)
         self.split = jax.ShapeDtypeStruct((pairs, PASSES * BOTH, 2 * LANES), bf16)
         self.signal = jax.ShapeDtypeStruct((pieces, rows_here, LANES), bf16)
         self.result = jax.ShapeDtypeStruct((pieces, 2, rows_here, LANES), bf16)
         self.square = jax.ShapeDtypeStruct((1, LANES), f32)
-        self.pair_work = pltpu.VMEM(self.result.shape, bf16)
-        self.work = pltpu.VMEM(self.spec.shape, f32)
+        self.result_work = pltpu.VMEM(self.result.shape, bf16)
+        self.work = pltpu.VMEM((pairs, BOTH, 2 * LANES), f32)
         self.split_work = pltpu.VMEM(self.split.shape, bf16)
         self.twist_work = pltpu.VMEM((2, outer, SPAN, LANES), f32)
         self.matrix_work = pltpu.VMEM(self.tables[2].shape, bf16)
 
-    def filter(self, signal):
+    def products(self, signals, taps):
         return call(
-            filter_kernel, self.spec, [self.twist_work, self.split_work],
-            signal, *self.tables,
-            in_specs=[IN_VMEM, IN_SMEM, IN_VMEM, IN_VMEM],
-            out_specs=IN_VMEM,
-        )
-
-    def products(self, signals, filter_spec):
-        return call(
-            products_kernel, (self.result, self.split),
-            [self.twist_work, self.matrix_work, self.pair_work, self.pair_work]
+            functools.partial(products_kernel, self.signal.shape[1]), (self.result, self.split),
+            [self.twist_work, self.matrix_work, pltpu.VMEM(signals.shape, bf16), self.result_work]
             + [self.split_work] * 3
             + [self.work] * 4
             + [pltpu.SemaphoreType.DMA((7,))],
-            signals, filter_spec, *self.tables,
-            in_specs=[ANYWHERE, ANYWHERE, IN_SMEM, IN_VMEM, ANYWHERE],
+            signals, taps, *self.tables,
+            in_specs=[ANYWHERE, IN_VMEM, IN_SMEM, IN_VMEM, ANYWHERE],
             out_specs=(ANYWHERE, ANYWHERE),
         )
 
@@ -416,11 +444,17 @@
         parts = from_leaves([(leaf_re[leaf], leaf_im[leaf]) for leaf in range(self.outer)], 1.0 / self.seq_len)
         return jnp.stack(parts).reshape(self.pieces, self.seq_len // self.pieces, -1)
 
-    def filter(self, signal):
-        return self.spectrum(signal[:, 0])
-
-    def products(self, signals, taps):
-        product, cotan = (self.spectrum(signals[:, kind]) for kind in range(2))
+    def products(self, signals, short_taps):
+        rows_here = self.seq_len // self.pieces
+        parts = [signals[:, kind * rows_here : (kind + 1) * rows_here] for kind in range(3)]
+        extra = signals[:, 3 * rows_here :].astype(f32)
+        rows = [extra[:, idx : idx + 1] for idx in range(extra.shape[1])]
+        ahead = [jnp.concatenate([jnp.zeros_like(row[:1]), row[:-1]], axis=0) for row in rows]
+        short_rows = [short_taps[shift][None, None, :] for shift in range(short_taps.shape[0])]
+        for kind, first in enumerate(first_signals(ahead, rows, short_rows)):
+            first = jnp.concatenate(first, axis=1)
+            parts[kind] = jnp.concatenate([first.astype(bf16), parts[kind][:, first.shape[1] :]], axis=1)
+        product, cotan, taps = (self.spectrum(part) for part in parts)
         conv = self.back(taps[0] * product[0] - taps[1] * product[1], taps[0] * product[1] + taps[1] * product[0])
         corr = self.back(taps[0] * cotan[0] + taps[1] * cotan[1], taps[0] * cotan[1] - taps[1] * cotan[0])
         lag = (
@@ -519,10 +553,6 @@
     return [slice(start, start + ROWS) for start in range(0, rows_here, ROWS)]
 
 
-def pack_work(idx, operands, results, scratch):
-    results[0][idx, 0] = operands[0][:, group(idx)].astype(bf16)
-
-
 def extend_rows(lead, in_ref, lanes, ext_ref):
     ext_ref[PAD - lead.shape[0] : PAD, :] = lead
     ext_ref[PAD:, :] = in_ref[:, lanes].astype(f32)
@@ -543,13 +573,24 @@
 
 
 def signals_work(idx, operands, results, exts):
-    q_ref, k_ref, v_ref, grad_ref, lead_ref, taps_ref = operands
-    taps = taps_ref[:, group(idx)]
-    extend_three(idx, operands, lead_ref, taps.shape[0] - 1, exts)
-    for rows in row_blocks(q_ref.shape[0]):
+    q_ref, k_ref, v_ref, grad_ref, kernel_ref, taps_ref = operands
+    lanes = group(idx)
+    taps = taps_ref[:, lanes]
+    halo_rows = taps.shape[0] - 1
+    rows_here = q_ref.shape[0]
+    for ext, in_ref in zip(exts, operands):
+        extend_rows(jnp.zeros((halo_rows, LANES), f32), in_ref, lanes, ext)
+    for rows in row_blocks(rows_here):
         q_short, k_short, v_short = (short_conv(ext, taps, rows) for ext in exts)
-        results[0][idx, 0, rows, :] = (k_short * v_short).astype(bf16)
-        results[0][idx, 1, rows, :] = (grad_ref[rows, group(idx)].astype(f32) * q_short).astype(bf16)
+        below = [slice(kind * rows_here + rows.start, kind * rows_here + rows.stop) for kind in range(3)]
+        results[0][idx, below[0], :] = (k_short * v_short).astype(bf16)
+        results[0][idx, below[1], :] = (grad_ref[rows, lanes].astype(f32) * q_short).astype(bf16)
+        results[0][idx, below[2], :] = kernel_ref[rows, lanes].astype(bf16)
+    top = grad_ref[0:TILE_ROWS, lanes].astype(f32)[:halo_rows]
+    extra = [ext[ext.shape[0] - halo_rows :, :] for ext in exts] + [ext[PAD : PAD + halo_rows, :] for ext in exts]
+    extra_count = results[0].shape[1] - 3 * rows_here
+    blank = jnp.zeros((extra_count - 7 * halo_rows, LANES), f32)
+    results[0][idx, 3 * rows_here :, :] = jnp.concatenate(extra + [top, blank], axis=0).astype(bf16)
 
 
 def short_work(idx, operands, results, exts):
@@ -616,7 +657,7 @@
         sums_ref[shift_idx : shift_idx + 1, lanes] = total
 
 
-def lead_kernel(q_ref, k_ref, v_ref, lead_ref):
+def lead_kernel(q_ref, k_ref, v_ref, after_ref, lead_ref):
     halo_rows = lead_ref.shape[0] // 3
     for place, ref in enumerate((q_ref, k_ref, v_ref)):
         rows = ref[...].astype(f32)
@@ -651,31 +692,14 @@
     square_ref[...] = jnp.full(square_ref.shape, square)
 
 
-def scale_kernel(limit, totals_ref, norm_ref, lag_hbm, taps_out, skip_out, kernel_hbm, lag_ref, kernel_ref, sems):
+def scale_kernel(limit, totals_ref, norm_ref, lag_ref, taps_out, skip_out, kernel_out):
     taps_count, channels = taps_out.shape
-    groups = lag_ref.shape[0]
-    per_step = max(groups // 4, 1)
-    steps = groups // per_step
-    arrivals = []
-    returns = []
-    for step in range(steps):
-        here = pl.ds(step * per_step, per_step)
-        lanes = pl.ds(step * per_step * LANES, per_step * LANES)
-        arrivals.append(pltpu.make_async_copy(lag_hbm.at[here], lag_ref.at[here], sems.at[0, step]))
-        returns.append(pltpu.make_async_copy(kernel_ref.at[:, lanes], kernel_hbm.at[:, lanes], sems.at[1, step]))
-        arrivals[step].start()
     factor = limit / jnp.maximum(jnp.sqrt(norm_ref[...]), limit)
-    for step in range(steps):
-        arrivals[step].wait()
-        for idx in range(step * per_step, (step + 1) * per_step):
-            kernel_ref[:, idx * LANES : (idx + 1) * LANES] = lag_ref[idx].astype(f32) * factor
-        returns[step].start()
-    for idx in range(groups):
+    for idx in range(channels // LANES):
         lanes = slice(idx * LANES, (idx + 1) * LANES)
         taps_out[:, lanes] = totals_ref[0:taps_count, lanes] * factor
         skip_out[:, lanes] = totals_ref[taps_count : taps_count + 1, lanes] * factor
-    for step in range(steps):
-        returns[step].wait()
+        kernel_out[:, lanes] = lag_ref[idx].astype(f32) * factor
 
 
 def exchange(pieces_first):
@@ -683,12 +707,12 @@
 
 
 def to_pieces(groups, pieces):
-    count, kinds, rows, lanes = groups.shape
+    count, rows, lanes = groups.shape
     if count == pieces:
         return groups
     share = count * lanes // pieces
-    split = groups.reshape(count, kinds, rows, lanes // share, share)
-    return split.transpose(0, 3, 1, 2, 4).reshape(pieces, kinds, rows, share)
+    split = groups.reshape(count, rows, lanes // share, share)
+    return split.transpose(0, 2, 1, 3).reshape(pieces, rows, share)
 
 
 def to_groups(parts):
@@ -737,8 +761,8 @@
 
     flat = jax.ShapeDtypeStruct((rows_here, channels), bf16)
     halo = jax.ShapeDtypeStruct((3 * halo_rows, channels), f32)
-    one_sent = jax.ShapeDtypeStruct((groups, 1, rows_here, LANES), bf16)
-    two_sent = jax.ShapeDtypeStruct((groups, 2, rows_here, LANES), bf16)
+    extra_rows = -(-7 * halo_rows // TILE_ROWS) * TILE_ROWS
+    sent = jax.ShapeDtypeStruct((groups, 3 * rows_here + extra_rows, LANES), bf16)
     exts = [pltpu.VMEM((rows_here + PAD, LANES), f32)] * 3
     last_block = 16
     last_spec = pl.BlockSpec((last_block, channels), lambda i: (rows_here // last_block - 1, 0))
@@ -746,35 +770,30 @@
     def whole(array):
         return pl.BlockSpec(array.shape, lambda i: (0,) * len(array.shape))
 
-    lead = call(
-        lead_kernel, halo, [], q_in, k_in, v_in,
-        grid=(1,), in_specs=[last_spec] * 3, out_specs=whole(halo),
-    )
-    lead = lax.ppermute(lead, "ctx", [(i, i + 1) for i in range(pieces - 1)])
-
-    (packed,) = stream(
-        pack_work,
-        operands=[(kernel, lanes2, None)],
-        results=[(one_sent, cut_groups(per_step), None)],
-    )
-    filter_here = exchange(to_pieces(packed, pieces))
     (signals,) = stream(
         signals_work,
-        operands=[(x, lanes2, None) for x in (q_in, k_in, v_in, grad_out, lead, short_filter)],
-        results=[(two_sent, cut_groups(per_step), None)],
+        operands=[(x, lanes2, None) for x in (q_in, k_in, v_in, grad_out, kernel, short_filter)],
+        results=[(sent, cut_groups(per_step), None)],
         scratch=exts,
     )
     signals_here = exchange(to_pieces(signals, pieces))
+    taps_here = lax.dynamic_slice_in_dim(short_filter, lax.axis_index("ctx") * share, share, axis=1)
+    long_here, lag_spec = transforms.products(signals_here, taps_here)
+    long = to_groups(exchange(long_here))
+    lag_here, lag_squares = transforms.lag(lag_spec)
+    lag = to_groups(exchange(lag_here[:, None]))[:, 0]
+
+    lead = call(
+        lead_kernel, halo, [], q_in, k_in, v_in, long_here,
+        grid=(1,), in_specs=[last_spec] * 3 + [ANYWHERE], out_specs=whole(halo),
+    )
+    lead = lax.ppermute(lead, "ctx", [(i, i + 1) for i in range(pieces - 1)])
     (short,) = stream(
         short_work,
         operands=[(x, lanes2, None) for x in (q_in, k_in, v_in, lead, short_filter)],
         results=[(jax.ShapeDtypeStruct((3, rows_here, channels), f32), lanes3, None)],
         scratch=exts,
     )
-    filter_spec = transforms.filter(filter_here)
-    long_here, lag_spec = transforms.products(signals_here, filter_spec)
-    long = to_groups(exchange(long_here))
-    lag_here, lag_squares = transforms.lag(lag_spec)
 
     mixed, grad_q, grad_k, grad_v, front, back, sums = stream(
         finish_work,
@@ -786,7 +805,6 @@
         scratch=exts,
         kept=[halo, halo, jax.ShapeDtypeStruct((taps_count + 1, channels + LANES), f32)],
     )
-    lag_here, sums = lax.optimization_barrier((lag_here, sums))
     lag = to_groups(exchange(lag_here[:, None]))[:, 0]
 
     totals = sums
@@ -827,11 +845,11 @@
             jax.ShapeDtypeStruct((1, channels), f32),
             jax.ShapeDtypeStruct((rows_here, channels), f32),
         ),
-        [pltpu.VMEM(lag.shape, bf16), pltpu.VMEM((rows_here, channels), f32), pltpu.SemaphoreType.DMA((2, 4))],
+        [],
         totals, norm_sq, lag,
         vmem_bytes=SMALL_VMEM_BYTES,
-        in_specs=[IN_VMEM, IN_VMEM, ANYWHERE],
-        out_specs=(IN_VMEM, IN_VMEM, ANYWHERE),
+        in_specs=[IN_VMEM] * 3,
+        out_specs=(IN_VMEM,) * 3,
     )
     return mixed, grad_q, grad_k, grad_v, grad_short, grad_skip.reshape(channels), grad_kernel
 

time: 139 us -> 140 us (level)
  Pallas kernels: 44.7 us -> 33.3 us
  waiting for transfers between devices: 47 us -> 57.3 us
  starting transfers between devices: 41.6 us -> 43.1 us
    all_to_all x4 -> x3, waiting for transfers between devices: 36.4 us -> 49.8 us  [exchange(): lax.all_to_all(pieces_first, 'ctx', split_axis=0, concat_axis=0, tiled=True)]
    pallas_call x11 -> x9, Pallas kernels: 44.7 us -> 33.3 us  [call(): pl.pallas_call(kernel, out_shape=outs, scratch_shapes=scratch, compiler_p...]
    ppermute x7, starting transfers between devices: 8.59 us -> 15.9 us  [partners(): lax.ppermute(value, axis, [(i, i ^ step) for i in range(size)])]
    all_to_all x4 -> x3, starting transfers between devices: 29.4 us -> 23.6 us  [exchange(): lax.all_to_all(pieces_first, 'ctx', split_axis=0, concat_axis=0, tiled=True)]
    ppermute x7, waiting for transfers between devices: 9.46 us -> 6.41 us  [partners(): lax.ppermute(value, axis, [(i, i ^ step) for i in range(size)])]
    unnamed x12 -> x10, local copies, waits for them, and re-layouts: 3.42 us -> 2.68 us
  transfers between devices with their start and end apart: 13 -> 12, of which waited for: 8 -> 7; matrix products, arithmetic and copies ran while one was open for 1% -> 1% of each run, Pallas kernels for 16% -> 13%
where the time goes in v6:
time: 140 us; the launch traced here: 139 us
  waiting for transfers between devices  57.3 us (41%)
  starting transfers between devices  43.1 us (31%)
  Pallas kernels  33.3 us (24%)
  local copies, waits for them, and re-layouts  3.95 us (3%)
    all_to_all x3, waiting for transfers between devices, exchange(): lax.all_to_all(pieces_first, 'ctx', split_axis=0, concat_axis=0, tiled=True)  49.8 us
    pallas_call x9, Pallas kernels, call(): pl.pallas_call(kernel, out_shape=outs, scratch_shapes=scratch, compiler_p...  33.3 us
    all_to_all x3, starting transfers between devices, exchange(): lax.all_to_all(pieces_first, 'ctx', split_axis=0, concat_axis=0, tiled=True)  23.6 us
    ppermute x7, starting transfers between devices, partners(): lax.ppermute(value, axis, [(i, i ^ step) for i in range(size)])  15.9 us
    ppermute x7, waiting for transfers between devices, partners(): lax.ppermute(value, axis, [(i, i ^ step) for i in range(size)])  6.41 us
  transfers between devices with their start and end apart: 12, of which 7 were waited for; matrix products, arithmetic and copies ran while one was open for 1% of the time, Pallas kernels for 13%

profile of v6, /device:TPU:0, one launch (start us, length us, event | category | flops | bytes accessed | tf_op | source)
XLA Modules:
  0.0 139.2 jit_solution(10179685607895261571)
XLA Ops:
  0.6 3.6 %shard_map.153 = bf16[16,400,128]{2,1,0:T(8,128)(2,1)} custom-call(bf16[128,2048]{1,0:T(8,128)(2,1)} %refs_0_.5, bf16[128,2048]{1,0:T(8,128)(2,1)} %refs_1_.5, bf16[128,2048]{1,0:T(8,128)(2,1)} %refs_2_.5, bf16[128,2048]{1,0:T(8,128)(2,1)} %refs_3_.3, f32[128,2048]{1,0:T(8,128)} %refs_4_.2, f32[3,2048]{1,0:T(4,128)} %taps_ref.1), custom_call_target="tpu_custom_call" | custom-call | tf_op jit(solution)/shard_map/pallas_call | solution.py:34
  4.2 7.4 %all-to-all-start = ((bf16[16,400,128]{2,1,0:T(8,128)(2,1)}), bf16[16,400,128]{2,1,0:T(8,128)(2,1)S(1)}, u32[]{:S(2)}, u32[]{:S(2)}) async-start(bf16[16,400,128]{2,1,0:T(8,128)(2,1)} %shard_map.153), calls=%async_computation | async-start | bytes 3276800 | tf_op jit(solution)/shard_map/all_to_all | solution.py:706
  11.6 1.3 constant_dynamic-slice_fusion.taps_ref
  12.9 31.8 %all-to-all-done.signals_hbm = bf16[16,400,128]{2,1,0:T(8,128)(2,1)S(1)} async-done(((bf16[16,400,128]{2,1,0:T(8,128)(2,1)}), bf16[16,400,128]{2,1,0:T(8,128)(2,1)S(1)}, u32[]{:S(2)}, u32[]{:S(2)}) %all-to-all-start) | async-done | bytes 1638432 | tf_op jit(solution)/shard_map/all_to_all | solution.py:706
  44.7 0.0 copy-start.2
  44.7 1.2 copy-done.2
  45.9 11.2 %shard_map.154 = (bf16[16,2,128,128]{3,2,1,0:T(8,128)(2,1)}, bf16[4,512,256]{2,1,0:T(8,128)(2,1)}) custom-call(bf16[16,400,128]{2,1,0:T(8,128)(2,1)} %copy-done.2, f32[3,128]{1,0:T(4,128)} %constant_dynamic-slice_fusion.taps_ref, f32[16,16]{1,0:T(8,128)} %constant.18.clone.coarse_ref, f32[2,8,16,128]{3,2,1,0:T(8,128)} %constant.19.clone.fine_ref, ...), custom_call_target="tpu_custom_call" | custom-call | tf_op jit(solution)/shard_map/pallas_call | solution.py:34
  57.1 9.3 %all-to-all-start.1 = ((bf16[16,2,128,128]{3,2,1,0:T(8,128)(2,1)}), bf16[16,2,128,128]{3,2,1,0:T(8,128)(2,1)S(1)}, u32[]{:S(2)}, u32[]{:S(2)}) async-start(bf16[16,2,128,128]{3,2,1,0:T(8,128)(2,1)} %get-tuple-element.33.after_ref), calls=%async_computation.1 | async-start | bytes 2097152 | tf_op jit(solution)/shard_map/all_to_all | solution.py:706
  66.5 5.0 %shard_map.157 = (bf16[16,128,128]{2,1,0:T(8,128)(2,1)}, f32[1,128]{1,0:T(1,128)}) custom-call(bf16[4,512,256]{2,1,0:T(8,128)(2,1)} %get-tuple-element.34.split_hbm, f32[16,16]{1,0:T(8,128)} %constant.18.clone.coarse_ref, f32[2,8,16,128]{3,2,1,0:T(8,128)} %constant.19.clone.fine_ref, bf16[512,512]{1,0:T(8,128)(2,1)} %constant.20.clone.matrix_hbm), custom_call_target="tpu_custom_call" | custom-call | tf_op jit(solution)/shard_map/pallas_call | solution.py:34
  71.5 18.0 %all-to-all-done.1.refs_8_ = bf16[16,2,128,128]{3,2,1,0:T(8,128)(2,1)S(1)} async-done(((bf16[16,2,128,128]{3,2,1,0:T(8,128)(2,1)}), bf16[16,2,128,128]{3,2,1,0:T(8,128)(2,1)S(1)}, u32[]{:S(2)}, u32[]{:S(2)}) %all-to-all-start.1) | async-done | bytes 1048608 | tf_op jit(solution)/shard_map/all_to_all | solution.py:706
  89.4 0.0 copy-start.3
  89.4 6.9 %all-to-all-start.2 = ((bf16[16,1,128,128]{3,2,1,0:T(8,128)(2,1)}), bf16[16,1,128,128]{3,2,1,0:T(8,128)(2,1)S(1)}, u32[]{:S(2)}, u32[]{:S(2)}) async-start(bf16[16,1,128,128]{3,2,1,0:T(8,128)(2,1)} %bitcast.7), calls=%async_computation.2 | async-start | bytes 1048576 | tf_op jit(solution)/shard_map/all_to_all | solution.py:706
  96.3 1.6 %shard_map.155 = f32[6,2048]{1,0:T(8,128)} custom-call(bf16[128,2048]{1,0:T(8,128)(2,1)} %refs_0_.5, bf16[128,2048]{1,0:T(8,128)(2,1)} %refs_1_.5, bf16[128,2048]{1,0:T(8,128)(2,1)} %refs_2_.5, bf16[16,2,128,128]{3,2,1,0:T(8,128)(2,1)} %get-tuple-element.33.after_ref), custom_call_target="tpu_custom_call" | custom-call | tf_op jit(solution)/shard_map/pallas_call | solution.py:34
  97.8 0.0 copy-done.3
  97.8 2.3 %collective-permute-start = (f32[6,2048]{1,0:T(8,128)}, f32[6,2048]{1,0:T(8,128)S(1)}, u32[]{:S(2)}, u32[]{:S(2)}) collective-permute-start(f32[6,2048]{1,0:T(8,128)} %shard_map.155), channel_id=1, source_target_pairs={{0,2},{2,4},{4,6},{6,8},{8,10},{10,12},{12,14},{14,16},{16,18},{18... | collective-permute-start | bytes 147464 | tf_op jit(solution)/shard_map/ppermute | solution.py:790
  100.2 1.1 collective-permute-done.refs_3_.refs_5_
  101.2 0.0 copy-start.4
  101.3 0.6 copy-done.4
  101.9 3.3 %shard_map.156.refs_4_ = f32[3,128,2048]{2,1,0:T(8,128)} custom-call(bf16[128,2048]{1,0:T(8,128)(2,1)} %refs_0_.5, bf16[128,2048]{1,0:T(8,128)(2,1)} %refs_1_.5, bf16[128,2048]{1,0:T(8,128)(2,1)} %refs_2_.5, f32[6,2048]{1,0:T(8,128)} %copy-done.4, f32[3,2048]{1,0:T(4,128)} %taps_ref.1), custom_call_target="tpu_custom_call" | custom-call | tf_op jit(solution)/shard_map/pallas_call | solution.py:34
  105.2 0.0 copy-start
  105.2 5.8 %shard_map.158 = (bf16[128,2048]{1,0:T(8,128)(2,1)}, bf16[128,2048]{1,0:T(8,128)(2,1)}, bf16[128,2048]{1,0:T(8,128)(2,1)}, bf16[128,2048]{1,0:T(8,128)(2,1)}, f3...) custom-call(bf16[128,2048]{1,0:T(8,128)(2,1)} %refs_0_.5, bf16[128,2048]{1,0:T(8,128)(2,1)} %refs_1_.5, ...), custom_call_target="tpu_custom_call" | custom-call | tf_op jit(solution)/shard_map/pallas_call | solution.py:34
  111.1 6.8 %collective-permute-start.4 = (f32[4,2176]{1,0:T(4,128)}, f32[4,2176]{1,0:T(4,128)S(1)}, u32[]{:S(2)}, u32[]{:S(2)}) collective-permute-start(f32[4,2176]{1,0:T(4,128)} %get-tuple-element.45), channel_id=1, source_target_pairs={{0,6},{2,4},{4,2},{6,0},{8,14},{10,12},{12,10},{14,8},{16,22},{18,... | collective-permute-start | bytes 104456 | tf_op jit(solution)/shard_map/ppermute | solution.py:728
  117.8 0.0 collective-permute-start.3
  117.8 0.2 collective-permute-start.2
  118.0 1.3 collective-permute-start.1
  119.3 0.5 collective-permute-done.4
  119.8 2.2 %collective-permute-done.3 = f32[4,2176]{1,0:T(4,128)S(1)} collective-permute-done((f32[4,2176]{1,0:T(4,128)}, f32[4,2176]{1,0:T(4,128)S(1)}, u32[]{:S(2)}, u32[]{:S(2)}) %collective-permute-start.3) | collective-permute-done | bytes 34848 | tf_op jit(solution)/shard_map/ppermute | solution.py:728
  122.0 0.0 collective-permute-done.2
  122.0 0.8 add_add_fusion.refs_0_
  122.8 6.7 %collective-permute-start.7 = (f32[4,2176]{1,0:T(4,128)S(1)}, f32[4,2176]{1,0:T(4,128)S(1)}, u32[]{:S(2)}, u32[]{:S(2)}) collective-permute-start(f32[4,2176]{1,0:T(4,128)S(1)} %add_add_fusion.refs_0_), channel_id=1, source_target_pairs={{0,24},{2,26},{4,28},{6,30},{8,16},{10,18},{12,20},{14,22},{16,8},... | collective-permute-start | bytes 104456 | tf_op jit(solution)/shard_map/ppermute | solution.py:728
  129.5 0.0 collective-permute-start.6
  129.5 0.6 collective-permute-start.5
  130.1 0.0 collective-permute-done.1.tail_ref
  130.1 0.0 copy-done
  130.1 0.0 copy-start.1
  130.1 0.8 copy-done.1
  131.0 1.6 %shard_map.159 = (bf16[128,2048]{1,0:T(8,128)(2,1)}, bf16[128,2048]{1,0:T(8,128)(2,1)}, bf16[128,2048]{1,0:T(8,128)(2,1)}) custom-call(f32[6,2048]{1,0:T(8,128)S(1)} %copy-done.1, f32[6,2048]{1,0:T(8,128)S(1)} %collective-permute-done.1.tail_ref, f32[3,2048]{1,0:T(4,128)S(1)} %copy-done, ...), custom_call_target="tpu_custom_call", output_to_operand_aliasing={{0}: (3, {}), {1}: (4, {}), {2}: (5, {})} | custom-call | tf_op jit(solution)/shard_map/pallas_call | solution.py:34
  132.6 0.0 collective-permute-done.7.refs_3_
  132.6 1.7 %collective-permute-done.6.refs_2_ = f32[4,2176]{1,0:T(4,128)S(1)} collective-permute-done((f32[4,2176]{1,0:T(4,128)S(1)}, f32[4,2176]{1,0:T(4,128)S(1)}, u32[]{:S(2)}, u32[]{:S(2)}) %collective-permute-start.6) | collective-permute-done | bytes 34848 | tf_op jit(solution)/shard_map/ppermute | solution.py:728
  134.3 0.0 collective-permute-done.5.refs_1_
  134.3 0.1 shard_map.160
  134.5 1.6 %collective-permute-start.8 = (f32[1,128]{1,0:T(1,128)S(1)}, f32[1,128]{1,0:T(1,128)S(1)}, u32[]{:S(2)}, u32[]{:S(2)}) collective-permute-start(f32[1,128]{1,0:T(1,128)S(1)} %get-tuple-element.54), channel_id=1, source_target_pairs={{0,1},{1,0},{2,3},{3,2},{4,5},{5,4},{6,7},{7,6},{8,9},{9,8},{10,11... | collective-permute-start | bytes 1544 | tf_op jit(solution)/shard_map/ppermute | solution.py:728
  136.1 2.0 %collective-permute-done.8 = f32[1,128]{1,0:T(1,128)S(1)} collective-permute-done((f32[1,128]{1,0:T(1,128)S(1)}, f32[1,128]{1,0:T(1,128)S(1)}, u32[]{:S(2)}, u32[]{:S(2)}) %collective-permute-start.8) | collective-permute-done | bytes 544 | tf_op jit(solution)/shard_map/ppermute | solution.py:728
  138.1 0.0 all-to-all-done.2
  138.1 1.1 shard_map.161
  (1 shorter events, 0.0 us)
Async XLA Ops:
  4.2 40.5 %all-to-all-start = ((bf16[16,400,128]{2,1,0:T(8,128)(2,1)}), bf16[16,400,128]{2,1,0:T(8,128)(2,1)S(1)}, u32[]{:S(2)}, u32[]{:S(2)}) async-start(bf16[16,400,128]{2,1,0:T(8,128)(2,1)} %shard_map.153), calls=%async_computation | async-start | bytes 3276800 | tf_op jit(solution)/shard_map/all_to_all | solution.py:706
  44.7 1.2 copy-start.2
  57.1 32.3 %all-to-all-start.1 = ((bf16[16,2,128,128]{3,2,1,0:T(8,128)(2,1)}), bf16[16,2,128,128]{3,2,1,0:T(8,128)(2,1)S(1)}, u32[]{:S(2)}, u32[]{:S(2)}) async-start(bf16[16,2,128,128]{3,2,1,0:T(8,128)(2,1)} %get-tuple-element.33.after_ref), calls=%async_computation.1 | async-start | bytes 2097152 | tf_op jit(solution)/shard_map/all_to_all | solution.py:706
  89.4 8.4 %copy-start.3 = (bf16[16,2,128,128]{3,2,1,0:T(8,128)(2,1)}, bf16[16,2,128,128]{3,2,1,0:T(8,128)(2,1)S(1)}, u32[]{:S(2)}) copy-start(bf16[16,2,128,128]{3,2,1,0:T(8,128)(2,1)S(1)} %all-to-all-done.1.refs_8_) | copy-start | bytes 3145732
  89.4 48.7 %all-to-all-start.2 = ((bf16[16,1,128,128]{3,2,1,0:T(8,128)(2,1)}), bf16[16,1,128,128]{3,2,1,0:T(8,128)(2,1)S(1)}, u32[]{:S(2)}, u32[]{:S(2)}) async-start(bf16[16,1,128,128]{3,2,1,0:T(8,128)(2,1)} %bitcast.7), calls=%async_computation.2 | async-start | bytes 1048576 | tf_op jit(solution)/shard_map/all_to_all | solution.py:706
  97.8 3.4 %collective-permute-start = (f32[6,2048]{1,0:T(8,128)}, f32[6,2048]{1,0:T(8,128)S(1)}, u32[]{:S(2)}, u32[]{:S(2)}) collective-permute-start(f32[6,2048]{1,0:T(8,128)} %shard_map.155), channel_id=1, source_target_pairs={{0,2},{2,4},{4,6},{6,8},{8,10},{10,12},{12,14},{14,16},{16,18},{18... | collective-permute-start | bytes 147464 | tf_op jit(solution)/shard_map/ppermute | solution.py:790
  101.2 0.6 copy-start.4
  105.2 24.9 %copy-start = (f32[3,2048]{1,0:T(4,128)S(1)}, f32[3,2048]{1,0:T(4,128)}, u32[]{:S(2)}) copy-start(f32[3,2048]{1,0:T(4,128)} %taps_ref.1) | copy-start | bytes 73732
  111.1 8.7 %collective-permute-start.4 = (f32[4,2176]{1,0:T(4,128)}, f32[4,2176]{1,0:T(4,128)S(1)}, u32[]{:S(2)}, u32[]{:S(2)}) collective-permute-start(f32[4,2176]{1,0:T(4,128)} %get-tuple-element.45), channel_id=1, source_target_pairs={{0,6},{2,4},{4,2},{6,0},{8,14},{10,12},{12,10},{14,8},{16,22},{18,... | collective-permute-start | bytes 104456 | tf_op jit(solution)/shard_map/ppermute | solution.py:728
  117.8 4.1 %collective-permute-start.3 = (f32[4,2176]{1,0:T(4,128)}, f32[4,2176]{1,0:T(4,128)S(1)}, u32[]{:S(2)}, u32[]{:S(2)}) collective-permute-start(f32[4,2176]{1,0:T(4,128)} %get-tuple-element.45), channel_id=1, source_target_pairs={{0,4},{2,6},{4,0},{6,2},{8,12},{10,14},{12,8},{14,10},{16,20},{18,... | collective-permute-start | bytes 104456 | tf_op jit(solution)/shard_map/ppermute | solution.py:728
  117.8 4.1 %collective-permute-start.2 = (f32[4,2176]{1,0:T(4,128)}, f32[4,2176]{1,0:T(4,128)S(1)}, u32[]{:S(2)}, u32[]{:S(2)}) collective-permute-start(f32[4,2176]{1,0:T(4,128)} %get-tuple-element.45), channel_id=1, source_target_pairs={{0,2},{2,0},{4,6},{6,4},{8,10},{10,8},{12,14},{14,12},{16,18},{18,... | collective-permute-start | bytes 104456 | tf_op jit(solution)/shard_map/ppermute | solution.py:728
  118.0 12.1 %collective-permute-start.1 = (f32[6,2048]{1,0:T(8,128)}, f32[6,2048]{1,0:T(8,128)S(1)}, u32[]{:S(2)}, u32[]{:S(2)}) collective-permute-start(f32[6,2048]{1,0:T(8,128)} %get-tuple-element.38), channel_id=1, source_target_pairs={{2,0},{4,2},{6,4},{8,6},{10,8},{12,10},{14,12},{16,14},{18,16},{20... | collective-permute-start | bytes 147464 | tf_op jit(solution)/shard_map/ppermute | solution.py:818
  122.8 9.8 %collective-permute-start.7 = (f32[4,2176]{1,0:T(4,128)S(1)}, f32[4,2176]{1,0:T(4,128)S(1)}, u32[]{:S(2)}, u32[]{:S(2)}) collective-permute-start(f32[4,2176]{1,0:T(4,128)S(1)} %add_add_fusion.refs_0_), channel_id=1, source_target_pairs={{0,24},{2,26},{4,28},{6,30},{8,16},{10,18},{12,20},{14,22},{16,8},... | collective-permute-start | bytes 104456 | tf_op jit(solution)/shard_map/ppermute | solution.py:728
  129.5 4.8 %collective-permute-start.6 = (f32[4,2176]{1,0:T(4,128)S(1)}, f32[4,2176]{1,0:T(4,128)S(1)}, u32[]{:S(2)}, u32[]{:S(2)}) collective-permute-start(f32[4,2176]{1,0:T(4,128)S(1)} %add_add_fusion.refs_0_), channel_id=1, source_target_pairs={{0,16},{2,18},{4,20},{6,22},{8,24},{10,26},{12,28},{14,30},{16,0},... | collective-permute-start | bytes 104456 | tf_op jit(solution)/shard_map/ppermute | solution.py:728
  129.5 4.8 %collective-permute-start.5 = (f32[4,2176]{1,0:T(4,128)S(1)}, f32[4,2176]{1,0:T(4,128)S(1)}, u32[]{:S(2)}, u32[]{:S(2)}) collective-permute-start(f32[4,2176]{1,0:T(4,128)S(1)} %add_add_fusion.refs_0_), channel_id=1, source_target_pairs={{0,8},{2,10},{4,12},{6,14},{8,0},{10,2},{12,4},{14,6},{16,24},{18,... | collective-permute-start | bytes 104456 | tf_op jit(solution)/shard_map/ppermute | solution.py:728
  130.1 0.8 copy-start.1
  134.5 3.6 %collective-permute-start.8 = (f32[1,128]{1,0:T(1,128)S(1)}, f32[1,128]{1,0:T(1,128)S(1)}, u32[]{:S(2)}, u32[]{:S(2)}) collective-permute-start(f32[1,128]{1,0:T(1,128)S(1)} %get-tuple-element.54), channel_id=1, source_target_pairs={{0,1},{1,0},{2,3},{3,2},{4,5},{5,4},{6,7},{7,6},{8,9},{9,8},{10,11... | collective-permute-start | bytes 1544 | tf_op jit(solution)/shard_map/ppermute | solution.py:728

commit v7 on v6

--- a/solution.py
+++ b/solution.py
@@ -173,14 +173,19 @@
     return stage
 
 
-def leaves_stage(signals_ref, first_row, rows_here, twist_ref, split_ref):
+def leaves_stage(signals_ref, first_row, heads_ref, rows_here, twist_ref, split_ref):
     outer = twist_ref.shape[1]
     ratio = SPAN // rows_here
 
     def stage(part, row, carry):
         here = in_span(part, row, rows_here)
         rows = pl.ds(pl.multiple_of(first_row + row, CHUNK), CHUNK)
-        parts = [signals_ref[place * ratio + part, rows, :].astype(f32) for place in range(outer)]
+        parts = [signals_ref[place * ratio + part, rows, :] for place in range(outer)]
+        if heads_ref is not None:
+            parts = [
+                jnp.where(row == 0, heads_ref[place * ratio + part], value) for place, value in enumerate(parts)
+            ]
+        parts = [value.astype(f32) for value in parts]
         for leaf, (re, im) in enumerate(to_leaves(parts)):
             cosine = twist_ref[0, leaf, here, :]
             sine = twist_ref[1, leaf, here, :]
@@ -262,7 +267,7 @@
     return product, cotan
 
 
-def patch_first_rows(signals_ref, taps_ref, rows_here):
+def patch_first_rows(signals_ref, heads_ref, taps_ref, rows_here):
     pieces, all_rows = signals_ref.shape[:2]
     taps = [taps_ref[shift : shift + 1, :] for shift in range(taps_ref.shape[0])]
     used = 7 * (len(taps) - 1)
@@ -272,30 +277,23 @@
         return [rows[idx : idx + 1] for idx in range(used)]
 
     row_idx = lax.broadcasted_iota(jnp.int32, (TILE_ROWS, LANES), 0)
-    ahead = extra(0)
-    for piece in range(1, pieces):
+    ahead = [jnp.zeros((1, LANES), f32)] * used
+    for piece in range(pieces):
         own = extra(piece)
         for kind, rows in enumerate(first_signals(ahead, own, taps)):
             place = slice(kind * rows_here, kind * rows_here + TILE_ROWS)
             tile = signals_ref[piece, place, :].astype(f32)
             for row, value in enumerate(rows):
                 tile = jnp.where(row_idx == row, value, tile)
-            signals_ref[piece, place, :] = tile.astype(bf16)
+            heads_ref[kind, piece] = tile.astype(bf16)
         ahead = own
 
 
 def products_kernel(
-    rows_here, signals_hbm, taps_ref, coarse_ref, fine_ref, matrix_hbm, results_hbm, lag_hbm,
-    twist_ref, matrix_ref, signals_ref, results_ref, one_split, two_split, lag_split,
+    rows_here, signals_ref, taps_ref, coarse_ref, fine_ref, matrix_hbm, after_ref, results_hbm, lag_hbm,
+    twist_ref, matrix_ref, heads_ref, results_ref, one_split, two_split, lag_split,
     filter_ref, product_ref, cotan_ref, time_ref, sems,
 ):
-    filter_rows = pl.ds(2 * rows_here, rows_here)
-    extra_rows = pl.ds(3 * rows_here, signals_ref.shape[1] - 3 * rows_here)
-    signal_rows = pl.ds(0, 2 * rows_here)
-    arrivals = [
-        pltpu.make_async_copy(signals_hbm.at[:, rows], signals_ref.at[:, rows], sems.at[idx])
-        for idx, rows in enumerate((filter_rows, extra_rows, signal_rows))
-    ]
     matrix_copy = pltpu.make_async_copy(matrix_hbm, matrix_ref, sems.at[3])
     lag_copy = pltpu.make_async_copy(lag_split, lag_hbm, sems.at[4])
     returns = [
@@ -303,7 +301,8 @@
     ]
 
     def leaves(kind, split_ref):
-        return leaves_stage(signals_ref, kind * rows_here, rows_here, twist_ref, split_ref)
+        heads = heads_ref.at[kind] if kind < 2 else None
+        return leaves_stage(signals_ref, kind * rows_here, heads, rows_here, twist_ref, split_ref)
 
     def combine(left_ref, right_ref, split_ref, conjugate):
         return combine_stage(left_ref, right_ref, split_ref, rows_here, conjugate)
@@ -315,14 +314,10 @@
 
         return signal_stage(from_ref, twist_ref, rows_here, write)
 
-    for copy in arrivals + [matrix_copy]:
-        copy.start()
+    matrix_copy.start()
     run_all([twist_stage(coarse_ref, fine_ref, twist_ref, rows_here)], rows_here)
-    arrivals[0].wait()
     run_all([leaves(2, one_split)], rows_here)
-    arrivals[1].wait()
-    arrivals[2].wait()
-    patch_first_rows(signals_ref, taps_ref, rows_here)
+    patch_first_rows(signals_ref, heads_ref, taps_ref, rows_here)
     matrix_copy.wait()
     run_all([leaves(0, two_split)], rows_here, (matrix_ref, one_split, filter_ref))
     run_all([leaves(1, one_split)], rows_here, (matrix_ref, two_split, product_ref))
@@ -387,15 +382,16 @@
         self.twist_work = pltpu.VMEM((2, outer, SPAN, LANES), f32)
         self.matrix_work = pltpu.VMEM(self.tables[2].shape, bf16)
 
-    def products(self, signals, taps):
+    def products(self, signals, taps, after):
         return call(
             functools.partial(products_kernel, self.signal.shape[1]), (self.result, self.split),
-            [self.twist_work, self.matrix_work, pltpu.VMEM(signals.shape, bf16), self.result_work]
+            [self.twist_work, self.matrix_work]
+            + [pltpu.VMEM((2, signals.shape[0], TILE_ROWS, LANES), bf16), self.result_work]
             + [self.split_work] * 3
             + [self.work] * 4
             + [pltpu.SemaphoreType.DMA((7,))],
-            signals, taps, *self.tables,
-            in_specs=[ANYWHERE, IN_VMEM, IN_SMEM, IN_VMEM, ANYWHERE],
+            signals, taps, *self.tables, after,
+            in_specs=[IN_VMEM, IN_VMEM, IN_SMEM, IN_VMEM, ANYWHERE, ANYWHERE],
             out_specs=(ANYWHERE, ANYWHERE),
         )
 
@@ -444,7 +440,7 @@
         parts = from_leaves([(leaf_re[leaf], leaf_im[leaf]) for leaf in range(self.outer)], 1.0 / self.seq_len)
         return jnp.stack(parts).reshape(self.pieces, self.seq_len // self.pieces, -1)
 
-    def products(self, signals, short_taps):
+    def products(self, signals, short_taps, after):
         rows_here = self.seq_len // self.pieces
         parts = [signals[:, kind * rows_here : (kind + 1) * rows_here] for kind in range(3)]
         extra = signals[:, 3 * rows_here :].astype(f32)
@@ -778,13 +774,8 @@
     )
     signals_here = exchange(to_pieces(signals, pieces))
     taps_here = lax.dynamic_slice_in_dim(short_filter, lax.axis_index("ctx") * share, share, axis=1)
-    long_here, lag_spec = transforms.products(signals_here, taps_here)
-    long = to_groups(exchange(long_here))
-    lag_here, lag_squares = transforms.lag(lag_spec)
-    lag = to_groups(exchange(lag_here[:, None]))[:, 0]
-
     lead = call(
-        lead_kernel, halo, [], q_in, k_in, v_in, long_here,
+        lead_kernel, halo, [], q_in, k_in, v_in, signals,
         grid=(1,), in_specs=[last_spec] * 3 + [ANYWHERE], out_specs=whole(halo),
     )
     lead = lax.ppermute(lead, "ctx", [(i, i + 1) for i in range(pieces - 1)])
@@ -794,6 +785,11 @@
         results=[(jax.ShapeDtypeStruct((3, rows_here, channels), f32), lanes3, None)],
         scratch=exts,
     )
+
+    long_here, lag_spec = transforms.products(signals_here, taps_here, short)
+    long = to_groups(exchange(long_here))
+    lag_here, lag_squares = transforms.lag(lag_spec)
+    lag = to_groups(exchange(lag_here[:, None]))[:, 0]
 
     mixed, grad_q, grad_k, grad_v, front, back, sums = stream(
         finish_work,
@@ -811,6 +807,7 @@
     rounds = rounds_of(pieces)
     for steps_of in rounds[:-1]:
         totals = add_up(partners(totals, "ctx", steps_of))
+    totals, front = lax.optimization_barrier((totals, front))
     last = partners(totals, "ctx", rounds[-1])
     if len(last) == 2:
         last = [last[0] + last[1]]

time: 140 us -> 129 us (0.921)
  waiting for transfers between devices: 57.3 us -> 49.6 us
  starting transfers between devices: 43.1 us -> 40.1 us
    all_to_all x3, waiting for transfers between devices: 49.8 us -> 42 us  [exchange(): lax.all_to_all(pieces_first, 'ctx', split_axis=0, concat_axis=0, tiled=True)]
    ppermute x7, starting transfers between devices: 15.9 us -> 8.65 us  [partners(): lax.ppermute(value, axis, [(i, i ^ step) for i in range(size)])]
    all_to_all x3, starting transfers between devices: 23.6 us -> 27.9 us  [exchange(): lax.all_to_all(pieces_first, 'ctx', split_axis=0, concat_axis=0, tiled=True)]
  transfers between devices with their start and end apart: 12 -> 12, of which waited for: 7 -> 6; matrix products, arithmetic and copies ran while one was open for 1% -> 2% of each run, Pallas kernels for 13% -> 14%
where the time goes in v7:
time: 129 us; the launch traced here: 128 us
  waiting for transfers between devices  49.6 us (38%)
  starting transfers between devices  40.1 us (31%)
  Pallas kernels  33.1 us (26%)
  local copies, waits for them, and re-layouts  3.93 us (3%)
    all_to_all x3, waiting for transfers between devices, exchange(): lax.all_to_all(pieces_first, 'ctx', split_axis=0, concat_axis=0, tiled=True)  42 us
    pallas_call x9, Pallas kernels, call(): pl.pallas_call(kernel, out_shape=outs, scratch_shapes=scratch, compiler_p...  33.1 us
    all_to_all x3, starting transfers between devices, exchange(): lax.all_to_all(pieces_first, 'ctx', split_axis=0, concat_axis=0, tiled=True)  27.9 us
    ppermute x7, starting transfers between devices, partners(): lax.ppermute(value, axis, [(i, i ^ step) for i in range(size)])  8.65 us
    ppermute x7, waiting for transfers between devices, partners(): lax.ppermute(value, axis, [(i, i ^ step) for i in range(size)])  7.55 us
    unnamed x10, local copies, waits for them, and re-layouts  2.67 us
  transfers between devices with their start and end apart: 12, of which 6 were waited for; matrix products, arithmetic and copies ran while one was open for 2% of the time, Pallas kernels for 14%

profile of v7, /device:TPU:0, one launch (start us, length us, event | category | flops | bytes accessed | tf_op | source)
XLA Modules:
  0.0 128.2 jit_solution(3795295041698337829)
XLA Ops:
  0.6 3.6 %shard_map.153.after_ref = bf16[16,400,128]{2,1,0:T(8,128)(2,1)} custom-call(bf16[128,2048]{1,0:T(8,128)(2,1)} %refs_0_.5, bf16[128,2048]{1,0:T(8,128)(2,1)} %refs_1_.5, bf16[128,2048]{1,0:T(8,128)(2,1)} %refs_2_.5, bf16[128,2048]{1,0:T(8,128)(2,1)} %refs_3_.3, f32[128,2048]{1,0:T(8,128)} %refs_4_.2, f32[3,2048]{1,0:T(4,128)} %taps_ref.1), custom_call_target="tpu_custom_call" | custom-call | tf_op jit(solution)/shard_map/pallas_call | solution.py:34
  4.2 7.4 %all-to-all-start = ((bf16[16,400,128]{2,1,0:T(8,128)(2,1)}), bf16[16,400,128]{2,1,0:T(8,128)(2,1)S(1)}, u32[]{:S(2)}, u32[]{:S(2)}) async-start(bf16[16,400,128]{2,1,0:T(8,128)(2,1)} %shard_map.153.after_ref), calls=%async_computation | async-start | bytes 3276800 | tf_op jit(solution)/shard_map/all_to_all | solution.py:702
  11.6 1.6 %shard_map.154 = f32[6,2048]{1,0:T(8,128)} custom-call(bf16[128,2048]{1,0:T(8,128)(2,1)} %refs_0_.5, bf16[128,2048]{1,0:T(8,128)(2,1)} %refs_1_.5, bf16[128,2048]{1,0:T(8,128)(2,1)} %refs_2_.5, bf16[16,400,128]{2,1,0:T(8,128)(2,1)} %shard_map.153.after_ref), custom_call_target="tpu_custom_call" | custom-call | tf_op jit(solution)/shard_map/pallas_call | solution.py:34
  13.2 2.3 %collective-permute-start = (f32[6,2048]{1,0:T(8,128)}, f32[6,2048]{1,0:T(8,128)S(1)}, u32[]{:S(2)}, u32[]{:S(2)}) collective-permute-start(f32[6,2048]{1,0:T(8,128)} %shard_map.154), channel_id=1, source_target_pairs={{0,2},{2,4},{4,6},{6,8},{8,10},{10,12},{12,14},{14,16},{16,18},{18... | collective-permute-start | bytes 147464 | tf_op jit(solution)/shard_map/ppermute | solution.py:781
  15.5 1.3 constant_dynamic-slice_fusion.taps_ref
  16.7 0.0 collective-permute-done.refs_3_.refs_5_
  16.8 0.0 copy-start.4
  16.8 0.6 copy-done.4
  17.4 3.3 %shard_map.155.after_ref.refs_4_ = f32[3,128,2048]{2,1,0:T(8,128)} custom-call(bf16[128,2048]{1,0:T(8,128)(2,1)} %refs_0_.5, bf16[128,2048]{1,0:T(8,128)(2,1)} %refs_1_.5, bf16[128,2048]{1,0:T(8,128)(2,1)} %refs_2_.5, f32[6,2048]{1,0:T(8,128)} %copy-done.4, f32[3,2048]{1,0:T(4,128)} %taps_ref.1), custom_call_target="tpu_custom_call" | custom-call | tf_op jit(solution)/shard_map/pallas_call | solution.py:34
  20.7 24.0 %all-to-all-done.signals_ref = bf16[16,400,128]{2,1,0:T(8,128)(2,1)S(1)} async-done(((bf16[16,400,128]{2,1,0:T(8,128)(2,1)}), bf16[16,400,128]{2,1,0:T(8,128)(2,1)S(1)}, u32[]{:S(2)}, u32[]{:S(2)}) %all-to-all-start) | async-done | bytes 1638432 | tf_op jit(solution)/shard_map/all_to_all | solution.py:702
  44.7 0.0 copy-start.2
  44.7 1.2 copy-done.2
  45.9 11.0 %shard_map.156 = (bf16[16,2,128,128]{3,2,1,0:T(8,128)(2,1)}, bf16[4,512,256]{2,1,0:T(8,128)(2,1)}) custom-call(bf16[16,400,128]{2,1,0:T(8,128)(2,1)} %copy-done.2, f32[3,128]{1,0:T(4,128)} %constant_dynamic-slice_fusion.taps_ref, f32[16,16]{1,0:T(8,128)} %constant.18.clone.coarse_ref, f32[2,8,16,128]{3,2,1,0:T(8,128)} %constant.19.clone.fine_ref, ...), custom_call_target="tpu_custom_call" | custom-call | tf_op jit(solution)/shard_map/pallas_call | solution.py:34
  57.0 13.6 %all-to-all-start.1 = ((bf16[16,2,128,128]{3,2,1,0:T(8,128)(2,1)}), bf16[16,2,128,128]{3,2,1,0:T(8,128)(2,1)S(1)}, u32[]{:S(2)}, u32[]{:S(2)}) async-start(bf16[16,2,128,128]{3,2,1,0:T(8,128)(2,1)} %get-tuple-element.35), calls=%async_computation.1 | async-start | bytes 2097152 | tf_op jit(solution)/shard_map/all_to_all | solution.py:702
  70.6 5.0 %shard_map.157 = (bf16[16,128,128]{2,1,0:T(8,128)(2,1)}, f32[1,128]{1,0:T(1,128)}) custom-call(bf16[4,512,256]{2,1,0:T(8,128)(2,1)} %get-tuple-element.36.split_hbm, f32[16,16]{1,0:T(8,128)} %constant.18.clone.coarse_ref, f32[2,8,16,128]{3,2,1,0:T(8,128)} %constant.19.clone.fine_ref, bf16[512,512]{1,0:T(8,128)(2,1)} %constant.20.clone.matrix_hbm), custom_call_target="tpu_custom_call" | custom-call | tf_op jit(solution)/shard_map/pallas_call | solution.py:34
  75.6 18.0 %all-to-all-done.1.refs_8_ = bf16[16,2,128,128]{3,2,1,0:T(8,128)(2,1)S(1)} async-done(((bf16[16,2,128,128]{3,2,1,0:T(8,128)(2,1)}), bf16[16,2,128,128]{3,2,1,0:T(8,128)(2,1)S(1)}, u32[]{:S(2)}, u32[]{:S(2)}) %all-to-all-start.1) | async-done | bytes 1048608 | tf_op jit(solution)/shard_map/all_to_all | solution.py:702
  93.5 0.0 copy-start.3
  93.5 6.9 %all-to-all-start.2 = ((bf16[16,1,128,128]{3,2,1,0:T(8,128)(2,1)}), bf16[16,1,128,128]{3,2,1,0:T(8,128)(2,1)S(1)}, u32[]{:S(2)}, u32[]{:S(2)}) async-start(bf16[16,1,128,128]{3,2,1,0:T(8,128)(2,1)} %bitcast.7), calls=%async_computation.2 | async-start | bytes 1048576 | tf_op jit(solution)/shard_map/all_to_all | solution.py:702
  100.4 0.0 copy-done.3
  100.4 0.0 copy-start
  100.4 5.8 %shard_map.158 = (bf16[128,2048]{1,0:T(8,128)(2,1)}, bf16[128,2048]{1,0:T(8,128)(2,1)}, bf16[128,2048]{1,0:T(8,128)(2,1)}, bf16[128,2048]{1,0:T(8,128)(2,1)}, f3...) custom-call(bf16[128,2048]{1,0:T(8,128)(2,1)} %refs_0_.5, bf16[128,2048]{1,0:T(8,128)(2,1)} %refs_1_.5, ...), custom_call_target="tpu_custom_call" | custom-call | tf_op jit(solution)/shard_map/pallas_call | solution.py:34
  106.2 1.7 %collective-permute-start.3 = (f32[4,2176]{1,0:T(4,128)}, f32[4,2176]{1,0:T(4,128)S(1)}, u32[]{:S(2)}, u32[]{:S(2)}) collective-permute-start(f32[4,2176]{1,0:T(4,128)} %get-tuple-element.40), channel_id=1, source_target_pairs={{0,6},{2,4},{4,2},{6,0},{8,14},{10,12},{12,10},{14,8},{16,22},{18,... | collective-permute-start | bytes 104456 | tf_op jit(solution)/shard_map/ppermute | solution.py:724
  108.0 0.4 collective-permute-start.2
  108.3 0.0 collective-permute-start.1
  108.3 1.8 %collective-permute-done.3 = f32[4,2176]{1,0:T(4,128)S(1)} collective-permute-done((f32[4,2176]{1,0:T(4,128)}, f32[4,2176]{1,0:T(4,128)S(1)}, u32[]{:S(2)}, u32[]{:S(2)}) %collective-permute-start.3) | collective-permute-done | bytes 34848 | tf_op jit(solution)/shard_map/ppermute | solution.py:724
  110.2 1.9 %collective-permute-done.2 = f32[4,2176]{1,0:T(4,128)S(1)} collective-permute-done((f32[4,2176]{1,0:T(4,128)}, f32[4,2176]{1,0:T(4,128)S(1)}, u32[]{:S(2)}, u32[]{:S(2)}) %collective-permute-start.2) | collective-permute-done | bytes 34848 | tf_op jit(solution)/shard_map/ppermute | solution.py:724
  112.1 0.0 collective-permute-done.1
  112.1 0.8 add_add_fusion.refs_0_
  112.9 1.3 %collective-permute-start.4 = (f32[6,2048]{1,0:T(8,128)}, f32[6,2048]{1,0:T(8,128)S(1)}, u32[]{:S(2)}, u32[]{:S(2)}) collective-permute-start(f32[6,2048]{1,0:T(8,128)} %get-tuple-element.42), channel_id=1, source_target_pairs={{2,0},{4,2},{6,4},{8,6},{10,8},{12,10},{14,12},{16,14},{18,16},{20... | collective-permute-start | bytes 147464 | tf_op jit(solution)/shard_map/ppermute | solution.py:815
  114.2 4.3 %collective-permute-start.7 = (f32[4,2176]{1,0:T(4,128)S(1)}, f32[4,2176]{1,0:T(4,128)S(1)}, u32[]{:S(2)}, u32[]{:S(2)}) collective-permute-start(f32[4,2176]{1,0:T(4,128)S(1)} %add_add_fusion.refs_0_), channel_id=1, source_target_pairs={{0,24},{2,26},{4,28},{6,30},{8,16},{10,18},{12,20},{14,22},{16,8},... | collective-permute-start | bytes 104456 | tf_op jit(solution)/shard_map/ppermute | solution.py:724
  118.5 0.2 collective-permute-start.6
  118.8 0.4 collective-permute-start.5
  119.2 0.0 collective-permute-done.4.tail_ref
  119.2 0.0 copy-done
  119.2 0.0 copy-start.1
  119.2 0.8 copy-done.1
  120.0 1.6 %shard_map.159 = (bf16[128,2048]{1,0:T(8,128)(2,1)}, bf16[128,2048]{1,0:T(8,128)(2,1)}, bf16[128,2048]{1,0:T(8,128)(2,1)}) custom-call(f32[6,2048]{1,0:T(8,128)S(1)} %copy-done.1, f32[6,2048]{1,0:T(8,128)S(1)} %collective-permute-done.4.tail_ref, f32[3,2048]{1,0:T(4,128)S(1)} %copy-done, ...), custom_call_target="tpu_custom_call", output_to_operand_aliasing={{0}: (3, {}), {1}: (4, {}), {2}: (5, {})} | custom-call | tf_op jit(solution)/shard_map/pallas_call | solution.py:34
  121.6 0.0 collective-permute-done.7.refs_3_
  121.6 1.7 %collective-permute-done.6.refs_2_ = f32[4,2176]{1,0:T(4,128)S(1)} collective-permute-done((f32[4,2176]{1,0:T(4,128)S(1)}, f32[4,2176]{1,0:T(4,128)S(1)}, u32[]{:S(2)}, u32[]{:S(2)}) %collective-permute-start.6) | collective-permute-done | bytes 34848 | tf_op jit(solution)/shard_map/ppermute | solution.py:724
  123.4 0.0 collective-permute-done.5.refs_1_
  123.4 0.1 shard_map.160
  123.5 1.6 %collective-permute-start.8 = (f32[1,128]{1,0:T(1,128)S(1)}, f32[1,128]{1,0:T(1,128)S(1)}, u32[]{:S(2)}, u32[]{:S(2)}) collective-permute-start(f32[1,128]{1,0:T(1,128)S(1)} %get-tuple-element.58), channel_id=1, source_target_pairs={{0,1},{1,0},{2,3},{3,2},{4,5},{5,4},{6,7},{7,6},{8,9},{9,8},{10,11... | collective-permute-start | bytes 1544 | tf_op jit(solution)/shard_map/ppermute | solution.py:724
  125.1 2.0 %collective-permute-done.8 = f32[1,128]{1,0:T(1,128)S(1)} collective-permute-done((f32[1,128]{1,0:T(1,128)S(1)}, f32[1,128]{1,0:T(1,128)S(1)}, u32[]{:S(2)}, u32[]{:S(2)}) %collective-permute-start.8) | collective-permute-done | bytes 544 | tf_op jit(solution)/shard_map/ppermute | solution.py:724
  127.1 0.0 all-to-all-done.2
  127.1 1.1 shard_map.161
  (1 shorter events, 0.0 us)
Async XLA Ops:
  4.2 40.5 %all-to-all-start = ((bf16[16,400,128]{2,1,0:T(8,128)(2,1)}), bf16[16,400,128]{2,1,0:T(8,128)(2,1)S(1)}, u32[]{:S(2)}, u32[]{:S(2)}) async-start(bf16[16,400,128]{2,1,0:T(8,128)(2,1)} %shard_map.153.after_ref), calls=%async_computation | async-start | bytes 3276800 | tf_op jit(solution)/shard_map/all_to_all | solution.py:702
  13.2 3.6 %collective-permute-start = (f32[6,2048]{1,0:T(8,128)}, f32[6,2048]{1,0:T(8,128)S(1)}, u32[]{:S(2)}, u32[]{:S(2)}) collective-permute-start(f32[6,2048]{1,0:T(8,128)} %shard_map.154), channel_id=1, source_target_pairs={{0,2},{2,4},{4,6},{6,8},{8,10},{10,12},{12,14},{14,16},{16,18},{18... | collective-permute-start | bytes 147464 | tf_op jit(solution)/shard_map/ppermute | solution.py:781
  16.8 0.6 copy-start.4
  44.7 1.2 copy-start.2
  57.0 36.6 %all-to-all-start.1 = ((bf16[16,2,128,128]{3,2,1,0:T(8,128)(2,1)}), bf16[16,2,128,128]{3,2,1,0:T(8,128)(2,1)S(1)}, u32[]{:S(2)}, u32[]{:S(2)}) async-start(bf16[16,2,128,128]{3,2,1,0:T(8,128)(2,1)} %get-tuple-element.35), calls=%async_computation.1 | async-start | bytes 2097152 | tf_op jit(solution)/shard_map/all_to_all | solution.py:702
  93.5 6.9 %copy-start.3 = (bf16[16,2,128,128]{3,2,1,0:T(8,128)(2,1)}, bf16[16,2,128,128]{3,2,1,0:T(8,128)(2,1)S(1)}, u32[]{:S(2)}) copy-start(bf16[16,2,128,128]{3,2,1,0:T(8,128)(2,1)S(1)} %all-to-all-done.1.refs_8_) | copy-start | bytes 3145732
  93.5 33.6 %all-to-all-start.2 = ((bf16[16,1,128,128]{3,2,1,0:T(8,128)(2,1)}), bf16[16,1,128,128]{3,2,1,0:T(8,128)(2,1)S(1)}, u32[]{:S(2)}, u32[]{:S(2)}) async-start(bf16[16,1,128,128]{3,2,1,0:T(8,128)(2,1)} %bitcast.7), calls=%async_computation.2 | async-start | bytes 1048576 | tf_op jit(solution)/shard_map/all_to_all | solution.py:702
  100.4 18.7 %copy-start = (f32[3,2048]{1,0:T(4,128)S(1)}, f32[3,2048]{1,0:T(4,128)}, u32[]{:S(2)}) copy-start(f32[3,2048]{1,0:T(4,128)} %taps_ref.1) | copy-start | bytes 73732
  106.2 4.0 %collective-permute-start.3 = (f32[4,2176]{1,0:T(4,128)}, f32[4,2176]{1,0:T(4,128)S(1)}, u32[]{:S(2)}, u32[]{:S(2)}) collective-permute-start(f32[4,2176]{1,0:T(4,128)} %get-tuple-element.40), channel_id=1, source_target_pairs={{0,6},{2,4},{4,2},{6,0},{8,14},{10,12},{12,10},{14,8},{16,22},{18,... | collective-permute-start | bytes 104456 | tf_op jit(solution)/shard_map/ppermute | solution.py:724
  108.0 4.2 %collective-permute-start.2 = (f32[4,2176]{1,0:T(4,128)}, f32[4,2176]{1,0:T(4,128)S(1)}, u32[]{:S(2)}, u32[]{:S(2)}) collective-permute-start(f32[4,2176]{1,0:T(4,128)} %get-tuple-element.40), channel_id=1, source_target_pairs={{0,4},{2,6},{4,0},{6,2},{8,12},{10,14},{12,8},{14,10},{16,20},{18,... | collective-permute-start | bytes 104456 | tf_op jit(solution)/shard_map/ppermute | solution.py:724
  108.3 3.8 %collective-permute-start.1 = (f32[4,2176]{1,0:T(4,128)}, f32[4,2176]{1,0:T(4,128)S(1)}, u32[]{:S(2)}, u32[]{:S(2)}) collective-permute-start(f32[4,2176]{1,0:T(4,128)} %get-tuple-element.40), channel_id=1, source_target_pairs={{0,2},{2,0},{4,6},{6,4},{8,10},{10,8},{12,14},{14,12},{16,18},{18,... | collective-permute-start | bytes 104456 | tf_op jit(solution)/shard_map/ppermute | solution.py:724
  112.9 6.3 %collective-permute-start.4 = (f32[6,2048]{1,0:T(8,128)}, f32[6,2048]{1,0:T(8,128)S(1)}, u32[]{:S(2)}, u32[]{:S(2)}) collective-permute-start(f32[6,2048]{1,0:T(8,128)} %get-tuple-element.42), channel_id=1, source_target_pairs={{2,0},{4,2},{6,4},{8,6},{10,8},{12,10},{14,12},{16,14},{18,16},{20... | collective-permute-start | bytes 147464 | tf_op jit(solution)/shard_map/ppermute | solution.py:815
  114.2 7.4 %collective-permute-start.7 = (f32[4,2176]{1,0:T(4,128)S(1)}, f32[4,2176]{1,0:T(4,128)S(1)}, u32[]{:S(2)}, u32[]{:S(2)}) collective-permute-start(f32[4,2176]{1,0:T(4,128)S(1)} %add_add_fusion.refs_0_), channel_id=1, source_target_pairs={{0,24},{2,26},{4,28},{6,30},{8,16},{10,18},{12,20},{14,22},{16,8},... | collective-permute-start | bytes 104456 | tf_op jit(solution)/shard_map/ppermute | solution.py:724
  118.5 4.8 %collective-permute-start.6 = (f32[4,2176]{1,0:T(4,128)S(1)}, f32[4,2176]{1,0:T(4,128)S(1)}, u32[]{:S(2)}, u32[]{:S(2)}) collective-permute-start(f32[4,2176]{1,0:T(4,128)S(1)} %add_add_fusion.refs_0_), channel_id=1, source_target_pairs={{0,16},{2,18},{4,20},{6,22},{8,24},{10,26},{12,28},{14,30},{16,0},... | collective-permute-start | bytes 104456 | tf_op jit(solution)/shard_map/ppermute | solution.py:724
  118.8 4.6 %collective-permute-start.5 = (f32[4,2176]{1,0:T(4,128)S(1)}, f32[4,2176]{1,0:T(4,128)S(1)}, u32[]{:S(2)}, u32[]{:S(2)}) collective-permute-start(f32[4,2176]{1,0:T(4,128)S(1)} %add_add_fusion.refs_0_), channel_id=1, source_target_pairs={{0,8},{2,10},{4,12},{6,14},{8,0},{10,2},{12,4},{14,6},{16,24},{18,... | collective-permute-start | bytes 104456 | tf_op jit(solution)/shard_map/ppermute | solution.py:724
  119.2 0.8 copy-start.1
  123.5 3.6 %collective-permute-start.8 = (f32[1,128]{1,0:T(1,128)S(1)}, f32[1,128]{1,0:T(1,128)S(1)}, u32[]{:S(2)}, u32[]{:S(2)}) collective-permute-start(f32[1,128]{1,0:T(1,128)S(1)} %get-tuple-element.58), channel_id=1, source_target_pairs={{0,1},{1,0},{2,3},{3,2},{4,5},{5,4},{6,7},{7,6},{8,9},{9,8},{10,11... | collective-permute-start | bytes 1544 | tf_op jit(solution)/shard_map/ppermute | solution.py:724

commit v8 on v7

--- a/solution.py
+++ b/solution.py
@@ -261,32 +261,72 @@
     def kind(rows, idx):
         return rows[idx * count : (idx + 1) * count]
 
-    q_short, k_short, v_short = (first_rows(kind(ahead, idx), kind(own, 3 + idx), taps) for idx in range(3))
-    product = [k_row * v_row for k_row, v_row in zip(k_short, v_short)]
-    cotan = [grad_row * q_row for grad_row, q_row in zip(kind(own, 6), q_short)]
-    return product, cotan
+    shorts = [first_rows(kind(ahead, idx), kind(own, 3 + idx), taps) for idx in range(3)]
+    product = [(k_row * v_row).astype(bf16) for k_row, v_row in zip(shorts[1], shorts[2])]
+    back_mix = [grad_row * q_row for grad_row, q_row in zip(kind(own, 6), shorts[0])]
+    return shorts, product, back_mix
+
+
+def first_backs(ahead, own, taps, skip, conv, corr):
+    count = len(taps) - 1
+    shorts, product, back_mix = first_signals(ahead, own, taps)
+    back_q = []
+    back_k = []
+    back_v = []
+    for row in range(count):
+        filtered = conv[row] + skip * product[row].astype(f32)
+        back_prod = corr[row] + skip * back_mix[row]
+        back_q.append(own[6 * count + row] * filtered)
+        back_k.append(back_prod * shorts[2][row])
+        back_v.append(back_prod * shorts[1][row])
+    return back_q + back_k + back_v
+
+
+def extra_of(signals_ref, piece, rows_here, used):
+    rows = signals_ref[piece, 3 * rows_here :, :].astype(f32)
+    return [rows[idx : idx + 1] for idx in range(used)]
+
+
+def tap_rows(taps_ref):
+    return [taps_ref[shift : shift + 1, :] for shift in range(taps_ref.shape[0])]
 
 
 def patch_first_rows(signals_ref, heads_ref, taps_ref, rows_here):
-    pieces, all_rows = signals_ref.shape[:2]
-    taps = [taps_ref[shift : shift + 1, :] for shift in range(taps_ref.shape[0])]
+    pieces = signals_ref.shape[0]
+    taps = tap_rows(taps_ref)[:-1]
     used = 7 * (len(taps) - 1)
-
-    def extra(piece):
-        rows = signals_ref[piece, 3 * rows_here : all_rows, :].astype(f32)
-        return [rows[idx : idx + 1] for idx in range(used)]
-
     row_idx = lax.broadcasted_iota(jnp.int32, (TILE_ROWS, LANES), 0)
     ahead = [jnp.zeros((1, LANES), f32)] * used
     for piece in range(pieces):
-        own = extra(piece)
-        for kind, rows in enumerate(first_signals(ahead, own, taps)):
-            place = slice(kind * rows_here, kind * rows_here + TILE_ROWS)
-            tile = signals_ref[piece, place, :].astype(f32)
+        own = extra_of(signals_ref, piece, rows_here, used)
+        for kind, rows in enumerate(first_signals(ahead, own, taps)[1:]):
+            tile = signals_ref[piece, kind * rows_here : kind * rows_here + TILE_ROWS, :].astype(f32)
             for row, value in enumerate(rows):
-                tile = jnp.where(row_idx == row, value, tile)
+                tile = jnp.where(row_idx == row, value.astype(f32), tile)
             heads_ref[kind, piece] = tile.astype(bf16)
         ahead = own
+
+
+def write_edges(signals_ref, results_ref, taps_ref, rows_here):
+    pieces = signals_ref.shape[0]
+    *taps, skip = tap_rows(taps_ref)
+    count = len(taps) - 1
+    nothing = jnp.zeros((1, LANES), f32)
+    extras = [extra_of(signals_ref, piece, rows_here, 7 * count) for piece in range(pieces)]
+    for piece in range(pieces):
+        rows = extras[piece - 1][: 3 * count] if piece else [nothing] * (3 * count)
+        if piece + 1 < pieces:
+            conv, corr = (
+                results_ref[piece + 1, kind * rows_here : kind * rows_here + TILE_ROWS, :].astype(f32)
+                for kind in range(2)
+            )
+            rows = rows + first_backs(
+                extras[piece], extras[piece + 1], taps, skip,
+                [conv[row : row + 1] for row in range(count)], [corr[row : row + 1] for row in range(count)],
+            )
+        spare = results_ref.shape[1] - 2 * rows_here - len(rows)
+        rows.append(jnp.zeros((spare, LANES), f32))
+        results_ref[piece, 2 * rows_here :, :] = jnp.concatenate(rows, axis=0).astype(bf16)
 
 
 def products_kernel(
@@ -297,7 +337,10 @@
     matrix_copy = pltpu.make_async_copy(matrix_hbm, matrix_ref, sems.at[3])
     lag_copy = pltpu.make_async_copy(lag_split, lag_hbm, sems.at[4])
     returns = [
-        pltpu.make_async_copy(results_ref.at[:, kind], results_hbm.at[:, kind], sems.at[5 + kind]) for kind in range(2)
+        pltpu.make_async_copy(results_ref.at[:, rows], results_hbm.at[:, rows], sems.at[5 + idx])
+        for idx, rows in enumerate(
+            (pl.ds(0, rows_here), pl.ds(rows_here, results_ref.shape[1] - rows_here))
+        )
     ]
 
     def leaves(kind, split_ref):
@@ -309,7 +352,8 @@
 
     def result(kind, from_ref):
         def write(piece, rows, value, carry):
-            results_ref[piece, kind, rows, :] = value.astype(bf16)
+            place = pl.ds(pl.multiple_of(kind * rows_here + rows.start, CHUNK), CHUNK)
+            results_ref[piece, place, :] = value.astype(bf16)
             return carry
 
         return signal_stage(from_ref, twist_ref, rows_here, write)
@@ -330,6 +374,7 @@
     lag_copy.start()
     returns[0].start()
     run_all([result(1, filter_ref)], rows_here)
+    write_edges(signals_ref, results_ref, taps_ref, rows_here)
     returns[1].start()
     lag_copy.wait()
     returns[0].wait()
@@ -374,7 +419,7 @@
         ]
         self.split = jax.ShapeDtypeStruct((pairs, PASSES * BOTH, 2 * LANES), bf16)
         self.signal = jax.ShapeDtypeStruct((pieces, rows_here, LANES), bf16)
-        self.result = jax.ShapeDtypeStruct((pieces, 2, rows_here, LANES), bf16)
+        self.result = jax.ShapeDtypeStruct((pieces, 2 * rows_here + TILE_ROWS, LANES), bf16)
         self.square = jax.ShapeDtypeStruct((1, LANES), f32)
         self.result_work = pltpu.VMEM(self.result.shape, bf16)
         self.work = pltpu.VMEM((pairs, BOTH, 2 * LANES), f32)
@@ -440,24 +485,37 @@
         parts = from_leaves([(leaf_re[leaf], leaf_im[leaf]) for leaf in range(self.outer)], 1.0 / self.seq_len)
         return jnp.stack(parts).reshape(self.pieces, self.seq_len // self.pieces, -1)
 
-    def products(self, signals, short_taps, after):
+    def products(self, signals, taps_and_skip, after):
         rows_here = self.seq_len // self.pieces
         parts = [signals[:, kind * rows_here : (kind + 1) * rows_here] for kind in range(3)]
         extra = signals[:, 3 * rows_here :].astype(f32)
         rows = [extra[:, idx : idx + 1] for idx in range(extra.shape[1])]
         ahead = [jnp.concatenate([jnp.zeros_like(row[:1]), row[:-1]], axis=0) for row in rows]
-        short_rows = [short_taps[shift][None, None, :] for shift in range(short_taps.shape[0])]
-        for kind, first in enumerate(first_signals(ahead, rows, short_rows)):
+        *taps, skip = [taps_and_skip[row][None, None, :] for row in range(taps_and_skip.shape[0])]
+        count = len(taps) - 1
+        for kind, first in enumerate(first_signals(ahead, rows, taps)[1:]):
             first = jnp.concatenate(first, axis=1)
             parts[kind] = jnp.concatenate([first.astype(bf16), parts[kind][:, first.shape[1] :]], axis=1)
-        product, cotan, taps = (self.spectrum(part) for part in parts)
-        conv = self.back(taps[0] * product[0] - taps[1] * product[1], taps[0] * product[1] + taps[1] * product[0])
-        corr = self.back(taps[0] * cotan[0] + taps[1] * cotan[1], taps[0] * cotan[1] - taps[1] * cotan[0])
+        product, cotan, taps_spec = (self.spectrum(part) for part in parts)
+        conv = self.back(
+            taps_spec[0] * product[0] - taps_spec[1] * product[1], taps_spec[0] * product[1] + taps_spec[1] * product[0]
+        ).astype(bf16)
+        corr = self.back(
+            taps_spec[0] * cotan[0] + taps_spec[1] * cotan[1], taps_spec[0] * cotan[1] - taps_spec[1] * cotan[0]
+        ).astype(bf16)
         lag = (
             product[0] * cotan[0] + product[1] * cotan[1],
             product[0] * cotan[1] - product[1] * cotan[0],
         )
-        return jnp.stack([conv, corr], axis=1).astype(bf16), lag
+        backs = first_backs(
+            ahead, rows, taps, skip,
+            [conv[:, row : row + 1].astype(f32) for row in range(count)],
+            [corr[:, row : row + 1].astype(f32) for row in range(count)],
+        )
+        behind = [jnp.concatenate([row[1:], jnp.zeros_like(row[:1])], axis=0) for row in backs]
+        edge = jnp.concatenate(ahead[: 3 * count] + behind, axis=1).astype(bf16)
+        edge = jnp.pad(edge, ((0, 0), (0, TILE_ROWS - edge.shape[1]), (0, 0)))
+        return jnp.concatenate([conv, corr, edge], axis=1), lag
 
     def lag(self, lag_spec):
         lag = self.back(*lag_spec)
@@ -478,13 +536,13 @@
     sems = refs[-1]
 
     def copy(place, step):
-        outside = hbm[place].at[places[place][0](step)]
-        inside = held[place].at[places[place][1](step)]
+        outside = hbm[place].at[places[place](step)]
+        inside = held[place].at[places[place](step)]
         ends = (outside, inside) if place < in_count else (inside, outside)
         return pltpu.make_async_copy(*ends, sems.at[place, step])
 
     def arrivals(step):
-        return [copy(place, step) for place in range(in_count) if places[place][0](step) is not None]
+        return [copy(place, step) for place in range(in_count) if places[place](step) is not None]
 
     for step in range(steps):
         for arrival in arrivals(step):
@@ -505,25 +563,24 @@
             copy(place, step).wait()
 
 
-def stream_call(work, steps, per_step, operands, results, scratch=(), aliases=(), kept=()):
+def stream_call(work, steps, per_step, operands, results, scratch=(), after=(), kept=()):
     arrays = [operand[0] for operand in operands]
     shapes = [jax.ShapeDtypeStruct(array.shape, array.dtype) for array in arrays] + [result[0] for result in results]
-    cuts = [entry[1] for entry in operands] + [entry[1] for entry in results]
-    held = [pltpu.VMEM(entry[2] or shape.shape, shape.dtype) for entry, shape in zip(operands + results, shapes)]
-    extra = list(aliases)
+    cuts = [entry[1] for entry in list(operands) + list(results)]
+    held = [pltpu.VMEM(shape.shape, shape.dtype) for shape in shapes]
+    extra = list(after)
     kernel = functools.partial(streamed, work, steps, per_step, cuts, len(arrays), len(results), len(kept))
 
-    def with_aliases(*refs):
+    def without_extra(*refs):
         kernel(*refs[: len(arrays)], *refs[len(arrays) + len(extra) :])
 
     return call(
-        with_aliases,
+        without_extra,
         tuple(result[0] for result in results) + tuple(kept),
         held + list(scratch) + [pltpu.SemaphoreType.DMA((len(shapes), steps))],
         *arrays, *extra,
         in_specs=[ANYWHERE] * (len(arrays) + len(extra)),
         out_specs=(ANYWHERE,) * len(results) + (IN_VMEM,) * len(kept),
-        input_output_aliases={len(arrays) + idx: idx for idx in range(len(extra))},
     )
 
 
@@ -531,14 +588,14 @@
     def place(step):
         return (slice(None),) * (rank - 1) + (pl.ds(step * width, width),)
 
-    return place, place
+    return place
 
 
 def cut_groups(per_step):
     def place(step):
         return (pl.ds(step * per_step, per_step),)
 
-    return place, place
+    return place
 
 
 def cut_none(step):
@@ -560,12 +617,6 @@
         term = taps[shift_idx : shift_idx + 1] * ext_ref[PAD + rows.start - shift_idx : PAD + rows.stop - shift_idx, :]
         result = term if result is None else result + term
     return result
-
-
-def extend_three(idx, operands, lead_ref, halo_rows, exts):
-    lead = lead_ref[:, group(idx)]
-    for place, ext in enumerate(exts):
-        extend_rows(lead[place * halo_rows : (place + 1) * halo_rows], operands[place], group(idx), ext)
 
 
 def signals_work(idx, operands, results, exts):
@@ -590,12 +641,13 @@
 
 
 def short_work(idx, operands, results, exts):
-    q_ref, k_ref, v_ref, lead_ref, taps_ref = operands
-    taps = taps_ref[:, group(idx)]
-    extend_three(idx, operands, lead_ref, taps.shape[0] - 1, exts)
-    for rows in row_blocks(q_ref.shape[0]):
+    lanes = group(idx)
+    taps = operands[3][:, lanes]
+    for ext, in_ref in zip(exts, operands):
+        extend_rows(jnp.zeros((taps.shape[0] - 1, LANES), f32), in_ref, lanes, ext)
+    for rows in row_blocks(operands[0].shape[0]):
         for place, ext in enumerate(exts):
-            results[0][place, rows, group(idx)] = short_conv(ext, taps, rows)
+            results[0][place, rows, lanes] = short_conv(ext, taps, rows)
 
 
 def fold(value):
@@ -603,33 +655,47 @@
 
 
 def finish_work(idx, operands, results, exts):
-    q_ref, k_ref, v_ref, grad_ref, short_ref, lead_ref, taps_ref, skip_ref, long_ref, squares_ref = operands
-    mixed_ref, grad_q_ref, grad_k_ref, grad_v_ref, front_ref, back_ref, sums_ref = results
+    q_ref, k_ref, v_ref, grad_ref, short_ref, taps_ref, skip_ref, long_ref, squares_ref = operands
+    mixed_ref, grad_q_ref, grad_k_ref, grad_v_ref, sums_ref = results
     lanes = group(idx)
     taps = taps_ref[:, lanes]
     skip = skip_ref[:, lanes]
-    lead = lead_ref[:, lanes]
     taps_count = taps.shape[0]
     halo_rows = taps_count - 1
     rows_here = q_ref.shape[0]
     sums = [jnp.zeros((8, LANES), f32) for _ in range(taps_count + 1)]
-    for ext in exts:
-        ext[rows_here:, :] = jnp.zeros((PAD, LANES), f32)
+    edge = long_ref[idx, 2 * rows_here :, :].astype(f32)
+    for place, ext in enumerate(exts):
+        at = (3 + place) * halo_rows
+        ext[rows_here : rows_here + halo_rows, :] = edge[at : at + halo_rows]
+    row_idx = lax.broadcasted_iota(jnp.int32, (ROWS, LANES), 0)
+
+    def short(place, rows):
+        value = short_ref[place, rows, lanes]
+        if rows.start == 0:
+            for shift_idx in range(1, taps_count):
+                terms = jnp.zeros((ROWS, LANES), f32)
+                for row in range(shift_idx):
+                    at = place * halo_rows + halo_rows + row - shift_idx
+                    term = taps[shift_idx : shift_idx + 1] * edge[at : at + 1]
+                    terms = jnp.where(row_idx == row, term, terms)
+                value = value + terms
+        return value
+
     for rows in row_blocks(rows_here):
-        q_short, k_short, v_short = (short_ref[place, rows, lanes] for place in range(3))
+        q_short, k_short, v_short = (short(place, rows) for place in range(3))
         product = (k_short * v_short).astype(bf16).astype(f32)
-        filtered = long_ref[idx, 0, rows, :].astype(f32) + skip * product
+        filtered = long_ref[idx, rows, :].astype(f32) + skip * product
         mixed_ref[rows, lanes] = (q_short * filtered).astype(bf16)
         upstream = grad_ref[rows, lanes].astype(f32)
         back_mix = upstream * q_short
-        back_prod = long_ref[idx, 1, rows, :].astype(f32) + skip * back_mix
+        below = slice(rows_here + rows.start, rows_here + rows.stop)
+        back_prod = long_ref[idx, below, :].astype(f32) + skip * back_mix
         sums[taps_count] = sums[taps_count] + fold(back_mix * product)
         exts[0][rows, :] = upstream * filtered
         exts[1][rows, :] = back_prod * v_short
         exts[2][rows, :] = back_prod * k_short
-    for place, (ext, in_ref, out_ref) in enumerate(
-        zip(exts, (q_ref, k_ref, v_ref), (grad_q_ref, grad_k_ref, grad_v_ref))
-    ):
+    for ext, in_ref, out_ref in zip(exts, (q_ref, k_ref, v_ref), (grad_q_ref, grad_k_ref, grad_v_ref)):
         for rows in row_blocks(rows_here):
             signal = in_ref[rows, lanes].astype(f32)
             grad = None
@@ -639,42 +705,11 @@
                 grad = term if grad is None else grad + term
                 sums[shift_idx] = sums[shift_idx] + fold(ahead * signal)
             out_ref[rows, lanes] = grad.astype(bf16)
-        back_ref[place * halo_rows : (place + 1) * halo_rows, lanes] = grad[ROWS - halo_rows :]
-        front_ref[place * halo_rows : (place + 1) * halo_rows, lanes] = ext[0:halo_rows, :]
     extra = slice(sums_ref.shape[1] - LANES, sums_ref.shape[1])
     sums_ref[:, extra] = jnp.zeros((taps_count + 1, LANES), f32)
     sums_ref[0:1, extra] = squares_ref[...]
     for shift_idx in range(taps_count + 1):
-        total = jnp.sum(sums[shift_idx], axis=0, keepdims=True)
-        for place in range(3 if shift_idx < taps_count else 0):
-            for row in range(shift_idx):
-                at = place * halo_rows + halo_rows - shift_idx + row
-                total = total + lead[at : at + 1] * exts[place][row : row + 1, :]
-        sums_ref[shift_idx : shift_idx + 1, lanes] = total
-
-
-def lead_kernel(q_ref, k_ref, v_ref, after_ref, lead_ref):
-    halo_rows = lead_ref.shape[0] // 3
-    for place, ref in enumerate((q_ref, k_ref, v_ref)):
-        rows = ref[...].astype(f32)
-        lead_ref[place * halo_rows : (place + 1) * halo_rows, :] = rows[rows.shape[0] - halo_rows :]
-
-
-def edges_kernel(back_ref, tail_ref, taps_ref, q_ref, k_ref, v_ref, q_out, k_out, v_out, work_ref):
-    taps_count = taps_ref.shape[0]
-    halo_rows = taps_count - 1
-    block_rows = q_ref.shape[0]
-    for place, (ref, out_ref) in enumerate(((q_ref, q_out), (k_ref, k_out), (v_ref, v_out))):
-        work_ref[...] = ref[...].astype(f32)
-        first = place * halo_rows
-        for row in range(halo_rows):
-            total = back_ref[first + row : first + row + 1, :]
-            for shift_idx in range(halo_rows - row, taps_count):
-                source = first + row + shift_idx - halo_rows
-                total = total + taps_ref[shift_idx : shift_idx + 1, :] * tail_ref[source : source + 1, :]
-            at = block_rows - halo_rows + row
-            work_ref[at : at + 1, :] = total
-        out_ref[...] = work_ref[...].astype(bf16)
+        sums_ref[shift_idx : shift_idx + 1, lanes] = jnp.sum(sums[shift_idx], axis=0, keepdims=True)
 
 
 def norm_kernel(*refs):
@@ -712,11 +747,11 @@
 
 
 def to_groups(parts):
-    pieces, kinds, rows, share = parts.shape
+    pieces, rows, share = parts.shape
     if share == LANES:
         return parts
-    joined = parts.reshape(pieces * share // LANES, LANES // share, kinds, rows, share)
-    return joined.transpose(0, 2, 3, 1, 4).reshape(-1, kinds, rows, LANES)
+    joined = parts.reshape(pieces * share // LANES, LANES // share, rows, share)
+    return joined.transpose(0, 2, 1, 3).reshape(-1, rows, LANES)
 
 
 def partners(value, axis, steps):
@@ -752,77 +787,53 @@
     steps = groups // per_step
     lanes2 = cut_lanes(per_step * LANES, 2)
     lanes3 = cut_lanes(per_step * LANES, 3)
+    skip_row = skip.reshape(1, channels)
     transforms = (Transforms if share == LANES else PlainTransforms)(pieces, rows_here)
     stream = functools.partial(stream_call, steps=steps, per_step=per_step)
 
     flat = jax.ShapeDtypeStruct((rows_here, channels), bf16)
-    halo = jax.ShapeDtypeStruct((3 * halo_rows, channels), f32)
     extra_rows = -(-7 * halo_rows // TILE_ROWS) * TILE_ROWS
     sent = jax.ShapeDtypeStruct((groups, 3 * rows_here + extra_rows, LANES), bf16)
     exts = [pltpu.VMEM((rows_here + PAD, LANES), f32)] * 3
-    last_block = 16
-    last_spec = pl.BlockSpec((last_block, channels), lambda i: (rows_here // last_block - 1, 0))
-
-    def whole(array):
-        return pl.BlockSpec(array.shape, lambda i: (0,) * len(array.shape))
 
     (signals,) = stream(
         signals_work,
-        operands=[(x, lanes2, None) for x in (q_in, k_in, v_in, grad_out, kernel, short_filter)],
-        results=[(sent, cut_groups(per_step), None)],
+        operands=[(x, lanes2) for x in (q_in, k_in, v_in, grad_out, kernel, short_filter)],
+        results=[(sent, cut_groups(per_step))],
         scratch=exts,
     )
     signals_here = exchange(to_pieces(signals, pieces))
-    taps_here = lax.dynamic_slice_in_dim(short_filter, lax.axis_index("ctx") * share, share, axis=1)
-    lead = call(
-        lead_kernel, halo, [], q_in, k_in, v_in, signals,
-        grid=(1,), in_specs=[last_spec] * 3 + [ANYWHERE], out_specs=whole(halo),
-    )
-    lead = lax.ppermute(lead, "ctx", [(i, i + 1) for i in range(pieces - 1)])
     (short,) = stream(
         short_work,
-        operands=[(x, lanes2, None) for x in (q_in, k_in, v_in, lead, short_filter)],
-        results=[(jax.ShapeDtypeStruct((3, rows_here, channels), f32), lanes3, None)],
+        operands=[(x, lanes2) for x in (q_in, k_in, v_in, short_filter)],
+        results=[(jax.ShapeDtypeStruct((3, rows_here, channels), f32), lanes3)],
         scratch=exts,
-    )
-
+        after=[signals],
+    )
+    taps_and_skip = jnp.concatenate([short_filter, skip_row], axis=0)
+    taps_here = lax.dynamic_slice_in_dim(taps_and_skip, lax.axis_index("ctx") * share, share, axis=1)
     long_here, lag_spec = transforms.products(signals_here, taps_here, short)
     long = to_groups(exchange(long_here))
     lag_here, lag_squares = transforms.lag(lag_spec)
-    lag = to_groups(exchange(lag_here[:, None]))[:, 0]
-
-    mixed, grad_q, grad_k, grad_v, front, back, sums = stream(
+    lag = to_groups(exchange(lag_here))
+
+    mixed, grad_q, grad_k, grad_v, sums = stream(
         finish_work,
-        operands=[(x, lanes2, None) for x in (q_in, k_in, v_in, grad_out)]
-        + [(short, lanes3, None)]
-        + [(x, lanes2, None) for x in (lead, short_filter, skip.reshape(1, channels))]
-        + [(long, cut_groups(per_step), None), (lag_squares, (cut_none, cut_none), None)],
-        results=[(flat, lanes2, None)] * 4,
+        operands=[(x, lanes2) for x in (q_in, k_in, v_in, grad_out)]
+        + [(short, lanes3), (short_filter, lanes2), (skip_row, lanes2)]
+        + [(long, cut_groups(per_step)), (lag_squares, cut_none)],
+        results=[(flat, lanes2)] * 4,
         scratch=exts,
-        kept=[halo, halo, jax.ShapeDtypeStruct((taps_count + 1, channels + LANES), f32)],
-    )
-    lag = to_groups(exchange(lag_here[:, None]))[:, 0]
+        kept=[jax.ShapeDtypeStruct((taps_count + 1, channels + LANES), f32)],
+    )
 
     totals = sums
     rounds = rounds_of(pieces)
     for steps_of in rounds[:-1]:
         totals = add_up(partners(totals, "ctx", steps_of))
-    totals, front = lax.optimization_barrier((totals, front))
     last = partners(totals, "ctx", rounds[-1])
     if len(last) == 2:
         last = [last[0] + last[1]]
-
-    tail = lax.ppermute(front, "ctx", [(i, i - 1) for i in range(1, pieces)])
-    grad_q, grad_k, grad_v = call(
-        edges_kernel, (flat, flat, flat), [pltpu.VMEM((last_block, channels), f32)],
-        back, tail, short_filter, grad_q, grad_k, grad_v,
-        vmem_bytes=SMALL_VMEM_BYTES,
-        grid=(1,),
-        in_specs=[whole(back), whole(tail), whole(short_filter)] + [last_spec] * 3,
-        out_specs=(last_spec,) * 3,
-        input_output_aliases={3: 0, 4: 1, 5: 2},
-    )
-    grad_q, grad_k, grad_v, *last = lax.optimization_barrier((grad_q, grad_k, grad_v, *last))
 
     totals, norm_sq = call(
         norm_kernel,

time: 129 us -> 124 us (0.961)
  waiting for transfers between devices: 49.6 us -> 57.7 us
  starting transfers between devices: 40.1 us -> 32.1 us
  Pallas kernels: 33.1 us -> 30.1 us
  local copies, waits for them, and re-layouts: 3.93 us -> 1.21 us
    all_to_all x3, waiting for transfers between devices: 42 us -> 48.1 us  [exchange(): lax.all_to_all(pieces_first, 'ctx', split_axis=0, concat_axis=0, tiled=True)]
    all_to_all x3, starting transfers between devices: 27.9 us -> 23.9 us  [exchange(): lax.all_to_all(pieces_first, 'ctx', split_axis=0, concat_axis=0, tiled=True)]
    ppermute x2 -> x0, starting transfers between devices: 3.59 us -> none  [the longest x1 2.3 us: body(): lead = lax.ppermute(lead, 'ctx', [(i, i + 1) for i in range(pieces - 1)])]
    pallas_call x9 -> x7, Pallas kernels: 33.1 us -> 30.1 us  [call(): pl.pallas_call(kernel, out_shape=outs, scratch_shapes=scratch, compiler_p...]
    ppermute x7, waiting for transfers between devices: 7.55 us -> 9.62 us  [partners(): lax.ppermute(value, axis, [(i, i ^ step) for i in range(size)])]
    unnamed x10 -> x8, local copies, waits for them, and re-layouts: 2.67 us -> 1.21 us
  transfers between devices with their start and end apart: 12 -> 10, of which waited for: 6 -> 7; matrix products, arithmetic and copies ran while one was open for 2% -> 1% of each run, Pallas kernels for 14% -> 11%
where the time goes in v8:
time: 124 us; the launch traced here: 123 us
  waiting for transfers between devices  57.7 us (47%)
  starting transfers between devices  32.1 us (26%)
  Pallas kernels  30.1 us (24%)
  other arithmetic  1.44 us (1%)
    all_to_all x3, waiting for transfers between devices, exchange(): lax.all_to_all(pieces_first, 'ctx', split_axis=0, concat_axis=0, tiled=True)  48.1 us
    pallas_call x7, Pallas kernels, call(): pl.pallas_call(kernel, out_shape=outs, scratch_shapes=scratch, compiler_p...  30.1 us
    all_to_all x3, starting transfers between devices, exchange(): lax.all_to_all(pieces_first, 'ctx', split_axis=0, concat_axis=0, tiled=True)  23.9 us
    ppermute x7, waiting for transfers between devices, partners(): lax.ppermute(value, axis, [(i, i ^ step) for i in range(size)])  9.62 us
    ppermute x7, starting transfers between devices, partners(): lax.ppermute(value, axis, [(i, i ^ step) for i in range(size)])  8.16 us
  transfers between devices with their start and end apart: 10, of which 7 were waited for; matrix products, arithmetic and copies ran while one was open for 1% of the time, Pallas kernels for 11%

profile of v8, /device:TPU:0, one launch (start us, length us, event | category | flops | bytes accessed | tf_op | source)
XLA Modules:
  0.0 123.3 jit_solution(530734329063573410)
XLA Ops:
  0.6 3.6 %shard_map.153.refs_4_ = bf16[16,400,128]{2,1,0:T(8,128)(2,1)} custom-call(bf16[128,2048]{1,0:T(8,128)(2,1)} %refs_0_.5, bf16[128,2048]{1,0:T(8,128)(2,1)} %refs_1_.5, bf16[128,2048]{1,0:T(8,128)(2,1)} %refs_2_.5, bf16[128,2048]{1,0:T(8,128)(2,1)} %refs_3_.5, f32[128,2048]{1,0:T(8,128)} %refs_4_.1, f32[3,2048]{1,0:T(4,128)} %refs_5_.3), custom_call_target="tpu_custom_call" | custom-call | tf_op jit(solution)/shard_map/pallas_call | solution.py:34
  4.2 7.4 %all-to-all-start = ((bf16[16,400,128]{2,1,0:T(8,128)(2,1)}), bf16[16,400,128]{2,1,0:T(8,128)(2,1)S(1)}, u32[]{:S(2)}, u32[]{:S(2)}) async-start(bf16[16,400,128]{2,1,0:T(8,128)(2,1)} %shard_map.153.refs_4_), calls=%async_computation | async-start | bytes 3276800 | tf_op jit(solution)/shard_map/all_to_all | solution.py:737
  11.6 0.0 copy-start.2
  11.6 0.0 copy-start.3
  11.6 3.3 %shard_map.154.after_ref.refs_4_ = f32[3,128,2048]{2,1,0:T(8,128)} custom-call(bf16[128,2048]{1,0:T(8,128)(2,1)} %refs_0_.5, bf16[128,2048]{1,0:T(8,128)(2,1)} %refs_1_.5, bf16[128,2048]{1,0:T(8,128)(2,1)} %refs_2_.5, f32[3,2048]{1,0:T(4,128)} %refs_5_.3, bf16[16,400,128]{2,1,0:T(8,128)(2,1)} %shard_map.153.refs_4_), custom_call_target="tpu_custom_call" | custom-call | tf_op jit(solution)/shard_map/pallas_call | solution.py:34
  15.0 0.0 copy-done.2
  15.0 0.0 copy-done.3
  15.0 0.7 fusion.taps_ref
  15.7 29.1 %all-to-all-done.signals_ref = bf16[16,400,128]{2,1,0:T(8,128)(2,1)S(1)} async-done(((bf16[16,400,128]{2,1,0:T(8,128)(2,1)}), bf16[16,400,128]{2,1,0:T(8,128)(2,1)S(1)}, u32[]{:S(2)}, u32[]{:S(2)}) %all-to-all-start) | async-done | bytes 1638432 | tf_op jit(solution)/shard_map/all_to_all | solution.py:737
  44.7 0.0 copy-start
  44.7 1.2 copy-done
  45.9 11.3 %shard_map.155 = (bf16[16,272,128]{2,1,0:T(8,128)(2,1)}, bf16[4,512,256]{2,1,0:T(8,128)(2,1)}) custom-call(bf16[16,400,128]{2,1,0:T(8,128)(2,1)} %copy-done, f32[4,128]{1,0:T(4,128)} %fusion.taps_ref, f32[16,16]{1,0:T(8,128)} %constant.18.clone.coarse_ref, f32[2,8,16,128]{3,2,1,0:T(8,128)} %constant.19.clone.fine_ref, ...), custom_call_target="tpu_custom_call" | custom-call | tf_op jit(solution)/shard_map/pallas_call | solution.py:34
  57.2 9.4 %all-to-all-start.1 = ((bf16[16,272,128]{2,1,0:T(8,128)(2,1)}), bf16[16,272,128]{2,1,0:T(8,128)(2,1)S(1)}, u32[]{:S(2)}, u32[]{:S(2)}) async-start(bf16[16,272,128]{2,1,0:T(8,128)(2,1)} %get-tuple-element.21), calls=%async_computation.1 | async-start | bytes 2228224 | tf_op jit(solution)/shard_map/all_to_all | solution.py:737
  66.6 5.0 %shard_map.156 = (bf16[16,128,128]{2,1,0:T(8,128)(2,1)}, f32[1,128]{1,0:T(1,128)}) custom-call(bf16[4,512,256]{2,1,0:T(8,128)(2,1)} %get-tuple-element.22.split_hbm, f32[16,16]{1,0:T(8,128)} %constant.18.clone.coarse_ref, f32[2,8,16,128]{3,2,1,0:T(8,128)} %constant.19.clone.fine_ref, bf16[512,512]{1,0:T(8,128)(2,1)} %constant.20.clone.matrix_hbm), custom_call_target="tpu_custom_call" | custom-call | tf_op jit(solution)/shard_map/pallas_call | solution.py:34
  71.6 19.0 %all-to-all-done.1.refs_7_ = bf16[16,272,128]{2,1,0:T(8,128)(2,1)S(1)} async-done(((bf16[16,272,128]{2,1,0:T(8,128)(2,1)}), bf16[16,272,128]{2,1,0:T(8,128)(2,1)S(1)}, u32[]{:S(2)}, u32[]{:S(2)}) %all-to-all-start.1) | async-done | bytes 1114144 | tf_op jit(solution)/shard_map/all_to_all | solution.py:737
  90.6 0.0 copy-start.1
  90.6 7.2 %all-to-all-start.2 = ((bf16[16,128,128]{2,1,0:T(8,128)(2,1)}), bf16[16,128,128]{2,1,0:T(8,128)(2,1)S(1)}, u32[]{:S(2)}, u32[]{:S(2)}) async-start(bf16[16,128,128]{2,1,0:T(8,128)(2,1)} %get-tuple-element.31), calls=%async_computation.2 | async-start | bytes 1048576 | tf_op jit(solution)/shard_map/all_to_all | solution.py:737
  97.8 0.0 copy-done.1
  97.9 5.6 %shard_map.157 = (bf16[128,2048]{1,0:T(8,128)(2,1)}, bf16[128,2048]{1,0:T(8,128)(2,1)}, bf16[128,2048]{1,0:T(8,128)(2,1)}, bf16[128,2048]{1,0:T(8,128)(2,1)}, f32[4,2176]{1,0:T(4,128)}) custom-call(bf16[128,2048]{1,0:T(8,128)(2,1)} %refs_0_.5, bf16[128,2048]{1,0:T(8,128)(2,1)} %refs_1_.5, bf16[128,2048]{1,0:T(8,128)(2,1)} %refs_2_.5, ...), custom_call_target="tpu_custom_call" | custom-call | tf_op jit(solution)/shard_map/pallas_call | solution.py:34
  103.5 1.7 %collective-permute-start.2 = (f32[4,2176]{1,0:T(4,128)}, f32[4,2176]{1,0:T(4,128)S(1)}, u32[]{:S(2)}, u32[]{:S(2)}) collective-permute-start(f32[4,2176]{1,0:T(4,128)} %get-tuple-element.28), channel_id=1, source_target_pairs={{0,6},{2,4},{4,2},{6,0},{8,14},{10,12},{12,10},{14,8},{16,22},{18,... | collective-permute-start | bytes 104456 | tf_op jit(solution)/shard_map/ppermute | solution.py:759
  105.2 0.4 collective-permute-start.1
  105.6 0.0 collective-permute-start
  105.6 1.9 %collective-permute-done.2 = f32[4,2176]{1,0:T(4,128)S(1)} collective-permute-done((f32[4,2176]{1,0:T(4,128)}, f32[4,2176]{1,0:T(4,128)S(1)}, u32[]{:S(2)}, u32[]{:S(2)}) %collective-permute-start.2) | collective-permute-done | bytes 34848 | tf_op jit(solution)/shard_map/ppermute | solution.py:759
  107.5 1.9 %collective-permute-done.1 = f32[4,2176]{1,0:T(4,128)S(1)} collective-permute-done((f32[4,2176]{1,0:T(4,128)}, f32[4,2176]{1,0:T(4,128)S(1)}, u32[]{:S(2)}, u32[]{:S(2)}) %collective-permute-start.1) | collective-permute-done | bytes 34848 | tf_op jit(solution)/shard_map/ppermute | solution.py:759
  109.4 0.0 collective-permute-done
  109.4 0.8 add_add_fusion.refs_0_
  110.2 3.3 %collective-permute-start.5 = (f32[4,2176]{1,0:T(4,128)S(1)}, f32[4,2176]{1,0:T(4,128)S(1)}, u32[]{:S(2)}, u32[]{:S(2)}) collective-permute-start(f32[4,2176]{1,0:T(4,128)S(1)} %add_add_fusion.refs_0_), channel_id=1, source_target_pairs={{0,24},{2,26},{4,28},{6,30},{8,16},{10,18},{12,20},{14,22},{16,8},... | collective-permute-start | bytes 104456 | tf_op jit(solution)/shard_map/ppermute | solution.py:759
  113.5 0.4 collective-permute-start.4
  113.9 0.7 collective-permute-start.3
  114.6 1.4 %collective-permute-done.5.refs_3_ = f32[4,2176]{1,0:T(4,128)S(1)} collective-permute-done((f32[4,2176]{1,0:T(4,128)S(1)}, f32[4,2176]{1,0:T(4,128)S(1)}, u32[]{:S(2)}, u32[]{:S(2)}) %collective-permute-start.5) | collective-permute-done | bytes 34848 | tf_op jit(solution)/shard_map/ppermute | solution.py:759
  116.1 2.4 %collective-permute-done.4.refs_2_ = f32[4,2176]{1,0:T(4,128)S(1)} collective-permute-done((f32[4,2176]{1,0:T(4,128)S(1)}, f32[4,2176]{1,0:T(4,128)S(1)}, u32[]{:S(2)}, u32[]{:S(2)}) %collective-permute-start.4) | collective-permute-done | bytes 34848 | tf_op jit(solution)/shard_map/ppermute | solution.py:759
  118.4 0.0 collective-permute-done.3.refs_1_
  118.4 0.1 shard_map.158
  118.6 1.6 %collective-permute-start.6 = (f32[1,128]{1,0:T(1,128)S(1)}, f32[1,128]{1,0:T(1,128)S(1)}, u32[]{:S(2)}, u32[]{:S(2)}) collective-permute-start(f32[1,128]{1,0:T(1,128)S(1)} %get-tuple-element.30), channel_id=1, source_target_pairs={{0,1},{1,0},{2,3},{3,2},{4,5},{5,4},{6,7},{7,6},{8,9},{9,8},{10,11... | collective-permute-start | bytes 1544 | tf_op jit(solution)/shard_map/ppermute | solution.py:759
  120.2 2.0 %collective-permute-done.6 = f32[1,128]{1,0:T(1,128)S(1)} collective-permute-done((f32[1,128]{1,0:T(1,128)S(1)}, f32[1,128]{1,0:T(1,128)S(1)}, u32[]{:S(2)}, u32[]{:S(2)}) %collective-permute-start.6) | collective-permute-done | bytes 544 | tf_op jit(solution)/shard_map/ppermute | solution.py:759
  122.2 0.0 all-to-all-done.2.lag_ref
  122.2 1.1 shard_map.159
  (1 shorter events, 0.0 us)
Async XLA Ops:
  4.2 40.5 %all-to-all-start = ((bf16[16,400,128]{2,1,0:T(8,128)(2,1)}), bf16[16,400,128]{2,1,0:T(8,128)(2,1)S(1)}, u32[]{:S(2)}, u32[]{:S(2)}) async-start(bf16[16,400,128]{2,1,0:T(8,128)(2,1)} %shard_map.153.refs_4_), calls=%async_computation | async-start | bytes 3276800 | tf_op jit(solution)/shard_map/all_to_all | solution.py:737
  11.6 3.4 %copy-start.2 = (f32[3,2048]{1,0:T(4,128)S(1)}, f32[3,2048]{1,0:T(4,128)}, u32[]{:S(2)}) copy-start(f32[3,2048]{1,0:T(4,128)} %refs_5_.3) | copy-start | bytes 73732
  11.6 3.4 %copy-start.3 = (f32[2048]{0:T(1024)S(1)}, f32[2048]{0:T(1024)}, u32[]{:S(2)}) copy-start(f32[2048]{0:T(1024)} %param.16) | copy-start | bytes 24580
  44.7 1.2 copy-start
  57.2 33.4 %all-to-all-start.1 = ((bf16[16,272,128]{2,1,0:T(8,128)(2,1)}), bf16[16,272,128]{2,1,0:T(8,128)(2,1)S(1)}, u32[]{:S(2)}, u32[]{:S(2)}) async-start(bf16[16,272,128]{2,1,0:T(8,128)(2,1)} %get-tuple-element.21), calls=%async_computation.1 | async-start | bytes 2228224 | tf_op jit(solution)/shard_map/all_to_all | solution.py:737
  90.6 7.2 %copy-start.1 = (bf16[16,272,128]{2,1,0:T(8,128)(2,1)}, bf16[16,272,128]{2,1,0:T(8,128)(2,1)S(1)}, u32[]{:S(2)}) copy-start(bf16[16,272,128]{2,1,0:T(8,128)(2,1)S(1)} %all-to-all-done.1.refs_7_) | copy-start | bytes 3342340
  90.6 31.6 %all-to-all-start.2 = ((bf16[16,128,128]{2,1,0:T(8,128)(2,1)}), bf16[16,128,128]{2,1,0:T(8,128)(2,1)S(1)}, u32[]{:S(2)}, u32[]{:S(2)}) async-start(bf16[16,128,128]{2,1,0:T(8,128)(2,1)} %get-tuple-element.31), calls=%async_computation.2 | async-start | bytes 1048576 | tf_op jit(solution)/shard_map/all_to_all | solution.py:737
  103.5 4.0 %collective-permute-start.2 = (f32[4,2176]{1,0:T(4,128)}, f32[4,2176]{1,0:T(4,128)S(1)}, u32[]{:S(2)}, u32[]{:S(2)}) collective-permute-start(f32[4,2176]{1,0:T(4,128)} %get-tuple-element.28), channel_id=1, source_target_pairs={{0,6},{2,4},{4,2},{6,0},{8,14},{10,12},{12,10},{14,8},{16,22},{18,... | collective-permute-start | bytes 104456 | tf_op jit(solution)/shard_map/ppermute | solution.py:759
  105.2 4.2 %collective-permute-start.1 = (f32[4,2176]{1,0:T(4,128)}, f32[4,2176]{1,0:T(4,128)S(1)}, u32[]{:S(2)}, u32[]{:S(2)}) collective-permute-start(f32[4,2176]{1,0:T(4,128)} %get-tuple-element.28), channel_id=1, source_target_pairs={{0,4},{2,6},{4,0},{6,2},{8,12},{10,14},{12,8},{14,10},{16,20},{18,... | collective-permute-start | bytes 104456 | tf_op jit(solution)/shard_map/ppermute | solution.py:759
  105.6 3.8 %collective-permute-start = (f32[4,2176]{1,0:T(4,128)}, f32[4,2176]{1,0:T(4,128)S(1)}, u32[]{:S(2)}, u32[]{:S(2)}) collective-permute-start(f32[4,2176]{1,0:T(4,128)} %get-tuple-element.28), channel_id=1, source_target_pairs={{0,2},{2,0},{4,6},{6,4},{8,10},{10,8},{12,14},{14,12},{16,18},{18,... | collective-permute-start | bytes 104456 | tf_op jit(solution)/shard_map/ppermute | solution.py:759
  110.2 5.9 %collective-permute-start.5 = (f32[4,2176]{1,0:T(4,128)S(1)}, f32[4,2176]{1,0:T(4,128)S(1)}, u32[]{:S(2)}, u32[]{:S(2)}) collective-permute-start(f32[4,2176]{1,0:T(4,128)S(1)} %add_add_fusion.refs_0_), channel_id=1, source_target_pairs={{0,24},{2,26},{4,28},{6,30},{8,16},{10,18},{12,20},{14,22},{16,8},... | collective-permute-start | bytes 104456 | tf_op jit(solution)/shard_map/ppermute | solution.py:759
  113.5 4.9 %collective-permute-start.4 = (f32[4,2176]{1,0:T(4,128)S(1)}, f32[4,2176]{1,0:T(4,128)S(1)}, u32[]{:S(2)}, u32[]{:S(2)}) collective-permute-start(f32[4,2176]{1,0:T(4,128)S(1)} %add_add_fusion.refs_0_), channel_id=1, source_target_pairs={{0,16},{2,18},{4,20},{6,22},{8,24},{10,26},{12,28},{14,30},{16,0},... | collective-permute-start | bytes 104456 | tf_op jit(solution)/shard_map/ppermute | solution.py:759
  113.9 4.5 %collective-permute-start.3 = (f32[4,2176]{1,0:T(4,128)S(1)}, f32[4,2176]{1,0:T(4,128)S(1)}, u32[]{:S(2)}, u32[]{:S(2)}) collective-permute-start(f32[4,2176]{1,0:T(4,128)S(1)} %add_add_fusion.refs_0_), channel_id=1, source_target_pairs={{0,8},{2,10},{4,12},{6,14},{8,0},{10,2},{12,4},{14,6},{16,24},{18,... | collective-permute-start | bytes 104456 | tf_op jit(solution)/shard_map/ppermute | solution.py:759
  118.6 3.6 %collective-permute-start.6 = (f32[1,128]{1,0:T(1,128)S(1)}, f32[1,128]{1,0:T(1,128)S(1)}, u32[]{:S(2)}, u32[]{:S(2)}) collective-permute-start(f32[1,128]{1,0:T(1,128)S(1)} %get-tuple-element.30), channel_id=1, source_target_pairs={{0,1},{1,0},{2,3},{3,2},{4,5},{5,4},{6,7},{7,6},{8,9},{9,8},{10,11... | collective-permute-start | bytes 1544 | tf_op jit(solution)/shard_map/ppermute | solution.py:759

commit v9 on v8

--- a/solution.py
+++ b/solution.py
@@ -128,31 +128,20 @@
 
 def run_all(stages, rows_here, matmul=None, carry=0):
     tiles = matmul[2].shape[0] if matmul else 4
-    ratio = SPAN // rows_here
-    in_part = tiles // ratio
     per_tile = CHUNKS // tiles
-    for part in range(ratio):
-
-        def step(tile, carry, part=part):
-            if matmul:
-                matrix_ref, split_ref, result_ref = matmul
-                place = part * in_part + tile
-                result_ref[place] = jnp.dot(matrix_ref[...], split_ref[place], preferred_element_type=f32)
-            for chunk in range(per_tile):
-                for stage in stages:
-                    carry = stage(part, chunk_row(tile * per_tile + chunk), carry)
-            return carry
-
-        carry = lax.fori_loop(0, in_part, step, carry)
+    in_part = rows_here // CHUNK
+    for tile in range(tiles):
+        if matmul:
+            matrix_ref, split_ref, result_ref = matmul
+            result_ref[tile] = jnp.dot(matrix_ref[...], split_ref[tile], preferred_element_type=f32)
+        for chunk in range(tile * per_tile, (tile + 1) * per_tile):
+            for stage in stages:
+                carry = stage(chunk // in_part, chunk % in_part * CHUNK, carry)
     return carry
 
 
-def chunk_row(idx):
-    return pl.multiple_of(idx * CHUNK, CHUNK)
-
-
 def in_span(part, row, rows_here):
-    return pl.ds(pl.multiple_of(part * rows_here + row, CHUNK), CHUNK)
+    return pl.ds(part * rows_here + row, CHUNK)
 
 
 def twist_stage(coarse_ref, fine_ref, twist_ref, rows_here):
@@ -179,12 +168,10 @@
 
     def stage(part, row, carry):
         here = in_span(part, row, rows_here)
-        rows = pl.ds(pl.multiple_of(first_row + row, CHUNK), CHUNK)
+        rows = pl.ds(first_row + row, CHUNK)
         parts = [signals_ref[place * ratio + part, rows, :] for place in range(outer)]
-        if heads_ref is not None:
-            parts = [
-                jnp.where(row == 0, heads_ref[place * ratio + part], value) for place, value in enumerate(parts)
-            ]
+        if heads_ref is not None and row == 0:
+            parts = [heads_ref[place * ratio + part] for place in range(outer)]
         parts = [value.astype(f32) for value in parts]
         for leaf, (re, im) in enumerate(to_leaves(parts)):
             cosine = twist_ref[0, leaf, here, :]
@@ -330,10 +317,17 @@
 
 
 def products_kernel(
-    rows_here, signals_ref, taps_ref, coarse_ref, fine_ref, matrix_hbm, after_ref, results_hbm, lag_hbm,
-    twist_ref, matrix_ref, heads_ref, results_ref, one_split, two_split, lag_split,
+    rows_here, signals_hbm, taps_ref, coarse_ref, fine_ref, matrix_hbm, after_ref, results_hbm, lag_hbm, same_hbm,
+    signals_ref, twist_ref, matrix_ref, heads_ref, results_ref, one_split, two_split, lag_split,
     filter_ref, product_ref, cotan_ref, time_ref, sems,
 ):
+    filter_rows = pl.ds(2 * rows_here, rows_here)
+    extra_rows = pl.ds(3 * rows_here, signals_ref.shape[1] - 3 * rows_here)
+    signal_rows = pl.ds(0, 2 * rows_here)
+    arrivals = [
+        pltpu.make_async_copy(signals_hbm.at[:, rows], signals_ref.at[:, rows], sems.at[idx])
+        for idx, rows in enumerate((filter_rows, extra_rows, signal_rows))
+    ]
     matrix_copy = pltpu.make_async_copy(matrix_hbm, matrix_ref, sems.at[3])
     lag_copy = pltpu.make_async_copy(lag_split, lag_hbm, sems.at[4])
     returns = [
@@ -352,15 +346,19 @@
 
     def result(kind, from_ref):
         def write(piece, rows, value, carry):
-            place = pl.ds(pl.multiple_of(kind * rows_here + rows.start, CHUNK), CHUNK)
+            place = pl.ds(kind * rows_here + rows.start, CHUNK)
             results_ref[piece, place, :] = value.astype(bf16)
             return carry
 
         return signal_stage(from_ref, twist_ref, rows_here, write)
 
-    matrix_copy.start()
+    for copy in arrivals + [matrix_copy]:
+        copy.start()
     run_all([twist_stage(coarse_ref, fine_ref, twist_ref, rows_here)], rows_here)
+    arrivals[0].wait()
     run_all([leaves(2, one_split)], rows_here)
+    arrivals[1].wait()
+    arrivals[2].wait()
     patch_first_rows(signals_ref, heads_ref, taps_ref, rows_here)
     matrix_copy.wait()
     run_all([leaves(0, two_split)], rows_here, (matrix_ref, one_split, filter_ref))
@@ -428,17 +426,20 @@
         self.matrix_work = pltpu.VMEM(self.tables[2].shape, bf16)
 
     def products(self, signals, taps, after):
-        return call(
-            functools.partial(products_kernel, self.signal.shape[1]), (self.result, self.split),
-            [self.twist_work, self.matrix_work]
+        results, lag_split, _ = call(
+            functools.partial(products_kernel, self.signal.shape[1]),
+            (self.result, self.split, jax.ShapeDtypeStruct(signals.shape, bf16)),
+            [pltpu.VMEM(signals.shape, bf16), self.twist_work, self.matrix_work]
             + [pltpu.VMEM((2, signals.shape[0], TILE_ROWS, LANES), bf16), self.result_work]
             + [self.split_work] * 3
             + [self.work] * 4
             + [pltpu.SemaphoreType.DMA((7,))],
             signals, taps, *self.tables, after,
-            in_specs=[IN_VMEM, IN_VMEM, IN_SMEM, IN_VMEM, ANYWHERE, ANYWHERE],
-            out_specs=(ANYWHERE, ANYWHERE),
+            in_specs=[ANYWHERE, IN_VMEM, IN_SMEM, IN_VMEM, ANYWHERE, ANYWHERE],
+            out_specs=(ANYWHERE, ANYWHERE, ANYWHERE),
+            input_output_aliases={0: 2},
         )
+        return results, lag_split
 
     def lag(self, lag_split):
         return call(
@@ -723,6 +724,10 @@
     square_ref[...] = jnp.full(square_ref.shape, square)
 
 
+def add_kernel(*refs):
+    refs[-1][...] = add_up([ref[...] for ref in refs[:-1]])
+
+
 def scale_kernel(limit, totals_ref, norm_ref, lag_ref, taps_out, skip_out, kernel_out):
     taps_count, channels = taps_out.shape
     factor = limit / jnp.maximum(jnp.sqrt(norm_ref[...]), limit)
@@ -830,7 +835,11 @@
     totals = sums
     rounds = rounds_of(pieces)
     for steps_of in rounds[:-1]:
-        totals = add_up(partners(totals, "ctx", steps_of))
+        values = partners(totals, "ctx", steps_of)
+        totals = call(
+            add_kernel, jax.ShapeDtypeStruct(totals.shape, f32), [], *values,
+            vmem_bytes=SMALL_VMEM_BYTES, in_specs=[IN_VMEM] * len(values), out_specs=IN_VMEM,
+        )
     last = partners(totals, "ctx", rounds[-1])
     if len(last) == 2:
         last = [last[0] + last[1]]

time: 124 us -> 122 us (0.984)
  Pallas kernels: 30.1 us -> 27.5 us
    pallas_call x7 -> x8, Pallas kernels: 30.1 us -> 27.5 us  [call(): pl.pallas_call(kernel, out_shape=outs, scratch_shapes=scratch, compiler_p...]
where the time goes in v9:
time: 122 us; the launch traced here: 121 us
  waiting for transfers between devices  58.4 us (48%)
  starting transfers between devices  32.1 us (26%)
  Pallas kernels  27.5 us (23%)
  local copies, waits for them, and re-layouts  1.99 us (2%)
    all_to_all x3, waiting for transfers between devices, exchange(): lax.all_to_all(pieces_first, 'ctx', split_axis=0, concat_axis=0, tiled=True)  48.7 us
    pallas_call x8, Pallas kernels, call(): pl.pallas_call(kernel, out_shape=outs, scratch_shapes=scratch, compiler_p...  27.5 us
    all_to_all x3, starting transfers between devices, exchange(): lax.all_to_all(pieces_first, 'ctx', split_axis=0, concat_axis=0, tiled=True)  23.9 us
    ppermute x7, waiting for transfers between devices, partners(): lax.ppermute(value, axis, [(i, i ^ step) for i in range(size)])  9.62 us
    ppermute x7, starting transfers between devices, partners(): lax.ppermute(value, axis, [(i, i ^ step) for i in range(size)])  8.17 us
  transfers between devices with their start and end apart: 10, of which 7 were waited for; matrix products, arithmetic and copies ran while one was open for 1% of the time, Pallas kernels for 11%

profile of v9, /device:TPU:0, one launch (start us, length us, event | category | flops | bytes accessed | tf_op | source)
XLA Modules:
  0.0 121.4 jit_solution(4894506170133226985)
XLA Ops:
  0.6 3.6 %shard_map.153.refs_4_ = bf16[16,400,128]{2,1,0:T(8,128)(2,1)} custom-call(bf16[128,2048]{1,0:T(8,128)(2,1)} %refs_0_.5, bf16[128,2048]{1,0:T(8,128)(2,1)} %refs_1_.5, bf16[128,2048]{1,0:T(8,128)(2,1)} %refs_2_.5, bf16[128,2048]{1,0:T(8,128)(2,1)} %refs_3_.5, f32[128,2048]{1,0:T(8,128)} %refs_4_.1, f32[3,2048]{1,0:T(4,128)} %refs_5_.3), custom_call_target="tpu_custom_call" | custom-call | tf_op jit(solution)/shard_map/pallas_call | solution.py:34
  4.2 7.4 %all-to-all-start = ((bf16[16,400,128]{2,1,0:T(8,128)(2,1)}), bf16[16,400,128]{2,1,0:T(8,128)(2,1)S(1)}, u32[]{:S(2)}, u32[]{:S(2)}) async-start(bf16[16,400,128]{2,1,0:T(8,128)(2,1)} %shard_map.153.refs_4_), calls=%async_computation | async-start | bytes 3276800 | tf_op jit(solution)/shard_map/all_to_all | solution.py:742
  11.6 0.0 copy-start.3
  11.6 0.0 copy-start.4
  11.6 3.3 %shard_map.154.after_ref.refs_4_ = f32[3,128,2048]{2,1,0:T(8,128)} custom-call(bf16[128,2048]{1,0:T(8,128)(2,1)} %refs_0_.5, bf16[128,2048]{1,0:T(8,128)(2,1)} %refs_1_.5, bf16[128,2048]{1,0:T(8,128)(2,1)} %refs_2_.5, f32[3,2048]{1,0:T(4,128)} %refs_5_.3, bf16[16,400,128]{2,1,0:T(8,128)(2,1)} %shard_map.153.refs_4_), custom_call_target="tpu_custom_call" | custom-call | tf_op jit(solution)/shard_map/pallas_call | solution.py:34
  14.9 0.0 copy-done.3
  14.9 0.0 copy-done.4
  14.9 0.7 fusion.taps_ref
  15.6 29.1 %all-to-all-done.signals_hbm = bf16[16,400,128]{2,1,0:T(8,128)(2,1)S(1)} async-done(((bf16[16,400,128]{2,1,0:T(8,128)(2,1)}), bf16[16,400,128]{2,1,0:T(8,128)(2,1)S(1)}, u32[]{:S(2)}, u32[]{:S(2)}) %all-to-all-start) | async-done | bytes 1638432 | tf_op jit(solution)/shard_map/all_to_all | solution.py:742
  44.7 0.0 copy-start.1
  44.7 1.2 copy-done.1
  45.9 9.3 %shard_map.155 = (bf16[16,272,128]{2,1,0:T(8,128)(2,1)}, bf16[4,512,256]{2,1,0:T(8,128)(2,1)}, bf16[16,400,128]{2,1,0:T(8,128)(2,1)}) custom-call(bf16[16,400,128]{2,1,0:T(8,128)(2,1)} %copy-done.1, f32[4,128]{1,0:T(4,128)} %fusion.taps_ref, f32[16,16]{1,0:T(8,128)} %constant.18.clone.coarse_ref, ...), custom_call_target="tpu_custom_call", output_to_operand_aliasing={{2}: (0, {})} | custom-call | tf_op jit(solution)/shard_map/pallas_call | solution.py:34
  55.3 9.4 %all-to-all-start.1 = ((bf16[16,272,128]{2,1,0:T(8,128)(2,1)}), bf16[16,272,128]{2,1,0:T(8,128)(2,1)S(1)}, u32[]{:S(2)}, u32[]{:S(2)}) async-start(bf16[16,272,128]{2,1,0:T(8,128)(2,1)} %get-tuple-element.21), calls=%async_computation.1 | async-start | bytes 2228224 | tf_op jit(solution)/shard_map/all_to_all | solution.py:742
  64.7 4.4 %shard_map.156 = (bf16[16,128,128]{2,1,0:T(8,128)(2,1)}, f32[1,128]{1,0:T(1,128)}) custom-call(bf16[4,512,256]{2,1,0:T(8,128)(2,1)} %get-tuple-element.22.split_hbm, f32[16,16]{1,0:T(8,128)} %constant.18.clone.coarse_ref, f32[2,8,16,128]{3,2,1,0:T(8,128)} %constant.19.clone.fine_ref, bf16[512,512]{1,0:T(8,128)(2,1)} %constant.20.clone.matrix_hbm), custom_call_target="tpu_custom_call" | custom-call | tf_op jit(solution)/shard_map/pallas_call | solution.py:34
  69.1 19.6 %all-to-all-done.1.refs_7_ = bf16[16,272,128]{2,1,0:T(8,128)(2,1)S(1)} async-done(((bf16[16,272,128]{2,1,0:T(8,128)(2,1)}), bf16[16,272,128]{2,1,0:T(8,128)(2,1)S(1)}, u32[]{:S(2)}, u32[]{:S(2)}) %all-to-all-start.1) | async-done | bytes 1114144 | tf_op jit(solution)/shard_map/all_to_all | solution.py:742
  88.7 0.0 copy-start.2
  88.7 7.2 %all-to-all-start.2 = ((bf16[16,128,128]{2,1,0:T(8,128)(2,1)}), bf16[16,128,128]{2,1,0:T(8,128)(2,1)S(1)}, u32[]{:S(2)}, u32[]{:S(2)}) async-start(bf16[16,128,128]{2,1,0:T(8,128)(2,1)} %get-tuple-element.31), calls=%async_computation.2 | async-start | bytes 1048576 | tf_op jit(solution)/shard_map/all_to_all | solution.py:742
  95.9 0.0 copy-done.2
  95.9 5.6 %shard_map.157 = (bf16[128,2048]{1,0:T(8,128)(2,1)}, bf16[128,2048]{1,0:T(8,128)(2,1)}, bf16[128,2048]{1,0:T(8,128)(2,1)}, bf16[128,2048]{1,0:T(8,128)(2,1)}, f32[4,2176]{1,0:T(4,128)}) custom-call(bf16[128,2048]{1,0:T(8,128)(2,1)} %refs_0_.5, bf16[128,2048]{1,0:T(8,128)(2,1)} %refs_1_.5, bf16[128,2048]{1,0:T(8,128)(2,1)} %refs_2_.5, ...), custom_call_target="tpu_custom_call" | custom-call | tf_op jit(solution)/shard_map/pallas_call | solution.py:34
  101.5 1.7 %collective-permute-start.2 = (f32[4,2176]{1,0:T(4,128)}, f32[4,2176]{1,0:T(4,128)S(1)}, u32[]{:S(2)}, u32[]{:S(2)}) collective-permute-start(f32[4,2176]{1,0:T(4,128)} %get-tuple-element.28.refs_0_), channel_id=1, source_target_pairs={{0,6},{2,4},{4,2},{6,0},{8,14},{10,12},{12,10},{14,8},{16,22},{18,... | collective-permute-start | bytes 104456 | tf_op jit(solution)/shard_map/ppermute | solution.py:764
  103.2 0.4 collective-permute-start.1
  103.6 0.0 collective-permute-start
  103.6 1.9 %collective-permute-done.2.refs_3_ = f32[4,2176]{1,0:T(4,128)S(1)} collective-permute-done((f32[4,2176]{1,0:T(4,128)}, f32[4,2176]{1,0:T(4,128)S(1)}, u32[]{:S(2)}, u32[]{:S(2)}) %collective-permute-start.2) | collective-permute-done | bytes 34848 | tf_op jit(solution)/shard_map/ppermute | solution.py:764
  105.5 1.9 %collective-permute-done.1.refs_2_ = f32[4,2176]{1,0:T(4,128)S(1)} collective-permute-done((f32[4,2176]{1,0:T(4,128)}, f32[4,2176]{1,0:T(4,128)S(1)}, u32[]{:S(2)}, u32[]{:S(2)}) %collective-permute-start.1) | collective-permute-done | bytes 34848 | tf_op jit(solution)/shard_map/ppermute | solution.py:764
  107.4 0.0 collective-permute-done.refs_1_
  107.4 0.0 copy-start
  107.4 0.8 copy-done
  108.2 3.3 %collective-permute-start.5 = (f32[4,2176]{1,0:T(4,128)S(1)}, f32[4,2176]{1,0:T(4,128)S(1)}, u32[]{:S(2)}, u32[]{:S(2)}) collective-permute-start(f32[4,2176]{1,0:T(4,128)S(1)} %shard_map.158.refs_0_), channel_id=1, source_target_pairs={{0,24},{2,26},{4,28},{6,30},{8,16},{10,18},{12,20},{14,22},{16,8},... | collective-permute-start | bytes 104456 | tf_op jit(solution)/shard_map/ppermute | solution.py:764
  111.5 0.4 collective-permute-start.4
  112.0 0.7 collective-permute-start.3
  112.6 1.4 %collective-permute-done.5.refs_3_ = f32[4,2176]{1,0:T(4,128)S(1)} collective-permute-done((f32[4,2176]{1,0:T(4,128)S(1)}, f32[4,2176]{1,0:T(4,128)S(1)}, u32[]{:S(2)}, u32[]{:S(2)}) %collective-permute-start.5) | collective-permute-done | bytes 34848 | tf_op jit(solution)/shard_map/ppermute | solution.py:764
  114.1 2.4 %collective-permute-done.4.refs_2_ = f32[4,2176]{1,0:T(4,128)S(1)} collective-permute-done((f32[4,2176]{1,0:T(4,128)S(1)}, f32[4,2176]{1,0:T(4,128)S(1)}, u32[]{:S(2)}, u32[]{:S(2)}) %collective-permute-start.4) | collective-permute-done | bytes 34848 | tf_op jit(solution)/shard_map/ppermute | solution.py:764
  116.5 0.0 collective-permute-done.3.refs_1_
  116.5 0.1 shard_map.159
  116.6 1.6 %collective-permute-start.6 = (f32[1,128]{1,0:T(1,128)S(1)}, f32[1,128]{1,0:T(1,128)S(1)}, u32[]{:S(2)}, u32[]{:S(2)}) collective-permute-start(f32[1,128]{1,0:T(1,128)S(1)} %get-tuple-element.30), channel_id=1, source_target_pairs={{0,1},{1,0},{2,3},{3,2},{4,5},{5,4},{6,7},{7,6},{8,9},{9,8},{10,11... | collective-permute-start | bytes 1544 | tf_op jit(solution)/shard_map/ppermute | solution.py:764
  118.2 2.0 %collective-permute-done.6 = f32[1,128]{1,0:T(1,128)S(1)} collective-permute-done((f32[1,128]{1,0:T(1,128)S(1)}, f32[1,128]{1,0:T(1,128)S(1)}, u32[]{:S(2)}, u32[]{:S(2)}) %collective-permute-start.6) | collective-permute-done | bytes 544 | tf_op jit(solution)/shard_map/ppermute | solution.py:764
  120.2 0.0 all-to-all-done.2.lag_ref
  120.2 1.1 shard_map.160
  (2 shorter events, 0.0 us)
Async XLA Ops:
  4.2 40.5 %all-to-all-start = ((bf16[16,400,128]{2,1,0:T(8,128)(2,1)}), bf16[16,400,128]{2,1,0:T(8,128)(2,1)S(1)}, u32[]{:S(2)}, u32[]{:S(2)}) async-start(bf16[16,400,128]{2,1,0:T(8,128)(2,1)} %shard_map.153.refs_4_), calls=%async_computation | async-start | bytes 3276800 | tf_op jit(solution)/shard_map/all_to_all | solution.py:742
  11.6 3.3 %copy-start.3 = (f32[3,2048]{1,0:T(4,128)S(1)}, f32[3,2048]{1,0:T(4,128)}, u32[]{:S(2)}) copy-start(f32[3,2048]{1,0:T(4,128)} %refs_5_.3) | copy-start | bytes 73732
  11.6 3.3 %copy-start.4 = (f32[2048]{0:T(1024)S(1)}, f32[2048]{0:T(1024)}, u32[]{:S(2)}) copy-start(f32[2048]{0:T(1024)} %param.16) | copy-start | bytes 24580
  44.7 1.2 copy-start.1
  55.3 33.4 %all-to-all-start.1 = ((bf16[16,272,128]{2,1,0:T(8,128)(2,1)}), bf16[16,272,128]{2,1,0:T(8,128)(2,1)S(1)}, u32[]{:S(2)}, u32[]{:S(2)}) async-start(bf16[16,272,128]{2,1,0:T(8,128)(2,1)} %get-tuple-element.21), calls=%async_computation.1 | async-start | bytes 2228224 | tf_op jit(solution)/shard_map/all_to_all | solution.py:742
  88.7 7.2 %copy-start.2 = (bf16[16,272,128]{2,1,0:T(8,128)(2,1)}, bf16[16,272,128]{2,1,0:T(8,128)(2,1)S(1)}, u32[]{:S(2)}) copy-start(bf16[16,272,128]{2,1,0:T(8,128)(2,1)S(1)} %all-to-all-done.1.refs_7_) | copy-start | bytes 3342340
  88.7 31.6 %all-to-all-start.2 = ((bf16[16,128,128]{2,1,0:T(8,128)(2,1)}), bf16[16,128,128]{2,1,0:T(8,128)(2,1)S(1)}, u32[]{:S(2)}, u32[]{:S(2)}) async-start(bf16[16,128,128]{2,1,0:T(8,128)(2,1)} %get-tuple-element.31), calls=%async_computation.2 | async-start | bytes 1048576 | tf_op jit(solution)/shard_map/all_to_all | solution.py:742
  101.5 4.0 %collective-permute-start.2 = (f32[4,2176]{1,0:T(4,128)}, f32[4,2176]{1,0:T(4,128)S(1)}, u32[]{:S(2)}, u32[]{:S(2)}) collective-permute-start(f32[4,2176]{1,0:T(4,128)} %get-tuple-element.28.refs_0_), channel_id=1, source_target_pairs={{0,6},{2,4},{4,2},{6,0},{8,14},{10,12},{12,10},{14,8},{16,22},{18,... | collective-permute-start | bytes 104456 | tf_op jit(solution)/shard_map/ppermute | solution.py:764
  103.2 4.2 %collective-permute-start.1 = (f32[4,2176]{1,0:T(4,128)}, f32[4,2176]{1,0:T(4,128)S(1)}, u32[]{:S(2)}, u32[]{:S(2)}) collective-permute-start(f32[4,2176]{1,0:T(4,128)} %get-tuple-element.28.refs_0_), channel_id=1, source_target_pairs={{0,4},{2,6},{4,0},{6,2},{8,12},{10,14},{12,8},{14,10},{16,20},{18,... | collective-permute-start | bytes 104456 | tf_op jit(solution)/shard_map/ppermute | solution.py:764
  103.6 3.8 %collective-permute-start = (f32[4,2176]{1,0:T(4,128)}, f32[4,2176]{1,0:T(4,128)S(1)}, u32[]{:S(2)}, u32[]{:S(2)}) collective-permute-start(f32[4,2176]{1,0:T(4,128)} %get-tuple-element.28.refs_0_), channel_id=1, source_target_pairs={{0,2},{2,0},{4,6},{6,4},{8,10},{10,8},{12,14},{14,12},{16,18},{18,... | collective-permute-start | bytes 104456 | tf_op jit(solution)/shard_map/ppermute | solution.py:764
  107.4 0.8 copy-start
  108.2 5.9 %collective-permute-start.5 = (f32[4,2176]{1,0:T(4,128)S(1)}, f32[4,2176]{1,0:T(4,128)S(1)}, u32[]{:S(2)}, u32[]{:S(2)}) collective-permute-start(f32[4,2176]{1,0:T(4,128)S(1)} %shard_map.158.refs_0_), channel_id=1, source_target_pairs={{0,24},{2,26},{4,28},{6,30},{8,16},{10,18},{12,20},{14,22},{16,8},... | collective-permute-start | bytes 104456 | tf_op jit(solution)/shard_map/ppermute | solution.py:764
  111.5 4.9 %collective-permute-start.4 = (f32[4,2176]{1,0:T(4,128)S(1)}, f32[4,2176]{1,0:T(4,128)S(1)}, u32[]{:S(2)}, u32[]{:S(2)}) collective-permute-start(f32[4,2176]{1,0:T(4,128)S(1)} %shard_map.158.refs_0_), channel_id=1, source_target_pairs={{0,16},{2,18},{4,20},{6,22},{8,24},{10,26},{12,28},{14,30},{16,0},... | collective-permute-start | bytes 104456 | tf_op jit(solution)/shard_map/ppermute | solution.py:764
  112.0 4.5 %collective-permute-start.3 = (f32[4,2176]{1,0:T(4,128)S(1)}, f32[4,2176]{1,0:T(4,128)S(1)}, u32[]{:S(2)}, u32[]{:S(2)}) collective-permute-start(f32[4,2176]{1,0:T(4,128)S(1)} %shard_map.158.refs_0_), channel_id=1, source_target_pairs={{0,8},{2,10},{4,12},{6,14},{8,0},{10,2},{12,4},{14,6},{16,24},{18,... | collective-permute-start | bytes 104456 | tf_op jit(solution)/shard_map/ppermute | solution.py:764
  116.6 3.6 %collective-permute-start.6 = (f32[1,128]{1,0:T(1,128)S(1)}, f32[1,128]{1,0:T(1,128)S(1)}, u32[]{:S(2)}, u32[]{:S(2)}) collective-permute-start(f32[1,128]{1,0:T(1,128)S(1)} %get-tuple-element.30), channel_id=1, source_target_pairs={{0,1},{1,0},{2,3},{3,2},{4,5},{5,4},{6,7},{7,6},{8,9},{9,8},{10,11... | collective-permute-start | bytes 1544 | tf_op jit(solution)/shard_map/ppermute | solution.py:764

commit v10 on v9

--- a/solution.py
+++ b/solution.py
@@ -19,7 +19,8 @@
 ROWS = 32
 PASSES = 1
 TILE_ROWS = 16
-VMEM_BYTES = 60 * 1024 * 1024
+VMEM_BYTES = 24 * 1024 * 1024
+MOST_VMEM_BYTES = 60 * 1024 * 1024
 SMALL_VMEM_BYTES = 8 * 1024 * 1024
 
 f32 = jnp.float32
@@ -317,17 +318,10 @@
 
 
 def products_kernel(
-    rows_here, signals_hbm, taps_ref, coarse_ref, fine_ref, matrix_hbm, after_ref, results_hbm, lag_hbm, same_hbm,
-    signals_ref, twist_ref, matrix_ref, heads_ref, results_ref, one_split, two_split, lag_split,
+    rows_here, signals_ref, taps_ref, coarse_ref, fine_ref, matrix_hbm, after_ref, results_hbm, lag_hbm,
+    twist_ref, matrix_ref, heads_ref, results_ref, one_split, two_split, lag_split,
     filter_ref, product_ref, cotan_ref, time_ref, sems,
 ):
-    filter_rows = pl.ds(2 * rows_here, rows_here)
-    extra_rows = pl.ds(3 * rows_here, signals_ref.shape[1] - 3 * rows_here)
-    signal_rows = pl.ds(0, 2 * rows_here)
-    arrivals = [
-        pltpu.make_async_copy(signals_hbm.at[:, rows], signals_ref.at[:, rows], sems.at[idx])
-        for idx, rows in enumerate((filter_rows, extra_rows, signal_rows))
-    ]
     matrix_copy = pltpu.make_async_copy(matrix_hbm, matrix_ref, sems.at[3])
     lag_copy = pltpu.make_async_copy(lag_split, lag_hbm, sems.at[4])
     returns = [
@@ -352,13 +346,9 @@
 
         return signal_stage(from_ref, twist_ref, rows_here, write)
 
-    for copy in arrivals + [matrix_copy]:
-        copy.start()
+    matrix_copy.start()
     run_all([twist_stage(coarse_ref, fine_ref, twist_ref, rows_here)], rows_here)
-    arrivals[0].wait()
     run_all([leaves(2, one_split)], rows_here)
-    arrivals[1].wait()
-    arrivals[2].wait()
     patch_first_rows(signals_ref, heads_ref, taps_ref, rows_here)
     matrix_copy.wait()
     run_all([leaves(0, two_split)], rows_here, (matrix_ref, one_split, filter_ref))
@@ -426,20 +416,17 @@
         self.matrix_work = pltpu.VMEM(self.tables[2].shape, bf16)
 
     def products(self, signals, taps, after):
-        results, lag_split, _ = call(
-            functools.partial(products_kernel, self.signal.shape[1]),
-            (self.result, self.split, jax.ShapeDtypeStruct(signals.shape, bf16)),
-            [pltpu.VMEM(signals.shape, bf16), self.twist_work, self.matrix_work]
+        return call(
+            functools.partial(products_kernel, self.signal.shape[1]), (self.result, self.split),
+            [self.twist_work, self.matrix_work]
             + [pltpu.VMEM((2, signals.shape[0], TILE_ROWS, LANES), bf16), self.result_work]
             + [self.split_work] * 3
             + [self.work] * 4
             + [pltpu.SemaphoreType.DMA((7,))],
             signals, taps, *self.tables, after,
-            in_specs=[ANYWHERE, IN_VMEM, IN_SMEM, IN_VMEM, ANYWHERE, ANYWHERE],
-            out_specs=(ANYWHERE, ANYWHERE, ANYWHERE),
-            input_output_aliases={0: 2},
+            in_specs=[IN_VMEM, IN_VMEM, IN_SMEM, IN_VMEM, ANYWHERE, ANYWHERE],
+            out_specs=(ANYWHERE, ANYWHERE),
         )
-        return results, lag_split
 
     def lag(self, lag_split):
         return call(
@@ -564,7 +551,7 @@
             copy(place, step).wait()
 
 
-def stream_call(work, steps, per_step, operands, results, scratch=(), after=(), kept=()):
+def stream_call(work, steps, per_step, operands, results, scratch=(), after=(), kept=(), vmem_bytes=VMEM_BYTES):
     arrays = [operand[0] for operand in operands]
     shapes = [jax.ShapeDtypeStruct(array.shape, array.dtype) for array in arrays] + [result[0] for result in results]
     cuts = [entry[1] for entry in list(operands) + list(results)]
@@ -580,6 +567,7 @@
         tuple(result[0] for result in results) + tuple(kept),
         held + list(scratch) + [pltpu.SemaphoreType.DMA((len(shapes), steps))],
         *arrays, *extra,
+        vmem_bytes=vmem_bytes,
         in_specs=[ANYWHERE] * (len(arrays) + len(extra)),
         out_specs=(ANYWHERE,) * len(results) + (IN_VMEM,) * len(kept),
     )
@@ -806,6 +794,7 @@
         operands=[(x, lanes2) for x in (q_in, k_in, v_in, grad_out, kernel, short_filter)],
         results=[(sent, cut_groups(per_step))],
         scratch=exts,
+        vmem_bytes=MOST_VMEM_BYTES,
     )
     signals_here = exchange(to_pieces(signals, pieces))
     (short,) = stream(

time: 122 us -> 127 us (1.041)
  local copies, waits for them, and re-layouts: 1.99 us -> 14.8 us
  Pallas kernels: 27.5 us -> 23.3 us
  waiting for transfers between devices: 58.4 us -> 54.6 us
    unnamed x10 -> x36, local copies, waits for them, and re-layouts: 1.99 us -> 14.8 us
    pallas_call x8, Pallas kernels: 27.5 us -> 23.3 us  [call(): pl.pallas_call(kernel, out_shape=outs, scratch_shapes=scratch, compiler_p...]
    all_to_all x3, waiting for transfers between devices: 48.7 us -> 45.3 us  [exchange(): lax.all_to_all(pieces_first, 'ctx', split_axis=0, concat_axis=0, tiled=True)]
  transfers between devices with their start and end apart: 10 -> 10, of which waited for: 7 -> 7; matrix products, arithmetic and copies ran while one was open for 1% -> 0% of each run, Pallas kernels for 11% -> 7%
where the time goes in v10:
time: 127 us; the launch traced here: 126 us
  waiting for transfers between devices  54.6 us (43%)
  starting transfers between devices  32.2 us (25%)
  Pallas kernels  23.3 us (18%)
  local copies, waits for them, and re-layouts  14.8 us (12%)
    all_to_all x3, waiting for transfers between devices, exchange(): lax.all_to_all(pieces_first, 'ctx', split_axis=0, concat_axis=0, tiled=True)  45.3 us
    all_to_all x3, starting transfers between devices, exchange(): lax.all_to_all(pieces_first, 'ctx', split_axis=0, concat_axis=0, tiled=True)  24.1 us
    pallas_call x8, Pallas kernels, call(): pl.pallas_call(kernel, out_shape=outs, scratch_shapes=scratch, compiler_p...  23.3 us
    unnamed x36, local copies, waits for them, and re-layouts  14.8 us
    ppermute x7, waiting for transfers between devices, partners(): lax.ppermute(value, axis, [(i, i ^ step) for i in range(size)])  9.31 us
    ppermute x7, starting transfers between devices, partners(): lax.ppermute(value, axis, [(i, i ^ step) for i in range(size)])  8.11 us
  transfers between devices with their start and end apart: 10, of which 7 were waited for; matrix products, arithmetic and copies ran while one was open for 0% of the time, Pallas kernels for 7%

profile of v10, /device:TPU:0, one launch (start us, length us, event | category | flops | bytes accessed | tf_op | source)
XLA Modules:
  0.0 125.7 jit_solution(4808380706721097598)
XLA Ops:
  0.6 3.6 %shard_map.153.refs_4_ = bf16[16,400,128]{2,1,0:T(8,128)(2,1)} custom-call(bf16[128,2048]{1,0:T(8,128)(2,1)} %refs_0_.5, bf16[128,2048]{1,0:T(8,128)(2,1)} %refs_1_.5, bf16[128,2048]{1,0:T(8,128)(2,1)} %refs_2_.5, bf16[128,2048]{1,0:T(8,128)(2,1)} %refs_3_.5, f32[128,2048]{1,0:T(8,128)} %refs_4_.1, f32[3,2048]{1,0:T(4,128)} %refs_5_.3), custom_call_target="tpu_custom_call" | custom-call | tf_op jit(solution)/shard_map/pallas_call | solution.py:35
  4.2 0.0 copy-start.13
  4.3 7.4 %all-to-all-start = ((bf16[16,400,128]{2,1,0:T(8,128)(2,1)}), bf16[16,400,128]{2,1,0:T(8,128)(2,1)}, u32[]{:S(2)}, u32[]{:S(2)}) async-start(bf16[16,400,128]{2,1,0:T(8,128)(2,1)} %shard_map.153.refs_4_), calls=%async_computation | async-start | bytes 3276800 | tf_op jit(solution)/shard_map/all_to_all | solution.py:730
  11.7 0.0 copy-done.13
  11.7 0.0 copy-start
  11.7 1.4 %copy-done = bf16[16,400,128]{2,1,0:T(8,128)(2,1)S(1)} copy-done((bf16[16,400,128]{2,1,0:T(8,128)(2,1)S(1)}, bf16[16,400,128]{2,1,0:T(8,128)(2,1)}, u32[]{:S(2)}) %copy-start) | copy-done | bytes 1638424
  13.2 0.0 copy-start.1
  13.2 1.0 copy-done.1
  14.2 0.0 copy-start.3
  14.2 1.0 copy-done.3
  15.2 0.0 copy-start.5
  15.2 1.0 copy-done.5
  16.3 0.0 copy-start.17
  16.3 0.0 copy-start.15
  16.3 0.0 copy-start.16
  16.3 1.9 %shard_map.154.after_ref.refs_4_ = f32[3,128,2048]{2,1,0:T(8,128)S(1)} custom-call(bf16[128,2048]{1,0:T(8,128)(2,1)S(1)} %copy-done.1, bf16[128,2048]{1,0:T(8,128)(2,1)S(1)} %copy-done.3, bf16[128,2048]{1,0:T(8,128)(2,1)S(1)} %copy-done.5, f32[3,2048]{1,0:T(4,128)S(1)} %copy-done.13, bf16[16,400,128]{2,1,0:T(8,128)(2,1)S(1)} %copy-done), custom_call_target="tpu_custom_call" | custom-call | tf_op jit(solution)/shard_map/pallas_call | solution.py:35
  18.2 0.0 copy-done.17
  18.2 0.1 fusion.taps_ref
  18.3 26.6 %all-to-all-done.signals_ref = bf16[16,400,128]{2,1,0:T(8,128)(2,1)} async-done(((bf16[16,400,128]{2,1,0:T(8,128)(2,1)}), bf16[16,400,128]{2,1,0:T(8,128)(2,1)}, u32[]{:S(2)}, u32[]{:S(2)}) %all-to-all-start) | async-done | bytes 1638432 | tf_op jit(solution)/shard_map/all_to_all | solution.py:730
  44.9 0.0 copy-done.15
  44.9 0.0 copy-done.16
  44.9 0.0 copy-start.8
  44.9 1.0 copy-done.8
  45.9 8.5 %shard_map.155 = (bf16[16,272,128]{2,1,0:T(8,128)(2,1)S(1)}, bf16[4,512,256]{2,1,0:T(8,128)(2,1)S(1)}) custom-call(bf16[16,400,128]{2,1,0:T(8,128)(2,1)} %all-to-all-done.signals_ref, f32[4,128]{1,0:T(4,128)S(1)} %fusion.taps_ref, f32[16,16]{1,0:T(8,128)S(1)} %copy-done.16, f32[2,8,16,128]{3,2,1,0:T(8,128)S(1)} %copy-done.15, ...), custom_call_target="tpu_custom_call" | custom-call | tf_op jit(solution)/shard_map/pallas_call | solution.py:35
  54.4 0.0 copy-start.10
  54.4 1.0 copy-done.10
  55.4 0.0 copy-start.11
  55.4 1.0 copy-done.11
  56.4 9.4 %all-to-all-start.1 = ((bf16[16,272,128]{2,1,0:T(8,128)(2,1)}), bf16[16,272,128]{2,1,0:T(8,128)(2,1)}, u32[]{:S(2)}, u32[]{:S(2)}) async-start(bf16[16,272,128]{2,1,0:T(8,128)(2,1)} %copy-done.10), calls=%async_computation.1 | async-start | bytes 2228224 | tf_op jit(solution)/shard_map/all_to_all | solution.py:730
  65.8 0.0 copy-start.9
  65.8 1.0 copy-done.9
  66.8 0.0 copy-start.12
  66.8 1.2 copy-done.12
  68.1 2.3 %shard_map.156 = (bf16[16,128,128]{2,1,0:T(8,128)(2,1)S(1)}, f32[1,128]{1,0:T(1,128)S(1)}) custom-call(bf16[4,512,256]{2,1,0:T(8,128)(2,1)S(1)} %copy-done.12, f32[16,16]{1,0:T(8,128)S(1)} %copy-done.16, f32[2,8,16,128]{3,2,1,0:T(8,128)S(1)} %copy-done.15, bf16[512,512]{1,0:T(8,128)(2,1)S(1)} %copy-done.9), custom_call_target="tpu_custom_call" | custom-call | tf_op jit(solution)/shard_map/pallas_call | solution.py:35
  70.4 0.0 copy-start.14
  70.4 0.8 copy-done.14
  71.2 18.7 %all-to-all-done.1.refs_7_ = bf16[16,272,128]{2,1,0:T(8,128)(2,1)} async-done(((bf16[16,272,128]{2,1,0:T(8,128)(2,1)}), bf16[16,272,128]{2,1,0:T(8,128)(2,1)}, u32[]{:S(2)}, u32[]{:S(2)}) %all-to-all-start.1) | async-done | bytes 1114144 | tf_op jit(solution)/shard_map/all_to_all | solution.py:730
  89.9 7.2 %all-to-all-start.2 = ((bf16[16,128,128]{2,1,0:T(8,128)(2,1)}), bf16[16,128,128]{2,1,0:T(8,128)(2,1)}, u32[]{:S(2)}, u32[]{:S(2)}) async-start(bf16[16,128,128]{2,1,0:T(8,128)(2,1)} %copy-done.14), calls=%async_computation.2 | async-start | bytes 1048576 | tf_op jit(solution)/shard_map/all_to_all | solution.py:730
  97.1 0.0 copy-start.2
  97.1 1.0 copy-done.2
  98.2 0.0 copy-start.4
  98.2 1.0 copy-done.4
  99.2 0.0 copy-start.6
  99.2 1.0 copy-done.6
  100.3 0.0 copy-start.7
  100.3 1.0 copy-done.7
  101.3 4.7 %shard_map.157 = (bf16[128,2048]{1,0:T(8,128)(2,1)}, bf16[128,2048]{1,0:T(8,128)(2,1)}, bf16[128,2048]{1,0:T(8,128)(2,1)}, bf16[128,2048]{1,0:T(8,128)(2,1)}, f32[4,2176]{1,0:T(4,128)S(1)}) custom-call(bf16[128,2048]{1,0:T(8,128)(2,1)S(1)} %copy-done.2, bf16[128,2048]{1,0:T(8,128)(2,1)S(1)} %copy-done.4, bf16[128,2048]{1,0:T(8,128)(2,1)S(1)} %copy-done.6, ...), custom_call_target="tpu_custom_call" | custom-call | tf_op jit(solution)/shard_map/pallas_call | solution.py:35
  106.0 1.7 %collective-permute-start.2 = (f32[4,2176]{1,0:T(4,128)S(1)}, f32[4,2176]{1,0:T(4,128)S(1)}, u32[]{:S(2)}, u32[]{:S(2)}) collective-permute-start(f32[4,2176]{1,0:T(4,128)S(1)} %get-tuple-element.28.refs_0_), channel_id=1, source_target_pairs={{0,6},{2,4},{4,2},{6,0},{8,14},{10,12},{12,10},{14,8},{16,22},{18,... | collective-permute-start | bytes 104456 | tf_op jit(solution)/shard_map/ppermute | solution.py:752
  107.7 0.4 collective-permute-start.1
  108.0 0.0 collective-permute-start
  108.0 1.7 %collective-permute-done.2.refs_3_ = f32[4,2176]{1,0:T(4,128)S(1)} collective-permute-done((f32[4,2176]{1,0:T(4,128)S(1)}, f32[4,2176]{1,0:T(4,128)S(1)}, u32[]{:S(2)}, u32[]{:S(2)}) %collective-permute-start.2) | collective-permute-done | bytes 34848 | tf_op jit(solution)/shard_map/ppermute | solution.py:752
  109.7 2.4 %collective-permute-done.1.refs_2_ = f32[4,2176]{1,0:T(4,128)S(1)} collective-permute-done((f32[4,2176]{1,0:T(4,128)S(1)}, f32[4,2176]{1,0:T(4,128)S(1)}, u32[]{:S(2)}, u32[]{:S(2)}) %collective-permute-start.1) | collective-permute-done | bytes 34848 | tf_op jit(solution)/shard_map/ppermute | solution.py:752
  112.1 0.0 collective-permute-done.refs_1_
  112.1 2.8 %collective-permute-start.5 = (f32[4,2176]{1,0:T(4,128)S(1)}, f32[4,2176]{1,0:T(4,128)S(1)}, u32[]{:S(2)}, u32[]{:S(2)}) collective-permute-start(f32[4,2176]{1,0:T(4,128)S(1)} %shard_map.158.refs_0_), channel_id=1, source_target_pairs={{0,24},{2,26},{4,28},{6,30},{8,16},{10,18},{12,20},{14,22},{16,8},... | collective-permute-start | bytes 104456 | tf_op jit(solution)/shard_map/ppermute | solution.py:752
  115.0 0.0 collective-permute-start.4
  115.0 1.6 %collective-permute-start.3 = (f32[4,2176]{1,0:T(4,128)S(1)}, f32[4,2176]{1,0:T(4,128)S(1)}, u32[]{:S(2)}, u32[]{:S(2)}) collective-permute-start(f32[4,2176]{1,0:T(4,128)S(1)} %shard_map.158.refs_0_), channel_id=1, source_target_pairs={{0,8},{2,10},{4,12},{6,14},{8,0},{10,2},{12,4},{14,6},{16,24},{18,... | collective-permute-start | bytes 104456 | tf_op jit(solution)/shard_map/ppermute | solution.py:752
  116.6 1.5 %collective-permute-done.5.refs_3_ = f32[4,2176]{1,0:T(4,128)S(1)} collective-permute-done((f32[4,2176]{1,0:T(4,128)S(1)}, f32[4,2176]{1,0:T(4,128)S(1)}, u32[]{:S(2)}, u32[]{:S(2)}) %collective-permute-start.5) | collective-permute-done | bytes 34848 | tf_op jit(solution)/shard_map/ppermute | solution.py:752
  118.1 1.7 %collective-permute-done.4.refs_2_ = f32[4,2176]{1,0:T(4,128)S(1)} collective-permute-done((f32[4,2176]{1,0:T(4,128)S(1)}, f32[4,2176]{1,0:T(4,128)S(1)}, u32[]{:S(2)}, u32[]{:S(2)}) %collective-permute-start.4) | collective-permute-done | bytes 34848 | tf_op jit(solution)/shard_map/ppermute | solution.py:752
  119.8 0.0 collective-permute-done.3.refs_1_
  119.8 0.1 shard_map.159
  120.0 1.6 %collective-permute-start.6 = (f32[1,128]{1,0:T(1,128)S(1)}, f32[1,128]{1,0:T(1,128)S(1)}, u32[]{:S(2)}, u32[]{:S(2)}) collective-permute-start(f32[1,128]{1,0:T(1,128)S(1)} %get-tuple-element.30), channel_id=1, source_target_pairs={{0,1},{1,0},{2,3},{3,2},{4,5},{5,4},{6,7},{7,6},{8,9},{9,8},{10,11... | collective-permute-start | bytes 1544 | tf_op jit(solution)/shard_map/ppermute | solution.py:752
  121.6 2.0 %collective-permute-done.6 = f32[1,128]{1,0:T(1,128)S(1)} collective-permute-done((f32[1,128]{1,0:T(1,128)S(1)}, f32[1,128]{1,0:T(1,128)S(1)}, u32[]{:S(2)}, u32[]{:S(2)}) %collective-permute-start.6) | collective-permute-done | bytes 544 | tf_op jit(solution)/shard_map/ppermute | solution.py:752
  123.6 0.0 all-to-all-done.2.lag_ref
  123.6 2.2 %shard_map.160 = (f32[3,2048]{1,0:T(4,128)}, f32[1,2048]{1,0:T(1,128)}, f32[128,2048]{1,0:T(8,128)}) custom-call(f32[4,2176]{1,0:T(4,128)S(1)} %get-tuple-element.29.totals_ref, f32[1,128]{1,0:T(1,128)S(1)} %add.7.norm_ref, bf16[16,128,128]{2,1,0:T(8,128)(2,1)} %all-to-all-done.2.lag_ref), custom_call_target="tpu_custom_call" | custom-call | tf_op jit(solution)/shard_map/pallas_call | solution.py:35
  (2 shorter events, 0.0 us)
Async XLA Ops:
  4.2 7.4 %copy-start.13 = (f32[3,2048]{1,0:T(4,128)S(1)}, f32[3,2048]{1,0:T(4,128)}, u32[]{:S(2)}) copy-start(f32[3,2048]{1,0:T(4,128)} %refs_5_.3) | copy-start | bytes 73732
  4.3 40.6 %all-to-all-start = ((bf16[16,400,128]{2,1,0:T(8,128)(2,1)}), bf16[16,400,128]{2,1,0:T(8,128)(2,1)}, u32[]{:S(2)}, u32[]{:S(2)}) async-start(bf16[16,400,128]{2,1,0:T(8,128)(2,1)} %shard_map.153.refs_4_), calls=%async_computation | async-start | bytes 3276800 | tf_op jit(solution)/shard_map/all_to_all | solution.py:730
  11.7 1.5 %copy-start = (bf16[16,400,128]{2,1,0:T(8,128)(2,1)S(1)}, bf16[16,400,128]{2,1,0:T(8,128)(2,1)}, u32[]{:S(2)}) copy-start(bf16[16,400,128]{2,1,0:T(8,128)(2,1)} %shard_map.153.refs_4_) | copy-start | bytes 4915204
  13.2 1.0 copy-start.1
  14.2 1.0 copy-start.3
  15.2 1.0 copy-start.5
  16.3 1.9 %copy-start.17 = (f32[2048]{0:T(1024)S(1)}, f32[2048]{0:T(1024)}, u32[]{:S(2)}) copy-start(f32[2048]{0:T(1024)} %param.16) | copy-start | bytes 24580
  16.3 28.6 %copy-start.15 = (f32[2,8,16,128]{3,2,1,0:T(8,128)S(1)}, f32[2,8,16,128]{3,2,1,0:T(8,128)}, u32[]{:S(2)}) copy-start(f32[2,8,16,128]{3,2,1,0:T(8,128)} %constant.19.clone.fine_ref) | copy-start | bytes 393220
  16.3 28.6 %copy-start.16 = (f32[16,16]{1,0:T(8,128)S(1)}, f32[16,16]{1,0:T(8,128)}, u32[]{:S(2)}) copy-start(f32[16,16]{1,0:T(8,128)} %constant.18.clone.coarse_ref) | copy-start | bytes 3076
  44.9 1.0 copy-start.8
  54.4 1.0 copy-start.10
  55.4 1.0 copy-start.11
  56.4 33.5 %all-to-all-start.1 = ((bf16[16,272,128]{2,1,0:T(8,128)(2,1)}), bf16[16,272,128]{2,1,0:T(8,128)(2,1)}, u32[]{:S(2)}, u32[]{:S(2)}) async-start(bf16[16,272,128]{2,1,0:T(8,128)(2,1)} %copy-done.10), calls=%async_computation.1 | async-start | bytes 2228224 | tf_op jit(solution)/shard_map/all_to_all | solution.py:730
  65.8 1.0 copy-start.9
  66.8 1.2 copy-start.12
  70.4 0.8 copy-start.14
  89.9 33.7 %all-to-all-start.2 = ((bf16[16,128,128]{2,1,0:T(8,128)(2,1)}), bf16[16,128,128]{2,1,0:T(8,128)(2,1)}, u32[]{:S(2)}, u32[]{:S(2)}) async-start(bf16[16,128,128]{2,1,0:T(8,128)(2,1)} %copy-done.14), calls=%async_computation.2 | async-start | bytes 1048576 | tf_op jit(solution)/shard_map/all_to_all | solution.py:730
  97.1 1.0 copy-start.2
  98.2 1.0 copy-start.4
  99.2 1.0 copy-start.6
  100.3 1.0 copy-start.7
  106.0 3.7 %collective-permute-start.2 = (f32[4,2176]{1,0:T(4,128)S(1)}, f32[4,2176]{1,0:T(4,128)S(1)}, u32[]{:S(2)}, u32[]{:S(2)}) collective-permute-start(f32[4,2176]{1,0:T(4,128)S(1)} %get-tuple-element.28.refs_0_), channel_id=1, source_target_pairs={{0,6},{2,4},{4,2},{6,0},{8,14},{10,12},{12,10},{14,8},{16,22},{18,... | collective-permute-start | bytes 104456 | tf_op jit(solution)/shard_map/ppermute | solution.py:752
  107.7 4.5 %collective-permute-start.1 = (f32[4,2176]{1,0:T(4,128)S(1)}, f32[4,2176]{1,0:T(4,128)S(1)}, u32[]{:S(2)}, u32[]{:S(2)}) collective-permute-start(f32[4,2176]{1,0:T(4,128)S(1)} %get-tuple-element.28.refs_0_), channel_id=1, source_target_pairs={{0,4},{2,6},{4,0},{6,2},{8,12},{10,14},{12,8},{14,10},{16,20},{18,... | collective-permute-start | bytes 104456 | tf_op jit(solution)/shard_map/ppermute | solution.py:752
  108.0 4.1 %collective-permute-start = (f32[4,2176]{1,0:T(4,128)S(1)}, f32[4,2176]{1,0:T(4,128)S(1)}, u32[]{:S(2)}, u32[]{:S(2)}) collective-permute-start(f32[4,2176]{1,0:T(4,128)S(1)} %get-tuple-element.28.refs_0_), channel_id=1, source_target_pairs={{0,2},{2,0},{4,6},{6,4},{8,10},{10,8},{12,14},{14,12},{16,18},{18,... | collective-permute-start | bytes 104456 | tf_op jit(solution)/shard_map/ppermute | solution.py:752
  112.1 6.0 %collective-permute-start.5 = (f32[4,2176]{1,0:T(4,128)S(1)}, f32[4,2176]{1,0:T(4,128)S(1)}, u32[]{:S(2)}, u32[]{:S(2)}) collective-permute-start(f32[4,2176]{1,0:T(4,128)S(1)} %shard_map.158.refs_0_), channel_id=1, source_target_pairs={{0,24},{2,26},{4,28},{6,30},{8,16},{10,18},{12,20},{14,22},{16,8},... | collective-permute-start | bytes 104456 | tf_op jit(solution)/shard_map/ppermute | solution.py:752
  115.0 4.8 %collective-permute-start.4 = (f32[4,2176]{1,0:T(4,128)S(1)}, f32[4,2176]{1,0:T(4,128)S(1)}, u32[]{:S(2)}, u32[]{:S(2)}) collective-permute-start(f32[4,2176]{1,0:T(4,128)S(1)} %shard_map.158.refs_0_), channel_id=1, source_target_pairs={{0,16},{2,18},{4,20},{6,22},{8,24},{10,26},{12,28},{14,30},{16,0},... | collective-permute-start | bytes 104456 | tf_op jit(solution)/shard_map/ppermute | solution.py:752
  115.0 4.8 %collective-permute-start.3 = (f32[4,2176]{1,0:T(4,128)S(1)}, f32[4,2176]{1,0:T(4,128)S(1)}, u32[]{:S(2)}, u32[]{:S(2)}) collective-permute-start(f32[4,2176]{1,0:T(4,128)S(1)} %shard_map.158.refs_0_), channel_id=1, source_target_pairs={{0,8},{2,10},{4,12},{6,14},{8,0},{10,2},{12,4},{14,6},{16,24},{18,... | collective-permute-start | bytes 104456 | tf_op jit(solution)/shard_map/ppermute | solution.py:752
  120.0 3.6 %collective-permute-start.6 = (f32[1,128]{1,0:T(1,128)S(1)}, f32[1,128]{1,0:T(1,128)S(1)}, u32[]{:S(2)}, u32[]{:S(2)}) collective-permute-start(f32[1,128]{1,0:T(1,128)S(1)} %get-tuple-element.30), channel_id=1, source_target_pairs={{0,1},{1,0},{2,3},{3,2},{4,5},{5,4},{6,7},{7,6},{8,9},{9,8},{10,11... | collective-permute-start | bytes 1544 | tf_op jit(solution)/shard_map/ppermute | solution.py:752

commit v11 on v9

--- a/solution.py
+++ b/solution.py
@@ -20,6 +20,7 @@
 PASSES = 1
 TILE_ROWS = 16
 VMEM_BYTES = 60 * 1024 * 1024
+MOST_VMEM_BYTES = 251 * 256 * 1024
 SMALL_VMEM_BYTES = 8 * 1024 * 1024
 
 f32 = jnp.float32
@@ -317,7 +318,7 @@
 
 
 def products_kernel(
-    rows_here, signals_hbm, taps_ref, coarse_ref, fine_ref, matrix_hbm, after_ref, results_hbm, lag_hbm, same_hbm,
+    rows_here, signals_hbm, taps_ref, coarse_ref, fine_ref, matrix_hbm, after_ref, results_hbm, lag_hbm,
     signals_ref, twist_ref, matrix_ref, heads_ref, results_ref, one_split, two_split, lag_split,
     filter_ref, product_ref, cotan_ref, time_ref, sems,
 ):
@@ -426,20 +427,18 @@
         self.matrix_work = pltpu.VMEM(self.tables[2].shape, bf16)
 
     def products(self, signals, taps, after):
-        results, lag_split, _ = call(
-            functools.partial(products_kernel, self.signal.shape[1]),
-            (self.result, self.split, jax.ShapeDtypeStruct(signals.shape, bf16)),
+        return call(
+            functools.partial(products_kernel, self.signal.shape[1]), (self.result, self.split),
             [pltpu.VMEM(signals.shape, bf16), self.twist_work, self.matrix_work]
             + [pltpu.VMEM((2, signals.shape[0], TILE_ROWS, LANES), bf16), self.result_work]
             + [self.split_work] * 3
             + [self.work] * 4
             + [pltpu.SemaphoreType.DMA((7,))],
             signals, taps, *self.tables, after,
+            vmem_bytes=MOST_VMEM_BYTES,
             in_specs=[ANYWHERE, IN_VMEM, IN_SMEM, IN_VMEM, ANYWHERE, ANYWHERE],
-            out_specs=(ANYWHERE, ANYWHERE, ANYWHERE),
-            input_output_aliases={0: 2},
+            out_specs=(ANYWHERE, ANYWHERE),
         )
-        return results, lag_split
 
     def lag(self, lag_split):
         return call(
@@ -525,7 +524,7 @@
 
 
 def group(idx):
-    return pl.ds(pl.multiple_of(idx * LANES, LANES), LANES)
+    return slice(idx * LANES, (idx + 1) * LANES)
 
 
 def streamed(work, steps, per_step, places, in_count, out_count, kept, *refs):
@@ -551,12 +550,9 @@
     for step in range(steps):
         for arrival in arrivals(step):
             arrival.wait()
-
-        def one(idx, carry):
-            work(idx, held[:in_count], held[in_count:] + kept_refs, scratch)
-            return carry
-
-        lax.fori_loop(step * per_step, (step + 1) * per_step, one, 0)
+        for idx in range(step * per_step, (step + 1) * per_step):
+            exts = scratch[idx % 2 :: 2]
+            work(idx, held[:in_count], held[in_count:] + kept_refs, exts)
         for place in range(in_count, moved):
             copy(place, step).start()
     for step in range(steps):
@@ -564,7 +560,7 @@
             copy(place, step).wait()
 
 
-def stream_call(work, steps, per_step, operands, results, scratch=(), after=(), kept=()):
+def stream_call(work, steps, per_step, operands, results, scratch=(), after=(), kept=(), vmem_bytes=VMEM_BYTES):
     arrays = [operand[0] for operand in operands]
     shapes = [jax.ShapeDtypeStruct(array.shape, array.dtype) for array in arrays] + [result[0] for result in results]
     cuts = [entry[1] for entry in list(operands) + list(results)]
@@ -580,6 +576,7 @@
         tuple(result[0] for result in results) + tuple(kept),
         held + list(scratch) + [pltpu.SemaphoreType.DMA((len(shapes), steps))],
         *arrays, *extra,
+        vmem_bytes=vmem_bytes,
         in_specs=[ANYWHERE] * (len(arrays) + len(extra)),
         out_specs=(ANYWHERE,) * len(results) + (IN_VMEM,) * len(kept),
     )
@@ -706,9 +703,10 @@
                 grad = term if grad is None else grad + term
                 sums[shift_idx] = sums[shift_idx] + fold(ahead * signal)
             out_ref[rows, lanes] = grad.astype(bf16)
-    extra = slice(sums_ref.shape[1] - LANES, sums_ref.shape[1])
-    sums_ref[:, extra] = jnp.zeros((taps_count + 1, LANES), f32)
-    sums_ref[0:1, extra] = squares_ref[...]
+    if idx == 0:
+        extra = slice(sums_ref.shape[1] - LANES, sums_ref.shape[1])
+        sums_ref[:, extra] = jnp.zeros((taps_count + 1, LANES), f32)
+        sums_ref[0:1, extra] = squares_ref[...]
     for shift_idx in range(taps_count + 1):
         sums_ref[shift_idx : shift_idx + 1, lanes] = jnp.sum(sums[shift_idx], axis=0, keepdims=True)
 
@@ -724,8 +722,12 @@
     square_ref[...] = jnp.full(square_ref.shape, square)
 
 
-def add_kernel(*refs):
-    refs[-1][...] = add_up([ref[...] for ref in refs[:-1]])
+def add_kernel(own_hbm, *refs):
+    *others, total_ref, own_ref, sem = refs
+    own_copy = pltpu.make_async_copy(own_hbm, own_ref, sem)
+    own_copy.start()
+    own_copy.wait()
+    total_ref[...] = add_up([own_ref[...]] + [ref[...] for ref in others])
 
 
 def scale_kernel(limit, totals_ref, norm_ref, lag_ref, taps_out, skip_out, kernel_out):
@@ -799,13 +801,14 @@
     flat = jax.ShapeDtypeStruct((rows_here, channels), bf16)
     extra_rows = -(-7 * halo_rows // TILE_ROWS) * TILE_ROWS
     sent = jax.ShapeDtypeStruct((groups, 3 * rows_here + extra_rows, LANES), bf16)
-    exts = [pltpu.VMEM((rows_here + PAD, LANES), f32)] * 3
+    exts = [pltpu.VMEM((rows_here + PAD, LANES), f32)] * 6
 
     (signals,) = stream(
         signals_work,
         operands=[(x, lanes2) for x in (q_in, k_in, v_in, grad_out, kernel, short_filter)],
         results=[(sent, cut_groups(per_step))],
         scratch=exts,
+        vmem_bytes=MOST_VMEM_BYTES,
     )
     signals_here = exchange(to_pieces(signals, pieces))
     (short,) = stream(
@@ -837,8 +840,10 @@
     for steps_of in rounds[:-1]:
         values = partners(totals, "ctx", steps_of)
         totals = call(
-            add_kernel, jax.ShapeDtypeStruct(totals.shape, f32), [], *values,
-            vmem_bytes=SMALL_VMEM_BYTES, in_specs=[IN_VMEM] * len(values), out_specs=IN_VMEM,
+            add_kernel, jax.ShapeDtypeStruct(totals.shape, f32),
+            [pltpu.VMEM(totals.shape, f32), pltpu.SemaphoreType.DMA], *values,
+            vmem_bytes=SMALL_VMEM_BYTES,
+            in_specs=[ANYWHERE] + [IN_VMEM] * (len(values) - 1), out_specs=IN_VMEM,
         )
     last = partners(totals, "ctx", rounds[-1])
     if len(last) == 2:

time: 122 us -> 121 us (level)
  no operation moved by 1% of the time
where the time goes in v11:
time: 121 us; the launch traced here: 120 us
  waiting for transfers between devices  58.4 us (48%)
  starting transfers between devices  32.2 us (27%)
  Pallas kernels  27.4 us (23%)
    all_to_all x3, waiting for transfers between devices, exchange(): lax.all_to_all(pieces_first, 'ctx', split_axis=0, concat_axis=0, tiled=True)  48.7 us
    pallas_call x8, Pallas kernels, call(): pl.pallas_call(kernel, out_shape=outs, scratch_shapes=scratch, compiler_p...  27.4 us
    all_to_all x3, starting transfers between devices, exchange(): lax.all_to_all(pieces_first, 'ctx', split_axis=0, concat_axis=0, tiled=True)  24 us
    ppermute x7, waiting for transfers between devices, partners(): lax.ppermute(value, axis, [(i, i ^ step) for i in range(size)])  9.7 us
    ppermute x7, starting transfers between devices, partners(): lax.ppermute(value, axis, [(i, i ^ step) for i in range(size)])  8.16 us
  transfers between devices with their start and end apart: 10, of which 7 were waited for; matrix products, arithmetic and copies ran while one was open for 1% of the time, Pallas kernels for 11%

profile of v11, /device:TPU:0, one launch (start us, length us, event | category | flops | bytes accessed | tf_op | source)
XLA Modules:
  0.0 120.2 jit_solution(157517924715626086)
XLA Ops:
  0.6 3.6 %shard_map.153.refs_4_ = bf16[16,400,128]{2,1,0:T(8,128)(2,1)} custom-call(bf16[128,2048]{1,0:T(8,128)(2,1)} %refs_0_.5, bf16[128,2048]{1,0:T(8,128)(2,1)} %refs_1_.5, bf16[128,2048]{1,0:T(8,128)(2,1)} %refs_2_.5, bf16[128,2048]{1,0:T(8,128)(2,1)} %refs_3_.5, f32[128,2048]{1,0:T(8,128)} %refs_4_.1, f32[3,2048]{1,0:T(4,128)} %refs_5_.3), custom_call_target="tpu_custom_call" | custom-call | tf_op jit(solution)/shard_map/pallas_call | solution.py:35
  4.2 7.4 %all-to-all-start = ((bf16[16,400,128]{2,1,0:T(8,128)(2,1)}), bf16[16,400,128]{2,1,0:T(8,128)(2,1)}, u32[]{:S(2)}, u32[]{:S(2)}) async-start(bf16[16,400,128]{2,1,0:T(8,128)(2,1)} %shard_map.153.refs_4_), calls=%async_computation | async-start | bytes 3276800 | tf_op jit(solution)/shard_map/all_to_all | solution.py:744
  11.7 0.0 copy-start.2
  11.7 0.0 copy-start.3
  11.7 3.4 %shard_map.154.after_ref.refs_4_ = f32[3,128,2048]{2,1,0:T(8,128)} custom-call(bf16[128,2048]{1,0:T(8,128)(2,1)} %refs_0_.5, bf16[128,2048]{1,0:T(8,128)(2,1)} %refs_1_.5, bf16[128,2048]{1,0:T(8,128)(2,1)} %refs_2_.5, f32[3,2048]{1,0:T(4,128)} %refs_5_.3, bf16[16,400,128]{2,1,0:T(8,128)(2,1)} %shard_map.153.refs_4_), custom_call_target="tpu_custom_call" | custom-call | tf_op jit(solution)/shard_map/pallas_call | solution.py:35
  15.1 0.0 copy-done.2
  15.1 0.0 copy-done.3
  15.1 0.7 fusion.taps_ref
  15.7 29.1 %all-to-all-done.signals_hbm = bf16[16,400,128]{2,1,0:T(8,128)(2,1)} async-done(((bf16[16,400,128]{2,1,0:T(8,128)(2,1)}), bf16[16,400,128]{2,1,0:T(8,128)(2,1)}, u32[]{:S(2)}, u32[]{:S(2)}) %all-to-all-start) | async-done | bytes 1638432 | tf_op jit(solution)/shard_map/all_to_all | solution.py:744
  44.8 9.3 %shard_map.155 = (bf16[16,272,128]{2,1,0:T(8,128)(2,1)}, bf16[4,512,256]{2,1,0:T(8,128)(2,1)}) custom-call(bf16[16,400,128]{2,1,0:T(8,128)(2,1)} %all-to-all-done.signals_hbm, f32[4,128]{1,0:T(4,128)} %fusion.taps_ref, f32[16,16]{1,0:T(8,128)} %constant.18.clone.coarse_ref, f32[2,8,16,128]{3,2,1,0:T(8,128)} %constant.19.clone.fine_ref, ...), custom_call_target="tpu_custom_call" | custom-call | tf_op jit(solution)/shard_map/pallas_call | solution.py:35
  54.1 9.4 %all-to-all-start.1 = ((bf16[16,272,128]{2,1,0:T(8,128)(2,1)}), bf16[16,272,128]{2,1,0:T(8,128)(2,1)S(1)}, u32[]{:S(2)}, u32[]{:S(2)}) async-start(bf16[16,272,128]{2,1,0:T(8,128)(2,1)} %get-tuple-element.21), calls=%async_computation.1 | async-start | bytes 2228224 | tf_op jit(solution)/shard_map/all_to_all | solution.py:744
  63.5 4.4 %shard_map.156 = (bf16[16,128,128]{2,1,0:T(8,128)(2,1)}, f32[1,128]{1,0:T(1,128)}) custom-call(bf16[4,512,256]{2,1,0:T(8,128)(2,1)} %get-tuple-element.22.split_hbm, f32[16,16]{1,0:T(8,128)} %constant.18.clone.coarse_ref, f32[2,8,16,128]{3,2,1,0:T(8,128)} %constant.19.clone.fine_ref, bf16[512,512]{1,0:T(8,128)(2,1)} %constant.20.clone.matrix_hbm), custom_call_target="tpu_custom_call" | custom-call | tf_op jit(solution)/shard_map/pallas_call | solution.py:35
  67.9 19.6 %all-to-all-done.1.refs_7_ = bf16[16,272,128]{2,1,0:T(8,128)(2,1)S(1)} async-done(((bf16[16,272,128]{2,1,0:T(8,128)(2,1)}), bf16[16,272,128]{2,1,0:T(8,128)(2,1)S(1)}, u32[]{:S(2)}, u32[]{:S(2)}) %all-to-all-start.1) | async-done | bytes 1114144 | tf_op jit(solution)/shard_map/all_to_all | solution.py:744
  87.6 0.0 copy-start.1
  87.6 7.2 %all-to-all-start.2 = ((bf16[16,128,128]{2,1,0:T(8,128)(2,1)}), bf16[16,128,128]{2,1,0:T(8,128)(2,1)S(1)}, u32[]{:S(2)}, u32[]{:S(2)}) async-start(bf16[16,128,128]{2,1,0:T(8,128)(2,1)} %get-tuple-element.31), calls=%async_computation.2 | async-start | bytes 1048576 | tf_op jit(solution)/shard_map/all_to_all | solution.py:744
  94.8 0.0 copy-done.1
  94.8 5.4 %shard_map.157 = (bf16[128,2048]{1,0:T(8,128)(2,1)}, bf16[128,2048]{1,0:T(8,128)(2,1)}, bf16[128,2048]{1,0:T(8,128)(2,1)}, bf16[128,2048]{1,0:T(8,128)(2,1)}, f32[4,2176]{1,0:T(4,128)}) custom-call(bf16[128,2048]{1,0:T(8,128)(2,1)} %refs_0_.5, bf16[128,2048]{1,0:T(8,128)(2,1)} %refs_1_.5, bf16[128,2048]{1,0:T(8,128)(2,1)} %refs_2_.5, ...), custom_call_target="tpu_custom_call" | custom-call | tf_op jit(solution)/shard_map/pallas_call | solution.py:35
  100.2 1.7 %collective-permute-start.2 = (f32[4,2176]{1,0:T(4,128)}, f32[4,2176]{1,0:T(4,128)S(1)}, u32[]{:S(2)}, u32[]{:S(2)}) collective-permute-start(f32[4,2176]{1,0:T(4,128)} %get-tuple-element.28.own_hbm), channel_id=1, source_target_pairs={{0,6},{2,4},{4,2},{6,0},{8,14},{10,12},{12,10},{14,8},{16,22},{18,... | collective-permute-start | bytes 104456 | tf_op jit(solution)/shard_map/ppermute | solution.py:766
  102.0 0.4 collective-permute-start.1
  102.4 0.0 collective-permute-start
  102.4 1.9 %collective-permute-done.2.refs_2_ = f32[4,2176]{1,0:T(4,128)S(1)} collective-permute-done((f32[4,2176]{1,0:T(4,128)}, f32[4,2176]{1,0:T(4,128)S(1)}, u32[]{:S(2)}, u32[]{:S(2)}) %collective-permute-start.2) | collective-permute-done | bytes 34848 | tf_op jit(solution)/shard_map/ppermute | solution.py:766
  104.2 1.9 %collective-permute-done.1.refs_1_ = f32[4,2176]{1,0:T(4,128)S(1)} collective-permute-done((f32[4,2176]{1,0:T(4,128)}, f32[4,2176]{1,0:T(4,128)S(1)}, u32[]{:S(2)}, u32[]{:S(2)}) %collective-permute-start.1) | collective-permute-done | bytes 34848 | tf_op jit(solution)/shard_map/ppermute | solution.py:766
  106.1 0.0 collective-permute-done.refs_0_
  106.1 0.0 copy-start
  106.1 0.8 copy-done
  106.9 3.3 %collective-permute-start.5 = (f32[4,2176]{1,0:T(4,128)S(1)}, f32[4,2176]{1,0:T(4,128)S(1)}, u32[]{:S(2)}, u32[]{:S(2)}) collective-permute-start(f32[4,2176]{1,0:T(4,128)S(1)} %shard_map.158.refs_0_), channel_id=1, source_target_pairs={{0,24},{2,26},{4,28},{6,30},{8,16},{10,18},{12,20},{14,22},{16,8},... | collective-permute-start | bytes 104456 | tf_op jit(solution)/shard_map/ppermute | solution.py:766
  110.3 0.5 collective-permute-start.4
  110.8 0.6 collective-permute-start.3
  111.4 1.7 %collective-permute-done.5.refs_3_ = f32[4,2176]{1,0:T(4,128)S(1)} collective-permute-done((f32[4,2176]{1,0:T(4,128)S(1)}, f32[4,2176]{1,0:T(4,128)S(1)}, u32[]{:S(2)}, u32[]{:S(2)}) %collective-permute-start.5) | collective-permute-done | bytes 34848 | tf_op jit(solution)/shard_map/ppermute | solution.py:766
  113.0 2.3 %collective-permute-done.4.refs_2_ = f32[4,2176]{1,0:T(4,128)S(1)} collective-permute-done((f32[4,2176]{1,0:T(4,128)S(1)}, f32[4,2176]{1,0:T(4,128)S(1)}, u32[]{:S(2)}, u32[]{:S(2)}) %collective-permute-start.4) | collective-permute-done | bytes 34848 | tf_op jit(solution)/shard_map/ppermute | solution.py:766
  115.3 0.0 collective-permute-done.3.refs_1_
  115.3 0.1 shard_map.159
  115.4 1.6 %collective-permute-start.6 = (f32[1,128]{1,0:T(1,128)S(1)}, f32[1,128]{1,0:T(1,128)S(1)}, u32[]{:S(2)}, u32[]{:S(2)}) collective-permute-start(f32[1,128]{1,0:T(1,128)S(1)} %get-tuple-element.30), channel_id=1, source_target_pairs={{0,1},{1,0},{2,3},{3,2},{4,5},{5,4},{6,7},{7,6},{8,9},{9,8},{10,11... | collective-permute-start | bytes 1544 | tf_op jit(solution)/shard_map/ppermute | solution.py:766
  117.0 2.0 %collective-permute-done.6 = f32[1,128]{1,0:T(1,128)S(1)} collective-permute-done((f32[1,128]{1,0:T(1,128)S(1)}, f32[1,128]{1,0:T(1,128)S(1)}, u32[]{:S(2)}, u32[]{:S(2)}) %collective-permute-start.6) | collective-permute-done | bytes 544 | tf_op jit(solution)/shard_map/ppermute | solution.py:766
  119.1 0.0 all-to-all-done.2.lag_ref
  119.1 1.1 shard_map.160
  (2 shorter events, 0.0 us)
Async XLA Ops:
  4.2 40.6 %all-to-all-start = ((bf16[16,400,128]{2,1,0:T(8,128)(2,1)}), bf16[16,400,128]{2,1,0:T(8,128)(2,1)}, u32[]{:S(2)}, u32[]{:S(2)}) async-start(bf16[16,400,128]{2,1,0:T(8,128)(2,1)} %shard_map.153.refs_4_), calls=%async_computation | async-start | bytes 3276800 | tf_op jit(solution)/shard_map/all_to_all | solution.py:744
  11.7 3.4 %copy-start.2 = (f32[3,2048]{1,0:T(4,128)S(1)}, f32[3,2048]{1,0:T(4,128)}, u32[]{:S(2)}) copy-start(f32[3,2048]{1,0:T(4,128)} %refs_5_.3) | copy-start | bytes 73732
  11.7 3.4 %copy-start.3 = (f32[2048]{0:T(1024)S(1)}, f32[2048]{0:T(1024)}, u32[]{:S(2)}) copy-start(f32[2048]{0:T(1024)} %param.16) | copy-start | bytes 24580
  54.1 33.4 %all-to-all-start.1 = ((bf16[16,272,128]{2,1,0:T(8,128)(2,1)}), bf16[16,272,128]{2,1,0:T(8,128)(2,1)S(1)}, u32[]{:S(2)}, u32[]{:S(2)}) async-start(bf16[16,272,128]{2,1,0:T(8,128)(2,1)} %get-tuple-element.21), calls=%async_computation.1 | async-start | bytes 2228224 | tf_op jit(solution)/shard_map/all_to_all | solution.py:744
  87.6 7.2 %copy-start.1 = (bf16[16,272,128]{2,1,0:T(8,128)(2,1)}, bf16[16,272,128]{2,1,0:T(8,128)(2,1)S(1)}, u32[]{:S(2)}) copy-start(bf16[16,272,128]{2,1,0:T(8,128)(2,1)S(1)} %all-to-all-done.1.refs_7_) | copy-start | bytes 3342340
  87.6 31.5 %all-to-all-start.2 = ((bf16[16,128,128]{2,1,0:T(8,128)(2,1)}), bf16[16,128,128]{2,1,0:T(8,128)(2,1)S(1)}, u32[]{:S(2)}, u32[]{:S(2)}) async-start(bf16[16,128,128]{2,1,0:T(8,128)(2,1)} %get-tuple-element.31), calls=%async_computation.2 | async-start | bytes 1048576 | tf_op jit(solution)/shard_map/all_to_all | solution.py:744
  100.2 4.0 %collective-permute-start.2 = (f32[4,2176]{1,0:T(4,128)}, f32[4,2176]{1,0:T(4,128)S(1)}, u32[]{:S(2)}, u32[]{:S(2)}) collective-permute-start(f32[4,2176]{1,0:T(4,128)} %get-tuple-element.28.own_hbm), channel_id=1, source_target_pairs={{0,6},{2,4},{4,2},{6,0},{8,14},{10,12},{12,10},{14,8},{16,22},{18,... | collective-permute-start | bytes 104456 | tf_op jit(solution)/shard_map/ppermute | solution.py:766
  102.0 4.2 %collective-permute-start.1 = (f32[4,2176]{1,0:T(4,128)}, f32[4,2176]{1,0:T(4,128)S(1)}, u32[]{:S(2)}, u32[]{:S(2)}) collective-permute-start(f32[4,2176]{1,0:T(4,128)} %get-tuple-element.28.own_hbm), channel_id=1, source_target_pairs={{0,4},{2,6},{4,0},{6,2},{8,12},{10,14},{12,8},{14,10},{16,20},{18,... | collective-permute-start | bytes 104456 | tf_op jit(solution)/shard_map/ppermute | solution.py:766
  102.4 3.8 %collective-permute-start = (f32[4,2176]{1,0:T(4,128)}, f32[4,2176]{1,0:T(4,128)S(1)}, u32[]{:S(2)}, u32[]{:S(2)}) collective-permute-start(f32[4,2176]{1,0:T(4,128)} %get-tuple-element.28.own_hbm), channel_id=1, source_target_pairs={{0,2},{2,0},{4,6},{6,4},{8,10},{10,8},{12,14},{14,12},{16,18},{18,... | collective-permute-start | bytes 104456 | tf_op jit(solution)/shard_map/ppermute | solution.py:766
  106.1 0.8 copy-start
  106.9 6.1 %collective-permute-start.5 = (f32[4,2176]{1,0:T(4,128)S(1)}, f32[4,2176]{1,0:T(4,128)S(1)}, u32[]{:S(2)}, u32[]{:S(2)}) collective-permute-start(f32[4,2176]{1,0:T(4,128)S(1)} %shard_map.158.refs_0_), channel_id=1, source_target_pairs={{0,24},{2,26},{4,28},{6,30},{8,16},{10,18},{12,20},{14,22},{16,8},... | collective-permute-start | bytes 104456 | tf_op jit(solution)/shard_map/ppermute | solution.py:766
  110.3 5.0 %collective-permute-start.4 = (f32[4,2176]{1,0:T(4,128)S(1)}, f32[4,2176]{1,0:T(4,128)S(1)}, u32[]{:S(2)}, u32[]{:S(2)}) collective-permute-start(f32[4,2176]{1,0:T(4,128)S(1)} %shard_map.158.refs_0_), channel_id=1, source_target_pairs={{0,16},{2,18},{4,20},{6,22},{8,24},{10,26},{12,28},{14,30},{16,0},... | collective-permute-start | bytes 104456 | tf_op jit(solution)/shard_map/ppermute | solution.py:766
  110.8 4.5 %collective-permute-start.3 = (f32[4,2176]{1,0:T(4,128)S(1)}, f32[4,2176]{1,0:T(4,128)S(1)}, u32[]{:S(2)}, u32[]{:S(2)}) collective-permute-start(f32[4,2176]{1,0:T(4,128)S(1)} %shard_map.158.refs_0_), channel_id=1, source_target_pairs={{0,8},{2,10},{4,12},{6,14},{8,0},{10,2},{12,4},{14,6},{16,24},{18,... | collective-permute-start | bytes 104456 | tf_op jit(solution)/shard_map/ppermute | solution.py:766
  115.4 3.6 %collective-permute-start.6 = (f32[1,128]{1,0:T(1,128)S(1)}, f32[1,128]{1,0:T(1,128)S(1)}, u32[]{:S(2)}, u32[]{:S(2)}) collective-permute-start(f32[1,128]{1,0:T(1,128)S(1)} %get-tuple-element.30), channel_id=1, source_target_pairs={{0,1},{1,0},{2,3},{3,2},{4,5},{5,4},{6,7},{7,6},{8,9},{9,8},{10,11... | collective-permute-start | bytes 1544 | tf_op jit(solution)/shard_map/ppermute | solution.py:766

commit v12 on v11

--- a/solution.py
+++ b/solution.py
@@ -353,10 +353,11 @@
 
         return signal_stage(from_ref, twist_ref, rows_here, write)
 
-    for copy in arrivals + [matrix_copy]:
-        copy.start()
+    arrivals[0].start()
     run_all([twist_stage(coarse_ref, fine_ref, twist_ref, rows_here)], rows_here)
     arrivals[0].wait()
+    for copy in (matrix_copy, arrivals[1], arrivals[2]):
+        copy.start()
     run_all([leaves(2, one_split)], rows_here)
     arrivals[1].wait()
     arrivals[2].wait()
@@ -722,12 +723,12 @@
     square_ref[...] = jnp.full(square_ref.shape, square)
 
 
-def add_kernel(own_hbm, *refs):
-    *others, total_ref, own_ref, sem = refs
-    own_copy = pltpu.make_async_copy(own_hbm, own_ref, sem)
-    own_copy.start()
-    own_copy.wait()
-    total_ref[...] = add_up([own_ref[...]] + [ref[...] for ref in others])
+def add_kernel(*refs):
+    refs[-1][...] = add_up([ref[...] for ref in refs[:-1]])
+
+
+def same_kernel(value_ref, same_ref):
+    same_ref[...] = value_ref[...]
 
 
 def scale_kernel(limit, totals_ref, norm_ref, lag_ref, taps_out, skip_out, kernel_out):
@@ -790,7 +791,7 @@
     halo_rows = taps_count - 1
     groups = channels // LANES
     share = channels // pieces
-    per_step = min(groups, 4)
+    per_step = min(groups, 8)
     steps = groups // per_step
     lanes2 = cut_lanes(per_step * LANES, 2)
     lanes3 = cut_lanes(per_step * LANES, 3)
@@ -839,11 +840,13 @@
     rounds = rounds_of(pieces)
     for steps_of in rounds[:-1]:
         values = partners(totals, "ctx", steps_of)
+        values[0] = call(
+            same_kernel, jax.ShapeDtypeStruct(totals.shape, f32), [], totals,
+            vmem_bytes=SMALL_VMEM_BYTES, in_specs=[IN_VMEM], out_specs=IN_VMEM,
+        )
         totals = call(
-            add_kernel, jax.ShapeDtypeStruct(totals.shape, f32),
-            [pltpu.VMEM(totals.shape, f32), pltpu.SemaphoreType.DMA], *values,
-            vmem_bytes=SMALL_VMEM_BYTES,
-            in_specs=[ANYWHERE] + [IN_VMEM] * (len(values) - 1), out_specs=IN_VMEM,
+            add_kernel, jax.ShapeDtypeStruct(totals.shape, f32), [], *values,
+            vmem_bytes=SMALL_VMEM_BYTES, in_specs=[IN_VMEM] * len(values), out_specs=IN_VMEM,
         )
     last = partners(totals, "ctx", rounds[-1])
     if len(last) == 2:

time: 121 us -> 121 us (level)
  Pallas kernels: 27.4 us -> 28.7 us
    pallas_call x8 -> x9, Pallas kernels: 27.4 us -> 28.7 us  [call(): pl.pallas_call(kernel, out_shape=outs, scratch_shapes=scratch, compiler_p...]
  transfers between devices with their start and end apart: 10 -> 10, of which waited for: 7 -> 7; matrix products, arithmetic and copies ran while one was open for 1% -> 1% of each run, Pallas kernels for 11% -> 12%
where the time goes in v12:
time: 121 us; the launch traced here: 120 us
  waiting for transfers between devices  57.2 us (47%)
  starting transfers between devices  32.2 us (27%)
  Pallas kernels  28.7 us (24%)
    all_to_all x3, waiting for transfers between devices, exchange(): lax.all_to_all(pieces_first, 'ctx', split_axis=0, concat_axis=0, tiled=True)  48.5 us
    pallas_call x9, Pallas kernels, call(): pl.pallas_call(kernel, out_shape=outs, scratch_shapes=scratch, compiler_p...  28.7 us
    all_to_all x3, starting transfers between devices, exchange(): lax.all_to_all(pieces_first, 'ctx', split_axis=0, concat_axis=0, tiled=True)  24 us
    ppermute x7, waiting for transfers between devices, partners(): lax.ppermute(value, axis, [(i, i ^ step) for i in range(size)])  8.77 us
    ppermute x7, starting transfers between devices, partners(): lax.ppermute(value, axis, [(i, i ^ step) for i in range(size)])  8.16 us
  transfers between devices with their start and end apart: 10, of which 7 were waited for; matrix products, arithmetic and copies ran while one was open for 1% of the time, Pallas kernels for 12%

profile of v12, /device:TPU:0, one launch (start us, length us, event | category | flops | bytes accessed | tf_op | source)
XLA Modules:
  0.0 120.4 jit_solution(8700213726053144921)
XLA Ops:
  0.6 3.7 %shard_map.153.refs_4_ = bf16[16,400,128]{2,1,0:T(8,128)(2,1)} custom-call(bf16[128,2048]{1,0:T(8,128)(2,1)} %refs_0_.5, bf16[128,2048]{1,0:T(8,128)(2,1)} %refs_1_.5, bf16[128,2048]{1,0:T(8,128)(2,1)} %refs_2_.5, bf16[128,2048]{1,0:T(8,128)(2,1)} %refs_3_.5, f32[128,2048]{1,0:T(8,128)} %refs_4_.1, f32[3,2048]{1,0:T(4,128)} %refs_5_.3), custom_call_target="tpu_custom_call" | custom-call | tf_op jit(solution)/shard_map/pallas_call | solution.py:35
  4.4 7.4 %all-to-all-start = ((bf16[16,400,128]{2,1,0:T(8,128)(2,1)}), bf16[16,400,128]{2,1,0:T(8,128)(2,1)}, u32[]{:S(2)}, u32[]{:S(2)}) async-start(bf16[16,400,128]{2,1,0:T(8,128)(2,1)} %shard_map.153.refs_4_), calls=%async_computation | async-start | bytes 3276800 | tf_op jit(solution)/shard_map/all_to_all | solution.py:745
  11.8 0.0 copy-start.2
  11.8 0.0 copy-start.3
  11.8 3.6 %shard_map.154.after_ref.refs_4_ = f32[3,128,2048]{2,1,0:T(8,128)} custom-call(bf16[128,2048]{1,0:T(8,128)(2,1)} %refs_0_.5, bf16[128,2048]{1,0:T(8,128)(2,1)} %refs_1_.5, bf16[128,2048]{1,0:T(8,128)(2,1)} %refs_2_.5, f32[3,2048]{1,0:T(4,128)} %refs_5_.3, bf16[16,400,128]{2,1,0:T(8,128)(2,1)} %shard_map.153.refs_4_), custom_call_target="tpu_custom_call" | custom-call | tf_op jit(solution)/shard_map/pallas_call | solution.py:35
  15.4 0.0 copy-done.2
  15.4 0.0 copy-done.3
  15.5 0.7 fusion.taps_ref
  16.1 28.9 %all-to-all-done.signals_hbm = bf16[16,400,128]{2,1,0:T(8,128)(2,1)} async-done(((bf16[16,400,128]{2,1,0:T(8,128)(2,1)}), bf16[16,400,128]{2,1,0:T(8,128)(2,1)}, u32[]{:S(2)}, u32[]{:S(2)}) %all-to-all-start) | async-done | bytes 1638432 | tf_op jit(solution)/shard_map/all_to_all | solution.py:745
  45.0 10.0 %shard_map.155 = (bf16[16,272,128]{2,1,0:T(8,128)(2,1)}, bf16[4,512,256]{2,1,0:T(8,128)(2,1)}) custom-call(bf16[16,400,128]{2,1,0:T(8,128)(2,1)} %all-to-all-done.signals_hbm, f32[4,128]{1,0:T(4,128)} %fusion.taps_ref, f32[16,16]{1,0:T(8,128)} %constant.18.clone.coarse_ref, f32[2,8,16,128]{3,2,1,0:T(8,128)} %constant.19.clone.fine_ref, ...), custom_call_target="tpu_custom_call" | custom-call | tf_op jit(solution)/shard_map/pallas_call | solution.py:35
  55.0 9.4 %all-to-all-start.1 = ((bf16[16,272,128]{2,1,0:T(8,128)(2,1)}), bf16[16,272,128]{2,1,0:T(8,128)(2,1)S(1)}, u32[]{:S(2)}, u32[]{:S(2)}) async-start(bf16[16,272,128]{2,1,0:T(8,128)(2,1)} %get-tuple-element.21), calls=%async_computation.1 | async-start | bytes 2228224 | tf_op jit(solution)/shard_map/all_to_all | solution.py:745
  64.4 4.4 %shard_map.156 = (bf16[16,128,128]{2,1,0:T(8,128)(2,1)}, f32[1,128]{1,0:T(1,128)}) custom-call(bf16[4,512,256]{2,1,0:T(8,128)(2,1)} %get-tuple-element.22.split_hbm, f32[16,16]{1,0:T(8,128)} %constant.18.clone.coarse_ref, f32[2,8,16,128]{3,2,1,0:T(8,128)} %constant.19.clone.fine_ref, bf16[512,512]{1,0:T(8,128)(2,1)} %constant.20.clone.matrix_hbm), custom_call_target="tpu_custom_call" | custom-call | tf_op jit(solution)/shard_map/pallas_call | solution.py:35
  68.8 19.6 %all-to-all-done.1.refs_7_ = bf16[16,272,128]{2,1,0:T(8,128)(2,1)S(1)} async-done(((bf16[16,272,128]{2,1,0:T(8,128)(2,1)}), bf16[16,272,128]{2,1,0:T(8,128)(2,1)S(1)}, u32[]{:S(2)}, u32[]{:S(2)}) %all-to-all-start.1) | async-done | bytes 1114144 | tf_op jit(solution)/shard_map/all_to_all | solution.py:745
  88.4 0.0 copy-start.1
  88.4 7.2 %all-to-all-start.2 = ((bf16[16,128,128]{2,1,0:T(8,128)(2,1)}), bf16[16,128,128]{2,1,0:T(8,128)(2,1)S(1)}, u32[]{:S(2)}, u32[]{:S(2)}) async-start(bf16[16,128,128]{2,1,0:T(8,128)(2,1)} %get-tuple-element.31), calls=%async_computation.2 | async-start | bytes 1048576 | tf_op jit(solution)/shard_map/all_to_all | solution.py:745
  95.6 0.0 copy-done.1
  95.6 5.7 %shard_map.157 = (bf16[128,2048]{1,0:T(8,128)(2,1)}, bf16[128,2048]{1,0:T(8,128)(2,1)}, bf16[128,2048]{1,0:T(8,128)(2,1)}, bf16[128,2048]{1,0:T(8,128)(2,1)}, f32[4,2176]{1,0:T(4,128)}) custom-call(bf16[128,2048]{1,0:T(8,128)(2,1)} %refs_0_.5, bf16[128,2048]{1,0:T(8,128)(2,1)} %refs_1_.5, bf16[128,2048]{1,0:T(8,128)(2,1)} %refs_2_.5, ...), custom_call_target="tpu_custom_call" | custom-call | tf_op jit(solution)/shard_map/pallas_call | solution.py:35
  101.3 1.7 %collective-permute-start.2 = (f32[4,2176]{1,0:T(4,128)}, f32[4,2176]{1,0:T(4,128)S(1)}, u32[]{:S(2)}, u32[]{:S(2)}) collective-permute-start(f32[4,2176]{1,0:T(4,128)} %get-tuple-element.28.value_ref), channel_id=1, source_target_pairs={{0,6},{2,4},{4,2},{6,0},{8,14},{10,12},{12,10},{14,8},{16,22},{18,... | collective-permute-start | bytes 104456 | tf_op jit(solution)/shard_map/ppermute | solution.py:767
  103.1 0.4 collective-permute-start.1
  103.5 0.0 collective-permute-start
  103.5 0.0 copy-start
  103.5 0.8 copy-done
  104.3 1.1 collective-permute-done.2.refs_3_
  105.4 1.9 %collective-permute-done.1.refs_2_ = f32[4,2176]{1,0:T(4,128)S(1)} collective-permute-done((f32[4,2176]{1,0:T(4,128)}, f32[4,2176]{1,0:T(4,128)S(1)}, u32[]{:S(2)}, u32[]{:S(2)}) %collective-permute-start.1) | collective-permute-done | bytes 34848 | tf_op jit(solution)/shard_map/ppermute | solution.py:767
  107.2 0.0 collective-permute-done.refs_1_
  107.2 3.3 %collective-permute-start.5 = (f32[4,2176]{1,0:T(4,128)S(1)}, f32[4,2176]{1,0:T(4,128)S(1)}, u32[]{:S(2)}, u32[]{:S(2)}) collective-permute-start(f32[4,2176]{1,0:T(4,128)S(1)} %shard_map.159.refs_0_), channel_id=1, source_target_pairs={{0,24},{2,26},{4,28},{6,30},{8,16},{10,18},{12,20},{14,22},{16,8},... | collective-permute-start | bytes 104456 | tf_op jit(solution)/shard_map/ppermute | solution.py:767
  110.6 0.4 collective-permute-start.4
  111.0 0.7 collective-permute-start.3
  111.7 1.4 %collective-permute-done.5.refs_3_ = f32[4,2176]{1,0:T(4,128)S(1)} collective-permute-done((f32[4,2176]{1,0:T(4,128)S(1)}, f32[4,2176]{1,0:T(4,128)S(1)}, u32[]{:S(2)}, u32[]{:S(2)}) %collective-permute-start.5) | collective-permute-done | bytes 34848 | tf_op jit(solution)/shard_map/ppermute | solution.py:767
  113.1 2.3 %collective-permute-done.4.refs_2_ = f32[4,2176]{1,0:T(4,128)S(1)} collective-permute-done((f32[4,2176]{1,0:T(4,128)S(1)}, f32[4,2176]{1,0:T(4,128)S(1)}, u32[]{:S(2)}, u32[]{:S(2)}) %collective-permute-start.4) | collective-permute-done | bytes 34848 | tf_op jit(solution)/shard_map/ppermute | solution.py:767
  115.5 0.0 collective-permute-done.3.refs_1_
  115.5 0.1 shard_map.160
  115.6 1.6 %collective-permute-start.6 = (f32[1,128]{1,0:T(1,128)S(1)}, f32[1,128]{1,0:T(1,128)S(1)}, u32[]{:S(2)}, u32[]{:S(2)}) collective-permute-start(f32[1,128]{1,0:T(1,128)S(1)} %get-tuple-element.30), channel_id=1, source_target_pairs={{0,1},{1,0},{2,3},{3,2},{4,5},{5,4},{6,7},{7,6},{8,9},{9,8},{10,11... | collective-permute-start | bytes 1544 | tf_op jit(solution)/shard_map/ppermute | solution.py:767
  117.2 2.0 %collective-permute-done.6 = f32[1,128]{1,0:T(1,128)S(1)} collective-permute-done((f32[1,128]{1,0:T(1,128)S(1)}, f32[1,128]{1,0:T(1,128)S(1)}, u32[]{:S(2)}, u32[]{:S(2)}) %collective-permute-start.6) | collective-permute-done | bytes 544 | tf_op jit(solution)/shard_map/ppermute | solution.py:767
  119.2 0.0 all-to-all-done.2.lag_ref
  119.2 1.1 shard_map.161
  (3 shorter events, 0.0 us)
Async XLA Ops:
  4.4 40.6 %all-to-all-start = ((bf16[16,400,128]{2,1,0:T(8,128)(2,1)}), bf16[16,400,128]{2,1,0:T(8,128)(2,1)}, u32[]{:S(2)}, u32[]{:S(2)}) async-start(bf16[16,400,128]{2,1,0:T(8,128)(2,1)} %shard_map.153.refs_4_), calls=%async_computation | async-start | bytes 3276800 | tf_op jit(solution)/shard_map/all_to_all | solution.py:745
  11.8 3.6 %copy-start.2 = (f32[3,2048]{1,0:T(4,128)S(1)}, f32[3,2048]{1,0:T(4,128)}, u32[]{:S(2)}) copy-start(f32[3,2048]{1,0:T(4,128)} %refs_5_.3) | copy-start | bytes 73732
  11.8 3.6 %copy-start.3 = (f32[2048]{0:T(1024)S(1)}, f32[2048]{0:T(1024)}, u32[]{:S(2)}) copy-start(f32[2048]{0:T(1024)} %param.16) | copy-start | bytes 24580
  55.0 33.4 %all-to-all-start.1 = ((bf16[16,272,128]{2,1,0:T(8,128)(2,1)}), bf16[16,272,128]{2,1,0:T(8,128)(2,1)S(1)}, u32[]{:S(2)}, u32[]{:S(2)}) async-start(bf16[16,272,128]{2,1,0:T(8,128)(2,1)} %get-tuple-element.21), calls=%async_computation.1 | async-start | bytes 2228224 | tf_op jit(solution)/shard_map/all_to_all | solution.py:745
  88.4 7.2 %copy-start.1 = (bf16[16,272,128]{2,1,0:T(8,128)(2,1)}, bf16[16,272,128]{2,1,0:T(8,128)(2,1)S(1)}, u32[]{:S(2)}) copy-start(bf16[16,272,128]{2,1,0:T(8,128)(2,1)S(1)} %all-to-all-done.1.refs_7_) | copy-start | bytes 3342340
  88.4 30.8 %all-to-all-start.2 = ((bf16[16,128,128]{2,1,0:T(8,128)(2,1)}), bf16[16,128,128]{2,1,0:T(8,128)(2,1)S(1)}, u32[]{:S(2)}, u32[]{:S(2)}) async-start(bf16[16,128,128]{2,1,0:T(8,128)(2,1)} %get-tuple-element.31), calls=%async_computation.2 | async-start | bytes 1048576 | tf_op jit(solution)/shard_map/all_to_all | solution.py:745
  101.3 4.0 %collective-permute-start.2 = (f32[4,2176]{1,0:T(4,128)}, f32[4,2176]{1,0:T(4,128)S(1)}, u32[]{:S(2)}, u32[]{:S(2)}) collective-permute-start(f32[4,2176]{1,0:T(4,128)} %get-tuple-element.28.value_ref), channel_id=1, source_target_pairs={{0,6},{2,4},{4,2},{6,0},{8,14},{10,12},{12,10},{14,8},{16,22},{18,... | collective-permute-start | bytes 104456 | tf_op jit(solution)/shard_map/ppermute | solution.py:767
  103.1 4.2 %collective-permute-start.1 = (f32[4,2176]{1,0:T(4,128)}, f32[4,2176]{1,0:T(4,128)S(1)}, u32[]{:S(2)}, u32[]{:S(2)}) collective-permute-start(f32[4,2176]{1,0:T(4,128)} %get-tuple-element.28.value_ref), channel_id=1, source_target_pairs={{0,4},{2,6},{4,0},{6,2},{8,12},{10,14},{12,8},{14,10},{16,20},{18,... | collective-permute-start | bytes 104456 | tf_op jit(solution)/shard_map/ppermute | solution.py:767
  103.5 3.8 %collective-permute-start = (f32[4,2176]{1,0:T(4,128)}, f32[4,2176]{1,0:T(4,128)S(1)}, u32[]{:S(2)}, u32[]{:S(2)}) collective-permute-start(f32[4,2176]{1,0:T(4,128)} %get-tuple-element.28.value_ref), channel_id=1, source_target_pairs={{0,2},{2,0},{4,6},{6,4},{8,10},{10,8},{12,14},{14,12},{16,18},{18,... | collective-permute-start | bytes 104456 | tf_op jit(solution)/shard_map/ppermute | solution.py:767
  103.5 0.8 copy-start
  107.2 5.9 %collective-permute-start.5 = (f32[4,2176]{1,0:T(4,128)S(1)}, f32[4,2176]{1,0:T(4,128)S(1)}, u32[]{:S(2)}, u32[]{:S(2)}) collective-permute-start(f32[4,2176]{1,0:T(4,128)S(1)} %shard_map.159.refs_0_), channel_id=1, source_target_pairs={{0,24},{2,26},{4,28},{6,30},{8,16},{10,18},{12,20},{14,22},{16,8},... | collective-permute-start | bytes 104456 | tf_op jit(solution)/shard_map/ppermute | solution.py:767
  110.6 4.9 %collective-permute-start.4 = (f32[4,2176]{1,0:T(4,128)S(1)}, f32[4,2176]{1,0:T(4,128)S(1)}, u32[]{:S(2)}, u32[]{:S(2)}) collective-permute-start(f32[4,2176]{1,0:T(4,128)S(1)} %shard_map.159.refs_0_), channel_id=1, source_target_pairs={{0,16},{2,18},{4,20},{6,22},{8,24},{10,26},{12,28},{14,30},{16,0},... | collective-permute-start | bytes 104456 | tf_op jit(solution)/shard_map/ppermute | solution.py:767
  111.0 4.5 %collective-permute-start.3 = (f32[4,2176]{1,0:T(4,128)S(1)}, f32[4,2176]{1,0:T(4,128)S(1)}, u32[]{:S(2)}, u32[]{:S(2)}) collective-permute-start(f32[4,2176]{1,0:T(4,128)S(1)} %shard_map.159.refs_0_), channel_id=1, source_target_pairs={{0,8},{2,10},{4,12},{6,14},{8,0},{10,2},{12,4},{14,6},{16,24},{18,... | collective-permute-start | bytes 104456 | tf_op jit(solution)/shard_map/ppermute | solution.py:767
  115.6 3.6 %collective-permute-start.6 = (f32[1,128]{1,0:T(1,128)S(1)}, f32[1,128]{1,0:T(1,128)S(1)}, u32[]{:S(2)}, u32[]{:S(2)}) collective-permute-start(f32[1,128]{1,0:T(1,128)S(1)} %get-tuple-element.30), channel_id=1, source_target_pairs={{0,1},{1,0},{2,3},{3,2},{4,5},{5,4},{6,7},{7,6},{8,9},{9,8},{10,11... | collective-permute-start | bytes 1544 | tf_op jit(solution)/shard_map/ppermute | solution.py:767

commit v13 on v12

--- a/solution.py
+++ b/solution.py
@@ -16,7 +16,8 @@
 CHUNK = 16
 CHUNKS = SPAN // CHUNK
 PAD = 8
-ROWS = 32
+ROWS = 16
+CUTS = 4
 PASSES = 1
 TILE_ROWS = 16
 VMEM_BYTES = 60 * 1024 * 1024
@@ -322,21 +323,41 @@
     signals_ref, twist_ref, matrix_ref, heads_ref, results_ref, one_split, two_split, lag_split,
     filter_ref, product_ref, cotan_ref, time_ref, sems,
 ):
-    filter_rows = pl.ds(2 * rows_here, rows_here)
-    extra_rows = pl.ds(3 * rows_here, signals_ref.shape[1] - 3 * rows_here)
-    signal_rows = pl.ds(0, 2 * rows_here)
-    arrivals = [
-        pltpu.make_async_copy(signals_hbm.at[:, rows], signals_ref.at[:, rows], sems.at[idx])
-        for idx, rows in enumerate((filter_rows, extra_rows, signal_rows))
+    all_rows = signals_ref.shape[1]
+    back_rows = results_ref.shape[1]
+    sem_idx = iter(range(sems.shape[0]))
+
+    def cut_copies(source, target, rows):
+        each = source.shape[0] // CUTS
+        places = [(pl.ds(cut * each, each), pl.ds(*rows)) for cut in range(CUTS)]
+        return [pltpu.make_async_copy(source.at[at], target.at[at], sems.at[next(sem_idx)]) for at in places]
+
+    filter_copies = cut_copies(signals_hbm, signals_ref, (2 * rows_here, all_rows - 2 * rows_here))
+    matrix_copies = [
+        pltpu.make_async_copy(
+            matrix_hbm.at[pl.ds(cut * BOTH // CUTS, BOTH // CUTS)],
+            matrix_ref.at[pl.ds(cut * BOTH // CUTS, BOTH // CUTS)],
+            sems.at[next(sem_idx)],
+        )
+        for cut in range(CUTS)
     ]
-    matrix_copy = pltpu.make_async_copy(matrix_hbm, matrix_ref, sems.at[3])
-    lag_copy = pltpu.make_async_copy(lag_split, lag_hbm, sems.at[4])
-    returns = [
-        pltpu.make_async_copy(results_ref.at[:, rows], results_hbm.at[:, rows], sems.at[5 + idx])
-        for idx, rows in enumerate(
-            (pl.ds(0, rows_here), pl.ds(rows_here, results_ref.shape[1] - rows_here))
-        )
+    signal_copies = [cut_copies(signals_hbm, signals_ref, (kind * rows_here, rows_here)) for kind in range(2)]
+    lag_copies = [
+        pltpu.make_async_copy(lag_split.at[pair], lag_hbm.at[pair], sems.at[next(sem_idx)])
+        for pair in range(lag_split.shape[0])
     ]
+    return_copies = [
+        cut_copies(results_ref, results_hbm, rows)
+        for rows in ((0, rows_here), (rows_here, back_rows - rows_here))
+    ]
+
+    def start_all(copies):
+        for copy in copies:
+            copy.start()
+
+    def wait_all(copies):
+        for copy in copies:
+            copy.wait()
 
     def leaves(kind, split_ref):
         heads = heads_ref.at[kind] if kind < 2 else None
@@ -353,16 +374,12 @@
 
         return signal_stage(from_ref, twist_ref, rows_here, write)
 
-    arrivals[0].start()
+    start_all(filter_copies + matrix_copies + signal_copies[0] + signal_copies[1])
     run_all([twist_stage(coarse_ref, fine_ref, twist_ref, rows_here)], rows_here)
-    arrivals[0].wait()
-    for copy in (matrix_copy, arrivals[1], arrivals[2]):
-        copy.start()
+    wait_all(filter_copies)
     run_all([leaves(2, one_split)], rows_here)
-    arrivals[1].wait()
-    arrivals[2].wait()
+    wait_all(signal_copies[0] + signal_copies[1] + matrix_copies)
     patch_first_rows(signals_ref, heads_ref, taps_ref, rows_here)
-    matrix_copy.wait()
     run_all([leaves(0, two_split)], rows_here, (matrix_ref, one_split, filter_ref))
     run_all([leaves(1, one_split)], rows_here, (matrix_ref, two_split, product_ref))
     run_all([combine(filter_ref, product_ref, two_split, False)], rows_here, (matrix_ref, one_split, cotan_ref))
@@ -371,14 +388,11 @@
         [combine(product_ref, cotan_ref, lag_split, True), result(0, time_ref)],
         rows_here, (matrix_ref, one_split, filter_ref),
     )
-    lag_copy.start()
-    returns[0].start()
+    start_all(return_copies[0] + lag_copies)
     run_all([result(1, filter_ref)], rows_here)
     write_edges(signals_ref, results_ref, taps_ref, rows_here)
-    returns[1].start()
-    lag_copy.wait()
-    returns[0].wait()
-    returns[1].wait()
+    start_all(return_copies[1])
+    wait_all(lag_copies + return_copies[0] + return_copies[1])
 
 
 def lag_kernel(
@@ -434,7 +448,7 @@
             + [pltpu.VMEM((2, signals.shape[0], TILE_ROWS, LANES), bf16), self.result_work]
             + [self.split_work] * 3
             + [self.work] * 4
-            + [pltpu.SemaphoreType.DMA((7,))],
+            + [pltpu.SemaphoreType.DMA((6 * CUTS + self.split.shape[0],))],
             signals, taps, *self.tables, after,
             vmem_bytes=MOST_VMEM_BYTES,
             in_specs=[ANYWHERE, IN_VMEM, IN_SMEM, IN_VMEM, ANYWHERE, ANYWHERE],
@@ -791,7 +805,7 @@
     halo_rows = taps_count - 1
     groups = channels // LANES
     share = channels // pieces
-    per_step = min(groups, 8)
+    per_step = min(groups, 2)
     steps = groups // per_step
     lanes2 = cut_lanes(per_step * LANES, 2)
     lanes3 = cut_lanes(per_step * LANES, 3)

time: 121 us -> 120 us (level)
  transfers between devices with their start and end apart: 10 -> 10, of which waited for: 7 -> 7; matrix products, arithmetic and copies ran while one was open for 1% -> 1% of each run, Pallas kernels for 12% -> 11%
where the time goes in v13:
time: 120 us
  waiting for transfers between devices  57.6 us (48%)
  starting transfers between devices  32.2 us (27%)
  Pallas kernels  27.8 us (23%)
    all_to_all x3, waiting for transfers between devices, exchange(): lax.all_to_all(pieces_first, 'ctx', split_axis=0, concat_axis=0, tiled=True)  48.9 us
    pallas_call x9, Pallas kernels, call(): pl.pallas_call(kernel, out_shape=outs, scratch_shapes=scratch, compiler_p...  27.8 us
    all_to_all x3, starting transfers between devices, exchange(): lax.all_to_all(pieces_first, 'ctx', split_axis=0, concat_axis=0, tiled=True)  24 us
    ppermute x7, waiting for transfers between devices, partners(): lax.ppermute(value, axis, [(i, i ^ step) for i in range(size)])  8.71 us
    ppermute x7, starting transfers between devices, partners(): lax.ppermute(value, axis, [(i, i ^ step) for i in range(size)])  8.16 us
  transfers between devices with their start and end apart: 10, of which 7 were waited for; matrix products, arithmetic and copies ran while one was open for 1% of the time, Pallas kernels for 11%

profile of v13, /device:TPU:0, one launch (start us, length us, event | category | flops | bytes accessed | tf_op | source)
XLA Modules:
  0.0 119.8 jit_solution(17935183463414920908)
XLA Ops:
  0.6 3.6 %shard_map.153.refs_4_ = bf16[16,400,128]{2,1,0:T(8,128)(2,1)} custom-call(bf16[128,2048]{1,0:T(8,128)(2,1)} %refs_0_.5, bf16[128,2048]{1,0:T(8,128)(2,1)} %refs_1_.5, bf16[128,2048]{1,0:T(8,128)(2,1)} %refs_2_.5, bf16[128,2048]{1,0:T(8,128)(2,1)} %refs_3_.5, f32[128,2048]{1,0:T(8,128)} %refs_4_.1, f32[3,2048]{1,0:T(4,128)} %refs_5_.3), custom_call_target="tpu_custom_call" | custom-call | tf_op jit(solution)/shard_map/pallas_call | solution.py:36
  4.3 7.4 %all-to-all-start = ((bf16[16,400,128]{2,1,0:T(8,128)(2,1)}), bf16[16,400,128]{2,1,0:T(8,128)(2,1)}, u32[]{:S(2)}, u32[]{:S(2)}) async-start(bf16[16,400,128]{2,1,0:T(8,128)(2,1)} %shard_map.153.refs_4_), calls=%async_computation | async-start | bytes 3276800 | tf_op jit(solution)/shard_map/all_to_all | solution.py:759
  11.7 0.0 copy-start.2
  11.7 0.0 copy-start.3
  11.7 3.2 %shard_map.154.after_ref.refs_4_ = f32[3,128,2048]{2,1,0:T(8,128)} custom-call(bf16[128,2048]{1,0:T(8,128)(2,1)} %refs_0_.5, bf16[128,2048]{1,0:T(8,128)(2,1)} %refs_1_.5, bf16[128,2048]{1,0:T(8,128)(2,1)} %refs_2_.5, f32[3,2048]{1,0:T(4,128)} %refs_5_.3, bf16[16,400,128]{2,1,0:T(8,128)(2,1)} %shard_map.153.refs_4_), custom_call_target="tpu_custom_call" | custom-call | tf_op jit(solution)/shard_map/pallas_call | solution.py:36
  14.9 0.0 copy-done.2
  14.9 0.0 copy-done.3
  14.9 0.7 fusion.taps_ref
  15.6 29.3 %all-to-all-done.signals_hbm = bf16[16,400,128]{2,1,0:T(8,128)(2,1)} async-done(((bf16[16,400,128]{2,1,0:T(8,128)(2,1)}), bf16[16,400,128]{2,1,0:T(8,128)(2,1)}, u32[]{:S(2)}, u32[]{:S(2)}) %all-to-all-start) | async-done | bytes 1638432 | tf_op jit(solution)/shard_map/all_to_all | solution.py:759
  44.9 9.5 %shard_map.155 = (bf16[16,272,128]{2,1,0:T(8,128)(2,1)}, bf16[4,512,256]{2,1,0:T(8,128)(2,1)}) custom-call(bf16[16,400,128]{2,1,0:T(8,128)(2,1)} %all-to-all-done.signals_hbm, f32[4,128]{1,0:T(4,128)} %fusion.taps_ref, f32[16,16]{1,0:T(8,128)} %constant.18.clone.coarse_ref, f32[2,8,16,128]{3,2,1,0:T(8,128)} %constant.19.clone.fine_ref, ...), custom_call_target="tpu_custom_call" | custom-call | tf_op jit(solution)/shard_map/pallas_call | solution.py:36
  54.4 9.4 %all-to-all-start.1 = ((bf16[16,272,128]{2,1,0:T(8,128)(2,1)}), bf16[16,272,128]{2,1,0:T(8,128)(2,1)S(1)}, u32[]{:S(2)}, u32[]{:S(2)}) async-start(bf16[16,272,128]{2,1,0:T(8,128)(2,1)} %get-tuple-element.21), calls=%async_computation.1 | async-start | bytes 2228224 | tf_op jit(solution)/shard_map/all_to_all | solution.py:759
  63.8 4.4 %shard_map.156 = (bf16[16,128,128]{2,1,0:T(8,128)(2,1)}, f32[1,128]{1,0:T(1,128)}) custom-call(bf16[4,512,256]{2,1,0:T(8,128)(2,1)} %get-tuple-element.22.split_hbm, f32[16,16]{1,0:T(8,128)} %constant.18.clone.coarse_ref, f32[2,8,16,128]{3,2,1,0:T(8,128)} %constant.19.clone.fine_ref, bf16[512,512]{1,0:T(8,128)(2,1)} %constant.20.clone.matrix_hbm), custom_call_target="tpu_custom_call" | custom-call | tf_op jit(solution)/shard_map/pallas_call | solution.py:36
  68.2 19.6 %all-to-all-done.1.refs_7_ = bf16[16,272,128]{2,1,0:T(8,128)(2,1)S(1)} async-done(((bf16[16,272,128]{2,1,0:T(8,128)(2,1)}), bf16[16,272,128]{2,1,0:T(8,128)(2,1)S(1)}, u32[]{:S(2)}, u32[]{:S(2)}) %all-to-all-start.1) | async-done | bytes 1114144 | tf_op jit(solution)/shard_map/all_to_all | solution.py:759
  87.8 0.0 copy-start.1
  87.8 7.2 %all-to-all-start.2 = ((bf16[16,128,128]{2,1,0:T(8,128)(2,1)}), bf16[16,128,128]{2,1,0:T(8,128)(2,1)S(1)}, u32[]{:S(2)}, u32[]{:S(2)}) async-start(bf16[16,128,128]{2,1,0:T(8,128)(2,1)} %get-tuple-element.31), calls=%async_computation.2 | async-start | bytes 1048576 | tf_op jit(solution)/shard_map/all_to_all | solution.py:759
  95.0 0.0 copy-done.1
  95.0 5.8 %shard_map.157 = (bf16[128,2048]{1,0:T(8,128)(2,1)}, bf16[128,2048]{1,0:T(8,128)(2,1)}, bf16[128,2048]{1,0:T(8,128)(2,1)}, bf16[128,2048]{1,0:T(8,128)(2,1)}, f32[4,2176]{1,0:T(4,128)}) custom-call(bf16[128,2048]{1,0:T(8,128)(2,1)} %refs_0_.5, bf16[128,2048]{1,0:T(8,128)(2,1)} %refs_1_.5, bf16[128,2048]{1,0:T(8,128)(2,1)} %refs_2_.5, ...), custom_call_target="tpu_custom_call" | custom-call | tf_op jit(solution)/shard_map/pallas_call | solution.py:36
  100.8 1.7 %collective-permute-start.2 = (f32[4,2176]{1,0:T(4,128)}, f32[4,2176]{1,0:T(4,128)S(1)}, u32[]{:S(2)}, u32[]{:S(2)}) collective-permute-start(f32[4,2176]{1,0:T(4,128)} %get-tuple-element.28.value_ref), channel_id=1, source_target_pairs={{0,6},{2,4},{4,2},{6,0},{8,14},{10,12},{12,10},{14,8},{16,22},{18,... | collective-permute-start | bytes 104456 | tf_op jit(solution)/shard_map/ppermute | solution.py:781
  102.6 0.4 collective-permute-start.1
  103.0 0.0 collective-permute-start
  103.0 0.0 copy-start
  103.0 0.8 copy-done
  103.8 1.0 collective-permute-done.2.refs_3_
  104.8 1.9 %collective-permute-done.1.refs_2_ = f32[4,2176]{1,0:T(4,128)S(1)} collective-permute-done((f32[4,2176]{1,0:T(4,128)}, f32[4,2176]{1,0:T(4,128)S(1)}, u32[]{:S(2)}, u32[]{:S(2)}) %collective-permute-start.1) | collective-permute-done | bytes 34848 | tf_op jit(solution)/shard_map/ppermute | solution.py:781
  106.7 0.0 collective-permute-done.refs_1_
  106.7 3.3 %collective-permute-start.5 = (f32[4,2176]{1,0:T(4,128)S(1)}, f32[4,2176]{1,0:T(4,128)S(1)}, u32[]{:S(2)}, u32[]{:S(2)}) collective-permute-start(f32[4,2176]{1,0:T(4,128)S(1)} %shard_map.159.refs_0_), channel_id=1, source_target_pairs={{0,24},{2,26},{4,28},{6,30},{8,16},{10,18},{12,20},{14,22},{16,8},... | collective-permute-start | bytes 104456 | tf_op jit(solution)/shard_map/ppermute | solution.py:781
  110.1 0.4 collective-permute-start.4
  110.5 0.7 collective-permute-start.3
  111.2 1.4 %collective-permute-done.5.refs_3_ = f32[4,2176]{1,0:T(4,128)S(1)} collective-permute-done((f32[4,2176]{1,0:T(4,128)S(1)}, f32[4,2176]{1,0:T(4,128)S(1)}, u32[]{:S(2)}, u32[]{:S(2)}) %collective-permute-start.5) | collective-permute-done | bytes 34848 | tf_op jit(solution)/shard_map/ppermute | solution.py:781
  112.6 2.3 %collective-permute-done.4.refs_2_ = f32[4,2176]{1,0:T(4,128)S(1)} collective-permute-done((f32[4,2176]{1,0:T(4,128)S(1)}, f32[4,2176]{1,0:T(4,128)S(1)}, u32[]{:S(2)}, u32[]{:S(2)}) %collective-permute-start.4) | collective-permute-done | bytes 34848 | tf_op jit(solution)/shard_map/ppermute | solution.py:781
  114.9 0.0 collective-permute-done.3.refs_1_
  114.9 0.1 shard_map.160
  115.1 1.6 %collective-permute-start.6 = (f32[1,128]{1,0:T(1,128)S(1)}, f32[1,128]{1,0:T(1,128)S(1)}, u32[]{:S(2)}, u32[]{:S(2)}) collective-permute-start(f32[1,128]{1,0:T(1,128)S(1)} %get-tuple-element.30), channel_id=1, source_target_pairs={{0,1},{1,0},{2,3},{3,2},{4,5},{5,4},{6,7},{7,6},{8,9},{9,8},{10,11... | collective-permute-start | bytes 1544 | tf_op jit(solution)/shard_map/ppermute | solution.py:781
  116.7 2.0 %collective-permute-done.6 = f32[1,128]{1,0:T(1,128)S(1)} collective-permute-done((f32[1,128]{1,0:T(1,128)S(1)}, f32[1,128]{1,0:T(1,128)S(1)}, u32[]{:S(2)}, u32[]{:S(2)}) %collective-permute-start.6) | collective-permute-done | bytes 544 | tf_op jit(solution)/shard_map/ppermute | solution.py:781
  118.7 0.0 all-to-all-done.2.lag_ref
  118.7 1.1 shard_map.161
  (3 shorter events, 0.0 us)
Async XLA Ops:
  4.3 40.6 %all-to-all-start = ((bf16[16,400,128]{2,1,0:T(8,128)(2,1)}), bf16[16,400,128]{2,1,0:T(8,128)(2,1)}, u32[]{:S(2)}, u32[]{:S(2)}) async-start(bf16[16,400,128]{2,1,0:T(8,128)(2,1)} %shard_map.153.refs_4_), calls=%async_computation | async-start | bytes 3276800 | tf_op jit(solution)/shard_map/all_to_all | solution.py:759
  11.7 3.2 %copy-start.2 = (f32[3,2048]{1,0:T(4,128)S(1)}, f32[3,2048]{1,0:T(4,128)}, u32[]{:S(2)}) copy-start(f32[3,2048]{1,0:T(4,128)} %refs_5_.3) | copy-start | bytes 73732
  11.7 3.2 %copy-start.3 = (f32[2048]{0:T(1024)S(1)}, f32[2048]{0:T(1024)}, u32[]{:S(2)}) copy-start(f32[2048]{0:T(1024)} %param.16) | copy-start | bytes 24580
  54.4 33.4 %all-to-all-start.1 = ((bf16[16,272,128]{2,1,0:T(8,128)(2,1)}), bf16[16,272,128]{2,1,0:T(8,128)(2,1)S(1)}, u32[]{:S(2)}, u32[]{:S(2)}) async-start(bf16[16,272,128]{2,1,0:T(8,128)(2,1)} %get-tuple-element.21), calls=%async_computation.1 | async-start | bytes 2228224 | tf_op jit(solution)/shard_map/all_to_all | solution.py:759
  87.8 7.2 %copy-start.1 = (bf16[16,272,128]{2,1,0:T(8,128)(2,1)}, bf16[16,272,128]{2,1,0:T(8,128)(2,1)S(1)}, u32[]{:S(2)}) copy-start(bf16[16,272,128]{2,1,0:T(8,128)(2,1)S(1)} %all-to-all-done.1.refs_7_) | copy-start | bytes 3342340
  87.8 30.9 %all-to-all-start.2 = ((bf16[16,128,128]{2,1,0:T(8,128)(2,1)}), bf16[16,128,128]{2,1,0:T(8,128)(2,1)S(1)}, u32[]{:S(2)}, u32[]{:S(2)}) async-start(bf16[16,128,128]{2,1,0:T(8,128)(2,1)} %get-tuple-element.31), calls=%async_computation.2 | async-start | bytes 1048576 | tf_op jit(solution)/shard_map/all_to_all | solution.py:759
  100.8 4.0 %collective-permute-start.2 = (f32[4,2176]{1,0:T(4,128)}, f32[4,2176]{1,0:T(4,128)S(1)}, u32[]{:S(2)}, u32[]{:S(2)}) collective-permute-start(f32[4,2176]{1,0:T(4,128)} %get-tuple-element.28.value_ref), channel_id=1, source_target_pairs={{0,6},{2,4},{4,2},{6,0},{8,14},{10,12},{12,10},{14,8},{16,22},{18,... | collective-permute-start | bytes 104456 | tf_op jit(solution)/shard_map/ppermute | solution.py:781
  102.6 4.2 %collective-permute-start.1 = (f32[4,2176]{1,0:T(4,128)}, f32[4,2176]{1,0:T(4,128)S(1)}, u32[]{:S(2)}, u32[]{:S(2)}) collective-permute-start(f32[4,2176]{1,0:T(4,128)} %get-tuple-element.28.value_ref), channel_id=1, source_target_pairs={{0,4},{2,6},{4,0},{6,2},{8,12},{10,14},{12,8},{14,10},{16,20},{18,... | collective-permute-start | bytes 104456 | tf_op jit(solution)/shard_map/ppermute | solution.py:781
  103.0 3.8 %collective-permute-start = (f32[4,2176]{1,0:T(4,128)}, f32[4,2176]{1,0:T(4,128)S(1)}, u32[]{:S(2)}, u32[]{:S(2)}) collective-permute-start(f32[4,2176]{1,0:T(4,128)} %get-tuple-element.28.value_ref), channel_id=1, source_target_pairs={{0,2},{2,0},{4,6},{6,4},{8,10},{10,8},{12,14},{14,12},{16,18},{18,... | collective-permute-start | bytes 104456 | tf_op jit(solution)/shard_map/ppermute | solution.py:781
  103.0 0.8 copy-start
  106.7 5.9 %collective-permute-start.5 = (f32[4,2176]{1,0:T(4,128)S(1)}, f32[4,2176]{1,0:T(4,128)S(1)}, u32[]{:S(2)}, u32[]{:S(2)}) collective-permute-start(f32[4,2176]{1,0:T(4,128)S(1)} %shard_map.159.refs_0_), channel_id=1, source_target_pairs={{0,24},{2,26},{4,28},{6,30},{8,16},{10,18},{12,20},{14,22},{16,8},... | collective-permute-start | bytes 104456 | tf_op jit(solution)/shard_map/ppermute | solution.py:781
  110.1 4.8 %collective-permute-start.4 = (f32[4,2176]{1,0:T(4,128)S(1)}, f32[4,2176]{1,0:T(4,128)S(1)}, u32[]{:S(2)}, u32[]{:S(2)}) collective-permute-start(f32[4,2176]{1,0:T(4,128)S(1)} %shard_map.159.refs_0_), channel_id=1, source_target_pairs={{0,16},{2,18},{4,20},{6,22},{8,24},{10,26},{12,28},{14,30},{16,0},... | collective-permute-start | bytes 104456 | tf_op jit(solution)/shard_map/ppermute | solution.py:781
  110.5 4.4 %collective-permute-start.3 = (f32[4,2176]{1,0:T(4,128)S(1)}, f32[4,2176]{1,0:T(4,128)S(1)}, u32[]{:S(2)}, u32[]{:S(2)}) collective-permute-start(f32[4,2176]{1,0:T(4,128)S(1)} %shard_map.159.refs_0_), channel_id=1, source_target_pairs={{0,8},{2,10},{4,12},{6,14},{8,0},{10,2},{12,4},{14,6},{16,24},{18,... | collective-permute-start | bytes 104456 | tf_op jit(solution)/shard_map/ppermute | solution.py:781
  115.1 3.6 %collective-permute-start.6 = (f32[1,128]{1,0:T(1,128)S(1)}, f32[1,128]{1,0:T(1,128)S(1)}, u32[]{:S(2)}, u32[]{:S(2)}) collective-permute-start(f32[1,128]{1,0:T(1,128)S(1)} %get-tuple-element.30), channel_id=1, source_target_pairs={{0,1},{1,0},{2,3},{3,2},{4,5},{5,4},{6,7},{7,6},{8,9},{9,8},{10,11... | collective-permute-start | bytes 1544 | tf_op jit(solution)/shard_map/ppermute | solution.py:781

commit v14 on v13

--- a/solution.py
+++ b/solution.py
@@ -16,7 +16,7 @@
 CHUNK = 16
 CHUNKS = SPAN // CHUNK
 PAD = 8
-ROWS = 16
+ROWS = 32
 CUTS = 4
 PASSES = 1
 TILE_ROWS = 16
@@ -729,9 +729,7 @@
 def norm_kernel(*refs):
     values, totals_ref, square_ref = refs[:-2], refs[-2], refs[-1]
     channels = totals_ref.shape[1] - LANES
-    totals = values[0][...]
-    if len(values) == 4:
-        totals = (totals + values[1][...]) + (values[2][...] + values[3][...])
+    totals = add_up([value[...] for value in values])
     totals_ref[...] = totals
     square = jnp.sum(totals[:, :channels] * totals[:, :channels]) + jnp.sum(totals[0:1, channels:])
     square_ref[...] = jnp.full(square_ref.shape, square)
@@ -782,12 +780,7 @@
 
 
 def rounds_of(size):
-    rounds = []
-    step = 1
-    while step < size:
-        rounds.append((step, 2 * step, 3 * step) if size // step >= 4 else (step,))
-        step *= 4 if size // step >= 4 else 2
-    return rounds
+    return [(1 << bit,) for bit in range(size.bit_length() - 1)]
 
 
 def add_up(values):
@@ -805,7 +798,7 @@
     halo_rows = taps_count - 1
     groups = channels // LANES
     share = channels // pieces
-    per_step = min(groups, 2)
+    per_step = min(groups, 4)
     steps = groups // per_step
     lanes2 = cut_lanes(per_step * LANES, 2)
     lanes3 = cut_lanes(per_step * LANES, 3)
@@ -852,19 +845,18 @@
 
     totals = sums
     rounds = rounds_of(pieces)
-    for steps_of in rounds[:-1]:
+    for idx, steps_of in enumerate(rounds[:-1]):
         values = partners(totals, "ctx", steps_of)
-        values[0] = call(
-            same_kernel, jax.ShapeDtypeStruct(totals.shape, f32), [], totals,
-            vmem_bytes=SMALL_VMEM_BYTES, in_specs=[IN_VMEM], out_specs=IN_VMEM,
-        )
+        if idx == 0:
+            values[0] = call(
+                same_kernel, jax.ShapeDtypeStruct(totals.shape, f32), [], totals,
+                vmem_bytes=SMALL_VMEM_BYTES, in_specs=[IN_VMEM], out_specs=IN_VMEM,
+            )
         totals = call(
             add_kernel, jax.ShapeDtypeStruct(totals.shape, f32), [], *values,
             vmem_bytes=SMALL_VMEM_BYTES, in_specs=[IN_VMEM] * len(values), out_specs=IN_VMEM,
         )
     last = partners(totals, "ctx", rounds[-1])
-    if len(last) == 2:
-        last = [last[0] + last[1]]
 
     totals, norm_sq = call(
         norm_kernel,

time: 120 us -> 121 us (level)
    ppermute x7 -> x5, starting transfers between devices: 8.16 us -> 9.27 us  [partners(): lax.ppermute(value, axis, [(i, i ^ step) for i in range(size)])]
    ppermute x7 -> x5, waiting for transfers between devices: 8.71 us -> 8.37 us  [partners(): lax.ppermute(value, axis, [(i, i ^ step) for i in range(size)])]
    pallas_call x9 -> x11, Pallas kernels: 27.8 us -> 27.6 us  [call(): pl.pallas_call(kernel, out_shape=outs, scratch_shapes=scratch, compiler_p...]
  transfers between devices with their start and end apart: 10 -> 8, of which waited for: 7 -> 7; matrix products, arithmetic and copies ran while one was open for 1% -> 1% of each run, Pallas kernels for 11% -> 11%
where the time goes in v14:
time: 121 us; the launch traced here: 120 us
  waiting for transfers between devices  57.1 us (47%)
  starting transfers between devices  33.3 us (28%)
  Pallas kernels  27.6 us (23%)
    all_to_all x3, waiting for transfers between devices, exchange(): lax.all_to_all(pieces_first, 'ctx', split_axis=0, concat_axis=0, tiled=True)  48.8 us
    pallas_call x11, Pallas kernels, call(): pl.pallas_call(kernel, out_shape=outs, scratch_shapes=scratch, compiler_p...  27.6 us
    all_to_all x3, starting transfers between devices, exchange(): lax.all_to_all(pieces_first, 'ctx', split_axis=0, concat_axis=0, tiled=True)  24 us
    ppermute x5, starting transfers between devices, partners(): lax.ppermute(value, axis, [(i, i ^ step) for i in range(size)])  9.27 us
    ppermute x5, waiting for transfers between devices, partners(): lax.ppermute(value, axis, [(i, i ^ step) for i in range(size)])  8.37 us
  transfers between devices with their start and end apart: 8, of which 7 were waited for; matrix products, arithmetic and copies ran while one was open for 1% of the time, Pallas kernels for 11%

profile of v14, /device:TPU:0, one launch (start us, length us, event | category | flops | bytes accessed | tf_op | source)
XLA Modules:
  0.0 120.2 jit_solution(6704204908425221152)
XLA Ops:
  0.6 3.6 %shard_map.153.refs_4_ = bf16[16,400,128]{2,1,0:T(8,128)(2,1)} custom-call(bf16[128,2048]{1,0:T(8,128)(2,1)} %refs_0_.5, bf16[128,2048]{1,0:T(8,128)(2,1)} %refs_1_.5, bf16[128,2048]{1,0:T(8,128)(2,1)} %refs_2_.5, bf16[128,2048]{1,0:T(8,128)(2,1)} %refs_3_.5, f32[128,2048]{1,0:T(8,128)} %refs_4_.1, f32[3,2048]{1,0:T(4,128)} %refs_5_.3), custom_call_target="tpu_custom_call" | custom-call | tf_op jit(solution)/shard_map/pallas_call | solution.py:36
  4.2 7.4 %all-to-all-start = ((bf16[16,400,128]{2,1,0:T(8,128)(2,1)}), bf16[16,400,128]{2,1,0:T(8,128)(2,1)}, u32[]{:S(2)}, u32[]{:S(2)}) async-start(bf16[16,400,128]{2,1,0:T(8,128)(2,1)} %shard_map.153.refs_4_), calls=%async_computation | async-start | bytes 3276800 | tf_op jit(solution)/shard_map/all_to_all | solution.py:757
  11.6 0.0 copy-start.2
  11.7 0.0 copy-start.3
  11.7 3.3 %shard_map.154.after_ref.refs_4_ = f32[3,128,2048]{2,1,0:T(8,128)} custom-call(bf16[128,2048]{1,0:T(8,128)(2,1)} %refs_0_.5, bf16[128,2048]{1,0:T(8,128)(2,1)} %refs_1_.5, bf16[128,2048]{1,0:T(8,128)(2,1)} %refs_2_.5, f32[3,2048]{1,0:T(4,128)} %refs_5_.3, bf16[16,400,128]{2,1,0:T(8,128)(2,1)} %shard_map.153.refs_4_), custom_call_target="tpu_custom_call" | custom-call | tf_op jit(solution)/shard_map/pallas_call | solution.py:36
  15.0 0.0 copy-done.2
  15.0 0.0 copy-done.3
  15.0 0.7 fusion.taps_ref
  15.7 29.1 %all-to-all-done.signals_hbm = bf16[16,400,128]{2,1,0:T(8,128)(2,1)} async-done(((bf16[16,400,128]{2,1,0:T(8,128)(2,1)}), bf16[16,400,128]{2,1,0:T(8,128)(2,1)}, u32[]{:S(2)}, u32[]{:S(2)}) %all-to-all-start) | async-done | bytes 1638432 | tf_op jit(solution)/shard_map/all_to_all | solution.py:757
  44.8 9.5 %shard_map.155 = (bf16[16,272,128]{2,1,0:T(8,128)(2,1)}, bf16[4,512,256]{2,1,0:T(8,128)(2,1)}) custom-call(bf16[16,400,128]{2,1,0:T(8,128)(2,1)} %all-to-all-done.signals_hbm, f32[4,128]{1,0:T(4,128)} %fusion.taps_ref, f32[16,16]{1,0:T(8,128)} %constant.18.clone.coarse_ref, f32[2,8,16,128]{3,2,1,0:T(8,128)} %constant.19.clone.fine_ref, ...), custom_call_target="tpu_custom_call" | custom-call | tf_op jit(solution)/shard_map/pallas_call | solution.py:36
  54.4 9.4 %all-to-all-start.1 = ((bf16[16,272,128]{2,1,0:T(8,128)(2,1)}), bf16[16,272,128]{2,1,0:T(8,128)(2,1)S(1)}, u32[]{:S(2)}, u32[]{:S(2)}) async-start(bf16[16,272,128]{2,1,0:T(8,128)(2,1)} %get-tuple-element.21), calls=%async_computation.1 | async-start | bytes 2228224 | tf_op jit(solution)/shard_map/all_to_all | solution.py:757
  63.8 4.4 %shard_map.156 = (bf16[16,128,128]{2,1,0:T(8,128)(2,1)}, f32[1,128]{1,0:T(1,128)}) custom-call(bf16[4,512,256]{2,1,0:T(8,128)(2,1)} %get-tuple-element.22.split_hbm, f32[16,16]{1,0:T(8,128)} %constant.18.clone.coarse_ref, f32[2,8,16,128]{3,2,1,0:T(8,128)} %constant.19.clone.fine_ref, bf16[512,512]{1,0:T(8,128)(2,1)} %constant.20.clone.matrix_hbm), custom_call_target="tpu_custom_call" | custom-call | tf_op jit(solution)/shard_map/pallas_call | solution.py:36
  68.2 19.6 %all-to-all-done.1.refs_7_ = bf16[16,272,128]{2,1,0:T(8,128)(2,1)S(1)} async-done(((bf16[16,272,128]{2,1,0:T(8,128)(2,1)}), bf16[16,272,128]{2,1,0:T(8,128)(2,1)S(1)}, u32[]{:S(2)}, u32[]{:S(2)}) %all-to-all-start.1) | async-done | bytes 1114144 | tf_op jit(solution)/shard_map/all_to_all | solution.py:757
  87.8 0.0 copy-start.1
  87.8 7.2 %all-to-all-start.2 = ((bf16[16,128,128]{2,1,0:T(8,128)(2,1)}), bf16[16,128,128]{2,1,0:T(8,128)(2,1)S(1)}, u32[]{:S(2)}, u32[]{:S(2)}) async-start(bf16[16,128,128]{2,1,0:T(8,128)(2,1)} %get-tuple-element.31), calls=%async_computation.2 | async-start | bytes 1048576 | tf_op jit(solution)/shard_map/all_to_all | solution.py:757
  95.0 0.0 copy-done.1
  95.0 5.4 %shard_map.157 = (bf16[128,2048]{1,0:T(8,128)(2,1)}, bf16[128,2048]{1,0:T(8,128)(2,1)}, bf16[128,2048]{1,0:T(8,128)(2,1)}, bf16[128,2048]{1,0:T(8,128)(2,1)}, f32[4,2176]{1,0:T(4,128)}) custom-call(bf16[128,2048]{1,0:T(8,128)(2,1)} %refs_0_.5, bf16[128,2048]{1,0:T(8,128)(2,1)} %refs_1_.5, bf16[128,2048]{1,0:T(8,128)(2,1)} %refs_2_.5, ...), custom_call_target="tpu_custom_call" | custom-call | tf_op jit(solution)/shard_map/pallas_call | solution.py:36
  100.5 0.5 collective-permute-start
  100.9 0.0 copy-start
  100.9 0.8 copy-done
  101.7 0.3 collective-permute-done.refs_1_
  102.0 1.9 %collective-permute-start.1 = (f32[4,2176]{1,0:T(4,128)S(1)}, f32[4,2176]{1,0:T(4,128)S(1)}, u32[]{:S(2)}, u32[]{:S(2)}) collective-permute-start(f32[4,2176]{1,0:T(4,128)S(1)} %shard_map.159.refs_0_), channel_id=1, source_target_pairs={{0,4},{2,6},{4,0},{6,2},{8,12},{10,14},{12,8},{14,10},{16,20},{18,... | collective-permute-start | bytes 104456 | tf_op jit(solution)/shard_map/ppermute | solution.py:779
  103.9 2.2 %collective-permute-done.1.refs_1_ = f32[4,2176]{1,0:T(4,128)S(1)} collective-permute-done((f32[4,2176]{1,0:T(4,128)S(1)}, f32[4,2176]{1,0:T(4,128)S(1)}, u32[]{:S(2)}, u32[]{:S(2)}) %collective-permute-start.1) | collective-permute-done | bytes 34848 | tf_op jit(solution)/shard_map/ppermute | solution.py:779
  106.1 2.5 %collective-permute-start.2 = (f32[4,2176]{1,0:T(4,128)S(1)}, f32[4,2176]{1,0:T(4,128)S(1)}, u32[]{:S(2)}, u32[]{:S(2)}) collective-permute-start(f32[4,2176]{1,0:T(4,128)S(1)} %shard_map.160.refs_0_), channel_id=1, source_target_pairs={{0,8},{2,10},{4,12},{6,14},{8,0},{10,2},{12,4},{14,6},{16,24},{18,... | collective-permute-start | bytes 104456 | tf_op jit(solution)/shard_map/ppermute | solution.py:779
  108.5 1.9 %collective-permute-done.2.refs_1_ = f32[4,2176]{1,0:T(4,128)S(1)} collective-permute-done((f32[4,2176]{1,0:T(4,128)S(1)}, f32[4,2176]{1,0:T(4,128)S(1)}, u32[]{:S(2)}, u32[]{:S(2)}) %collective-permute-start.2) | collective-permute-done | bytes 34848 | tf_op jit(solution)/shard_map/ppermute | solution.py:779
  110.5 2.9 %collective-permute-start.3 = (f32[4,2176]{1,0:T(4,128)S(1)}, f32[4,2176]{1,0:T(4,128)S(1)}, u32[]{:S(2)}, u32[]{:S(2)}) collective-permute-start(f32[4,2176]{1,0:T(4,128)S(1)} %shard_map.161.refs_0_), channel_id=1, source_target_pairs={{0,16},{2,18},{4,20},{6,22},{8,24},{10,26},{12,28},{14,30},{16,0},... | collective-permute-start | bytes 104456 | tf_op jit(solution)/shard_map/ppermute | solution.py:779
  113.3 1.9 %collective-permute-done.3.refs_1_ = f32[4,2176]{1,0:T(4,128)S(1)} collective-permute-done((f32[4,2176]{1,0:T(4,128)S(1)}, f32[4,2176]{1,0:T(4,128)S(1)}, u32[]{:S(2)}, u32[]{:S(2)}) %collective-permute-start.3) | collective-permute-done | bytes 34848 | tf_op jit(solution)/shard_map/ppermute | solution.py:779
  115.3 0.1 shard_map.162
  115.4 1.6 %collective-permute-start.4 = (f32[1,128]{1,0:T(1,128)S(1)}, f32[1,128]{1,0:T(1,128)S(1)}, u32[]{:S(2)}, u32[]{:S(2)}) collective-permute-start(f32[1,128]{1,0:T(1,128)S(1)} %get-tuple-element.30), channel_id=1, source_target_pairs={{0,1},{1,0},{2,3},{3,2},{4,5},{5,4},{6,7},{7,6},{8,9},{9,8},{10,11... | collective-permute-start | bytes 1544 | tf_op jit(solution)/shard_map/ppermute | solution.py:779
  117.0 2.0 %collective-permute-done.4 = f32[1,128]{1,0:T(1,128)S(1)} collective-permute-done((f32[1,128]{1,0:T(1,128)S(1)}, f32[1,128]{1,0:T(1,128)S(1)}, u32[]{:S(2)}, u32[]{:S(2)}) %collective-permute-start.4) | collective-permute-done | bytes 544 | tf_op jit(solution)/shard_map/ppermute | solution.py:779
  119.0 0.0 all-to-all-done.2.lag_ref
  119.0 1.1 shard_map.163
  (5 shorter events, 0.0 us)
Async XLA Ops:
  4.2 40.6 %all-to-all-start = ((bf16[16,400,128]{2,1,0:T(8,128)(2,1)}), bf16[16,400,128]{2,1,0:T(8,128)(2,1)}, u32[]{:S(2)}, u32[]{:S(2)}) async-start(bf16[16,400,128]{2,1,0:T(8,128)(2,1)} %shard_map.153.refs_4_), calls=%async_computation | async-start | bytes 3276800 | tf_op jit(solution)/shard_map/all_to_all | solution.py:757
  11.6 3.4 %copy-start.2 = (f32[3,2048]{1,0:T(4,128)S(1)}, f32[3,2048]{1,0:T(4,128)}, u32[]{:S(2)}) copy-start(f32[3,2048]{1,0:T(4,128)} %refs_5_.3) | copy-start | bytes 73732
  11.7 3.3 %copy-start.3 = (f32[2048]{0:T(1024)S(1)}, f32[2048]{0:T(1024)}, u32[]{:S(2)}) copy-start(f32[2048]{0:T(1024)} %param.16) | copy-start | bytes 24580
  54.4 33.4 %all-to-all-start.1 = ((bf16[16,272,128]{2,1,0:T(8,128)(2,1)}), bf16[16,272,128]{2,1,0:T(8,128)(2,1)S(1)}, u32[]{:S(2)}, u32[]{:S(2)}) async-start(bf16[16,272,128]{2,1,0:T(8,128)(2,1)} %get-tuple-element.21), calls=%async_computation.1 | async-start | bytes 2228224 | tf_op jit(solution)/shard_map/all_to_all | solution.py:757
  87.8 7.2 %copy-start.1 = (bf16[16,272,128]{2,1,0:T(8,128)(2,1)}, bf16[16,272,128]{2,1,0:T(8,128)(2,1)S(1)}, u32[]{:S(2)}) copy-start(bf16[16,272,128]{2,1,0:T(8,128)(2,1)S(1)} %all-to-all-done.1.refs_7_) | copy-start | bytes 3342340
  87.8 31.3 %all-to-all-start.2 = ((bf16[16,128,128]{2,1,0:T(8,128)(2,1)}), bf16[16,128,128]{2,1,0:T(8,128)(2,1)S(1)}, u32[]{:S(2)}, u32[]{:S(2)}) async-start(bf16[16,128,128]{2,1,0:T(8,128)(2,1)} %get-tuple-element.31), calls=%async_computation.2 | async-start | bytes 1048576 | tf_op jit(solution)/shard_map/all_to_all | solution.py:757
  100.5 1.5 %collective-permute-start = (f32[4,2176]{1,0:T(4,128)}, f32[4,2176]{1,0:T(4,128)S(1)}, u32[]{:S(2)}, u32[]{:S(2)}) collective-permute-start(f32[4,2176]{1,0:T(4,128)} %get-tuple-element.28.value_ref), channel_id=1, source_target_pairs={{0,2},{2,0},{4,6},{6,4},{8,10},{10,8},{12,14},{14,12},{16,18},{18,... | collective-permute-start | bytes 104456 | tf_op jit(solution)/shard_map/ppermute | solution.py:779
  100.9 0.8 copy-start
  102.0 4.0 %collective-permute-start.1 = (f32[4,2176]{1,0:T(4,128)S(1)}, f32[4,2176]{1,0:T(4,128)S(1)}, u32[]{:S(2)}, u32[]{:S(2)}) collective-permute-start(f32[4,2176]{1,0:T(4,128)S(1)} %shard_map.159.refs_0_), channel_id=1, source_target_pairs={{0,4},{2,6},{4,0},{6,2},{8,12},{10,14},{12,8},{14,10},{16,20},{18,... | collective-permute-start | bytes 104456 | tf_op jit(solution)/shard_map/ppermute | solution.py:779
  106.1 4.4 %collective-permute-start.2 = (f32[4,2176]{1,0:T(4,128)S(1)}, f32[4,2176]{1,0:T(4,128)S(1)}, u32[]{:S(2)}, u32[]{:S(2)}) collective-permute-start(f32[4,2176]{1,0:T(4,128)S(1)} %shard_map.160.refs_0_), channel_id=1, source_target_pairs={{0,8},{2,10},{4,12},{6,14},{8,0},{10,2},{12,4},{14,6},{16,24},{18,... | collective-permute-start | bytes 104456 | tf_op jit(solution)/shard_map/ppermute | solution.py:779
  110.5 4.8 %collective-permute-start.3 = (f32[4,2176]{1,0:T(4,128)S(1)}, f32[4,2176]{1,0:T(4,128)S(1)}, u32[]{:S(2)}, u32[]{:S(2)}) collective-permute-start(f32[4,2176]{1,0:T(4,128)S(1)} %shard_map.161.refs_0_), channel_id=1, source_target_pairs={{0,16},{2,18},{4,20},{6,22},{8,24},{10,26},{12,28},{14,30},{16,0},... | collective-permute-start | bytes 104456 | tf_op jit(solution)/shard_map/ppermute | solution.py:779
  115.4 3.6 %collective-permute-start.4 = (f32[1,128]{1,0:T(1,128)S(1)}, f32[1,128]{1,0:T(1,128)S(1)}, u32[]{:S(2)}, u32[]{:S(2)}) collective-permute-start(f32[1,128]{1,0:T(1,128)S(1)} %get-tuple-element.30), channel_id=1, source_target_pairs={{0,1},{1,0},{2,3},{3,2},{4,5},{5,4},{6,7},{7,6},{8,9},{9,8},{10,11... | collective-permute-start | bytes 1544 | tf_op jit(solution)/shard_map/ppermute | solution.py:779

commit v15 on v13

--- a/solution.py
+++ b/solution.py
@@ -16,8 +16,8 @@
 CHUNK = 16
 CHUNKS = SPAN // CHUNK
 PAD = 8
-ROWS = 16
-CUTS = 4
+ROWS = 32
+CUTS = 1
 PASSES = 1
 TILE_ROWS = 16
 VMEM_BYTES = 60 * 1024 * 1024
@@ -729,9 +729,7 @@
 def norm_kernel(*refs):
     values, totals_ref, square_ref = refs[:-2], refs[-2], refs[-1]
     channels = totals_ref.shape[1] - LANES
-    totals = values[0][...]
-    if len(values) == 4:
-        totals = (totals + values[1][...]) + (values[2][...] + values[3][...])
+    totals = add_up([value[...] for value in values]) if len(values) > 1 else values[0][...]
     totals_ref[...] = totals
     square = jnp.sum(totals[:, :channels] * totals[:, :channels]) + jnp.sum(totals[0:1, channels:])
     square_ref[...] = jnp.full(square_ref.shape, square)
@@ -739,6 +737,12 @@
 
 def add_kernel(*refs):
     refs[-1][...] = add_up([ref[...] for ref in refs[:-1]])
+
+
+def halves_kernel(odd_ref, own_ref, one_ref, two_ref, three_ref, four_ref, total_ref):
+    even_sum = (own_ref[...] + one_ref[...]) + (two_ref[...] + three_ref[...])
+    odd_sum = (one_ref[...] + two_ref[...]) + (three_ref[...] + four_ref[...])
+    total_ref[...] = jnp.where(odd_ref[0] == 1, odd_sum, even_sum)
 
 
 def same_kernel(value_ref, same_ref):
@@ -788,6 +792,15 @@
         rounds.append((step, 2 * step, 3 * step) if size // step >= 4 else (step,))
         step *= 4 if size // step >= 4 else 2
     return rounds
+
+
+def halved_partners(value, axis):
+    size = lax.axis_size(axis)
+    heard = [value]
+    for idx in range(1, 4):
+        heard.append(lax.ppermute(value, axis, [(i, i ^ 2 * (idx + 3 * (i % 2))) for i in range(size)]))
+    heard.append(lax.ppermute(value, axis, [(i, i ^ 14) for i in range(1, size, 2)]))
+    return heard
 
 
 def add_up(values):
@@ -805,7 +818,7 @@
     halo_rows = taps_count - 1
     groups = channels // LANES
     share = channels // pieces
-    per_step = min(groups, 2)
+    per_step = min(groups, 4)
     steps = groups // per_step
     lanes2 = cut_lanes(per_step * LANES, 2)
     lanes3 = cut_lanes(per_step * LANES, 3)
@@ -850,25 +863,36 @@
         kept=[jax.ShapeDtypeStruct((taps_count + 1, channels + LANES), f32)],
     )
 
-    totals = sums
-    rounds = rounds_of(pieces)
-    for steps_of in rounds[:-1]:
-        values = partners(totals, "ctx", steps_of)
+    total_shape = jax.ShapeDtypeStruct(sums.shape, f32)
+
+    def add(values):
+        return call(
+            add_kernel, total_shape, [], *values,
+            vmem_bytes=SMALL_VMEM_BYTES, in_specs=[IN_VMEM] * len(values), out_specs=IN_VMEM,
+        )
+
+    if pieces >= 16:
+        values = partners(sums, "ctx", (1,))
         values[0] = call(
-            same_kernel, jax.ShapeDtypeStruct(totals.shape, f32), [], totals,
+            same_kernel, total_shape, [], sums,
             vmem_bytes=SMALL_VMEM_BYTES, in_specs=[IN_VMEM], out_specs=IN_VMEM,
         )
-        totals = call(
-            add_kernel, jax.ShapeDtypeStruct(totals.shape, f32), [], *values,
-            vmem_bytes=SMALL_VMEM_BYTES, in_specs=[IN_VMEM] * len(values), out_specs=IN_VMEM,
+        odd = (lax.axis_index("ctx") % 2).reshape(1)
+        halves = call(
+            halves_kernel, total_shape, [], odd, *halved_partners(add(values), "ctx"),
+            vmem_bytes=SMALL_VMEM_BYTES, in_specs=[IN_SMEM] + [IN_VMEM] * 5, out_specs=IN_VMEM,
         )
-    last = partners(totals, "ctx", rounds[-1])
-    if len(last) == 2:
-        last = [last[0] + last[1]]
+        last = partners(halves, "ctx", (1,))
+        rounds = [tuple(16 * step for step in steps_of) for steps_of in rounds_of(pieces // 16)]
+    else:
+        last = [sums]
+        rounds = rounds_of(pieces)
+    for steps_of in rounds:
+        last = partners(add(last) if len(last) > 1 else last[0], "ctx", steps_of)
 
     totals, norm_sq = call(
         norm_kernel,
-        (jax.ShapeDtypeStruct(totals.shape, f32), jax.ShapeDtypeStruct((1, LANES), f32)),
+        (total_shape, jax.ShapeDtypeStruct((1, LANES), f32)),
         [], *last,
         vmem_bytes=SMALL_VMEM_BYTES,
         in_specs=[IN_VMEM] * len(last), out_specs=(IN_VMEM, IN_VMEM),

time: 120 us -> 120 us (level)
  waiting for transfers between devices: 57.6 us -> 56 us
  starting transfers between devices: 32.2 us -> 33.7 us
    ppermute x7 -> x3, waiting for transfers between devices: 8.71 us -> 3.19 us  [partners(): lax.ppermute(value, axis, [(i, i ^ step) for i in range(size)])]
    ppermute x0 -> x4, starting transfers between devices: none -> 4.21 us  [the longest x3 3.55 us: halved_partners(): lax.ppermute(value, axis, [(i, i ^ 2 * (idx + 3 * (i % 2))) for i in rang...]
    ppermute x0 -> x4, waiting for transfers between devices: none -> 4.13 us  [the longest x3 4.13 us: halved_partners(): lax.ppermute(value, axis, [(i, i ^ 2 * (idx + 3 * (i % 2))) for i in rang...]
    ppermute x7 -> x3, starting transfers between devices: 8.16 us -> 5.52 us  [partners(): lax.ppermute(value, axis, [(i, i ^ step) for i in range(size)])]
    pallas_call x9 -> x10, Pallas kernels: 27.8 us -> 27.4 us  [call(): pl.pallas_call(kernel, out_shape=outs, scratch_shapes=scratch, compiler_p...]
  transfers between devices with their start and end apart: 10 -> 10, of which waited for: 7 -> 8; matrix products, arithmetic and copies ran while one was open for 1% -> 1% of each run, Pallas kernels for 11% -> 11%
where the time goes in v15:
time: 120 us; the launch traced here: 119 us
  waiting for transfers between devices  56 us (47%)
  starting transfers between devices  33.7 us (28%)
  Pallas kernels  27.4 us (23%)
    all_to_all x3, waiting for transfers between devices, exchange(): lax.all_to_all(pieces_first, 'ctx', split_axis=0, concat_axis=0, tiled=True)  48.7 us
    pallas_call x10, Pallas kernels, call(): pl.pallas_call(kernel, out_shape=outs, scratch_shapes=scratch, compiler_p...  27.4 us
    all_to_all x3, starting transfers between devices, exchange(): lax.all_to_all(pieces_first, 'ctx', split_axis=0, concat_axis=0, tiled=True)  24 us
    ppermute x3, starting transfers between devices, partners(): lax.ppermute(value, axis, [(i, i ^ step) for i in range(size)])  5.52 us
    ppermute x3, waiting for transfers between devices, halved_partners(): lax.ppermute(value, axis, [(i, i ^ 2 * (idx + 3 * (i % 2))) for i in rang...  4.13 us
    ppermute x3, starting transfers between devices, halved_partners(): lax.ppermute(value, axis, [(i, i ^ 2 * (idx + 3 * (i % 2))) for i in rang...  3.55 us
    ppermute x3, waiting for transfers between devices, partners(): lax.ppermute(value, axis, [(i, i ^ step) for i in range(size)])  3.19 us
  transfers between devices with their start and end apart: 10, of which 8 were waited for; matrix products, arithmetic and copies ran while one was open for 1% of the time, Pallas kernels for 11%

profile of v15, /device:TPU:0, one launch (start us, length us, event | category | flops | bytes accessed | tf_op | source)
XLA Modules:
  0.0 119.4 jit_solution(12713394030449287022)
XLA Ops:
  0.6 3.6 %shard_map.153.refs_4_ = bf16[16,400,128]{2,1,0:T(8,128)(2,1)} custom-call(bf16[128,2048]{1,0:T(8,128)(2,1)} %refs_0_.5, bf16[128,2048]{1,0:T(8,128)(2,1)} %refs_1_.5, bf16[128,2048]{1,0:T(8,128)(2,1)} %refs_2_.5, bf16[128,2048]{1,0:T(8,128)(2,1)} %refs_3_.5, f32[128,2048]{1,0:T(8,128)} %refs_4_.1, f32[3,2048]{1,0:T(4,128)} %refs_5_.3), custom_call_target="tpu_custom_call" | custom-call | tf_op jit(solution)/shard_map/pallas_call | solution.py:36
  4.2 7.4 %all-to-all-start = ((bf16[16,400,128]{2,1,0:T(8,128)(2,1)}), bf16[16,400,128]{2,1,0:T(8,128)(2,1)}, u32[]{:S(2)}, u32[]{:S(2)}) async-start(bf16[16,400,128]{2,1,0:T(8,128)(2,1)} %shard_map.153.refs_4_), calls=%async_computation | async-start | bytes 3276800 | tf_op jit(solution)/shard_map/all_to_all | solution.py:763
  11.7 0.0 copy-start.2
  11.7 0.0 copy-start.3
  11.7 3.4 %shard_map.154.after_ref.refs_4_ = f32[3,128,2048]{2,1,0:T(8,128)} custom-call(bf16[128,2048]{1,0:T(8,128)(2,1)} %refs_0_.5, bf16[128,2048]{1,0:T(8,128)(2,1)} %refs_1_.5, bf16[128,2048]{1,0:T(8,128)(2,1)} %refs_2_.5, f32[3,2048]{1,0:T(4,128)} %refs_5_.3, bf16[16,400,128]{2,1,0:T(8,128)(2,1)} %shard_map.153.refs_4_), custom_call_target="tpu_custom_call" | custom-call | tf_op jit(solution)/shard_map/pallas_call | solution.py:36
  15.1 0.0 copy-done.2
  15.1 0.0 copy-done.3
  15.1 0.7 fusion.taps_ref
  15.7 29.1 %all-to-all-done.signals_hbm = bf16[16,400,128]{2,1,0:T(8,128)(2,1)} async-done(((bf16[16,400,128]{2,1,0:T(8,128)(2,1)}), bf16[16,400,128]{2,1,0:T(8,128)(2,1)}, u32[]{:S(2)}, u32[]{:S(2)}) %all-to-all-start) | async-done | bytes 1638432 | tf_op jit(solution)/shard_map/all_to_all | solution.py:763
  44.8 9.4 %shard_map.155 = (bf16[16,272,128]{2,1,0:T(8,128)(2,1)}, bf16[4,512,256]{2,1,0:T(8,128)(2,1)}) custom-call(bf16[16,400,128]{2,1,0:T(8,128)(2,1)} %all-to-all-done.signals_hbm, f32[4,128]{1,0:T(4,128)} %fusion.taps_ref, f32[16,16]{1,0:T(8,128)} %constant.30.clone.coarse_ref, f32[2,8,16,128]{3,2,1,0:T(8,128)} %constant.31.clone.fine_ref, ...), custom_call_target="tpu_custom_call" | custom-call | tf_op jit(solution)/shard_map/pallas_call | solution.py:36
  54.2 9.4 %all-to-all-start.1 = ((bf16[16,272,128]{2,1,0:T(8,128)(2,1)}), bf16[16,272,128]{2,1,0:T(8,128)(2,1)S(1)}, u32[]{:S(2)}, u32[]{:S(2)}) async-start(bf16[16,272,128]{2,1,0:T(8,128)(2,1)} %get-tuple-element.21), calls=%async_computation.1 | async-start | bytes 2228224 | tf_op jit(solution)/shard_map/all_to_all | solution.py:763
  63.6 4.4 %shard_map.156 = (bf16[16,128,128]{2,1,0:T(8,128)(2,1)}, f32[1,128]{1,0:T(1,128)}) custom-call(bf16[4,512,256]{2,1,0:T(8,128)(2,1)} %get-tuple-element.22.split_hbm, f32[16,16]{1,0:T(8,128)} %constant.30.clone.coarse_ref, f32[2,8,16,128]{3,2,1,0:T(8,128)} %constant.31.clone.fine_ref, bf16[512,512]{1,0:T(8,128)(2,1)} %constant.32.clone.matrix_hbm), custom_call_target="tpu_custom_call" | custom-call | tf_op jit(solution)/shard_map/pallas_call | solution.py:36
  68.0 19.6 %all-to-all-done.1.refs_7_ = bf16[16,272,128]{2,1,0:T(8,128)(2,1)S(1)} async-done(((bf16[16,272,128]{2,1,0:T(8,128)(2,1)}), bf16[16,272,128]{2,1,0:T(8,128)(2,1)S(1)}, u32[]{:S(2)}, u32[]{:S(2)}) %all-to-all-start.1) | async-done | bytes 1114144 | tf_op jit(solution)/shard_map/all_to_all | solution.py:763
  87.6 0.0 copy-start.1
  87.6 7.2 %all-to-all-start.2 = ((bf16[16,128,128]{2,1,0:T(8,128)(2,1)}), bf16[16,128,128]{2,1,0:T(8,128)(2,1)S(1)}, u32[]{:S(2)}, u32[]{:S(2)}) async-start(bf16[16,128,128]{2,1,0:T(8,128)(2,1)} %get-tuple-element.31), calls=%async_computation.2 | async-start | bytes 1048576 | tf_op jit(solution)/shard_map/all_to_all | solution.py:763
  94.8 0.0 copy-done.1
  94.8 5.4 %shard_map.157 = (bf16[128,2048]{1,0:T(8,128)(2,1)}, bf16[128,2048]{1,0:T(8,128)(2,1)}, bf16[128,2048]{1,0:T(8,128)(2,1)}, bf16[128,2048]{1,0:T(8,128)(2,1)}, f32[4,2176]{1,0:T(4,128)}) custom-call(bf16[128,2048]{1,0:T(8,128)(2,1)} %refs_0_.5, bf16[128,2048]{1,0:T(8,128)(2,1)} %refs_1_.5, bf16[128,2048]{1,0:T(8,128)(2,1)} %refs_2_.5, ...), custom_call_target="tpu_custom_call" | custom-call | tf_op jit(solution)/shard_map/pallas_call | solution.py:36
  100.3 0.5 collective-permute-start
  100.8 0.0 copy-start
  100.8 0.8 copy-done
  101.5 0.3 collective-permute-done.refs_1_
  101.8 0.7 collective-permute-start.4
  102.5 2.8 %collective-permute-start.3 = (f32[4,2176]{1,0:T(4,128)S(1)}, f32[4,2176]{1,0:T(4,128)S(1)}, u32[]{:S(2)}, u32[]{:S(2)}) collective-permute-start(f32[4,2176]{1,0:T(4,128)S(1)} %shard_map.159.own_ref), channel_id=1, source_target_pairs={{0,12},{2,26},{4,8},{6,30},{8,4},{10,18},{12,0},{14,22},{16,28},{1... | collective-permute-start | bytes 104456 | tf_op jit(solution)/shard_map/ppermute | solution.py:801
  105.3 0.6 collective-permute-start.2
  105.9 0.2 collective-permute-start.1
  106.1 0.0 collective-permute-done.4.four_ref
  106.1 1.5 %collective-permute-done.3.three_ref = f32[4,2176]{1,0:T(4,128)S(1)} collective-permute-done((f32[4,2176]{1,0:T(4,128)S(1)}, f32[4,2176]{1,0:T(4,128)S(1)}, u32[]{:S(2)}, u32[]{:S(2)}) %collective-permute-start.3) | collective-permute-done | bytes 34848 | tf_op jit(solution)/shard_map/ppermute | solution.py:801
  107.5 1.9 %collective-permute-done.2.two_ref = f32[4,2176]{1,0:T(4,128)S(1)} collective-permute-done((f32[4,2176]{1,0:T(4,128)S(1)}, f32[4,2176]{1,0:T(4,128)S(1)}, u32[]{:S(2)}, u32[]{:S(2)}) %collective-permute-start.2) | collective-permute-done | bytes 34848 | tf_op jit(solution)/shard_map/ppermute | solution.py:801
  109.4 0.8 collective-permute-done.1.one_ref
  110.2 3.5 %collective-permute-start.5 = (f32[4,2176]{1,0:T(4,128)S(1)}, f32[4,2176]{1,0:T(4,128)S(1)}, u32[]{:S(2)}, u32[]{:S(2)}) collective-permute-start(f32[4,2176]{1,0:T(4,128)S(1)} %shard_map.160.refs_0_), channel_id=1, source_target_pairs={{0,2},{2,0},{4,6},{6,4},{8,10},{10,8},{12,14},{14,12},{16,18},{18,... | collective-permute-start | bytes 104456 | tf_op jit(solution)/shard_map/ppermute | solution.py:785
  113.7 0.9 collective-permute-done.5.refs_1_
  114.5 0.1 shard_map.161
  114.7 1.6 %collective-permute-start.6 = (f32[1,128]{1,0:T(1,128)S(1)}, f32[1,128]{1,0:T(1,128)S(1)}, u32[]{:S(2)}, u32[]{:S(2)}) collective-permute-start(f32[1,128]{1,0:T(1,128)S(1)} %get-tuple-element.30), channel_id=1, source_target_pairs={{0,1},{1,0},{2,3},{3,2},{4,5},{5,4},{6,7},{7,6},{8,9},{9,8},{10,11... | collective-permute-start | bytes 1544 | tf_op jit(solution)/shard_map/ppermute | solution.py:785
  116.3 2.0 %collective-permute-done.6 = f32[1,128]{1,0:T(1,128)S(1)} collective-permute-done((f32[1,128]{1,0:T(1,128)S(1)}, f32[1,128]{1,0:T(1,128)S(1)}, u32[]{:S(2)}, u32[]{:S(2)}) %collective-permute-start.6) | collective-permute-done | bytes 544 | tf_op jit(solution)/shard_map/ppermute | solution.py:785
  118.3 0.0 all-to-all-done.2.lag_ref
  118.3 1.1 shard_map.162
  (4 shorter events, 0.0 us)
Async XLA Ops:
  4.2 40.6 %all-to-all-start = ((bf16[16,400,128]{2,1,0:T(8,128)(2,1)}), bf16[16,400,128]{2,1,0:T(8,128)(2,1)}, u32[]{:S(2)}, u32[]{:S(2)}) async-start(bf16[16,400,128]{2,1,0:T(8,128)(2,1)} %shard_map.153.refs_4_), calls=%async_computation | async-start | bytes 3276800 | tf_op jit(solution)/shard_map/all_to_all | solution.py:763
  11.7 3.4 %copy-start.2 = (f32[3,2048]{1,0:T(4,128)S(1)}, f32[3,2048]{1,0:T(4,128)}, u32[]{:S(2)}) copy-start(f32[3,2048]{1,0:T(4,128)} %refs_5_.3) | copy-start | bytes 73732
  11.7 3.4 %copy-start.3 = (f32[2048]{0:T(1024)S(1)}, f32[2048]{0:T(1024)}, u32[]{:S(2)}) copy-start(f32[2048]{0:T(1024)} %param.16) | copy-start | bytes 24580
  54.2 33.4 %all-to-all-start.1 = ((bf16[16,272,128]{2,1,0:T(8,128)(2,1)}), bf16[16,272,128]{2,1,0:T(8,128)(2,1)S(1)}, u32[]{:S(2)}, u32[]{:S(2)}) async-start(bf16[16,272,128]{2,1,0:T(8,128)(2,1)} %get-tuple-element.21), calls=%async_computation.1 | async-start | bytes 2228224 | tf_op jit(solution)/shard_map/all_to_all | solution.py:763
  87.6 7.2 %copy-start.1 = (bf16[16,272,128]{2,1,0:T(8,128)(2,1)}, bf16[16,272,128]{2,1,0:T(8,128)(2,1)S(1)}, u32[]{:S(2)}) copy-start(bf16[16,272,128]{2,1,0:T(8,128)(2,1)S(1)} %all-to-all-done.1.refs_7_) | copy-start | bytes 3342340
  87.6 30.7 %all-to-all-start.2 = ((bf16[16,128,128]{2,1,0:T(8,128)(2,1)}), bf16[16,128,128]{2,1,0:T(8,128)(2,1)S(1)}, u32[]{:S(2)}, u32[]{:S(2)}) async-start(bf16[16,128,128]{2,1,0:T(8,128)(2,1)} %get-tuple-element.31), calls=%async_computation.2 | async-start | bytes 1048576 | tf_op jit(solution)/shard_map/all_to_all | solution.py:763
  100.3 1.5 %collective-permute-start = (f32[4,2176]{1,0:T(4,128)}, f32[4,2176]{1,0:T(4,128)S(1)}, u32[]{:S(2)}, u32[]{:S(2)}) collective-permute-start(f32[4,2176]{1,0:T(4,128)} %get-tuple-element.28.value_ref), channel_id=1, source_target_pairs={{0,2},{2,0},{4,6},{6,4},{8,10},{10,8},{12,14},{14,12},{16,18},{18,... | collective-permute-start | bytes 104456 | tf_op jit(solution)/shard_map/ppermute | solution.py:785
  100.8 0.8 copy-start
  101.8 4.2 %collective-permute-start.4 = (f32[4,2176]{1,0:T(4,128)S(1)}, f32[4,2176]{1,0:T(4,128)S(1)}, u32[]{:S(2)}, u32[]{:S(2)}) collective-permute-start(f32[4,2176]{1,0:T(4,128)S(1)} %shard_map.159.own_ref), channel_id=1, source_target_pairs={{2,30},{6,26},{10,22},{14,18},{18,14},{22,10},{26,6},{30,2},{3,31}... | collective-permute-start | bytes 104456 | tf_op jit(solution)/shard_map/ppermute | solution.py:802
  102.5 5.0 %collective-permute-start.3 = (f32[4,2176]{1,0:T(4,128)S(1)}, f32[4,2176]{1,0:T(4,128)S(1)}, u32[]{:S(2)}, u32[]{:S(2)}) collective-permute-start(f32[4,2176]{1,0:T(4,128)S(1)} %shard_map.159.own_ref), channel_id=1, source_target_pairs={{0,12},{2,26},{4,8},{6,30},{8,4},{10,18},{12,0},{14,22},{16,28},{1... | collective-permute-start | bytes 104456 | tf_op jit(solution)/shard_map/ppermute | solution.py:801
  105.3 4.1 %collective-permute-start.2 = (f32[4,2176]{1,0:T(4,128)S(1)}, f32[4,2176]{1,0:T(4,128)S(1)}, u32[]{:S(2)}, u32[]{:S(2)}) collective-permute-start(f32[4,2176]{1,0:T(4,128)S(1)} %shard_map.159.own_ref), channel_id=1, source_target_pairs={{0,8},{2,22},{4,12},{6,18},{8,0},{10,30},{12,4},{14,26},{16,24},{1... | collective-permute-start | bytes 104456 | tf_op jit(solution)/shard_map/ppermute | solution.py:801
  105.9 4.3 %collective-permute-start.1 = (f32[4,2176]{1,0:T(4,128)S(1)}, f32[4,2176]{1,0:T(4,128)S(1)}, u32[]{:S(2)}, u32[]{:S(2)}) collective-permute-start(f32[4,2176]{1,0:T(4,128)S(1)} %shard_map.159.own_ref), channel_id=1, source_target_pairs={{0,4},{2,18},{4,0},{6,22},{8,12},{10,26},{12,8},{14,30},{16,20},{1... | collective-permute-start | bytes 104456 | tf_op jit(solution)/shard_map/ppermute | solution.py:801
  110.2 4.3 %collective-permute-start.5 = (f32[4,2176]{1,0:T(4,128)S(1)}, f32[4,2176]{1,0:T(4,128)S(1)}, u32[]{:S(2)}, u32[]{:S(2)}) collective-permute-start(f32[4,2176]{1,0:T(4,128)S(1)} %shard_map.160.refs_0_), channel_id=1, source_target_pairs={{0,2},{2,0},{4,6},{6,4},{8,10},{10,8},{12,14},{14,12},{16,18},{18,... | collective-permute-start | bytes 104456 | tf_op jit(solution)/shard_map/ppermute | solution.py:785
  114.7 3.6 %collective-permute-start.6 = (f32[1,128]{1,0:T(1,128)S(1)}, f32[1,128]{1,0:T(1,128)S(1)}, u32[]{:S(2)}, u32[]{:S(2)}) collective-permute-start(f32[1,128]{1,0:T(1,128)S(1)} %get-tuple-element.30), channel_id=1, source_target_pairs={{0,1},{1,0},{2,3},{3,2},{4,5},{5,4},{6,7},{7,6},{8,9},{9,8},{10,11... | collective-permute-start | bytes 1544 | tf_op jit(solution)/shard_map/ppermute | solution.py:785

commit v16 on v15

--- a/solution.py
+++ b/solution.py
@@ -313,13 +313,13 @@
                 extras[piece], extras[piece + 1], taps, skip,
                 [conv[row : row + 1] for row in range(count)], [corr[row : row + 1] for row in range(count)],
             )
-        spare = results_ref.shape[1] - 2 * rows_here - len(rows)
+        spare = results_ref.shape[1] - 3 * rows_here - len(rows)
         rows.append(jnp.zeros((spare, LANES), f32))
-        results_ref[piece, 2 * rows_here :, :] = jnp.concatenate(rows, axis=0).astype(bf16)
+        results_ref[piece, 3 * rows_here :, :] = jnp.concatenate(rows, axis=0).astype(bf16)
 
 
 def products_kernel(
-    rows_here, signals_hbm, taps_ref, coarse_ref, fine_ref, matrix_hbm, after_ref, results_hbm, lag_hbm,
+    rows_here, signals_hbm, taps_ref, coarse_ref, fine_ref, matrix_hbm, after_ref, results_hbm, square_ref,
     signals_ref, twist_ref, matrix_ref, heads_ref, results_ref, one_split, two_split, lag_split,
     filter_ref, product_ref, cotan_ref, time_ref, sems,
 ):
@@ -342,13 +342,9 @@
         for cut in range(CUTS)
     ]
     signal_copies = [cut_copies(signals_hbm, signals_ref, (kind * rows_here, rows_here)) for kind in range(2)]
-    lag_copies = [
-        pltpu.make_async_copy(lag_split.at[pair], lag_hbm.at[pair], sems.at[next(sem_idx)])
-        for pair in range(lag_split.shape[0])
-    ]
     return_copies = [
         cut_copies(results_ref, results_hbm, rows)
-        for rows in ((0, rows_here), (rows_here, back_rows - rows_here))
+        for rows in ((0, rows_here), (rows_here, rows_here), (2 * rows_here, back_rows - 2 * rows_here))
     ]
 
     def start_all(copies):
@@ -370,7 +366,7 @@
         def write(piece, rows, value, carry):
             place = pl.ds(kind * rows_here + rows.start, CHUNK)
             results_ref[piece, place, :] = value.astype(bf16)
-            return carry
+            return carry + value * value if kind == 2 else carry
 
         return signal_stage(from_ref, twist_ref, rows_here, write)
 
@@ -388,36 +384,14 @@
         [combine(product_ref, cotan_ref, lag_split, True), result(0, time_ref)],
         rows_here, (matrix_ref, one_split, filter_ref),
     )
-    start_all(return_copies[0] + lag_copies)
-    run_all([result(1, filter_ref)], rows_here)
+    start_all(return_copies[0])
+    run_all([result(1, filter_ref)], rows_here, (matrix_ref, lag_split, time_ref))
+    start_all(return_copies[1])
     write_edges(signals_ref, results_ref, taps_ref, rows_here)
-    start_all(return_copies[1])
-    wait_all(lag_copies + return_copies[0] + return_copies[1])
-
-
-def lag_kernel(
-    split_hbm, coarse_ref, fine_ref, matrix_hbm, lag_ref, square_ref, twist_ref, matrix_ref, split_ref, time_ref, sems
-):
-    rows_here = lag_ref.shape[1]
-    copies = [
-        pltpu.make_async_copy(matrix_hbm, matrix_ref, sems.at[0]),
-        pltpu.make_async_copy(split_hbm, split_ref, sems.at[1]),
-    ]
-    for copy in copies:
-        copy.start()
-    run_all([twist_stage(coarse_ref, fine_ref, twist_ref, rows_here)], rows_here)
-    for copy in copies:
-        copy.wait()
-    run_all([], rows_here, (matrix_ref, split_ref, time_ref))
-
-    def write(piece, rows, value, carry):
-        lag_ref[piece, rows, :] = value.astype(bf16)
-        return carry + value * value
-
-    square = run_all(
-        [signal_stage(time_ref, twist_ref, rows_here, write)], rows_here, None, jnp.zeros((CHUNK, LANES), f32)
-    )
+    square = run_all([result(2, time_ref)], rows_here, None, jnp.zeros((CHUNK, LANES), f32))
+    start_all(return_copies[2])
     square_ref[...] = jnp.sum(square, axis=0, keepdims=True)
+    wait_all(return_copies[0] + return_copies[1] + return_copies[2])
 
 
 class Transforms:
@@ -433,7 +407,7 @@
         ]
         self.split = jax.ShapeDtypeStruct((pairs, PASSES * BOTH, 2 * LANES), bf16)
         self.signal = jax.ShapeDtypeStruct((pieces, rows_here, LANES), bf16)
-        self.result = jax.ShapeDtypeStruct((pieces, 2 * rows_here + TILE_ROWS, LANES), bf16)
+        self.result = jax.ShapeDtypeStruct((pieces, 3 * rows_here + TILE_ROWS, LANES), bf16)
         self.square = jax.ShapeDtypeStruct((1, LANES), f32)
         self.result_work = pltpu.VMEM(self.result.shape, bf16)
         self.work = pltpu.VMEM((pairs, BOTH, 2 * LANES), f32)
@@ -443,25 +417,16 @@
 
     def products(self, signals, taps, after):
         return call(
-            functools.partial(products_kernel, self.signal.shape[1]), (self.result, self.split),
+            functools.partial(products_kernel, self.signal.shape[1]), (self.result, self.square),
             [pltpu.VMEM(signals.shape, bf16), self.twist_work, self.matrix_work]
             + [pltpu.VMEM((2, signals.shape[0], TILE_ROWS, LANES), bf16), self.result_work]
             + [self.split_work] * 3
             + [self.work] * 4
-            + [pltpu.SemaphoreType.DMA((6 * CUTS + self.split.shape[0],))],
+            + [pltpu.SemaphoreType.DMA((7 * CUTS,))],
             signals, taps, *self.tables, after,
             vmem_bytes=MOST_VMEM_BYTES,
             in_specs=[ANYWHERE, IN_VMEM, IN_SMEM, IN_VMEM, ANYWHERE, ANYWHERE],
-            out_specs=(ANYWHERE, ANYWHERE),
-        )
-
-    def lag(self, lag_split):
-        return call(
-            lag_kernel, (self.signal, self.square),
-            [self.twist_work, self.matrix_work, self.split_work, self.work, pltpu.SemaphoreType.DMA((2,))],
-            lag_split, *self.tables,
-            in_specs=[ANYWHERE, IN_SMEM, IN_VMEM, ANYWHERE],
-            out_specs=(IN_VMEM, IN_VMEM),
+            out_specs=(ANYWHERE, IN_VMEM),
         )
 
 
@@ -518,10 +483,11 @@
         corr = self.back(
             taps_spec[0] * cotan[0] + taps_spec[1] * cotan[1], taps_spec[0] * cotan[1] - taps_spec[1] * cotan[0]
         ).astype(bf16)
-        lag = (
-            product[0] * cotan[0] + product[1] * cotan[1],
-            product[0] * cotan[1] - product[1] * cotan[0],
+        lag = self.back(
+            product[0] * cotan[0] + product[1] * cotan[1], product[0] * cotan[1] - product[1] * cotan[0]
         )
+        squares = jnp.sum(lag * lag, axis=(0, 1))
+        squares = jnp.zeros((1, LANES), f32).at[0, : squares.shape[0]].set(squares)
         backs = first_backs(
             ahead, rows, taps, skip,
             [conv[:, row : row + 1].astype(f32) for row in range(count)],
@@ -530,12 +496,7 @@
         behind = [jnp.concatenate([row[1:], jnp.zeros_like(row[:1])], axis=0) for row in backs]
         edge = jnp.concatenate(ahead[: 3 * count] + behind, axis=1).astype(bf16)
         edge = jnp.pad(edge, ((0, 0), (0, TILE_ROWS - edge.shape[1]), (0, 0)))
-        return jnp.concatenate([conv, corr, edge], axis=1), lag
-
-    def lag(self, lag_spec):
-        lag = self.back(*lag_spec)
-        squares = jnp.sum(lag * lag, axis=(0, 1))
-        return lag.astype(bf16), jnp.zeros((1, LANES), f32).at[0, : squares.shape[0]].set(squares)
+        return jnp.concatenate([conv, corr, lag.astype(bf16), edge], axis=1), squares
 
 
 def group(idx):
@@ -604,9 +565,9 @@
     return place
 
 
-def cut_groups(per_step):
+def cut_groups(per_step, first_row, rows):
     def place(step):
-        return (pl.ds(step * per_step, per_step),)
+        return (pl.ds(step * per_step, per_step), pl.ds(first_row, rows))
 
     return place
 
@@ -668,7 +629,7 @@
 
 
 def finish_work(idx, operands, results, exts):
-    q_ref, k_ref, v_ref, grad_ref, short_ref, taps_ref, skip_ref, long_ref, squares_ref = operands
+    q_ref, k_ref, v_ref, grad_ref, short_ref, taps_ref, skip_ref, long_ref, edge_ref, squares_ref = operands
     mixed_ref, grad_q_ref, grad_k_ref, grad_v_ref, sums_ref = results
     lanes = group(idx)
     taps = taps_ref[:, lanes]
@@ -677,7 +638,7 @@
     halo_rows = taps_count - 1
     rows_here = q_ref.shape[0]
     sums = [jnp.zeros((8, LANES), f32) for _ in range(taps_count + 1)]
-    edge = long_ref[idx, 2 * rows_here :, :].astype(f32)
+    edge = edge_ref[idx, 3 * rows_here :, :].astype(f32)
     for place, ext in enumerate(exts):
         at = (3 + place) * halo_rows
         ext[rows_here : rows_here + halo_rows, :] = edge[at : at + halo_rows]
@@ -834,7 +795,7 @@
     (signals,) = stream(
         signals_work,
         operands=[(x, lanes2) for x in (q_in, k_in, v_in, grad_out, kernel, short_filter)],
-        results=[(sent, cut_groups(per_step))],
+        results=[(sent, cut_groups(per_step, 0, sent.shape[1]))],
         scratch=exts,
         vmem_bytes=MOST_VMEM_BYTES,
     )
@@ -848,19 +809,20 @@
     )
     taps_and_skip = jnp.concatenate([short_filter, skip_row], axis=0)
     taps_here = lax.dynamic_slice_in_dim(taps_and_skip, lax.axis_index("ctx") * share, share, axis=1)
-    long_here, lag_spec = transforms.products(signals_here, taps_here, short)
+    long_here, lag_squares = transforms.products(signals_here, taps_here, short)
     long = to_groups(exchange(long_here))
-    lag_here, lag_squares = transforms.lag(lag_spec)
-    lag = to_groups(exchange(lag_here))
+    lag = long[:, 2 * rows_here : 3 * rows_here]
 
     mixed, grad_q, grad_k, grad_v, sums = stream(
         finish_work,
         operands=[(x, lanes2) for x in (q_in, k_in, v_in, grad_out)]
         + [(short, lanes3), (short_filter, lanes2), (skip_row, lanes2)]
-        + [(long, cut_groups(per_step)), (lag_squares, cut_none)],
+        + [(long, cut_groups(per_step, 0, 2 * rows_here)), (long, cut_groups(per_step, 3 * rows_here, TILE_ROWS))]
+        + [(lag_squares, cut_none)],
         results=[(flat, lanes2)] * 4,
         scratch=exts,
         kept=[jax.ShapeDtypeStruct((taps_count + 1, channels + LANES), f32)],
+        vmem_bytes=MOST_VMEM_BYTES,
     )
 
     total_shape = jax.ShapeDtypeStruct(sums.shape, f32)

time: 120 us -> 129 us (1.075)
  blocking collectives: 0 us -> 49.3 us
  waiting for transfers between devices: 56 us -> 34 us
  starting transfers between devices: 33.7 us -> 17.1 us
  Pallas kernels: 27.4 us -> 24.7 us
    all_to_all x0 -> x1, blocking collectives: none -> 49.3 us  [exchange(): lax.all_to_all(pieces_first, 'ctx', split_axis=0, concat_axis=0, tiled=True)]
    all_to_all x3 -> x1, waiting for transfers between devices: 48.7 us -> 29.1 us  [exchange(): lax.all_to_all(pieces_first, 'ctx', split_axis=0, concat_axis=0, tiled=True)]
    all_to_all x3 -> x1, starting transfers between devices: 24 us -> 7.41 us  [exchange(): lax.all_to_all(pieces_first, 'ctx', split_axis=0, concat_axis=0, tiled=True)]
    pallas_call x10 -> x9, Pallas kernels: 27.4 us -> 24.7 us  [call(): pl.pallas_call(kernel, out_shape=outs, scratch_shapes=scratch, compiler_p...]
    ppermute x3, waiting for transfers between devices: 4.13 us -> 2.51 us  [halved_partners(): lax.ppermute(value, axis, [(i, i ^ 2 * (idx + 3 * (i % 2))) for i in rang...]
  transfers between devices with their start and end apart: 10 -> 8, of which waited for: 8 -> 6; matrix products, arithmetic and copies ran while one was open for 1% -> 1% of each run, Pallas kernels for 11% -> 3%
where the time goes in v16:
time: 129 us; the launch traced here: 128 us
  blocking collectives  49.3 us (38%)
  waiting for transfers between devices  34 us (26%)
  Pallas kernels  24.7 us (19%)
  starting transfers between devices  17.1 us (13%)
  local copies, waits for them, and re-layouts  1.85 us (1%)
    all_to_all x1, blocking collectives, exchange(): lax.all_to_all(pieces_first, 'ctx', split_axis=0, concat_axis=0, tiled=True)  49.3 us
    all_to_all x1, waiting for transfers between devices, exchange(): lax.all_to_all(pieces_first, 'ctx', split_axis=0, concat_axis=0, tiled=True)  29.1 us
    pallas_call x9, Pallas kernels, call(): pl.pallas_call(kernel, out_shape=outs, scratch_shapes=scratch, compiler_p...  24.7 us
    all_to_all x1, starting transfers between devices, exchange(): lax.all_to_all(pieces_first, 'ctx', split_axis=0, concat_axis=0, tiled=True)  7.41 us
    ppermute x3, starting transfers between devices, partners(): lax.ppermute(value, axis, [(i, i ^ step) for i in range(size)])  5.45 us
    ppermute x3, starting transfers between devices, halved_partners(): lax.ppermute(value, axis, [(i, i ^ 2 * (idx + 3 * (i % 2))) for i in rang...  3.55 us
  transfers between devices with their start and end apart: 8, of which 6 were waited for; matrix products, arithmetic and copies ran while one was open for 1% of the time, Pallas kernels for 3%

profile of v16, /device:TPU:0, one launch (start us, length us, event | category | flops | bytes accessed | tf_op | source)
XLA Modules:
  0.0 128.2 jit_solution(16989009484710839261)
XLA Ops:
  0.6 3.6 %shard_map.153.refs_4_ = bf16[16,400,128]{2,1,0:T(8,128)(2,1)} custom-call(bf16[128,2048]{1,0:T(8,128)(2,1)} %refs_0_.5, bf16[128,2048]{1,0:T(8,128)(2,1)} %refs_1_.5, bf16[128,2048]{1,0:T(8,128)(2,1)} %refs_2_.5, bf16[128,2048]{1,0:T(8,128)(2,1)} %refs_3_.5, f32[128,2048]{1,0:T(8,128)} %refs_4_.1, f32[3,2048]{1,0:T(4,128)} %refs_5_.3), custom_call_target="tpu_custom_call" | custom-call | tf_op jit(solution)/shard_map/pallas_call | solution.py:36
  4.2 7.4 %all-to-all-start = ((bf16[16,400,128]{2,1,0:T(8,128)(2,1)}), bf16[16,400,128]{2,1,0:T(8,128)(2,1)}, u32[]{:S(2)}, u32[]{:S(2)}) async-start(bf16[16,400,128]{2,1,0:T(8,128)(2,1)} %shard_map.153.refs_4_), calls=%async_computation | async-start | bytes 3276800 | tf_op jit(solution)/shard_map/all_to_all | solution.py:724
  11.7 0.0 copy-start.1
  11.7 0.0 copy-start.2
  11.7 3.3 %shard_map.154.after_ref.refs_4_ = f32[3,128,2048]{2,1,0:T(8,128)} custom-call(bf16[128,2048]{1,0:T(8,128)(2,1)} %refs_0_.5, bf16[128,2048]{1,0:T(8,128)(2,1)} %refs_1_.5, bf16[128,2048]{1,0:T(8,128)(2,1)} %refs_2_.5, f32[3,2048]{1,0:T(4,128)} %refs_5_.3, bf16[16,400,128]{2,1,0:T(8,128)(2,1)} %shard_map.153.refs_4_), custom_call_target="tpu_custom_call" | custom-call | tf_op jit(solution)/shard_map/pallas_call | solution.py:36
  15.0 0.0 copy-done.1
  15.0 0.0 copy-done.2
  15.1 0.7 fusion.taps_ref
  15.7 29.1 %all-to-all-done.signals_hbm = bf16[16,400,128]{2,1,0:T(8,128)(2,1)} async-done(((bf16[16,400,128]{2,1,0:T(8,128)(2,1)}), bf16[16,400,128]{2,1,0:T(8,128)(2,1)}, u32[]{:S(2)}, u32[]{:S(2)}) %all-to-all-start) | async-done | bytes 1638432 | tf_op jit(solution)/shard_map/all_to_all | solution.py:724
  44.8 11.0 %shard_map.155 = (bf16[16,400,128]{2,1,0:T(8,128)(2,1)}, f32[1,128]{1,0:T(1,128)}) custom-call(bf16[16,400,128]{2,1,0:T(8,128)(2,1)} %all-to-all-done.signals_hbm, f32[4,128]{1,0:T(4,128)} %fusion.taps_ref, f32[16,16]{1,0:T(8,128)} %constant.30.clone.coarse_ref, f32[2,8,16,128]{3,2,1,0:T(8,128)} %constant.31.clone.fine_ref, ...), custom_call_target="tpu_custom_call" | custom-call | tf_op jit(solution)/shard_map/pallas_call | solution.py:36
  55.8 49.3 %all_to_all.10.refs_7_.refs_8_ = bf16[16,400,128]{2,1,0:T(8,128)(2,1)} all-to-all(bf16[16,400,128]{2,1,0:T(8,128)(2,1)} %get-tuple-element.19), channel_id=1, replica_groups=mesh['ctx'=16,'ch'=2] {'ctx'}, dimensions={0} | all-to-all | bytes 3276800 | tf_op jit(solution)/shard_map/all_to_all | solution.py:724
  105.1 5.5 %shard_map.156 = (bf16[128,2048]{1,0:T(8,128)(2,1)}, bf16[128,2048]{1,0:T(8,128)(2,1)}, bf16[128,2048]{1,0:T(8,128)(2,1)}, bf16[128,2048]{1,0:T(8,128)(2,1)}, f32[4,2176]{1,0:T(4,128)}) custom-call(bf16[128,2048]{1,0:T(8,128)(2,1)} %refs_0_.5, bf16[128,2048]{1,0:T(8,128)(2,1)} %refs_1_.5, bf16[128,2048]{1,0:T(8,128)(2,1)} %refs_2_.5, ...), custom_call_target="tpu_custom_call" | custom-call | tf_op jit(solution)/shard_map/pallas_call | solution.py:36
  110.6 0.2 collective-permute-start
  110.8 0.0 copy-start
  110.8 0.8 copy-done
  111.5 0.5 collective-permute-done.refs_1_
  112.1 0.7 collective-permute-start.4
  112.7 0.8 collective-permute-start.3
  113.5 1.4 %collective-permute-start.2 = (f32[4,2176]{1,0:T(4,128)S(1)}, f32[4,2176]{1,0:T(4,128)S(1)}, u32[]{:S(2)}, u32[]{:S(2)}) collective-permute-start(f32[4,2176]{1,0:T(4,128)S(1)} %shard_map.158.own_ref), channel_id=1, source_target_pairs={{0,8},{2,22},{4,12},{6,18},{8,0},{10,30},{12,4},{14,26},{16,24},{1... | collective-permute-start | bytes 104456 | tf_op jit(solution)/shard_map/ppermute | solution.py:762
  114.9 1.4 %collective-permute-start.1 = (f32[4,2176]{1,0:T(4,128)S(1)}, f32[4,2176]{1,0:T(4,128)S(1)}, u32[]{:S(2)}, u32[]{:S(2)}) collective-permute-start(f32[4,2176]{1,0:T(4,128)S(1)} %shard_map.158.own_ref), channel_id=1, source_target_pairs={{0,4},{2,18},{4,0},{6,22},{8,12},{10,26},{12,8},{14,30},{16,20},{1... | collective-permute-start | bytes 104456 | tf_op jit(solution)/shard_map/ppermute | solution.py:762
  116.3 0.0 collective-permute-done.4.four_ref
  116.3 1.3 %collective-permute-done.3.three_ref = f32[4,2176]{1,0:T(4,128)S(1)} collective-permute-done((f32[4,2176]{1,0:T(4,128)S(1)}, f32[4,2176]{1,0:T(4,128)S(1)}, u32[]{:S(2)}, u32[]{:S(2)}) %collective-permute-start.3) | collective-permute-done | bytes 34848 | tf_op jit(solution)/shard_map/ppermute | solution.py:762
  117.6 0.0 collective-permute-done.2.two_ref
  117.6 1.2 collective-permute-done.1.one_ref
  118.8 3.7 %collective-permute-start.5 = (f32[4,2176]{1,0:T(4,128)S(1)}, f32[4,2176]{1,0:T(4,128)S(1)}, u32[]{:S(2)}, u32[]{:S(2)}) collective-permute-start(f32[4,2176]{1,0:T(4,128)S(1)} %shard_map.159.refs_0_), channel_id=1, source_target_pairs={{0,2},{2,0},{4,6},{6,4},{8,10},{10,8},{12,14},{14,12},{16,18},{18,... | collective-permute-start | bytes 104456 | tf_op jit(solution)/shard_map/ppermute | solution.py:746
  122.5 0.9 collective-permute-done.5.refs_1_
  123.4 0.1 shard_map.160
  123.5 1.6 %collective-permute-start.6 = (f32[1,128]{1,0:T(1,128)S(1)}, f32[1,128]{1,0:T(1,128)S(1)}, u32[]{:S(2)}, u32[]{:S(2)}) collective-permute-start(f32[1,128]{1,0:T(1,128)S(1)} %get-tuple-element.27), channel_id=1, source_target_pairs={{0,1},{1,0},{2,3},{3,2},{4,5},{5,4},{6,7},{7,6},{8,9},{9,8},{10,11... | collective-permute-start | bytes 1544 | tf_op jit(solution)/shard_map/ppermute | solution.py:746
  125.1 1.1 slice.4.lag_ref
  126.2 0.9 collective-permute-done.6
  127.1 1.1 shard_map.161
  (4 shorter events, 0.0 us)
Async XLA Ops:
  4.2 40.6 %all-to-all-start = ((bf16[16,400,128]{2,1,0:T(8,128)(2,1)}), bf16[16,400,128]{2,1,0:T(8,128)(2,1)}, u32[]{:S(2)}, u32[]{:S(2)}) async-start(bf16[16,400,128]{2,1,0:T(8,128)(2,1)} %shard_map.153.refs_4_), calls=%async_computation | async-start | bytes 3276800 | tf_op jit(solution)/shard_map/all_to_all | solution.py:724
  11.7 3.4 %copy-start.1 = (f32[3,2048]{1,0:T(4,128)S(1)}, f32[3,2048]{1,0:T(4,128)}, u32[]{:S(2)}) copy-start(f32[3,2048]{1,0:T(4,128)} %refs_5_.3) | copy-start | bytes 73732
  11.7 3.4 %copy-start.2 = (f32[2048]{0:T(1024)S(1)}, f32[2048]{0:T(1024)}, u32[]{:S(2)}) copy-start(f32[2048]{0:T(1024)} %param.16) | copy-start | bytes 24580
  110.6 1.5 %collective-permute-start = (f32[4,2176]{1,0:T(4,128)}, f32[4,2176]{1,0:T(4,128)S(1)}, u32[]{:S(2)}, u32[]{:S(2)}) collective-permute-start(f32[4,2176]{1,0:T(4,128)} %get-tuple-element.25.value_ref), channel_id=1, source_target_pairs={{0,2},{2,0},{4,6},{6,4},{8,10},{10,8},{12,14},{14,12},{16,18},{18,... | collective-permute-start | bytes 104456 | tf_op jit(solution)/shard_map/ppermute | solution.py:746
  110.8 0.8 copy-start
  112.1 4.2 %collective-permute-start.4 = (f32[4,2176]{1,0:T(4,128)S(1)}, f32[4,2176]{1,0:T(4,128)S(1)}, u32[]{:S(2)}, u32[]{:S(2)}) collective-permute-start(f32[4,2176]{1,0:T(4,128)S(1)} %shard_map.158.own_ref), channel_id=1, source_target_pairs={{2,30},{6,26},{10,22},{14,18},{18,14},{22,10},{26,6},{30,2},{3,31}... | collective-permute-start | bytes 104456 | tf_op jit(solution)/shard_map/ppermute | solution.py:763
  112.7 4.9 %collective-permute-start.3 = (f32[4,2176]{1,0:T(4,128)S(1)}, f32[4,2176]{1,0:T(4,128)S(1)}, u32[]{:S(2)}, u32[]{:S(2)}) collective-permute-start(f32[4,2176]{1,0:T(4,128)S(1)} %shard_map.158.own_ref), channel_id=1, source_target_pairs={{0,12},{2,26},{4,8},{6,30},{8,4},{10,18},{12,0},{14,22},{16,28},{1... | collective-permute-start | bytes 104456 | tf_op jit(solution)/shard_map/ppermute | solution.py:762
  113.5 4.1 %collective-permute-start.2 = (f32[4,2176]{1,0:T(4,128)S(1)}, f32[4,2176]{1,0:T(4,128)S(1)}, u32[]{:S(2)}, u32[]{:S(2)}) collective-permute-start(f32[4,2176]{1,0:T(4,128)S(1)} %shard_map.158.own_ref), channel_id=1, source_target_pairs={{0,8},{2,22},{4,12},{6,18},{8,0},{10,30},{12,4},{14,26},{16,24},{1... | collective-permute-start | bytes 104456 | tf_op jit(solution)/shard_map/ppermute | solution.py:762
  114.9 3.9 %collective-permute-start.1 = (f32[4,2176]{1,0:T(4,128)S(1)}, f32[4,2176]{1,0:T(4,128)S(1)}, u32[]{:S(2)}, u32[]{:S(2)}) collective-permute-start(f32[4,2176]{1,0:T(4,128)S(1)} %shard_map.158.own_ref), channel_id=1, source_target_pairs={{0,4},{2,18},{4,0},{6,22},{8,12},{10,26},{12,8},{14,30},{16,20},{1... | collective-permute-start | bytes 104456 | tf_op jit(solution)/shard_map/ppermute | solution.py:762
  118.8 4.5 %collective-permute-start.5 = (f32[4,2176]{1,0:T(4,128)S(1)}, f32[4,2176]{1,0:T(4,128)S(1)}, u32[]{:S(2)}, u32[]{:S(2)}) collective-permute-start(f32[4,2176]{1,0:T(4,128)S(1)} %shard_map.159.refs_0_), channel_id=1, source_target_pairs={{0,2},{2,0},{4,6},{6,4},{8,10},{10,8},{12,14},{14,12},{16,18},{18,... | collective-permute-start | bytes 104456 | tf_op jit(solution)/shard_map/ppermute | solution.py:746
  123.5 3.6 %collective-permute-start.6 = (f32[1,128]{1,0:T(1,128)S(1)}, f32[1,128]{1,0:T(1,128)S(1)}, u32[]{:S(2)}, u32[]{:S(2)}) collective-permute-start(f32[1,128]{1,0:T(1,128)S(1)} %get-tuple-element.27), channel_id=1, source_target_pairs={{0,1},{1,0},{2,3},{3,2},{4,5},{5,4},{6,7},{7,6},{8,9},{9,8},{10,11... | collective-permute-start | bytes 1544 | tf_op jit(solution)/shard_map/ppermute | solution.py:746

commit v17 on v14

--- a/solution.py
+++ b/solution.py
@@ -17,7 +17,7 @@
 CHUNKS = SPAN // CHUNK
 PAD = 8
 ROWS = 32
-CUTS = 4
+CUTS = 1
 PASSES = 1
 TILE_ROWS = 16
 VMEM_BYTES = 60 * 1024 * 1024
@@ -729,7 +729,7 @@
 def norm_kernel(*refs):
     values, totals_ref, square_ref = refs[:-2], refs[-2], refs[-1]
     channels = totals_ref.shape[1] - LANES
-    totals = add_up([value[...] for value in values])
+    totals = add_up([value[...] for value in values]) if len(values) > 1 else values[0][...]
     totals_ref[...] = totals
     square = jnp.sum(totals[:, :channels] * totals[:, :channels]) + jnp.sum(totals[0:1, channels:])
     square_ref[...] = jnp.full(square_ref.shape, square)
@@ -780,7 +780,12 @@
 
 
 def rounds_of(size):
-    return [(1 << bit,) for bit in range(size.bit_length() - 1)]
+    rounds = [(1,)] if size > 1 else []
+    step = 2
+    while step < size:
+        rounds.append((step, 2 * step, 3 * step) if size // step >= 4 else (step,))
+        step *= 4 if size // step >= 4 else 2
+    return rounds
 
 
 def add_up(values):
@@ -843,24 +848,26 @@
         kept=[jax.ShapeDtypeStruct((taps_count + 1, channels + LANES), f32)],
     )
 
-    totals = sums
-    rounds = rounds_of(pieces)
-    for idx, steps_of in enumerate(rounds[:-1]):
-        values = partners(totals, "ctx", steps_of)
+    total_shape = jax.ShapeDtypeStruct(sums.shape, f32)
+
+    def add(values):
+        return call(
+            add_kernel, total_shape, [], *values,
+            vmem_bytes=SMALL_VMEM_BYTES, in_specs=[IN_VMEM] * len(values), out_specs=IN_VMEM,
+        )
+
+    last = [sums]
+    for idx, steps_of in enumerate(rounds_of(pieces)):
+        last = partners(add(last) if idx else sums, "ctx", steps_of)
         if idx == 0:
-            values[0] = call(
-                same_kernel, jax.ShapeDtypeStruct(totals.shape, f32), [], totals,
+            last[0] = call(
+                same_kernel, total_shape, [], sums,
                 vmem_bytes=SMALL_VMEM_BYTES, in_specs=[IN_VMEM], out_specs=IN_VMEM,
             )
-        totals = call(
-            add_kernel, jax.ShapeDtypeStruct(totals.shape, f32), [], *values,
-            vmem_bytes=SMALL_VMEM_BYTES, in_specs=[IN_VMEM] * len(values), out_specs=IN_VMEM,
-        )
-    last = partners(totals, "ctx", rounds[-1])
 
     totals, norm_sq = call(
         norm_kernel,
-        (jax.ShapeDtypeStruct(totals.shape, f32), jax.ShapeDtypeStruct((1, LANES), f32)),
+        (total_shape, jax.ShapeDtypeStruct((1, LANES), f32)),
         [], *last,
         vmem_bytes=SMALL_VMEM_BYTES,
         in_specs=[IN_VMEM] * len(last), out_specs=(IN_VMEM, IN_VMEM),

time: 121 us -> 120 us (level)
  starting transfers between devices: 33.3 us -> 31.8 us
    ppermute x5 -> x6, starting transfers between devices: 9.27 us -> 7.85 us  [partners(): lax.ppermute(value, axis, [(i, i ^ step) for i in range(size)])]
    ppermute x5 -> x6, waiting for transfers between devices: 8.37 us -> 9.19 us  [partners(): lax.ppermute(value, axis, [(i, i ^ step) for i in range(size)])]
    pallas_call x11 -> x10, Pallas kernels: 27.6 us -> 27.4 us  [call(): pl.pallas_call(kernel, out_shape=outs, scratch_shapes=scratch, compiler_p...]
  transfers between devices with their start and end apart: 8 -> 9, of which waited for: 7 -> 8; matrix products, arithmetic and copies ran while one was open for 1% -> 1% of each run, Pallas kernels for 11% -> 11%
where the time goes in v17:
time: 120 us; the launch traced here: 119 us
  waiting for transfers between devices  57.9 us (48%)
  starting transfers between devices  31.8 us (26%)
  Pallas kernels  27.4 us (23%)
    all_to_all x3, waiting for transfers between devices, exchange(): lax.all_to_all(pieces_first, 'ctx', split_axis=0, concat_axis=0, tiled=True)  48.7 us
    pallas_call x10, Pallas kernels, call(): pl.pallas_call(kernel, out_shape=outs, scratch_shapes=scratch, compiler_p...  27.4 us
    all_to_all x3, starting transfers between devices, exchange(): lax.all_to_all(pieces_first, 'ctx', split_axis=0, concat_axis=0, tiled=True)  24 us
    ppermute x6, waiting for transfers between devices, partners(): lax.ppermute(value, axis, [(i, i ^ step) for i in range(size)])  9.19 us
    ppermute x6, starting transfers between devices, partners(): lax.ppermute(value, axis, [(i, i ^ step) for i in range(size)])  7.85 us
  transfers between devices with their start and end apart: 9, of which 8 were waited for; matrix products, arithmetic and copies ran while one was open for 1% of the time, Pallas kernels for 11%

profile of v17, /device:TPU:0, one launch (start us, length us, event | category | flops | bytes accessed | tf_op | source)
XLA Modules:
  0.0 119.4 jit_solution(10373787947803563309)
XLA Ops:
  0.6 3.6 %shard_map.153.refs_4_ = bf16[16,400,128]{2,1,0:T(8,128)(2,1)} custom-call(bf16[128,2048]{1,0:T(8,128)(2,1)} %refs_0_.5, bf16[128,2048]{1,0:T(8,128)(2,1)} %refs_1_.5, bf16[128,2048]{1,0:T(8,128)(2,1)} %refs_2_.5, bf16[128,2048]{1,0:T(8,128)(2,1)} %refs_3_.5, f32[128,2048]{1,0:T(8,128)} %refs_4_.1, f32[3,2048]{1,0:T(4,128)} %refs_5_.3), custom_call_target="tpu_custom_call" | custom-call | tf_op jit(solution)/shard_map/pallas_call | solution.py:36
  4.2 7.4 %all-to-all-start = ((bf16[16,400,128]{2,1,0:T(8,128)(2,1)}), bf16[16,400,128]{2,1,0:T(8,128)(2,1)}, u32[]{:S(2)}, u32[]{:S(2)}) async-start(bf16[16,400,128]{2,1,0:T(8,128)(2,1)} %shard_map.153.refs_4_), calls=%async_computation | async-start | bytes 3276800 | tf_op jit(solution)/shard_map/all_to_all | solution.py:757
  11.7 0.0 copy-start.2
  11.7 0.0 copy-start.3
  11.7 3.3 %shard_map.154.after_ref.refs_4_ = f32[3,128,2048]{2,1,0:T(8,128)} custom-call(bf16[128,2048]{1,0:T(8,128)(2,1)} %refs_0_.5, bf16[128,2048]{1,0:T(8,128)(2,1)} %refs_1_.5, bf16[128,2048]{1,0:T(8,128)(2,1)} %refs_2_.5, f32[3,2048]{1,0:T(4,128)} %refs_5_.3, bf16[16,400,128]{2,1,0:T(8,128)(2,1)} %shard_map.153.refs_4_), custom_call_target="tpu_custom_call" | custom-call | tf_op jit(solution)/shard_map/pallas_call | solution.py:36
  15.0 0.0 copy-done.2
  15.1 0.0 copy-done.3
  15.1 0.7 fusion.taps_ref
  15.7 29.1 %all-to-all-done.signals_hbm = bf16[16,400,128]{2,1,0:T(8,128)(2,1)} async-done(((bf16[16,400,128]{2,1,0:T(8,128)(2,1)}), bf16[16,400,128]{2,1,0:T(8,128)(2,1)}, u32[]{:S(2)}, u32[]{:S(2)}) %all-to-all-start) | async-done | bytes 1638432 | tf_op jit(solution)/shard_map/all_to_all | solution.py:757
  44.8 9.4 %shard_map.155 = (bf16[16,272,128]{2,1,0:T(8,128)(2,1)}, bf16[4,512,256]{2,1,0:T(8,128)(2,1)}) custom-call(bf16[16,400,128]{2,1,0:T(8,128)(2,1)} %all-to-all-done.signals_hbm, f32[4,128]{1,0:T(4,128)} %fusion.taps_ref, f32[16,16]{1,0:T(8,128)} %constant.18.clone.coarse_ref, f32[2,8,16,128]{3,2,1,0:T(8,128)} %constant.19.clone.fine_ref, ...), custom_call_target="tpu_custom_call" | custom-call | tf_op jit(solution)/shard_map/pallas_call | solution.py:36
  54.2 9.4 %all-to-all-start.1 = ((bf16[16,272,128]{2,1,0:T(8,128)(2,1)}), bf16[16,272,128]{2,1,0:T(8,128)(2,1)S(1)}, u32[]{:S(2)}, u32[]{:S(2)}) async-start(bf16[16,272,128]{2,1,0:T(8,128)(2,1)} %get-tuple-element.21), calls=%async_computation.1 | async-start | bytes 2228224 | tf_op jit(solution)/shard_map/all_to_all | solution.py:757
  63.6 4.4 %shard_map.156 = (bf16[16,128,128]{2,1,0:T(8,128)(2,1)}, f32[1,128]{1,0:T(1,128)}) custom-call(bf16[4,512,256]{2,1,0:T(8,128)(2,1)} %get-tuple-element.22.split_hbm, f32[16,16]{1,0:T(8,128)} %constant.18.clone.coarse_ref, f32[2,8,16,128]{3,2,1,0:T(8,128)} %constant.19.clone.fine_ref, bf16[512,512]{1,0:T(8,128)(2,1)} %constant.20.clone.matrix_hbm), custom_call_target="tpu_custom_call" | custom-call | tf_op jit(solution)/shard_map/pallas_call | solution.py:36
  68.0 19.6 %all-to-all-done.1.refs_7_ = bf16[16,272,128]{2,1,0:T(8,128)(2,1)S(1)} async-done(((bf16[16,272,128]{2,1,0:T(8,128)(2,1)}), bf16[16,272,128]{2,1,0:T(8,128)(2,1)S(1)}, u32[]{:S(2)}, u32[]{:S(2)}) %all-to-all-start.1) | async-done | bytes 1114144 | tf_op jit(solution)/shard_map/all_to_all | solution.py:757
  87.6 0.0 copy-start.1
  87.6 7.2 %all-to-all-start.2 = ((bf16[16,128,128]{2,1,0:T(8,128)(2,1)}), bf16[16,128,128]{2,1,0:T(8,128)(2,1)S(1)}, u32[]{:S(2)}, u32[]{:S(2)}) async-start(bf16[16,128,128]{2,1,0:T(8,128)(2,1)} %get-tuple-element.31), calls=%async_computation.2 | async-start | bytes 1048576 | tf_op jit(solution)/shard_map/all_to_all | solution.py:757
  94.8 0.0 copy-done.1
  94.9 5.4 %shard_map.157 = (bf16[128,2048]{1,0:T(8,128)(2,1)}, bf16[128,2048]{1,0:T(8,128)(2,1)}, bf16[128,2048]{1,0:T(8,128)(2,1)}, bf16[128,2048]{1,0:T(8,128)(2,1)}, f32[4,2176]{1,0:T(4,128)}) custom-call(bf16[128,2048]{1,0:T(8,128)(2,1)} %refs_0_.5, bf16[128,2048]{1,0:T(8,128)(2,1)} %refs_1_.5, bf16[128,2048]{1,0:T(8,128)(2,1)} %refs_2_.5, ...), custom_call_target="tpu_custom_call" | custom-call | tf_op jit(solution)/shard_map/pallas_call | solution.py:36
  100.3 0.5 collective-permute-start
  100.8 0.0 copy-start
  100.8 0.8 copy-done
  101.5 0.3 collective-permute-done.refs_1_
  101.9 2.8 %collective-permute-start.3 = (f32[4,2176]{1,0:T(4,128)S(1)}, f32[4,2176]{1,0:T(4,128)S(1)}, u32[]{:S(2)}, u32[]{:S(2)}) collective-permute-start(f32[4,2176]{1,0:T(4,128)S(1)} %shard_map.159.refs_0_), channel_id=1, source_target_pairs={{0,12},{2,14},{4,8},{6,10},{8,4},{10,6},{12,0},{14,2},{16,28},{18,... | collective-permute-start | bytes 104456 | tf_op jit(solution)/shard_map/ppermute | solution.py:779
  104.6 0.6 collective-permute-start.2
  105.2 0.2 collective-permute-start.1
  105.3 1.4 %collective-permute-done.3.refs_3_ = f32[4,2176]{1,0:T(4,128)S(1)} collective-permute-done((f32[4,2176]{1,0:T(4,128)S(1)}, f32[4,2176]{1,0:T(4,128)S(1)}, u32[]{:S(2)}, u32[]{:S(2)}) %collective-permute-start.3) | collective-permute-done | bytes 34848 | tf_op jit(solution)/shard_map/ppermute | solution.py:779
  106.7 2.4 %collective-permute-done.2.refs_2_ = f32[4,2176]{1,0:T(4,128)S(1)} collective-permute-done((f32[4,2176]{1,0:T(4,128)S(1)}, f32[4,2176]{1,0:T(4,128)S(1)}, u32[]{:S(2)}, u32[]{:S(2)}) %collective-permute-start.2) | collective-permute-done | bytes 34848 | tf_op jit(solution)/shard_map/ppermute | solution.py:779
  109.1 0.6 collective-permute-done.1.refs_1_
  109.6 2.3 %collective-permute-start.4 = (f32[4,2176]{1,0:T(4,128)S(1)}, f32[4,2176]{1,0:T(4,128)S(1)}, u32[]{:S(2)}, u32[]{:S(2)}) collective-permute-start(f32[4,2176]{1,0:T(4,128)S(1)} %shard_map.160.refs_0_), channel_id=1, source_target_pairs={{0,16},{2,18},{4,20},{6,22},{8,24},{10,26},{12,28},{14,30},{16,0},... | collective-permute-start | bytes 104456 | tf_op jit(solution)/shard_map/ppermute | solution.py:779
  111.9 2.6 %collective-permute-done.4.refs_1_ = f32[4,2176]{1,0:T(4,128)S(1)} collective-permute-done((f32[4,2176]{1,0:T(4,128)S(1)}, f32[4,2176]{1,0:T(4,128)S(1)}, u32[]{:S(2)}, u32[]{:S(2)}) %collective-permute-start.4) | collective-permute-done | bytes 34848 | tf_op jit(solution)/shard_map/ppermute | solution.py:779
  114.5 0.1 shard_map.161
  114.7 1.6 %collective-permute-start.5 = (f32[1,128]{1,0:T(1,128)S(1)}, f32[1,128]{1,0:T(1,128)S(1)}, u32[]{:S(2)}, u32[]{:S(2)}) collective-permute-start(f32[1,128]{1,0:T(1,128)S(1)} %get-tuple-element.30), channel_id=1, source_target_pairs={{0,1},{1,0},{2,3},{3,2},{4,5},{5,4},{6,7},{7,6},{8,9},{9,8},{10,11... | collective-permute-start | bytes 1544 | tf_op jit(solution)/shard_map/ppermute | solution.py:779
  116.3 2.0 %collective-permute-done.5 = f32[1,128]{1,0:T(1,128)S(1)} collective-permute-done((f32[1,128]{1,0:T(1,128)S(1)}, f32[1,128]{1,0:T(1,128)S(1)}, u32[]{:S(2)}, u32[]{:S(2)}) %collective-permute-start.5) | collective-permute-done | bytes 544 | tf_op jit(solution)/shard_map/ppermute | solution.py:779
  118.3 0.0 all-to-all-done.2.lag_ref
  118.3 1.1 shard_map.162
  (4 shorter events, 0.0 us)
Async XLA Ops:
  4.2 40.6 %all-to-all-start = ((bf16[16,400,128]{2,1,0:T(8,128)(2,1)}), bf16[16,400,128]{2,1,0:T(8,128)(2,1)}, u32[]{:S(2)}, u32[]{:S(2)}) async-start(bf16[16,400,128]{2,1,0:T(8,128)(2,1)} %shard_map.153.refs_4_), calls=%async_computation | async-start | bytes 3276800 | tf_op jit(solution)/shard_map/all_to_all | solution.py:757
  11.7 3.4 %copy-start.2 = (f32[3,2048]{1,0:T(4,128)S(1)}, f32[3,2048]{1,0:T(4,128)}, u32[]{:S(2)}) copy-start(f32[3,2048]{1,0:T(4,128)} %refs_5_.3) | copy-start | bytes 73732
  11.7 3.4 %copy-start.3 = (f32[2048]{0:T(1024)S(1)}, f32[2048]{0:T(1024)}, u32[]{:S(2)}) copy-start(f32[2048]{0:T(1024)} %param.16) | copy-start | bytes 24580
  54.2 33.4 %all-to-all-start.1 = ((bf16[16,272,128]{2,1,0:T(8,128)(2,1)}), bf16[16,272,128]{2,1,0:T(8,128)(2,1)S(1)}, u32[]{:S(2)}, u32[]{:S(2)}) async-start(bf16[16,272,128]{2,1,0:T(8,128)(2,1)} %get-tuple-element.21), calls=%async_computation.1 | async-start | bytes 2228224 | tf_op jit(solution)/shard_map/all_to_all | solution.py:757
  87.6 7.2 %copy-start.1 = (bf16[16,272,128]{2,1,0:T(8,128)(2,1)}, bf16[16,272,128]{2,1,0:T(8,128)(2,1)S(1)}, u32[]{:S(2)}) copy-start(bf16[16,272,128]{2,1,0:T(8,128)(2,1)S(1)} %all-to-all-done.1.refs_7_) | copy-start | bytes 3342340
  87.6 30.7 %all-to-all-start.2 = ((bf16[16,128,128]{2,1,0:T(8,128)(2,1)}), bf16[16,128,128]{2,1,0:T(8,128)(2,1)S(1)}, u32[]{:S(2)}, u32[]{:S(2)}) async-start(bf16[16,128,128]{2,1,0:T(8,128)(2,1)} %get-tuple-element.31), calls=%async_computation.2 | async-start | bytes 1048576 | tf_op jit(solution)/shard_map/all_to_all | solution.py:757
  100.3 1.5 %collective-permute-start = (f32[4,2176]{1,0:T(4,128)}, f32[4,2176]{1,0:T(4,128)S(1)}, u32[]{:S(2)}, u32[]{:S(2)}) collective-permute-start(f32[4,2176]{1,0:T(4,128)} %get-tuple-element.28.value_ref), channel_id=1, source_target_pairs={{0,2},{2,0},{4,6},{6,4},{8,10},{10,8},{12,14},{14,12},{16,18},{18,... | collective-permute-start | bytes 104456 | tf_op jit(solution)/shard_map/ppermute | solution.py:779
  100.8 0.8 copy-start
  101.9 4.8 %collective-permute-start.3 = (f32[4,2176]{1,0:T(4,128)S(1)}, f32[4,2176]{1,0:T(4,128)S(1)}, u32[]{:S(2)}, u32[]{:S(2)}) collective-permute-start(f32[4,2176]{1,0:T(4,128)S(1)} %shard_map.159.refs_0_), channel_id=1, source_target_pairs={{0,12},{2,14},{4,8},{6,10},{8,4},{10,6},{12,0},{14,2},{16,28},{18,... | collective-permute-start | bytes 104456 | tf_op jit(solution)/shard_map/ppermute | solution.py:779
  104.6 4.5 %collective-permute-start.2 = (f32[4,2176]{1,0:T(4,128)S(1)}, f32[4,2176]{1,0:T(4,128)S(1)}, u32[]{:S(2)}, u32[]{:S(2)}) collective-permute-start(f32[4,2176]{1,0:T(4,128)S(1)} %shard_map.159.refs_0_), channel_id=1, source_target_pairs={{0,8},{2,10},{4,12},{6,14},{8,0},{10,2},{12,4},{14,6},{16,24},{18,... | collective-permute-start | bytes 104456 | tf_op jit(solution)/shard_map/ppermute | solution.py:779
  105.2 4.4 %collective-permute-start.1 = (f32[4,2176]{1,0:T(4,128)S(1)}, f32[4,2176]{1,0:T(4,128)S(1)}, u32[]{:S(2)}, u32[]{:S(2)}) collective-permute-start(f32[4,2176]{1,0:T(4,128)S(1)} %shard_map.159.refs_0_), channel_id=1, source_target_pairs={{0,4},{2,6},{4,0},{6,2},{8,12},{10,14},{12,8},{14,10},{16,20},{18,... | collective-permute-start | bytes 104456 | tf_op jit(solution)/shard_map/ppermute | solution.py:779
  109.6 4.9 %collective-permute-start.4 = (f32[4,2176]{1,0:T(4,128)S(1)}, f32[4,2176]{1,0:T(4,128)S(1)}, u32[]{:S(2)}, u32[]{:S(2)}) collective-permute-start(f32[4,2176]{1,0:T(4,128)S(1)} %shard_map.160.refs_0_), channel_id=1, source_target_pairs={{0,16},{2,18},{4,20},{6,22},{8,24},{10,26},{12,28},{14,30},{16,0},... | collective-permute-start | bytes 104456 | tf_op jit(solution)/shard_map/ppermute | solution.py:779
  114.7 3.6 %collective-permute-start.5 = (f32[1,128]{1,0:T(1,128)S(1)}, f32[1,128]{1,0:T(1,128)S(1)}, u32[]{:S(2)}, u32[]{:S(2)}) collective-permute-start(f32[1,128]{1,0:T(1,128)S(1)} %get-tuple-element.30), channel_id=1, source_target_pairs={{0,1},{1,0},{2,3},{3,2},{4,5},{5,4},{6,7},{7,6},{8,9},{9,8},{10,11... | collective-permute-start | bytes 1544 | tf_op jit(solution)/shard_map/ppermute | solution.py:779
